TPU v7x, 32 devices: a whole 2x2x4 slice. The times are simulated.
32 devices in a mesh: gx: 4 (over y, x), gy: 2 (over core), gz: 4 (over z).
Axes of the slice: x: 2, y: 2, z: 4, core: 2. Of those that a mesh axis runs over, the one named last changes fastest.
Arguments:
- activations: bfloat16 [64, 32, 16, 512], P(None, 'gx', 'gy', 'gz'), may hold values from -6 to 6
- preact: bfloat16 [64, 32, 16, 512], P(None, 'gx', 'gy', 'gz'), may hold values from -6 to 6
- upstream: bfloat16 [64, 32, 16, 512], P(None, 'gx', 'gy', 'gz'), may hold values from -6 to 6
- master: float32 [110592], P(('gx', 'gy', 'gz')), may hold values from -0.15625 to 0.15625
- first_moment: float32 [110592], P(('gx', 'gy', 'gz')), may hold values from -4 to 4
- second_moment: float32 [110592], P(('gx', 'gy', 'gz')), may hold values from 0.05 to 2
Outputs:
- grad_input: bfloat16 [64, 32, 16, 512], P(None, 'gx', 'gy', 'gz')
- weight_grad: float32 [110592], P(('gx', 'gy', 'gz'))
- new_master: float32 [110592], P(('gx', 'gy', 'gz'))
- new_first: float32 [110592], P(('gx', 'gy', 'gz'))
- new_second: float32 [110592], P(('gx', 'gy', 'gz'))
All inputs are finite; a program needn't handle non-finite values.
Results may differ from a plain program's by a relative error of at most 0.0049.
Values may be sent and summed in bfloat16 or wider, within the bound.
No kernel may reach another device: no remote copies, remote signals or barrier semaphores. Data moves between devices by JAX's collectives and lax.ppermute only.
A program may use at most 64 MiB of HBM per device.

v0:
```python
import functools
import math

import jax
import jax.numpy as jnp
from jax import lax
from jax.experimental import pallas as pl
from jax.experimental.pallas import tpu as pltpu
from jax.sharding import PartitionSpec as P

AXES = ("gx", "gy", "gz")
LANES = 128
VMEM = pl.BlockSpec(memory_space=pltpu.VMEM)
HBM = pl.BlockSpec(memory_space=pltpu.HBM)
F32 = jnp.float32
BF16 = jnp.bfloat16
ALL_VMEM = 64 * 2**20


def params(limit=24 * 2**20):
    return pltpu.CompilerParams(vmem_limit_bytes=limit)


def cost(flops, moved):
    return pl.CostEstimate(flops=flops, bytes_accessed=moved, transcendentals=0)


def to_planes(value, tile, write):
    channels, size_y, size_z = value.shape
    tile[...] = value.astype(F32).reshape(channels * size_y, size_z)
    for y in range(size_y):
        write(y, tile[pl.ds(y, channels, stride=size_y), :].astype(BF16))


def masked(p, u):
    return jnp.where(p > 0, u, jnp.zeros_like(u))


def face_kernel(p_ref, u_ref, low_ref, high_ref, p_buf, u_buf, tile, sems):
    size_x, size_z = p_ref.shape[1], p_ref.shape[3]
    copies = []
    for k, x in enumerate((0, size_x - 1)):
        pair = (
            pltpu.make_async_copy(p_ref.at[:, x], p_buf.at[k], sems.at[2 * k]),
            pltpu.make_async_copy(u_ref.at[:, x], u_buf.at[k], sems.at[2 * k + 1]),
        )
        for copy in pair:
            copy.start()
        copies.append(pair)
    for k, out_ref in enumerate((low_ref, high_ref)):
        for copy in copies[k]:
            copy.wait()

        def write(y, value):
            out_ref[:, y * size_z : (y + 1) * size_z] = value

        to_planes(masked(p_buf[k], u_buf[k]), tile.at[k], write)


def faces(preact, upstream):
    channels, size_x, size_y, size_z = preact.shape
    face = jax.ShapeDtypeStruct((channels, size_y * size_z), BF16)
    buffer = pltpu.VMEM((2, channels, size_y, size_z), BF16)
    return pl.pallas_call(
        face_kernel,
        in_specs=[HBM, HBM],
        out_specs=[VMEM] * 2,
        out_shape=[face, face],
        scratch_shapes=[
            buffer,
            buffer,
            pltpu.VMEM((2, channels * size_y, size_z), F32),
            pltpu.SemaphoreType.DMA((4,)),
        ],
        compiler_params=params(ALL_VMEM - 900_000),
        cost_estimate=cost(0, 2**20),
        name="faces",
    )(preact, upstream)


def inner_kernel(p_ref, u_ref, a_ref, m_ref, g_ref, x_ref, sent_ref, p_buf, u_buf, a_buf, tile, sems):
    channels, size_x, size_y, size_z = a_ref.shape
    inner = size_x - 2
    copies = []
    for x in range(inner):
        copies.append(
            (
                pltpu.make_async_copy(p_ref.at[:, x + 1], p_buf.at[x], sems.at[x]),
                pltpu.make_async_copy(u_ref.at[:, x + 1], u_buf.at[x], sems.at[inner + x]),
            )
        )
    for x in range(size_x):
        copies.append(
            (pltpu.make_async_copy(a_ref.at[:, x], a_buf.at[x], sems.at[2 * inner + x]),)
        )
    for group in copies:
        for copy in group:
            copy.start()
    share = m_ref[...]
    count, height, width = sent_ref.shape
    if height > share.shape[0]:
        share = jnp.concatenate([share, jnp.zeros((height - share.shape[0], width), F32)], axis=0)
    sent_ref[...] = jnp.broadcast_to(share.astype(BF16)[None], sent_ref.shape)
    for x in range(inner):
        for copy in copies[x]:
            copy.wait()

        def write(y, value):
            g_ref[x, :, y * size_z : (y + 1) * size_z] = value

        to_planes(masked(p_buf[x], u_buf[x]), tile.at[x % 2], write)
    for x in range(size_x):
        copies[inner + x][0].wait()

        def write(y, value):
            x_ref[x, :, y * size_z : (y + 1) * size_z] = value

        to_planes(a_buf[x], tile.at[x % 2], write)


def inner_planes(preact, upstream, activations, share, sent_shape):
    channels, size_x, size_y, size_z = preact.shape
    plane = size_y * size_z
    return pl.pallas_call(
        inner_kernel,
        in_specs=[HBM] * 3 + [VMEM],
        out_specs=[VMEM] * 3,
        out_shape=[
            jax.ShapeDtypeStruct((size_x - 2, channels, plane), BF16),
            jax.ShapeDtypeStruct((size_x, channels, plane), BF16),
            jax.ShapeDtypeStruct(sent_shape, BF16),
        ],
        scratch_shapes=[
            pltpu.VMEM((size_x - 2, channels, size_y, size_z), BF16),
            pltpu.VMEM((size_x - 2, channels, size_y, size_z), BF16),
            pltpu.VMEM((size_x, channels, size_y, size_z), BF16),
            pltpu.VMEM((2, channels * size_y, size_z), F32),
            pltpu.SemaphoreType.DMA((3 * size_x - 4,)),
        ],
        compiler_params=params(ALL_VMEM - 3_600_000),
        cost_estimate=cost(0, 6 * 2**20),
        name="inner",
    )(preact, upstream, activations, share)


def body_of(refs, index):
    planes = refs[2].shape[0] + 4
    if 2 <= index < planes - 2:
        return refs[2].at[index - 2]
    return refs[{0: 0, 1: 1, planes - 2: 3, planes - 1: 4}[index]]


def y_halo(refs, index):
    me = lax.axis_index("gy")
    low = jnp.where(me > 0, refs[0][index].astype(F32), 0.0)
    high = jnp.where(me < lax.axis_size("gy") - 1, refs[1][index].astype(F32), 0.0)
    return low, high


def z_picker(rows_y, size_z):
    shape = (rows_y * size_z, 2 * LANES)
    voxel = lax.broadcasted_iota(jnp.int32, shape, 0)
    lane = lax.broadcasted_iota(jnp.int32, shape, 1)
    wanted = jnp.where(lane < LANES, lane * size_z, (lane - LANES) * size_z + size_z - 1)
    return (voxel == wanted).astype(F32).astype(BF16)


def z_tiles(planes, rows_y, size_z):
    channels = planes[0].shape[0]
    columns = jnp.dot(
        jnp.concatenate(planes, axis=0), z_picker(rows_y, size_z), preferred_element_type=F32
    )
    low = jnp.zeros((channels, LANES), F32)
    high = jnp.zeros((channels, LANES), F32)
    for index in range(len(planes)):
        rows = columns[index * channels : (index + 1) * channels]
        low = low + pltpu.roll(rows[:, :LANES], index * rows_y, 1)
        high = high + pltpu.roll(rows[:, LANES:], index * rows_y, 1)
    return low, high


def put_columns(columns, row_of, rows_y, size_z):
    shape = (2 * LANES, rows_y * size_z)
    source = lax.broadcasted_iota(jnp.int32, shape, 0)
    voxel = lax.broadcasted_iota(jnp.int32, shape, 1)
    number = source % LANES
    place = row_of(number) * size_z + jnp.where(source < LANES, 0, size_z - 1)
    place = jnp.where(number < rows_y, place, -1)
    put = (voxel == place).astype(F32).astype(BF16)
    rows = [jnp.concatenate(pair, axis=1) for pair in columns]
    return jnp.dot(
        jnp.concatenate(rows, axis=0).astype(BF16), put, preferred_element_type=F32
    )


def z_halo(low_ref, high_ref, planes, rows_y, size_z):
    columns = []
    for index in range(planes):
        shift = -index * rows_y % LANES
        columns.append(
            [pltpu.roll(ref[...].astype(F32), shift, 1) for ref in (low_ref, high_ref)]
        )
    return put_columns(columns, lambda number: number, rows_y, size_z)


def pair_z_halo(low_ref, high_ref, planes, size_y, size_z):
    me = lax.axis_index("gy")
    sides = []
    for ref in (low_ref, high_ref):
        first, second = ref[0].astype(F32), ref[1].astype(F32)
        lane = lax.broadcasted_iota(jnp.int32, first.shape, 1)
        own = jnp.where(me == 0, first, second)
        before = jnp.where(me == 0, 0.0, first)
        after = jnp.where(me == 0, second, 0.0)
        columns = []
        for index in range(planes):
            start = index * size_y
            columns.append(
                jnp.where(
                    lane < size_y,
                    pltpu.roll(own, -start % LANES, 1),
                    jnp.where(
                        lane == size_y,
                        pltpu.roll(before, (1 - start) % LANES, 1),
                        pltpu.roll(after, (size_y + 1 - start) % LANES, 1),
                    ),
                )
            )
        sides.append(columns)

    def row_of(number):
        return jnp.where(number < size_y, number + 1, jnp.where(number == size_y, 0, size_y + 1))

    return put_columns(list(zip(*sides)), row_of, size_y + 2, size_z)


def shifted_plane(index, refs, halo, g3):
    channels, plane = refs[0].shape
    size_z = refs[5].shape[-1]
    rows_y = plane // size_z + 2
    base = 3 * channels * index
    lane = lax.broadcasted_iota(jnp.int32, (channels, size_z), 1)
    low, high = y_halo(refs[5:7], index)
    body = body_of(refs[:5], index)
    for row in range(rows_y):
        cols = slice(row * size_z, (row + 1) * size_z)
        if row == 0:
            wide = low
        elif row == rows_y - 1:
            wide = high
        else:
            wide = body[:, (row - 1) * size_z : row * size_z].astype(F32)
        edge = 0.0 if halo is None else halo[index * channels : (index + 1) * channels, cols]
        before = jnp.where(lane == 0, edge, pltpu.roll(wide, 1, 1))
        after = jnp.where(lane == size_z - 1, edge, pltpu.roll(wide, size_z - 1, 1))
        g3[base : base + channels, cols] = before.astype(BF16)
        g3[base + channels : base + 2 * channels, cols] = wide.astype(BF16)
        g3[base + 2 * channels : base + 3 * channels, cols] = after.astype(BF16)


def weight_products(refs, halo, x_ref, g3, x3, acc):
    size_x, channels, plane = x_ref.shape
    size_z = refs[5].shape[-1]
    group = 3 * channels
    zero = jnp.zeros((channels, 2 * size_z), BF16)
    done = 0
    for x in range(size_x):
        while done < x + 3:
            shifted_plane(done, refs, halo, g3)
            done += 1
        value = x_ref[x]
        for b in range(3):
            at = slice(b * channels, (b + 1) * channels)
            start = (2 - b) * size_z
            x3[x, at, start : start + plane] = value
            if start:
                x3[x, at, :start] = zero[:, :start]
            if start < 2 * size_z:
                x3[x, at, start + plane :] = zero[:, start:]
        product = lax.dot_general(
            g3[x * group : (x + 3) * group, :],
            x3[x],
            (((1,), (1,)), ((), ())),
            preferred_element_type=F32,
        )
        if x == 0:
            acc[...] = product
        else:
            acc[...] += product


def to_flat(value, count, channels, flat):
    height, width = value.shape
    wide = jnp.concatenate([value, jnp.zeros((-height % LANES, width), F32)], axis=0)
    wide = jnp.concatenate([wide, jnp.zeros((wide.shape[0], -width % LANES), F32)], axis=1)
    turned = wide.T
    for b in range(3):
        rows = turned[b * channels : (b + 1) * channels]
        for block in range(9):
            start = block * count
            cell = rows[:, start // LANES * LANES : (start // LANES + 1) * LANES]
            tap = (2 - block // 3) * 9 + b * 3 + 2 - block % 3
            shift = -start % LANES
            flat[pl.ds(tap, channels, stride=27), :] = pltpu.roll(cell, shift, 1) if shift else cell
    return flat[...].T[:count]


def spread_weights(whole, turned, weights):
    channels, taps = whole.shape
    group = 3 * channels
    whole = jnp.concatenate([whole, jnp.zeros((LANES - channels, taps), F32)], axis=0)
    whole = jnp.concatenate([whole, jnp.zeros((LANES, -taps % LANES), F32)], axis=1)
    turned[...] = whole.T
    for b in range(3):
        blocks = []
        for a in range(3):
            for c in range(3):
                tap = (2 - a) * 9 + (2 - b) * 3 + 2 - c
                blocks.append(turned[pl.ds(tap, channels, stride=27), :][:, :channels])
        zero = jnp.zeros((channels, group), F32)
        weights[b, :channels] = jnp.concatenate(blocks + [zero], axis=1).astype(BF16)
        weights[b, channels:] = jnp.concatenate([zero] + blocks, axis=1).astype(BF16)


def input_products(refs, halo, g3, weights, tile, out_ref):
    channels, size_x, size_y, size_z = out_ref.shape
    group = 3 * channels
    plane = size_y * size_z
    done = 0
    for pair in range(size_x // 2):
        while done < 2 * pair + 4:
            shifted_plane(done, refs, halo, g3)
            done += 1
        at = slice(2 * pair * group, (2 * pair + 4) * group)
        total = None
        for b in range(3):
            product = jnp.dot(
                weights[b],
                g3[at, b * size_z : b * size_z + plane],
                preferred_element_type=F32,
            )
            total = product if total is None else total + product
        for half in range(2):
            for y in range(size_y):
                tile[half, pl.ds(y, channels, stride=size_y), :] = total[
                    half * channels : (half + 1) * channels, y * size_z : (y + 1) * size_z
                ]
            out_ref[:, 2 * pair + half] = (
                tile[half].reshape(channels, size_y, size_z).astype(BF16)
            )


def g3_scratch(channels, size_x, size_y, size_z):
    return pltpu.VMEM(((size_x + 2) * 3 * channels, (size_y + 2) * size_z), BF16)


def x3_scratch(channels, size_x, size_y, size_z):
    return pltpu.VMEM((size_x, 3 * channels, (size_y + 2) * size_z), BF16)


def acc_scratch(channels):
    return pltpu.VMEM((9 * channels, 3 * channels), F32)


def flat_scratch(channels):
    return pltpu.VMEM((-(-27 * channels // LANES) * LANES, LANES), F32)


def dgrad_scratch(channels, size_x, size_y, size_z):
    return [
        g3_scratch(channels, size_x, size_y, size_z),
        flat_scratch(channels),
        pltpu.VMEM((3, 2 * channels, 12 * channels), BF16),
        pltpu.VMEM((2, channels * size_y, size_z), F32),
    ]


def wgrad_cost(channels, size_x, size_y, size_z):
    return cost(54 * channels * channels * size_x * (size_y + 2) * size_z, 4 * 2**20)


def dgrad_cost(channels, size_x, size_y, size_z):
    return cost(72 * channels * channels * size_x * size_y * size_z, 4 * 2**20)


def side_kernel(*refs):
    sent_ref = refs[5]
    planes = refs[2].shape[0] + 4
    plane = refs[0].shape[-1]
    size_z = sent_ref.shape[-1]
    is_first = lax.axis_index("gy") == 0
    whole = []
    for index in range(planes):
        body = body_of(refs[:5], index)[...]
        whole.append(body)
        low, high = body[:, :size_z], body[:, plane - size_z :]
        picked = jnp.where(is_first, high.astype(F32), low.astype(F32))
        sent_ref[index] = picked.astype(BF16)
    low, high = z_tiles(whole, plane // size_z, size_z)
    sent_ref[planes] = low.astype(BF16)
    sent_ref[planes + 1] = high.astype(BF16)


def side(planes, size_z):
    inner, channels, _ = planes[2].shape
    return pl.pallas_call(
        side_kernel,
        in_specs=[VMEM] * 5,
        out_specs=VMEM,
        out_shape=jax.ShapeDtypeStruct((inner + 6, channels, size_z), BF16),
        compiler_params=params(),
        cost_estimate=cost(2**27, 2**21),
        name="side",
    )(*planes)


def join_kernel(own_ref, other_ref, low_ref, high_ref):
    at = own_ref.shape[0] - 2
    me = lax.axis_index("gy")
    for k, out_ref in enumerate((low_ref, high_ref)):
        out_ref[me] = own_ref[at + k]
        out_ref[1 - me] = other_ref[at + k]


def join(own, other):
    tiles = jax.ShapeDtypeStruct((2, *own.shape[1:]), BF16)
    return pl.pallas_call(
        join_kernel,
        in_specs=[VMEM] * 2,
        out_specs=[VMEM] * 2,
        out_shape=[tiles, tiles],
        compiler_params=params(),
        cost_estimate=cost(0, 2**17),
        name="join",
    )(own, other)


def pair_wgrad_kernel(span, *refs):
    x_ref, mine_ref, theirs_ref, g3, x3, acc = refs[7:]
    size_x, channels, plane = x_ref.shape
    size_z = refs[5].shape[-1]
    weight_products(refs, None, x_ref, g3, x3, acc)
    me = lax.axis_index("gy")
    rows = 9 * channels // 2
    width = 3 * channels
    spare = jnp.zeros((rows, mine_ref.shape[1] - width), F32)
    halves = []
    for half in range(2):
        at = range(half * span, 9 * channels, 2 * span)
        halves.append(jnp.concatenate([acc[start : start + span, :] for start in at], axis=0))
    low, high = z_tiles([x_ref[x] for x in range(size_x)], plane // size_z, size_z)
    for ref, own in ((mine_ref, True), (theirs_ref, False)):
        picked = jnp.where((me == 0) == own, halves[0], halves[1])
        ref[:rows, :] = jnp.concatenate([picked, spare], axis=1)
        ref[rows:, :LANES] = low
        ref[rows:, LANES:] = high


def pair_wgrad(sources, planes_x, shape, span):
    channels = shape[0]
    part = jax.ShapeDtypeStruct((9 * channels // 2 + channels, 2 * LANES), F32)
    return pl.pallas_call(
        functools.partial(pair_wgrad_kernel, span),
        in_specs=[VMEM] * 8,
        out_specs=[VMEM] * 2,
        out_shape=[part, part],
        scratch_shapes=[g3_scratch(*shape), x3_scratch(*shape), acc_scratch(channels)],
        compiler_params=params(32 * 2**20),
        cost_estimate=wgrad_cost(*shape),
        name="wgrad",
    )(*sources, planes_x)


def finish_kernel(scale, span, rows, sizes, *refs):
    mine_ref, other_ref, zlo_ref, zhi_ref, part_ref, flat, lines, chunks = refs
    size_x, size_y = sizes
    channels = zlo_ref.shape[1]
    count = channels // 2
    height = 9 * count
    area = size_x * size_y
    me = lax.axis_index("gy")
    total = (mine_ref[:height, :] + other_ref[:height, :])[:, : 3 * channels]
    own, other = mine_ref[height:, :], other_ref[height:, :]
    inputs = (jnp.where(me == 0, own, other), jnp.where(me == 0, other, own))
    lane = lax.broadcasted_iota(jnp.int32, (channels, LANES), 1)
    row = lane % size_y
    few = lax.broadcasted_iota(jnp.int32, (count, LANES), 1)
    edge = {}
    for side_z, tile_ref in ((0, zlo_ref), (2, zhi_ref)):
        cols = slice(0, LANES) if side_z == 0 else slice(LANES, 2 * LANES)
        value = jnp.where(
            lane < area, inputs[0][:, cols], pltpu.roll(inputs[1][:, cols], area, 1)
        )
        jump = area - size_y + 1
        below = jnp.where(lane >= area, pltpu.roll(value, jump, 1), 0.0)
        above = jnp.where(lane < area, pltpu.roll(value, LANES - jump, 1), 0.0)
        right = jnp.concatenate(
            [
                jnp.where(row > 0, pltpu.roll(value, 1, 1), below),
                value,
                jnp.where(row < size_y - 1, pltpu.roll(value, LANES - 1, 1), above),
            ],
            axis=0,
        )
        tiles = []
        for device in range(2):
            tile = tile_ref[device].astype(F32)
            halves = [
                jnp.concatenate(
                    [tile[at : at + span] for at in range(half * span, channels, 2 * span)], axis=0
                )
                for half in range(2)
            ]
            tiles.append(jnp.where(me == 0, halves[0], halves[1]))
        left = []
        for a in range(3):
            first = pltpu.roll(tiles[0], -a * size_y % LANES, 1)
            second = pltpu.roll(tiles[1], (area - a * size_y) % LANES, 1)
            left.append(jnp.where(few < area, first, jnp.where(few < 2 * area, second, 0.0)))
        edge[side_z] = lax.dot_general(
            jnp.concatenate(left, axis=0).astype(BF16),
            right.astype(BF16),
            (((1,), (1,)), ((), ())),
            preferred_element_type=F32,
        )
    blocks = []
    for a in range(3):
        for c in range(3):
            block = total[(3 * a + c) * count : (3 * a + c + 1) * count]
            blocks.append(block if c == 1 else block + edge[c][a * count : (a + 1) * count])
    taps = 27 * channels
    whole = to_flat(jnp.concatenate(blocks, axis=0) * scale, count, channels, flat)
    pieces = whole.shape[1] // LANES
    for k in range(pieces):
        lines[k * count : (k + 1) * count, :] = whole[:, k * LANES : (k + 1) * LANES]
    number, tall, width = part_ref.shape
    parts = []
    for r in range(rows):
        found = [lines[pl.ds(k * count + r, number, stride=rows), :] for k in range(pieces)]
        parts.append(jnp.concatenate(found, axis=1)[:, :taps])
    line = jnp.concatenate(parts, axis=1)
    chunks[...] = jnp.zeros_like(chunks)
    for k in range(line.shape[1] // width):
        chunks[pl.ds(k, number, stride=tall), :] = line[:, k * width : (k + 1) * width]
    part_ref[...] = chunks[...].reshape(part_ref.shape).astype(BF16)


def finish(mine, other, z_halos, scale, span, rows, sizes, part_shape):
    channels = z_halos[0].shape[1]
    return pl.pallas_call(
        functools.partial(finish_kernel, scale, span, rows, sizes),
        in_specs=[VMEM] * 4,
        out_specs=VMEM,
        out_shape=jax.ShapeDtypeStruct(part_shape, BF16),
        scratch_shapes=[
            flat_scratch(channels),
            pltpu.VMEM((-(-27 * channels // LANES) * channels // 2, LANES), F32),
            pltpu.VMEM((part_shape[0] * part_shape[1], part_shape[2]), F32),
        ],
        compiler_params=params(),
        cost_estimate=cost(2**24, 2**20),
        name="finish",
    )(mine, other, *z_halos)


def pair_dgrad_kernel(rows, *refs):
    w_ref, out_ref, g3, turned, weights, tile, chunks, lines = refs[9:]
    channels, size_x, size_y, size_z = out_ref.shape
    taps = 27 * channels
    count, height, width = w_ref.shape
    chunks[...] = w_ref[...].astype(F32).reshape(chunks.shape)
    line = jnp.concatenate(
        [chunks[pl.ds(k, count, stride=height), :] for k in range(rows * taps // width)], axis=1
    )
    pieces = lines.shape[0] // channels
    spare = jnp.zeros((count, pieces * LANES - taps), F32)
    for r in range(rows):
        found = jnp.concatenate([line[:, r * taps : (r + 1) * taps], spare], axis=1)
        for k in range(pieces):
            lines[pl.ds(k * channels + r, count, stride=rows), :] = found[
                :, k * LANES : (k + 1) * LANES
            ]
    whole = [lines[k * channels : (k + 1) * channels, :] for k in range(pieces)]
    spread_weights(jnp.concatenate(whole, axis=1)[:, :taps], turned, weights)
    halo = pair_z_halo(refs[7], refs[8], size_x + 2, size_y, size_z)
    input_products(refs, halo, g3, weights, tile, out_ref)


def pair_dgrad(sources, kernel, shape, rows):
    channels = shape[0]
    return pl.pallas_call(
        functools.partial(pair_dgrad_kernel, rows),
        in_specs=[VMEM] * 10,
        out_specs=VMEM,
        out_shape=jax.ShapeDtypeStruct(shape, BF16),
        scratch_shapes=dgrad_scratch(*shape)
        + [
            pltpu.VMEM((kernel.shape[0] * kernel.shape[1], kernel.shape[2]), F32),
            pltpu.VMEM((-(-27 * channels // LANES) * channels, LANES), F32),
        ],
        compiler_params=params(32 * 2**20),
        cost_estimate=dgrad_cost(*shape),
        name="dgrad",
    )(*sources, kernel)


def pair_gradients(activations, preact, upstream, master, scale):
    shape = activations.shape
    channels, size_x, size_y, size_z = shape
    devices = math.prod(lax.axis_size(a) for a in AXES)
    rows = channels // devices
    span = lax.axis_size("gz") * rows
    used = master.shape[0] // LANES
    tall = -(-used // 16) * 16
    first, last = faces(preact, upstream)
    x_halos = (shifted(last, {"gx": 1}), shifted(first, {"gx": -1}))
    inner, planes_x, sent = inner_planes(
        preact, upstream, activations, master.reshape(used, LANES), (devices, tall, LANES)
    )
    kernel = lax.all_to_all(sent, AXES, 0, 0, tiled=True)
    planes = (x_halos[0], first, inner, last, x_halos[1])
    own = side(planes, size_z)
    other = shifted(own, {"gy": "swap"})
    zlo, zhi = join(own, other)
    z_halos = (shifted(zhi, {"gz": 1}), shifted(zlo, {"gz": -1}))
    sources = (*planes, other, other)
    mine, theirs = pair_wgrad(sources, planes_x, shape, span)
    theirs = shifted(theirs, {"gy": "swap"})
    part = finish(
        mine,
        theirs,
        z_halos,
        scale,
        span,
        rows,
        (size_x, size_y),
        (devices // 2, tall, LANES),
    )
    part, kernel = lax.optimization_barrier((part, kernel))
    parts = lax.all_to_all(part, ("gx", "gz"), 0, 0, tiled=True)
    grad_input = pair_dgrad((*sources, *z_halos), kernel, shape, rows)
    return grad_input, parts


def yface_kernel(*refs):
    low_ref, high_ref = refs[5:]
    size_z = low_ref.shape[-1]
    for index in range(low_ref.shape[0]):
        body = body_of(refs[:5], index)
        plane = body.shape[-1]
        low_ref[index] = body[:, :size_z]
        high_ref[index] = body[:, plane - size_z :]


def y_faces(planes, size_z):
    inner, channels, _ = planes[2].shape
    face = jax.ShapeDtypeStruct((inner + 4, channels, size_z), BF16)
    return pl.pallas_call(
        yface_kernel,
        in_specs=[VMEM] * 5,
        out_specs=[VMEM] * 2,
        out_shape=[face] * 2,
        compiler_params=params(),
        cost_estimate=cost(0, 2**19),
        name="yfaces",
    )(*planes)


def zface_kernel(*refs):
    zlo_ref, zhi_ref = refs[7:]
    size_z = refs[5].shape[-1]
    whole = []
    for index in range(refs[5].shape[0]):
        low, high = y_halo(refs[5:7], index)
        body = body_of(refs[:5], index)[...]
        whole.append(jnp.concatenate([low.astype(BF16), body, high.astype(BF16)], axis=1))
    low, high = z_tiles(whole, whole[0].shape[1] // size_z, size_z)
    zlo_ref[...] = low.astype(BF16)
    zhi_ref[...] = high.astype(BF16)


def z_faces(planes, y_halos):
    face = jax.ShapeDtypeStruct((planes[0].shape[0], LANES), BF16)
    return pl.pallas_call(
        zface_kernel,
        in_specs=[VMEM] * 7,
        out_specs=[VMEM] * 2,
        out_shape=[face, face],
        compiler_params=params(),
        cost_estimate=cost(2**27, 2**21),
        name="zfaces",
    )(*planes, *y_halos)


def wgrad_kernel(scale, *refs):
    x_ref, part_ref, g3, x3, acc, flat = refs[9:]
    size_x, channels, plane = x_ref.shape
    size_z = refs[5].shape[-1]
    halo = z_halo(refs[7], refs[8], size_x + 2, plane // size_z + 2, size_z)
    weight_products(refs, halo, x_ref, g3, x3, acc)
    whole = to_flat(acc[...] * scale, channels, channels, flat)
    part_ref[...] = whole[:, : part_ref.shape[1]].astype(BF16)


def wgrad(sources, planes_x, shape, scale):
    channels = shape[0]
    return pl.pallas_call(
        functools.partial(wgrad_kernel, scale),
        in_specs=[VMEM] * 10,
        out_specs=VMEM,
        out_shape=jax.ShapeDtypeStruct((channels, 27 * channels), BF16),
        scratch_shapes=[
            g3_scratch(*shape),
            x3_scratch(*shape),
            acc_scratch(channels),
            flat_scratch(channels),
        ],
        compiler_params=params(32 * 2**20),
        cost_estimate=wgrad_cost(*shape),
        name="wgrad",
    )(*sources, planes_x)


def dgrad_kernel(*refs):
    w_ref, out_ref, g3, turned, weights, tile = refs[9:]
    _, size_x, size_y, size_z = out_ref.shape
    spread_weights(w_ref[...].astype(F32), turned, weights)
    halo = z_halo(refs[7], refs[8], size_x + 2, size_y + 2, size_z)
    input_products(refs, halo, g3, weights, tile, out_ref)


def dgrad(sources, kernel, shape):
    return pl.pallas_call(
        dgrad_kernel,
        in_specs=[VMEM] * 10,
        out_specs=VMEM,
        out_shape=jax.ShapeDtypeStruct(shape, BF16),
        scratch_shapes=dgrad_scratch(*shape),
        compiler_params=params(32 * 2**20),
        cost_estimate=dgrad_cost(*shape),
        name="dgrad",
    )(*sources, kernel)


def general_gradients(activations, preact, upstream, master, scale):
    shape = activations.shape
    channels, _, _, size_z = shape
    devices = math.prod(lax.axis_size(a) for a in AXES)
    share = master.shape[0]
    first, last = faces(preact, upstream)
    x_halos = (shifted(last, {"gx": 1}), shifted(first, {"gx": -1}))
    inner, planes_x, sent = inner_planes(
        preact, upstream, activations, master.reshape(1, share), (devices, 1, share)
    )
    kernel = lax.all_to_all(sent, AXES, 0, 0, tiled=True).reshape(channels, 27 * channels)
    planes = (x_halos[0], first, inner, last, x_halos[1])
    y_sent = y_faces(planes, size_z)
    y_halos = (shifted(y_sent[1], {"gy": 1}), shifted(y_sent[0], {"gy": -1}))
    zlo, zhi = z_faces(planes, y_halos)
    z_halos = (shifted(zhi, {"gz": 1}), shifted(zlo, {"gz": -1}))
    sources = (*planes, *y_halos, *z_halos)
    part = wgrad(sources, planes_x, shape, scale)
    part, kernel = lax.optimization_barrier((part, kernel))
    parts = lax.all_to_all(part.reshape(devices, 1, share), AXES, 0, 0, tiled=True)
    grad_input = dgrad(sources, kernel, shape)
    return grad_input, parts


def shifted(value, moves):
    names = tuple(moves)
    sizes = [lax.axis_size(name) for name in names]
    pairs = []
    for source in range(math.prod(sizes)):
        rest, coords = source, []
        for size in reversed(sizes):
            coords.insert(0, rest % size)
            rest //= size
        coords = [
            (at + moves[name]) if moves[name] != "swap" else 1 - at
            for at, name in zip(coords, names)
        ]
        if all(0 <= at < size for at, size in zip(coords, sizes)):
            target = 0
            for at, size in zip(coords, sizes):
                target = target * size + at
            pairs.append((source, target))
    return lax.ppermute(value, names if len(names) > 1 else names[0], pairs)


def local(activations, preact, upstream, master, first_moment, second_moment):
    channels, size_x, size_y, size_z = activations.shape
    devices = math.prod(lax.axis_size(a) for a in AXES)
    share = master.shape[0]
    scale = 1.0 / math.sqrt(size_x * size_y * size_z * devices)
    in_pairs = (
        lax.axis_size("gy") == 2
        and channels % devices == 0
        and share % LANES == 0
        and channels // devices * lax.axis_size("gz") % 8 == 0
        and 2 * size_x * size_y <= LANES
        and (size_x + 2) * size_y <= LANES
    )
    gradients = pair_gradients if in_pairs else general_gradients
    grad_input, parts = gradients(activations, preact, upstream, master, scale)
    weight_grad = jnp.sum(parts.astype(F32), axis=0).reshape(-1)[:share]
    new_first = 0.9 * first_moment + 0.1 * weight_grad
    new_second = 0.999 * second_moment + 0.001 * weight_grad * weight_grad
    corr_first = 1.0 - (0.9**10) ** 10
    corr_second = 1.0 - (0.999**10) ** 10
    update = new_first / corr_first / (jnp.sqrt(new_second / corr_second) + 1e-08) + 0.01 * master
    new_master = master - 0.05 * update
    return (grad_input, weight_grad, new_master, new_first, new_second)


def solution(mesh):
    volume = P(None, "gx", "gy", "gz")
    flat = P(AXES)
    return jax.shard_map(
        local,
        mesh=mesh,
        in_specs=(volume, volume, volume, flat, flat, flat),
        out_specs=(volume, flat, flat, flat, flat),
        check_vma=False,
    )
```

profile of v0, /device:TPU:0, one launch (start us, length us, event | category | flops | bytes accessed | tf_op | source)
XLA Modules:
  0.0 51.6 jit_solution(2034520370207733459)
XLA Ops:
  0.6 1.9 %faces.1 = (bf16[64,1024]{1,0:T(8,128)(2,1)}, bf16[64,1024]{1,0:T(8,128)(2,1)}) custom-call(bf16[64,8,8,128]{3,2,1,0:T(8,128)(2,1)} %p_ref.3, bf16[64,8,8,128]{3,2,1,0:T(8,128)(2,1)} %u_ref.3), custom_call_target="tpu_custom_call" | custom-call | bytes 1048576 | tf_op jit(solution)/shard_map/faces/pallas_call | solution.py:64
  2.5 4.8 %collective-permute-start = (bf16[64,1024]{1,0:T(8,128)(2,1)}, bf16[64,1024]{1,0:T(8,128)(2,1)S(1)}, u32[]{:S(2)}, u32[]{:S(2)}) collective-permute-start(bf16[64,1024]{1,0:T(8,128)(2,1)} %get-tuple-element.16.refs_3_), channel_id=1, source_target_pairs={{0,8},{8,16},{16,24},{1,9},{9,17},{17,25},{2,10},{10,18},{18,26},{... | collective-permute-start | bytes 393224 | tf_op jit(solution)/shard_map/ppermute | solution.py:787
  7.4 1.3 %collective-permute-start.1 = (bf16[64,1024]{1,0:T(8,128)(2,1)}, bf16[64,1024]{1,0:T(8,128)(2,1)S(1)}, u32[]{:S(2)}, u32[]{:S(2)}) collective-permute-start(bf16[64,1024]{1,0:T(8,128)(2,1)} %get-tuple-element.17.refs_1_), channel_id=1, source_target_pairs={{8,0},{16,8},{24,16},{9,1},{17,9},{25,17},{10,2},{18,10},{26,18},{... | collective-permute-start | bytes 393224 | tf_op jit(solution)/shard_map/ppermute | solution.py:787
  8.7 0.0 copy-start.2
  8.7 0.0 copy-start.3
  8.7 4.4 %inner.1 = (bf16[6,64,1024]{2,1,0:T(8,128)(2,1)}, bf16[8,64,1024]{2,1,0:T(8,128)(2,1)}, bf16[32,32,128]{2,1,0:T(8,128)(2,1)}) custom-call(bf16[64,8,8,128]{3,2,1,0:T(8,128)(2,1)} %p_ref.3, bf16[64,8,8,128]{3,2,1,0:T(8,128)(2,1)} %u_ref.3, bf16[64,8,8,128]{3,2,1,0:T(8,128)(2,1)} %a_ref.1, f32[27,128]{1,0:T(8,128)} %bitcast.4), custom_call_target="tpu_custom_call" | custom-call | bytes 6291456 | tf_op jit(solution)/shard_map/inner/pallas_call | solution.py:124
  13.2 0.0 collective-permute-done.refs_0_
  13.2 1.9 %collective-permute-done.1.refs_4_ = bf16[64,1024]{1,0:T(8,128)(2,1)S(1)} collective-permute-done((bf16[64,1024]{1,0:T(8,128)(2,1)}, bf16[64,1024]{1,0:T(8,128)(2,1)S(1)}, u32[]{:S(2)}, u32[]{:S(2)}) %collective-permute-start.1) | collective-permute-done | bytes 131104 | tf_op jit(solution)/shard_map/ppermute | solution.py:787
  15.1 0.0 copy-done.2
  15.1 0.0 copy-done.3
  15.1 1.1 %copy-done = bf16[6,64,1024]{2,1,0:T(8,128)(2,1)S(1)} copy-done((bf16[6,64,1024]{2,1,0:T(8,128)(2,1)S(1)}, bf16[6,64,1024]{2,1,0:T(8,128)(2,1)}, u32[]{:S(2)}) %copy-start) | copy-done | bytes 786456
  16.2 0.6 %side.1.own_ref = bf16[12,64,128]{2,1,0:T(8,128)(2,1)S(1)} custom-call(bf16[64,1024]{1,0:T(8,128)(2,1)S(1)} %collective-permute-done.refs_0_, bf16[64,1024]{1,0:T(8,128)(2,1)S(1)} %copy-done.2, bf16[6,64,1024]{2,1,0:T(8,128)(2,1)S(1)} %copy-done, bf16[64,1024]{1,0:T(8,128)(2,1)S(1)} %copy-done.3, bf16[64,1024]{1,0:T(8,128)(2,1)S(1)} %collective-permute-done.1.refs_4_), custom_call_target="tpu_custom_call" | custom-call | flops 134217728 | bytes 2097152 | tf_op jit(solution)/shard_map/side/pallas_call | solution.py:406
  16.8 0.1 collective-permute-start.2
  16.9 5.3 %all-to-all-start = ((bf16[32,32,128]{2,1,0:T(8,128)(2,1)}), bf16[32,32,128]{2,1,0:T(8,128)(2,1)S(1)}, u32[]{:S(2)}, u32[]{:S(2)}) async-start(bf16[32,32,128]{2,1,0:T(8,128)(2,1)} %get-tuple-element.24), calls=%async_computation | async-start | bytes 524288 | tf_op jit(solution)/shard_map/all_to_all | solution.py:620
  22.2 0.0 collective-permute-done.2.other_ref.refs_5_.refs_6_
  22.2 0.0 copy-done.1
  22.2 3.9 %wgrad.1 = (f32[352,256]{1,0:T(8,128)S(1)}, f32[352,256]{1,0:T(8,128)S(1)}) custom-call(bf16[64,1024]{1,0:T(8,128)(2,1)S(1)} %collective-permute-done.refs_0_, bf16[64,1024]{1,0:T(8,128)(2,1)S(1)} %copy-done.2, bf16[6,64,1024]{2,1,0:T(8,128)(2,1)S(1)} %copy-done.1, bf16[64,1024]{1,0:T(8,128)(2,1)S(1)} %copy-done.3, ...), custom_call_target="tpu_custom_call" | custom-call | flops 2264924160 | bytes 4194304 | tf_op jit(solution)/shard_map/wgrad/pallas_call | solution.py:462
  26.1 0.3 collective-permute-start.5
  26.4 3.6 %collective-permute-start.3 = (bf16[2,64,128]{2,1,0:T(8,128)(2,1)S(1)}, bf16[2,64,128]{2,1,0:T(8,128)(2,1)S(1)}, u32[]{:S(2)}, u32[]{:S(2)}) collective-permute-start(bf16[2,64,128]{2,1,0:T(8,128)(2,1)S(1)} %get-tuple-element.19), channel_id=1, source_target_pairs={{0,1},{1,2},{2,3},{4,5},{5,6},{6,7},{8,9},{9,10},{10,11},{12,13},{... | collective-permute-start | bytes 98312 | tf_op jit(solution)/shard_map/ppermute | solution.py:787
  30.0 1.3 %collective-permute-start.4 = (bf16[2,64,128]{2,1,0:T(8,128)(2,1)S(1)}, bf16[2,64,128]{2,1,0:T(8,128)(2,1)S(1)}, u32[]{:S(2)}, u32[]{:S(2)}) collective-permute-start(bf16[2,64,128]{2,1,0:T(8,128)(2,1)S(1)} %get-tuple-element.20), channel_id=1, source_target_pairs={{1,0},{2,1},{3,2},{5,4},{6,5},{7,6},{9,8},{10,9},{11,10},{13,12},{... | collective-permute-start | bytes 98312 | tf_op jit(solution)/shard_map/ppermute | solution.py:787
  31.3 0.3 collective-permute-done.3.refs_2_.refs_7_
  31.6 4.2 %collective-permute-done.4.refs_3_.refs_8_ = bf16[2,64,128]{2,1,0:T(8,128)(2,1)S(1)} collective-permute-done((bf16[2,64,128]{2,1,0:T(8,128)(2,1)S(1)}, bf16[2,64,128]{2,1,0:T(8,128)(2,1)S(1)}, u32[]{:S(2)}, u32[]{:S(2)}) %collective-permute-start.4) | collective-permute-done | bytes 32800 | tf_op jit(solution)/shard_map/ppermute | solution.py:787
  35.8 0.0 collective-permute-done.5.refs_1_
  35.8 1.8 %finish.1 = bf16[16,32,128]{2,1,0:T(8,128)(2,1)} custom-call(f32[352,256]{1,0:T(8,128)S(1)} %get-tuple-element.22.refs_0_, f32[352,256]{1,0:T(8,128)S(1)} %collective-permute-done.5.refs_1_, bf16[2,64,128]{2,1,0:T(8,128)(2,1)S(1)} %collective-permute-done.3.refs_2_.refs_7_, bf16[2,64,128]{2,1,0:T(8,128)(2,1)S(1)} %collective-permute-done.4.refs_3_.refs_8_), custom_call_target="tpu_custom_call" | custom-call | flops 16777216 | bytes 1048576 | tf_op jit(solution)/shard_map/finish/pallas_call | solution.py:550
  37.6 0.0 all-to-all-done.refs_9_
  37.6 5.7 %all-to-all-start.1 = ((bf16[16,32,128]{2,1,0:T(8,128)(2,1)}), bf16[16,32,128]{2,1,0:T(8,128)(2,1)S(1)}, u32[]{:S(2)}, u32[]{:S(2)}) async-start(bf16[16,32,128]{2,1,0:T(8,128)(2,1)} %finish.1), calls=%async_computation.1 | async-start | bytes 262144 | tf_op jit(solution)/shard_map/all_to_all | solution.py:640
  43.3 5.4 %dgrad.1 = bf16[64,8,8,128]{3,2,1,0:T(8,128)(2,1)} custom-call(bf16[64,1024]{1,0:T(8,128)(2,1)S(1)} %collective-permute-done.refs_0_, bf16[64,1024]{1,0:T(8,128)(2,1)S(1)} %copy-done.2, bf16[6,64,1024]{2,1,0:T(8,128)(2,1)S(1)} %copy-done.1, bf16[64,1024]{1,0:T(8,128)(2,1)S(1)} %copy-done.3, bf16[64,1024]{1,0:T(8,128)(2,1)S(1)} %collective-permute-done.1.refs_4_, ...), custom_call_target="tpu_custom_call" | custom-call | flops 2415919104 | bytes 4194304 | tf_op jit(solution)/shard_map/dgrad/pallas_call | solution.py:591
  48.6 2.3 %all-to-all-done.1 = bf16[16,32,128]{2,1,0:T(8,128)(2,1)S(1)} async-done(((bf16[16,32,128]{2,1,0:T(8,128)(2,1)}), bf16[16,32,128]{2,1,0:T(8,128)(2,1)S(1)}, u32[]{:S(2)}, u32[]{:S(2)}) %all-to-all-start.1) | async-done | bytes 131104 | tf_op jit(solution)/shard_map/all_to_all | solution.py:640
  50.9 0.0 copy-done.5
  50.9 0.0 copy-done.6
  50.9 0.0 copy-done.7
  50.9 0.6 %multiply_subtract_fusion = (f32[3456]{0:T(1024)}, f32[3456]{0:T(1024)}, f32[3456]{0:T(1024)}, f32[3456]{0:T(1024)}) fusion(f32[3456]{0:T(1024)S(1)} %copy-done.5, f32[3456]{0:T(1024)S(1)} %copy-done.6, f32[3456]{0:T(1024)S(1)} %copy-done.7, f32[32,128]{1,0:T(8,128)S(1)} %convert_reduce_fusion), kind=kLoop, calls=%fused_computation.4 | loop fusion | flops 51840 | bytes 110592 | tf_op jit(solution)/shard_map/sub | solution.py:811
  (9 shorter events, 0.0 us)
Async XLA Ops:
  2.5 10.6 %collective-permute-start = (bf16[64,1024]{1,0:T(8,128)(2,1)}, bf16[64,1024]{1,0:T(8,128)(2,1)S(1)}, u32[]{:S(2)}, u32[]{:S(2)}) collective-permute-start(bf16[64,1024]{1,0:T(8,128)(2,1)} %get-tuple-element.16.refs_3_), channel_id=1, source_target_pairs={{0,8},{8,16},{16,24},{1,9},{9,17},{17,25},{2,10},{10,18},{18,26},{... | collective-permute-start | bytes 393224 | tf_op jit(solution)/shard_map/ppermute | solution.py:787
  7.4 7.7 %collective-permute-start.1 = (bf16[64,1024]{1,0:T(8,128)(2,1)}, bf16[64,1024]{1,0:T(8,128)(2,1)S(1)}, u32[]{:S(2)}, u32[]{:S(2)}) collective-permute-start(bf16[64,1024]{1,0:T(8,128)(2,1)} %get-tuple-element.17.refs_1_), channel_id=1, source_target_pairs={{8,0},{16,8},{24,16},{9,1},{17,9},{25,17},{10,2},{18,10},{26,18},{... | collective-permute-start | bytes 393224 | tf_op jit(solution)/shard_map/ppermute | solution.py:787
  8.7 6.4 %copy-start.2 = (bf16[64,1024]{1,0:T(8,128)(2,1)S(1)}, bf16[64,1024]{1,0:T(8,128)(2,1)}, u32[]{:S(2)}) copy-start(bf16[64,1024]{1,0:T(8,128)(2,1)} %get-tuple-element.17.refs_1_) | copy-start | bytes 393220
  8.7 6.4 %copy-start.3 = (bf16[64,1024]{1,0:T(8,128)(2,1)S(1)}, bf16[64,1024]{1,0:T(8,128)(2,1)}, u32[]{:S(2)}) copy-start(bf16[64,1024]{1,0:T(8,128)(2,1)} %get-tuple-element.16.refs_3_) | copy-start | bytes 393220
  15.1 1.1 %copy-start = (bf16[6,64,1024]{2,1,0:T(8,128)(2,1)S(1)}, bf16[6,64,1024]{2,1,0:T(8,128)(2,1)}, u32[]{:S(2)}) copy-start(bf16[6,64,1024]{2,1,0:T(8,128)(2,1)} %get-tuple-element.18.refs_2_) | copy-start | bytes 2359300
  16.2 6.0 %copy-start.1 = (bf16[6,64,1024]{2,1,0:T(8,128)(2,1)S(1)}, bf16[6,64,1024]{2,1,0:T(8,128)(2,1)}, u32[]{:S(2)}) copy-start(bf16[6,64,1024]{2,1,0:T(8,128)(2,1)} %get-tuple-element.18.refs_2_) | copy-start | bytes 2359300
  16.2 6.0 %copy-start.4 = (bf16[8,64,1024]{2,1,0:T(8,128)(2,1)S(1)}, bf16[8,64,1024]{2,1,0:T(8,128)(2,1)}, u32[]{:S(2)}) copy-start(bf16[8,64,1024]{2,1,0:T(8,128)(2,1)} %get-tuple-element.21.refs_7_) | copy-start | bytes 3145732
  16.8 5.4 %collective-permute-start.2 = (bf16[12,64,128]{2,1,0:T(8,128)(2,1)S(1)}, bf16[12,64,128]{2,1,0:T(8,128)(2,1)S(1)}, u32[]{:S(2)}, u32[]{:S(2)}) collective-permute-start(bf16[12,64,128]{2,1,0:T(8,128)(2,1)S(1)} %side.1.own_ref), channel_id=1, source_target_pairs={{0,4},{4,0},{1,5},{5,1},{2,6},{6,2},{3,7},{7,3},{8,12},{12,8},{9,1... | collective-permute-start | bytes 589832 | tf_op jit(solution)/shard_map/ppermute | solution.py:787
  16.9 20.7 %all-to-all-start = ((bf16[32,32,128]{2,1,0:T(8,128)(2,1)}), bf16[32,32,128]{2,1,0:T(8,128)(2,1)S(1)}, u32[]{:S(2)}, u32[]{:S(2)}) async-start(bf16[32,32,128]{2,1,0:T(8,128)(2,1)} %get-tuple-element.24), calls=%async_computation | async-start | bytes 524288 | tf_op jit(solution)/shard_map/all_to_all | solution.py:620
  26.1 9.7 %collective-permute-start.5 = (f32[352,256]{1,0:T(8,128)S(1)}, f32[352,256]{1,0:T(8,128)S(1)}, u32[]{:S(2)}, u32[]{:S(2)}) collective-permute-start(f32[352,256]{1,0:T(8,128)S(1)} %get-tuple-element.23), channel_id=1, source_target_pairs={{0,4},{4,0},{1,5},{5,1},{2,6},{6,2},{3,7},{7,3},{8,12},{12,8},{9,1... | collective-permute-start | bytes 1081352 | tf_op jit(solution)/shard_map/ppermute | solution.py:787
  26.4 5.2 %collective-permute-start.3 = (bf16[2,64,128]{2,1,0:T(8,128)(2,1)S(1)}, bf16[2,64,128]{2,1,0:T(8,128)(2,1)S(1)}, u32[]{:S(2)}, u32[]{:S(2)}) collective-permute-start(bf16[2,64,128]{2,1,0:T(8,128)(2,1)S(1)} %get-tuple-element.19), channel_id=1, source_target_pairs={{0,1},{1,2},{2,3},{4,5},{5,6},{6,7},{8,9},{9,10},{10,11},{12,13},{... | collective-permute-start | bytes 98312 | tf_op jit(solution)/shard_map/ppermute | solution.py:787
  30.0 5.8 %collective-permute-start.4 = (bf16[2,64,128]{2,1,0:T(8,128)(2,1)S(1)}, bf16[2,64,128]{2,1,0:T(8,128)(2,1)S(1)}, u32[]{:S(2)}, u32[]{:S(2)}) collective-permute-start(bf16[2,64,128]{2,1,0:T(8,128)(2,1)S(1)} %get-tuple-element.20), channel_id=1, source_target_pairs={{1,0},{2,1},{3,2},{5,4},{6,5},{7,6},{9,8},{10,9},{11,10},{13,12},{... | collective-permute-start | bytes 98312 | tf_op jit(solution)/shard_map/ppermute | solution.py:787
  37.6 13.3 %all-to-all-start.1 = ((bf16[16,32,128]{2,1,0:T(8,128)(2,1)}), bf16[16,32,128]{2,1,0:T(8,128)(2,1)S(1)}, u32[]{:S(2)}, u32[]{:S(2)}) async-start(bf16[16,32,128]{2,1,0:T(8,128)(2,1)} %finish.1), calls=%async_computation.1 | async-start | bytes 262144 | tf_op jit(solution)/shard_map/all_to_all | solution.py:640
  48.6 2.3 %copy-start.5 = (f32[3456]{0:T(1024)S(1)}, f32[3456]{0:T(1024)}, u32[]{:S(2)}) copy-start(f32[3456]{0:T(1024)} %param.9) | copy-start | bytes 41476
  48.6 2.3 %copy-start.6 = (f32[3456]{0:T(1024)S(1)}, f32[3456]{0:T(1024)}, u32[]{:S(2)}) copy-start(f32[3456]{0:T(1024)} %param.10) | copy-start | bytes 41476
  48.6 2.3 %copy-start.7 = (f32[3456]{0:T(1024)S(1)}, f32[3456]{0:T(1024)}, u32[]{:S(2)}) copy-start(f32[3456]{0:T(1024)} %param.11) | copy-start | bytes 41476
where the time goes:
time: 52.1 us; the launch traced here: 51.6 us
  starting transfers between devices  22.3 us (43%)
  Pallas kernels  17.9 us (34%)
  waiting for transfers between devices  8.69 us (17%)
  local copies, waits for them, and re-layouts  1.16 us (2%)
  between operations  0.8 us (2%)
  other arithmetic  0.66 us (1%)
    ppermute x6, starting transfers between devices, shifted(): return lax.ppermute(value, names if len(names) > 1 else names[0], pairs)  11.4 us
    ppermute x6, waiting for transfers between devices, shifted(): return lax.ppermute(value, names if len(names) > 1 else names[0], pairs)  6.43 us
    all_to_all x1, starting transfers between devices, pair_gradients(): parts = lax.all_to_all(part, ('gx', 'gz'), 0, 0, tiled=True)  5.65 us
    pallas_call x1, Pallas kernels, pair_dgrad(): pl.pallas_call(functools.partial(pair_dgrad_kernel, rows), in_specs=[VMEM...  5.36 us
    all_to_all x1, starting transfers between devices, pair_gradients(): kernel = lax.all_to_all(sent, AXES, 0, 0, tiled=True)  5.27 us
    pallas_call x1, Pallas kernels, inner_planes(): pl.pallas_call(inner_kernel, in_specs=[HBM] * 3 + [VMEM], out_specs=[VMEM...  4.44 us
    pallas_call x1, Pallas kernels, pair_wgrad(): pl.pallas_call(functools.partial(pair_wgrad_kernel, span), in_specs=[VMEM...  3.88 us
    all_to_all x1, waiting for transfers between devices, pair_gradients(): parts = lax.all_to_all(part, ('gx', 'gz'), 0, 0, tiled=True)  2.26 us
  transfers between devices with their start and end apart: 8, of which 4 were waited for; matrix products, arithmetic and copies ran while one was open for 0% of the time, Pallas kernels for 30%

commit v1 on v0

--- a/solution.py
+++ b/solution.py
@@ -78,7 +78,7 @@
     )(preact, upstream)
 
 
-def inner_kernel(p_ref, u_ref, a_ref, m_ref, g_ref, x_ref, sent_ref, p_buf, u_buf, a_buf, tile, sems):
+def read_inner(p_ref, u_ref, a_ref, g_ref, x_ref, p_buf, u_buf, a_buf, tile, sems):
     channels, size_x, size_y, size_z = a_ref.shape
     inner = size_x - 2
     copies = []
@@ -96,11 +96,6 @@
     for group in copies:
         for copy in group:
             copy.start()
-    share = m_ref[...]
-    count, height, width = sent_ref.shape
-    if height > share.shape[0]:
-        share = jnp.concatenate([share, jnp.zeros((height - share.shape[0], width), F32)], axis=0)
-    sent_ref[...] = jnp.broadcast_to(share.astype(BF16)[None], sent_ref.shape)
     for x in range(inner):
         for copy in copies[x]:
             copy.wait()
@@ -118,29 +113,40 @@
         to_planes(a_buf[x], tile.at[x % 2], write)
 
 
-def inner_planes(preact, upstream, activations, share, sent_shape):
-    channels, size_x, size_y, size_z = preact.shape
+def inner_kernel(*refs):
+    read_inner(*refs)
+
+
+def inner_outputs(channels, size_x, size_y, size_z):
     plane = size_y * size_z
+    return [
+        jax.ShapeDtypeStruct((size_x - 2, channels, plane), BF16),
+        jax.ShapeDtypeStruct((size_x, channels, plane), BF16),
+    ]
+
+
+def inner_scratch(channels, size_x, size_y, size_z):
+    return [
+        pltpu.VMEM((size_x - 2, channels, size_y, size_z), BF16),
+        pltpu.VMEM((size_x - 2, channels, size_y, size_z), BF16),
+        pltpu.VMEM((size_x, channels, size_y, size_z), BF16),
+        pltpu.VMEM((2, channels * size_y, size_z), F32),
+        pltpu.SemaphoreType.DMA((3 * size_x - 4,)),
+    ]
+
+
+def inner_planes(preact, upstream, activations):
+    shape = preact.shape
     return pl.pallas_call(
         inner_kernel,
-        in_specs=[HBM] * 3 + [VMEM],
-        out_specs=[VMEM] * 3,
-        out_shape=[
-            jax.ShapeDtypeStruct((size_x - 2, channels, plane), BF16),
-            jax.ShapeDtypeStruct((size_x, channels, plane), BF16),
-            jax.ShapeDtypeStruct(sent_shape, BF16),
-        ],
-        scratch_shapes=[
-            pltpu.VMEM((size_x - 2, channels, size_y, size_z), BF16),
-            pltpu.VMEM((size_x - 2, channels, size_y, size_z), BF16),
-            pltpu.VMEM((size_x, channels, size_y, size_z), BF16),
-            pltpu.VMEM((2, channels * size_y, size_z), F32),
-            pltpu.SemaphoreType.DMA((3 * size_x - 4,)),
-        ],
+        in_specs=[HBM] * 3,
+        out_specs=[VMEM] * 2,
+        out_shape=inner_outputs(*shape),
+        scratch_shapes=inner_scratch(*shape),
         compiler_params=params(ALL_VMEM - 3_600_000),
         cost_estimate=cost(0, 6 * 2**20),
         name="inner",
-    )(preact, upstream, activations, share)
+    )(preact, upstream, activations)
 
 
 def body_of(refs, index):
@@ -165,17 +171,17 @@
     return (voxel == wanted).astype(F32).astype(BF16)
 
 
-def z_tiles(planes, rows_y, size_z):
+def z_tiles(planes, rows_y, size_z, numbers):
     channels = planes[0].shape[0]
     columns = jnp.dot(
         jnp.concatenate(planes, axis=0), z_picker(rows_y, size_z), preferred_element_type=F32
     )
     low = jnp.zeros((channels, LANES), F32)
     high = jnp.zeros((channels, LANES), F32)
-    for index in range(len(planes)):
+    for index, number in enumerate(numbers):
         rows = columns[index * channels : (index + 1) * channels]
-        low = low + pltpu.roll(rows[:, :LANES], index * rows_y, 1)
-        high = high + pltpu.roll(rows[:, LANES:], index * rows_y, 1)
+        low = low + pltpu.roll(rows[:, :LANES], number * rows_y, 1)
+        high = high + pltpu.roll(rows[:, LANES:], number * rows_y, 1)
     return low, high
 
 
@@ -291,8 +297,11 @@
 
 def to_flat(value, count, channels, flat):
     height, width = value.shape
-    wide = jnp.concatenate([value, jnp.zeros((-height % LANES, width), F32)], axis=0)
-    wide = jnp.concatenate([wide, jnp.zeros((wide.shape[0], -width % LANES), F32)], axis=1)
+    wide = value
+    if height % LANES:
+        wide = jnp.concatenate([wide, jnp.zeros((-height % LANES, width), F32)], axis=0)
+    if width % LANES:
+        wide = jnp.concatenate([wide, jnp.zeros((wide.shape[0], -width % LANES), F32)], axis=1)
     turned = wide.T
     for b in range(3):
         rows = turned[b * channels : (b + 1) * channels]
@@ -383,39 +392,73 @@
     return cost(72 * channels * channels * size_x * size_y * size_z, 4 * 2**20)
 
 
-def side_kernel(*refs):
-    sent_ref = refs[5]
-    planes = refs[2].shape[0] + 4
-    plane = refs[0].shape[-1]
-    size_z = sent_ref.shape[-1]
-    is_first = lax.axis_index("gy") == 0
-    whole = []
-    for index in range(planes):
-        body = body_of(refs[:5], index)[...]
-        whole.append(body)
-        low, high = body[:, :size_z], body[:, plane - size_z :]
-        picked = jnp.where(is_first, high.astype(F32), low.astype(F32))
-        sent_ref[index] = picked.astype(BF16)
-    low, high = z_tiles(whole, plane // size_z, size_z)
-    sent_ref[planes] = low.astype(BF16)
-    sent_ref[planes + 1] = high.astype(BF16)
-
-
-def side(planes, size_z):
-    inner, channels, _ = planes[2].shape
+def row_for_other(body, size_z):
+    plane = body.shape[-1]
+    low, high = body[:, :size_z].astype(F32), body[:, plane - size_z :].astype(F32)
+    return jnp.where(lax.axis_index("gy") == 0, high, low).astype(BF16)
+
+
+def pair_inner_kernel(*refs):
+    first_ref, last_ref = refs[3:5]
+    g_ref, x_ref, side_ref = refs[5:8]
+    read_inner(*refs[:3], g_ref, x_ref, *refs[8:])
+    size_z = side_ref.shape[-1]
+    size_x, channels, plane = x_ref.shape
+    size_y = plane // size_z
+    bodies = [first_ref] + [g_ref.at[x] for x in range(size_x - 2)] + [last_ref]
+    for x, body in enumerate(bodies):
+        side_ref[x] = row_for_other(body, size_z)
+    low, high = z_tiles([body[...] for body in bodies], size_y, size_z, range(1, size_x + 1))
+    side_ref[size_x] = low.astype(BF16)
+    side_ref[size_x + 1] = high.astype(BF16)
+    low, high = z_tiles([x_ref[x] for x in range(size_x)], size_y, size_z, range(size_x))
+    side_ref[size_x + 2] = (low + pltpu.roll(high, size_x * size_y, 1)).astype(BF16)
+
+
+def pair_inner(preact, upstream, activations, first, last):
+    shape = preact.shape
+    channels, size_x, _, size_z = shape
+    return pl.pallas_call(
+        pair_inner_kernel,
+        in_specs=[HBM] * 3 + [VMEM] * 2,
+        out_specs=[VMEM] * 3,
+        out_shape=inner_outputs(*shape)
+        + [jax.ShapeDtypeStruct((size_x + 3, channels, size_z), BF16)],
+        scratch_shapes=inner_scratch(*shape),
+        compiler_params=params(ALL_VMEM - 3_600_000),
+        cost_estimate=cost(0, 6 * 2**20),
+        name="inner",
+    )(preact, upstream, activations, first, last)
+
+
+def side_kernel(xlo_ref, xhi_ref, own_ref, sent_ref):
+    size_x = own_ref.shape[0] - 3
+    size_z = own_ref.shape[-1]
+    size_y = xlo_ref.shape[-1] // size_z
+    sent_ref[0] = row_for_other(xlo_ref, size_z)
+    for x in range(size_x):
+        sent_ref[x + 1] = own_ref[x]
+    sent_ref[size_x + 1] = row_for_other(xhi_ref, size_z)
+    tiles = z_tiles([xlo_ref[...], xhi_ref[...]], size_y, size_z, (0, size_x + 1))
+    for k in range(2):
+        sent_ref[size_x + 2 + k] = (own_ref[size_x + k].astype(F32) + tiles[k]).astype(BF16)
+    sent_ref[size_x + 4] = own_ref[size_x + 2]
+
+
+def side(x_halos, own):
     return pl.pallas_call(
         side_kernel,
-        in_specs=[VMEM] * 5,
+        in_specs=[VMEM] * 3,
         out_specs=VMEM,
-        out_shape=jax.ShapeDtypeStruct((inner + 6, channels, size_z), BF16),
+        out_shape=jax.ShapeDtypeStruct((own.shape[0] + 2, *own.shape[1:]), BF16),
         compiler_params=params(),
-        cost_estimate=cost(2**27, 2**21),
+        cost_estimate=cost(2**25, 2**19),
         name="side",
-    )(*planes)
+    )(*x_halos, own)
 
 
 def join_kernel(own_ref, other_ref, low_ref, high_ref):
-    at = own_ref.shape[0] - 2
+    at = own_ref.shape[0] - 3
     me = lax.axis_index("gy")
     for k, out_ref in enumerate((low_ref, high_ref)):
         out_ref[me] = own_ref[at + k]
@@ -437,28 +480,24 @@
 
 def pair_wgrad_kernel(span, *refs):
     x_ref, mine_ref, theirs_ref, g3, x3, acc = refs[7:]
-    size_x, channels, plane = x_ref.shape
-    size_z = refs[5].shape[-1]
+    channels = x_ref.shape[1]
     weight_products(refs, None, x_ref, g3, x3, acc)
-    me = lax.axis_index("gy")
-    rows = 9 * channels // 2
+    is_first = lax.axis_index("gy") == 0
     width = 3 * channels
-    spare = jnp.zeros((rows, mine_ref.shape[1] - width), F32)
     halves = []
     for half in range(2):
         at = range(half * span, 9 * channels, 2 * span)
         halves.append(jnp.concatenate([acc[start : start + span, :] for start in at], axis=0))
-    low, high = z_tiles([x_ref[x] for x in range(size_x)], plane // size_z, size_z)
-    for ref, own in ((mine_ref, True), (theirs_ref, False)):
-        picked = jnp.where((me == 0) == own, halves[0], halves[1])
-        ref[:rows, :] = jnp.concatenate([picked, spare], axis=1)
-        ref[rows:, :LANES] = low
-        ref[rows:, LANES:] = high
+    spare = jnp.zeros((halves[0].shape[0], mine_ref.shape[1] - width), F32)
+    for ref, order in ((mine_ref, halves), (theirs_ref, halves[::-1])):
+        picked = jnp.where(is_first, order[0], order[1])
+        ref[...] = jnp.concatenate([picked, spare], axis=1)
 
 
 def pair_wgrad(sources, planes_x, shape, span):
     channels = shape[0]
-    part = jax.ShapeDtypeStruct((9 * channels // 2 + channels, 2 * LANES), F32)
+    width = -(-3 * channels // LANES) * LANES
+    part = jax.ShapeDtypeStruct((9 * channels // 2, width), F32)
     return pl.pallas_call(
         functools.partial(pair_wgrad_kernel, span),
         in_specs=[VMEM] * 8,
@@ -471,25 +510,23 @@
     )(*sources, planes_x)
 
 
-def finish_kernel(scale, span, rows, sizes, *refs):
-    mine_ref, other_ref, zlo_ref, zhi_ref, part_ref, flat, lines, chunks = refs
+def edge_kernel(span, sizes, own_ref, other_ref, zlo_ref, zhi_ref, edge_ref):
     size_x, size_y = sizes
     channels = zlo_ref.shape[1]
     count = channels // 2
-    height = 9 * count
     area = size_x * size_y
-    me = lax.axis_index("gy")
-    total = (mine_ref[:height, :] + other_ref[:height, :])[:, : 3 * channels]
-    own, other = mine_ref[height:, :], other_ref[height:, :]
-    inputs = (jnp.where(me == 0, own, other), jnp.where(me == 0, other, own))
+    is_first = lax.axis_index("gy") == 0
+    at = own_ref.shape[0] - 1
+    own, other = own_ref[at].astype(F32), other_ref[at].astype(F32)
+    inputs = (jnp.where(is_first, own, other), jnp.where(is_first, other, own))
     lane = lax.broadcasted_iota(jnp.int32, (channels, LANES), 1)
     row = lane % size_y
     few = lax.broadcasted_iota(jnp.int32, (count, LANES), 1)
-    edge = {}
-    for side_z, tile_ref in ((0, zlo_ref), (2, zhi_ref)):
-        cols = slice(0, LANES) if side_z == 0 else slice(LANES, 2 * LANES)
+    for number, tile_ref in enumerate((zlo_ref, zhi_ref)):
         value = jnp.where(
-            lane < area, inputs[0][:, cols], pltpu.roll(inputs[1][:, cols], area, 1)
+            lane < area,
+            pltpu.roll(inputs[0], -number * area % LANES, 1),
+            pltpu.roll(inputs[1], (1 - number) * area % LANES, 1),
         )
         jump = area - size_y + 1
         below = jnp.where(lane >= area, pltpu.roll(value, jump, 1), 0.0)
@@ -507,28 +544,50 @@
             tile = tile_ref[device].astype(F32)
             halves = [
                 jnp.concatenate(
-                    [tile[at : at + span] for at in range(half * span, channels, 2 * span)], axis=0
+                    [tile[s : s + span] for s in range(half * span, channels, 2 * span)], axis=0
                 )
                 for half in range(2)
             ]
-            tiles.append(jnp.where(me == 0, halves[0], halves[1]))
+            tiles.append(jnp.where(is_first, halves[0], halves[1]))
         left = []
         for a in range(3):
             first = pltpu.roll(tiles[0], -a * size_y % LANES, 1)
             second = pltpu.roll(tiles[1], (area - a * size_y) % LANES, 1)
             left.append(jnp.where(few < area, first, jnp.where(few < 2 * area, second, 0.0)))
-        edge[side_z] = lax.dot_general(
+        product = lax.dot_general(
             jnp.concatenate(left, axis=0).astype(BF16),
             right.astype(BF16),
             (((1,), (1,)), ((), ())),
             preferred_element_type=F32,
         )
+        spare = jnp.zeros((3 * count, edge_ref.shape[2] - 3 * channels), F32)
+        edge_ref[number] = jnp.concatenate([product, spare], axis=1)
+
+
+def z_edges(own, other, z_halos, span, sizes, width):
+    channels = own.shape[1]
+    return pl.pallas_call(
+        functools.partial(edge_kernel, span, sizes),
+        in_specs=[VMEM] * 4,
+        out_specs=VMEM,
+        out_shape=jax.ShapeDtypeStruct((2, 3 * channels // 2, width), F32),
+        compiler_params=params(),
+        cost_estimate=cost(2**27, 2**20),
+        name="edges",
+    )(own, other, *z_halos)
+
+
+def finish_kernel(scale, rows, channels, mine_ref, other_ref, edge_ref, part_ref, flat, lines, chunks):
+    count = channels // 2
+    taps = 27 * channels
+    total = mine_ref[...] + other_ref[...]
     blocks = []
     for a in range(3):
         for c in range(3):
             block = total[(3 * a + c) * count : (3 * a + c + 1) * count]
-            blocks.append(block if c == 1 else block + edge[c][a * count : (a + 1) * count])
-    taps = 27 * channels
+            if c != 1:
+                block = block + edge_ref[c // 2, a * count : (a + 1) * count, :]
+            blocks.append(block)
     whole = to_flat(jnp.concatenate(blocks, axis=0) * scale, count, channels, flat)
     pieces = whole.shape[1] // LANES
     for k in range(pieces):
@@ -545,11 +604,10 @@
     part_ref[...] = chunks[...].reshape(part_ref.shape).astype(BF16)
 
 
-def finish(mine, other, z_halos, scale, span, rows, sizes, part_shape):
-    channels = z_halos[0].shape[1]
-    return pl.pallas_call(
-        functools.partial(finish_kernel, scale, span, rows, sizes),
-        in_specs=[VMEM] * 4,
+def finish(mine, other, edge, scale, rows, channels, part_shape):
+    return pl.pallas_call(
+        functools.partial(finish_kernel, scale, rows, channels),
+        in_specs=[VMEM] * 3,
         out_specs=VMEM,
         out_shape=jax.ShapeDtypeStruct(part_shape, BF16),
         scratch_shapes=[
@@ -560,7 +618,42 @@
         compiler_params=params(),
         cost_estimate=cost(2**24, 2**20),
         name="finish",
-    )(mine, other, *z_halos)
+    )(mine, other, edge)
+
+
+def adam_step(master, first, second, weight_grad):
+    new_first = 0.9 * first + 0.1 * weight_grad
+    new_second = 0.999 * second + 0.001 * weight_grad * weight_grad
+    corr_first = 1.0 - (0.9**10) ** 10
+    corr_second = 1.0 - (0.999**10) ** 10
+    update = new_first / corr_first / (jnp.sqrt(new_second / corr_second) + 1e-08) + 0.01 * master
+    return master - 0.05 * update, new_first, new_second
+
+
+def adam_kernel(parts_ref, master_ref, first_ref, second_ref, *out_refs):
+    weight_grad = parts_ref[0].astype(F32)
+    for source in range(1, parts_ref.shape[0]):
+        weight_grad = weight_grad + parts_ref[source].astype(F32)
+    weight_grad = weight_grad[: master_ref.shape[0]]
+    results = adam_step(master_ref[...], first_ref[...], second_ref[...], weight_grad)
+    for out_ref, result in zip(out_refs, (weight_grad, *results)):
+        out_ref[...] = result
+
+
+def adam(parts, *states):
+    share = states[0].shape[0]
+    tiled = [state.reshape(share // LANES, LANES) for state in states]
+    result = jax.ShapeDtypeStruct(tiled[0].shape, F32)
+    outs = pl.pallas_call(
+        adam_kernel,
+        in_specs=[VMEM] * 4,
+        out_specs=[VMEM] * 4,
+        out_shape=[result] * 4,
+        compiler_params=params(),
+        cost_estimate=cost(2**18, 2**18),
+        name="adam",
+    )(parts, *tiled)
+    return tuple(out.reshape(share) for out in outs)
 
 
 def pair_dgrad_kernel(rows, *refs):
@@ -604,9 +697,9 @@
     )(*sources, kernel)
 
 
-def pair_gradients(activations, preact, upstream, master, scale):
+def pair_program(activations, preact, upstream, master, first_moment, second_moment, scale):
     shape = activations.shape
-    channels, size_x, size_y, size_z = shape
+    channels, size_x, size_y, _ = shape
     devices = math.prod(lax.axis_size(a) for a in AXES)
     rows = channels // devices
     span = lax.axis_size("gz") * rows
@@ -614,32 +707,26 @@
     tall = -(-used // 16) * 16
     first, last = faces(preact, upstream)
     x_halos = (shifted(last, {"gx": 1}), shifted(first, {"gx": -1}))
-    inner, planes_x, sent = inner_planes(
-        preact, upstream, activations, master.reshape(used, LANES), (devices, tall, LANES)
+    inner, planes_x, own = pair_inner(preact, upstream, activations, first, last)
+    sent = jnp.pad(master.astype(BF16).reshape(used, LANES), ((0, tall - used), (0, 0)))
+    kernel = lax.all_to_all(
+        jnp.broadcast_to(sent[None], (devices, tall, LANES)), AXES, 0, 0, tiled=True
     )
-    kernel = lax.all_to_all(sent, AXES, 0, 0, tiled=True)
     planes = (x_halos[0], first, inner, last, x_halos[1])
-    own = side(planes, size_z)
+    own = side(x_halos, own)
     other = shifted(own, {"gy": "swap"})
     zlo, zhi = join(own, other)
     z_halos = (shifted(zhi, {"gz": 1}), shifted(zlo, {"gz": -1}))
     sources = (*planes, other, other)
     mine, theirs = pair_wgrad(sources, planes_x, shape, span)
+    theirs, *z_halos = lax.optimization_barrier((theirs, *z_halos))
     theirs = shifted(theirs, {"gy": "swap"})
-    part = finish(
-        mine,
-        theirs,
-        z_halos,
-        scale,
-        span,
-        rows,
-        (size_x, size_y),
-        (devices // 2, tall, LANES),
-    )
+    edge = z_edges(own, other, z_halos, span, (size_x, size_y), mine.shape[1])
+    part = finish(mine, theirs, edge, scale, rows, channels, (devices // 2, tall, LANES))
     part, kernel = lax.optimization_barrier((part, kernel))
     parts = lax.all_to_all(part, ("gx", "gz"), 0, 0, tiled=True)
     grad_input = pair_dgrad((*sources, *z_halos), kernel, shape, rows)
-    return grad_input, parts
+    return grad_input, *adam(parts, master, first_moment, second_moment)
 
 
 def yface_kernel(*refs):
@@ -674,7 +761,7 @@
         low, high = y_halo(refs[5:7], index)
         body = body_of(refs[:5], index)[...]
         whole.append(jnp.concatenate([low.astype(BF16), body, high.astype(BF16)], axis=1))
-    low, high = z_tiles(whole, whole[0].shape[1] // size_z, size_z)
+    low, high = z_tiles(whole, whole[0].shape[1] // size_z, size_z, range(len(whole)))
     zlo_ref[...] = low.astype(BF16)
     zhi_ref[...] = high.astype(BF16)
 
@@ -742,16 +829,15 @@
     )(*sources, kernel)
 
 
-def general_gradients(activations, preact, upstream, master, scale):
+def general_program(activations, preact, upstream, master, first_moment, second_moment, scale):
     shape = activations.shape
     channels, _, _, size_z = shape
     devices = math.prod(lax.axis_size(a) for a in AXES)
     share = master.shape[0]
     first, last = faces(preact, upstream)
     x_halos = (shifted(last, {"gx": 1}), shifted(first, {"gx": -1}))
-    inner, planes_x, sent = inner_planes(
-        preact, upstream, activations, master.reshape(1, share), (devices, 1, share)
-    )
+    inner, planes_x = inner_planes(preact, upstream, activations)
+    sent = jnp.broadcast_to(master.astype(BF16).reshape(1, 1, share), (devices, 1, share))
     kernel = lax.all_to_all(sent, AXES, 0, 0, tiled=True).reshape(channels, 27 * channels)
     planes = (x_halos[0], first, inner, last, x_halos[1])
     y_sent = y_faces(planes, size_z)
@@ -763,7 +849,9 @@
     part, kernel = lax.optimization_barrier((part, kernel))
     parts = lax.all_to_all(part.reshape(devices, 1, share), AXES, 0, 0, tiled=True)
     grad_input = dgrad(sources, kernel, shape)
-    return grad_input, parts
+    weight_grad = jnp.sum(parts.astype(F32), axis=0).reshape(-1)
+    results = adam_step(master, first_moment, second_moment, weight_grad)
+    return grad_input, weight_grad, *results
 
 
 def shifted(value, moves):
@@ -800,16 +888,10 @@
         and 2 * size_x * size_y <= LANES
         and (size_x + 2) * size_y <= LANES
     )
-    gradients = pair_gradients if in_pairs else general_gradients
-    grad_input, parts = gradients(activations, preact, upstream, master, scale)
-    weight_grad = jnp.sum(parts.astype(F32), axis=0).reshape(-1)[:share]
-    new_first = 0.9 * first_moment + 0.1 * weight_grad
-    new_second = 0.999 * second_moment + 0.001 * weight_grad * weight_grad
-    corr_first = 1.0 - (0.9**10) ** 10
-    corr_second = 1.0 - (0.999**10) ** 10
-    update = new_first / corr_first / (jnp.sqrt(new_second / corr_second) + 1e-08) + 0.01 * master
-    new_master = master - 0.05 * update
-    return (grad_input, weight_grad, new_master, new_first, new_second)
+    program = pair_program if in_pairs else general_program
+    return program(
+        activations, preact, upstream, master, first_moment, second_moment, scale
+    )
 
 
 def solution(mesh):

time: 52.1 us -> 53.2 us (1.021)
  waiting for transfers between devices: 8.69 us -> 5.52 us
  starting transfers between devices: 22.3 us -> 24.7 us
  local copies, waits for them, and re-layouts: 1.16 us -> 3.14 us
  other arithmetic: 0.66 us -> 0.01 us
  Pallas kernels: 17.9 us -> 18.5 us
    ppermute x6, waiting for transfers between devices: 6.43 us -> 2.63 us  [shifted(): return lax.ppermute(value, names if len(names) > 1 else names[0], pairs)]
    all_to_all x2, starting transfers between devices: 10.9 us -> 13.3 us  [the longest x1 7.72 us: pair_program(): parts = lax.all_to_all(part, ('gx', 'gz'), 0, 0, tiled=True)]
    unnamed x16 -> x18, local copies, waits for them, and re-layouts: 1.16 us -> 2.39 us
    pallas_call x3 -> x5, Pallas kernels: 6.78 us -> 7.74 us  [the longest x1 4.97 us: pair_inner(): pl.pallas_call(pair_inner_kernel, in_specs=[HBM] * 3 + [VMEM] * 2, out_sp...]
    broadcast_in_dim x0 -> x1, local copies, waits for them, and re-layouts: none -> 0.74 us  [pair_program(): jnp.broadcast_to(sent[None], (devices, tall, LANES))]
    sub x1 -> x0, other arithmetic: 0.64 us -> none  [local(): new_master = master - 0.05 * update]
    all_to_all x2, waiting for transfers between devices: 2.26 us -> 2.89 us  [the longest x1 2.89 us: pair_program(): parts = lax.all_to_all(part, ('gx', 'gz'), 0, 0, tiled=True)]
  transfers between devices with their start and end apart: 8 -> 8, of which waited for: 4 -> 3; matrix products, arithmetic and copies ran while one was open for 0% -> 1% of each run, Pallas kernels for 30% -> 30%
where the time goes in v1:
time: 53.2 us; the launch traced here: 52.7 us
  starting transfers between devices  24.7 us (46%)
  Pallas kernels  18.5 us (35%)
  waiting for transfers between devices  5.52 us (10%)
  local copies, waits for them, and re-layouts  3.14 us (6%)
  between operations  0.86 us (2%)
    ppermute x6, starting transfers between devices, shifted(): return lax.ppermute(value, names if len(names) > 1 else names[0], pairs)  11.4 us
    all_to_all x1, starting transfers between devices, pair_program(): parts = lax.all_to_all(part, ('gx', 'gz'), 0, 0, tiled=True)  7.72 us
    all_to_all x1, starting transfers between devices, pair_program(): lax.all_to_all(jnp.broadcast_to(sent[None], (devices, tall, LANES)), AXES...  5.6 us
    pallas_call x1, Pallas kernels, pair_dgrad(): pl.pallas_call(functools.partial(pair_dgrad_kernel, rows), in_specs=[VMEM...  5.25 us
    pallas_call x1, Pallas kernels, pair_inner(): pl.pallas_call(pair_inner_kernel, in_specs=[HBM] * 3 + [VMEM] * 2, out_sp...  4.97 us
    pallas_call x1, Pallas kernels, pair_wgrad(): pl.pallas_call(functools.partial(pair_wgrad_kernel, span), in_specs=[VMEM...  3.6 us
    all_to_all x1, waiting for transfers between devices, pair_program(): parts = lax.all_to_all(part, ('gx', 'gz'), 0, 0, tiled=True)  2.89 us
    ppermute x6, waiting for transfers between devices, shifted(): return lax.ppermute(value, names if len(names) > 1 else names[0], pairs)  2.63 us
  transfers between devices with their start and end apart: 8, of which 3 were waited for; matrix products, arithmetic and copies ran while one was open for 1% of the time, Pallas kernels for 30%

profile of v1, /device:TPU:0, one launch (start us, length us, event | category | flops | bytes accessed | tf_op | source)
XLA Modules:
  0.0 52.7 jit_solution(5083451745726506586)
XLA Ops:
  0.6 1.9 %faces.1 = (bf16[64,1024]{1,0:T(8,128)(2,1)}, bf16[64,1024]{1,0:T(8,128)(2,1)}) custom-call(bf16[64,8,8,128]{3,2,1,0:T(8,128)(2,1)} %refs_0_.1, bf16[64,8,8,128]{3,2,1,0:T(8,128)(2,1)} %refs_1_.1), custom_call_target="tpu_custom_call" | custom-call | bytes 1048576 | tf_op jit(solution)/shard_map/faces/pallas_call | solution.py:64
  2.5 4.8 %collective-permute-start = (bf16[64,1024]{1,0:T(8,128)(2,1)}, bf16[64,1024]{1,0:T(8,128)(2,1)S(1)}, u32[]{:S(2)}, u32[]{:S(2)}) collective-permute-start(bf16[64,1024]{1,0:T(8,128)(2,1)} %get-tuple-element.23.refs_4_.refs_3_), channel_id=1, source_target_pairs={{0,8},{8,16},{16,24},{1,9},{9,17},{17,25},{2,10},{10,18},{18,26},{... | collective-permute-start | bytes 393224 | tf_op jit(solution)/shard_map/ppermute | solution.py:875
  7.4 1.3 %collective-permute-start.1 = (bf16[64,1024]{1,0:T(8,128)(2,1)}, bf16[64,1024]{1,0:T(8,128)(2,1)S(1)}, u32[]{:S(2)}, u32[]{:S(2)}) collective-permute-start(bf16[64,1024]{1,0:T(8,128)(2,1)} %get-tuple-element.24.refs_3_.refs_1_), channel_id=1, source_target_pairs={{8,0},{16,8},{24,16},{9,1},{17,9},{25,17},{10,2},{18,10},{26,18},{... | collective-permute-start | bytes 393224 | tf_op jit(solution)/shard_map/ppermute | solution.py:875
  8.7 5.0 %inner.1 = (bf16[6,64,1024]{2,1,0:T(8,128)(2,1)}, bf16[8,64,1024]{2,1,0:T(8,128)(2,1)}, bf16[11,64,128]{2,1,0:T(8,128)(2,1)}) custom-call(bf16[64,8,8,128]{3,2,1,0:T(8,128)(2,1)} %refs_0_.1, bf16[64,8,8,128]{3,2,1,0:T(8,128)(2,1)} %refs_1_.1, bf16[64,8,8,128]{3,2,1,0:T(8,128)(2,1)} %refs_2_.1, bf16[64,1024]{1,0:T(8,128)(2,1)} %get-tuple-element.24.refs_3_.refs_1_, ...), custom_call_target="tpu_custom_call" | custom-call | bytes 6291456 | tf_op jit(solution)/shard_map/inner/pallas_call | solution.py:421
  13.7 0.0 collective-permute-done.xlo_ref.refs_0_
  13.7 1.4 %collective-permute-done.1.xhi_ref.refs_4_ = bf16[64,1024]{1,0:T(8,128)(2,1)S(1)} collective-permute-done((bf16[64,1024]{1,0:T(8,128)(2,1)}, bf16[64,1024]{1,0:T(8,128)(2,1)S(1)}, u32[]{:S(2)}, u32[]{:S(2)}) %collective-permute-start.1) | collective-permute-done | bytes 131104 | tf_op jit(solution)/shard_map/ppermute | solution.py:875
  15.1 0.9 %copy-done = bf16[11,64,128]{2,1,0:T(8,128)(2,1)S(1)} copy-done((bf16[11,64,128]{2,1,0:T(8,128)(2,1)S(1)}, bf16[11,64,128]{2,1,0:T(8,128)(2,1)}, u32[]{:S(2)}) %copy-start) | copy-done | bytes 180248
  16.0 0.3 side.1.own_ref
  16.3 0.1 collective-permute-start.2
  16.4 0.3 copy-done.3
  16.7 0.7 %broadcast_in_dim.2 = bf16[32,32,128]{2,1,0:T(8,128)(2,1)} broadcast(bf16[32,128]{1,0:T(8,128)(2,1)S(1)} %pad.4), dimensions={1,2} | broadcast | bytes 270336 | tf_op jit(solution)/shard_map/broadcast_in_dim | solution.py:713
  17.5 5.6 %all-to-all-start = ((bf16[32,32,128]{2,1,0:T(8,128)(2,1)}), bf16[32,32,128]{2,1,0:T(8,128)(2,1)S(1)}, u32[]{:S(2)}, u32[]{:S(2)}) async-start(bf16[32,32,128]{2,1,0:T(8,128)(2,1)} %broadcast_in_dim.2), calls=%async_computation | async-start | bytes 524288 | tf_op jit(solution)/shard_map/all_to_all | solution.py:712
  23.1 0.0 collective-permute-done.2.refs_5_.refs_6_.other_ref
  23.1 3.8 %collective-permute-start.3 = (bf16[2,64,128]{2,1,0:T(8,128)(2,1)S(1)}, bf16[2,64,128]{2,1,0:T(8,128)(2,1)S(1)}, u32[]{:S(2)}, u32[]{:S(2)}) collective-permute-start(bf16[2,64,128]{2,1,0:T(8,128)(2,1)S(1)} %get-tuple-element.29), channel_id=1, source_target_pairs={{0,1},{1,2},{2,3},{4,5},{5,6},{6,7},{8,9},{9,10},{10,11},{12,13},{... | collective-permute-start | bytes 98312 | tf_op jit(solution)/shard_map/ppermute | solution.py:875
  27.0 1.3 %collective-permute-start.4 = (bf16[2,64,128]{2,1,0:T(8,128)(2,1)S(1)}, bf16[2,64,128]{2,1,0:T(8,128)(2,1)S(1)}, u32[]{:S(2)}, u32[]{:S(2)}) collective-permute-start(bf16[2,64,128]{2,1,0:T(8,128)(2,1)S(1)} %get-tuple-element.30), channel_id=1, source_target_pairs={{1,0},{2,1},{3,2},{5,4},{6,5},{7,6},{9,8},{10,9},{11,10},{13,12},{... | collective-permute-start | bytes 98312 | tf_op jit(solution)/shard_map/ppermute | solution.py:875
  28.3 0.0 copy-done.6
  28.3 0.0 copy-done.1
  28.3 1.1 %copy-done.7 = bf16[6,64,1024]{2,1,0:T(8,128)(2,1)S(1)} copy-done((bf16[6,64,1024]{2,1,0:T(8,128)(2,1)S(1)}, bf16[6,64,1024]{2,1,0:T(8,128)(2,1)}, u32[]{:S(2)}) %copy-start.7) | copy-done | bytes 786456
  29.4 3.6 %wgrad.1 = (f32[288,256]{1,0:T(8,128)S(1)}, f32[288,256]{1,0:T(8,128)S(1)}) custom-call(bf16[64,1024]{1,0:T(8,128)(2,1)S(1)} %collective-permute-done.xlo_ref.refs_0_, bf16[64,1024]{1,0:T(8,128)(2,1)S(1)} %copy-done.1, bf16[6,64,1024]{2,1,0:T(8,128)(2,1)S(1)} %copy-done.7, bf16[64,1024]{1,0:T(8,128)(2,1)S(1)} %copy-done.2, ...), custom_call_target="tpu_custom_call" | custom-call | flops 2264924160 | bytes 4194304 | tf_op jit(solution)/shard_map/wgrad/pallas_call | solution.py:501
  33.0 0.0 collective-permute-done.3.zlo_ref.refs_7_
  33.0 0.0 collective-permute-done.4.zhi_ref.refs_8_
  33.1 0.1 collective-permute-start.5
  33.1 0.4 edges.1.edge_ref
  33.5 1.2 %collective-permute-done.5.other_ref = f32[288,256]{1,0:T(8,128)S(1)} collective-permute-done((f32[288,256]{1,0:T(8,128)S(1)}, f32[288,256]{1,0:T(8,128)S(1)}, u32[]{:S(2)}, u32[]{:S(2)}) %collective-permute-start.5) | collective-permute-done | bytes 294944 | tf_op jit(solution)/shard_map/ppermute | solution.py:875
  34.7 1.4 %finish.1 = bf16[16,32,128]{2,1,0:T(8,128)(2,1)} custom-call(f32[288,256]{1,0:T(8,128)S(1)} %get-tuple-element.33.mine_ref, f32[288,256]{1,0:T(8,128)S(1)} %collective-permute-done.5.other_ref, f32[2,96,256]{2,1,0:T(8,128)S(1)} %edges.1.edge_ref), custom_call_target="tpu_custom_call" | custom-call | flops 16777216 | bytes 1048576 | tf_op jit(solution)/shard_map/finish/pallas_call | solution.py:608
  36.1 0.0 all-to-all-done.refs_9_
  36.1 7.7 %all-to-all-start.1 = ((bf16[16,32,128]{2,1,0:T(8,128)(2,1)}), bf16[16,32,128]{2,1,0:T(8,128)(2,1)S(1)}, u32[]{:S(2)}, u32[]{:S(2)}) async-start(bf16[16,32,128]{2,1,0:T(8,128)(2,1)} %finish.1), calls=%async_computation.1 | async-start | bytes 262144 | tf_op jit(solution)/shard_map/all_to_all | solution.py:727
  43.9 0.0 copy-start.4
  43.9 0.0 copy-start.5
  43.9 5.2 %dgrad.1 = bf16[64,8,8,128]{3,2,1,0:T(8,128)(2,1)} custom-call(bf16[64,1024]{1,0:T(8,128)(2,1)S(1)} %collective-permute-done.xlo_ref.refs_0_, bf16[64,1024]{1,0:T(8,128)(2,1)S(1)} %copy-done.1, bf16[6,64,1024]{2,1,0:T(8,128)(2,1)S(1)} %copy-done.8, bf16[64,1024]{1,0:T(8,128)(2,1)S(1)} %copy-done.2, ...), custom_call_target="tpu_custom_call" | custom-call | flops 2415919104 | bytes 4194304 | tf_op jit(solution)/shard_map/dgrad/pallas_call | solution.py:684
  49.2 2.9 %all-to-all-done.1.parts_ref = bf16[16,32,128]{2,1,0:T(8,128)(2,1)S(1)} async-done(((bf16[16,32,128]{2,1,0:T(8,128)(2,1)}), bf16[16,32,128]{2,1,0:T(8,128)(2,1)S(1)}, u32[]{:S(2)}, u32[]{:S(2)}) %all-to-all-start.1) | async-done | bytes 131104 | tf_op jit(solution)/shard_map/all_to_all | solution.py:727
  52.1 0.7 %adam.1 = (f32[27,128]{1,0:T(8,128)}, f32[27,128]{1,0:T(8,128)}, f32[27,128]{1,0:T(8,128)}, f32[27,128]{1,0:T(8,128)}) custom-call(bf16[16,32,128]{2,1,0:T(8,128)(2,1)S(1)} %all-to-all-done.1.parts_ref, f32[27,128]{1,0:T(8,128)S(1)} %bitcast.9, f32[27,128]{1,0:T(8,128)S(1)} %bitcast.10, f32[27,128]{1,0:T(8,128)S(1)} %bitcast.11), custom_call_target="tpu_custom_call" | custom-call | flops 262144 | bytes 262144 | tf_op jit(solution)/shard_map/adam/pallas_call | solution.py:647
  (14 shorter events, 0.1 us)
Async XLA Ops:
  2.5 11.1 %collective-permute-start = (bf16[64,1024]{1,0:T(8,128)(2,1)}, bf16[64,1024]{1,0:T(8,128)(2,1)S(1)}, u32[]{:S(2)}, u32[]{:S(2)}) collective-permute-start(bf16[64,1024]{1,0:T(8,128)(2,1)} %get-tuple-element.23.refs_4_.refs_3_), channel_id=1, source_target_pairs={{0,8},{8,16},{16,24},{1,9},{9,17},{17,25},{2,10},{10,18},{18,26},{... | collective-permute-start | bytes 393224 | tf_op jit(solution)/shard_map/ppermute | solution.py:875
  7.4 7.7 %collective-permute-start.1 = (bf16[64,1024]{1,0:T(8,128)(2,1)}, bf16[64,1024]{1,0:T(8,128)(2,1)S(1)}, u32[]{:S(2)}, u32[]{:S(2)}) collective-permute-start(bf16[64,1024]{1,0:T(8,128)(2,1)} %get-tuple-element.24.refs_3_.refs_1_), channel_id=1, source_target_pairs={{8,0},{16,8},{24,16},{9,1},{17,9},{25,17},{10,2},{18,10},{26,18},{... | collective-permute-start | bytes 393224 | tf_op jit(solution)/shard_map/ppermute | solution.py:875
  15.1 0.9 %copy-start = (bf16[11,64,128]{2,1,0:T(8,128)(2,1)S(1)}, bf16[11,64,128]{2,1,0:T(8,128)(2,1)}, u32[]{:S(2)}) copy-start(bf16[11,64,128]{2,1,0:T(8,128)(2,1)} %get-tuple-element.26.own_ref) | copy-start | bytes 540676
  16.0 0.7 %copy-start.3 = (f32[3456]{0:T(1024)S(1)}, f32[3456]{0:T(1024)}, u32[]{:S(2)}) copy-start(f32[3456]{0:T(1024)} %param.9) | copy-start | bytes 41476
  16.0 12.2 %copy-start.6 = (bf16[8,64,1024]{2,1,0:T(8,128)(2,1)S(1)}, bf16[8,64,1024]{2,1,0:T(8,128)(2,1)}, u32[]{:S(2)}) copy-start(bf16[8,64,1024]{2,1,0:T(8,128)(2,1)} %get-tuple-element.27.refs_7_) | copy-start | bytes 3145732
  16.3 6.8 %collective-permute-start.2 = (bf16[13,64,128]{2,1,0:T(8,128)(2,1)S(1)}, bf16[13,64,128]{2,1,0:T(8,128)(2,1)S(1)}, u32[]{:S(2)}, u32[]{:S(2)}) collective-permute-start(bf16[13,64,128]{2,1,0:T(8,128)(2,1)S(1)} %side.1.own_ref), channel_id=1, source_target_pairs={{0,4},{4,0},{1,5},{5,1},{2,6},{6,2},{3,7},{7,3},{8,12},{12,8},{9,1... | collective-permute-start | bytes 638984 | tf_op jit(solution)/shard_map/ppermute | solution.py:875
  17.5 18.7 %all-to-all-start = ((bf16[32,32,128]{2,1,0:T(8,128)(2,1)}), bf16[32,32,128]{2,1,0:T(8,128)(2,1)S(1)}, u32[]{:S(2)}, u32[]{:S(2)}) async-start(bf16[32,32,128]{2,1,0:T(8,128)(2,1)} %broadcast_in_dim.2), calls=%async_computation | async-start | bytes 524288 | tf_op jit(solution)/shard_map/all_to_all | solution.py:712
  23.1 5.2 %copy-start.1 = (bf16[64,1024]{1,0:T(8,128)(2,1)S(1)}, bf16[64,1024]{1,0:T(8,128)(2,1)}, u32[]{:S(2)}) copy-start(bf16[64,1024]{1,0:T(8,128)(2,1)} %get-tuple-element.24.refs_3_.refs_1_) | copy-start | bytes 393220
  23.1 5.2 %copy-start.2 = (bf16[64,1024]{1,0:T(8,128)(2,1)S(1)}, bf16[64,1024]{1,0:T(8,128)(2,1)}, u32[]{:S(2)}) copy-start(bf16[64,1024]{1,0:T(8,128)(2,1)} %get-tuple-element.23.refs_4_.refs_3_) | copy-start | bytes 393220
  23.1 9.9 %collective-permute-start.3 = (bf16[2,64,128]{2,1,0:T(8,128)(2,1)S(1)}, bf16[2,64,128]{2,1,0:T(8,128)(2,1)S(1)}, u32[]{:S(2)}, u32[]{:S(2)}) collective-permute-start(bf16[2,64,128]{2,1,0:T(8,128)(2,1)S(1)} %get-tuple-element.29), channel_id=1, source_target_pairs={{0,1},{1,2},{2,3},{4,5},{5,6},{6,7},{8,9},{9,10},{10,11},{12,13},{... | collective-permute-start | bytes 98312 | tf_op jit(solution)/shard_map/ppermute | solution.py:875
  27.0 6.1 %collective-permute-start.4 = (bf16[2,64,128]{2,1,0:T(8,128)(2,1)S(1)}, bf16[2,64,128]{2,1,0:T(8,128)(2,1)S(1)}, u32[]{:S(2)}, u32[]{:S(2)}) collective-permute-start(bf16[2,64,128]{2,1,0:T(8,128)(2,1)S(1)} %get-tuple-element.30), channel_id=1, source_target_pairs={{1,0},{2,1},{3,2},{5,4},{6,5},{7,6},{9,8},{10,9},{11,10},{13,12},{... | collective-permute-start | bytes 98312 | tf_op jit(solution)/shard_map/ppermute | solution.py:875
  28.3 1.1 %copy-start.7 = (bf16[6,64,1024]{2,1,0:T(8,128)(2,1)S(1)}, bf16[6,64,1024]{2,1,0:T(8,128)(2,1)}, u32[]{:S(2)}) copy-start(bf16[6,64,1024]{2,1,0:T(8,128)(2,1)} %get-tuple-element.25.refs_2_) | copy-start | bytes 2359300
  33.1 10.8 %copy-start.8 = (bf16[6,64,1024]{2,1,0:T(8,128)(2,1)S(1)}, bf16[6,64,1024]{2,1,0:T(8,128)(2,1)}, u32[]{:S(2)}) copy-start(bf16[6,64,1024]{2,1,0:T(8,128)(2,1)} %get-tuple-element.25.refs_2_) | copy-start | bytes 2359300
  33.1 1.6 %collective-permute-start.5 = (f32[288,256]{1,0:T(8,128)S(1)}, f32[288,256]{1,0:T(8,128)S(1)}, u32[]{:S(2)}, u32[]{:S(2)}) collective-permute-start(f32[288,256]{1,0:T(8,128)S(1)} %get-tuple-element.34), channel_id=1, source_target_pairs={{0,4},{4,0},{1,5},{5,1},{2,6},{6,2},{3,7},{7,3},{8,12},{12,8},{9,1... | collective-permute-start | bytes 884744 | tf_op jit(solution)/shard_map/ppermute | solution.py:875
  36.1 15.9 %all-to-all-start.1 = ((bf16[16,32,128]{2,1,0:T(8,128)(2,1)}), bf16[16,32,128]{2,1,0:T(8,128)(2,1)S(1)}, u32[]{:S(2)}, u32[]{:S(2)}) async-start(bf16[16,32,128]{2,1,0:T(8,128)(2,1)} %finish.1), calls=%async_computation.1 | async-start | bytes 262144 | tf_op jit(solution)/shard_map/all_to_all | solution.py:727
  43.9 8.2 %copy-start.4 = (f32[3456]{0:T(1024)S(1)}, f32[3456]{0:T(1024)}, u32[]{:S(2)}) copy-start(f32[3456]{0:T(1024)} %param.10) | copy-start | bytes 41476
  43.9 8.2 %copy-start.5 = (f32[3456]{0:T(1024)S(1)}, f32[3456]{0:T(1024)}, u32[]{:S(2)}) copy-start(f32[3456]{0:T(1024)} %param.11) | copy-start | bytes 41476

commit v2 on v1

--- a/solution.py
+++ b/solution.py
@@ -14,7 +14,8 @@
 HBM = pl.BlockSpec(memory_space=pltpu.HBM)
 F32 = jnp.float32
 BF16 = jnp.bfloat16
-ALL_VMEM = 64 * 2**20
+FACES_VMEM = 56_200_000
+INNER_VMEM = 53_000_000
 
 
 def params(limit=24 * 2**20):
@@ -72,7 +73,7 @@
             pltpu.VMEM((2, channels * size_y, size_z), F32),
             pltpu.SemaphoreType.DMA((4,)),
         ],
-        compiler_params=params(ALL_VMEM - 900_000),
+        compiler_params=params(FACES_VMEM),
         cost_estimate=cost(0, 2**20),
         name="faces",
     )(preact, upstream)
@@ -143,7 +144,7 @@
         out_specs=[VMEM] * 2,
         out_shape=inner_outputs(*shape),
         scratch_shapes=inner_scratch(*shape),
-        compiler_params=params(ALL_VMEM - 3_600_000),
+        compiler_params=params(INNER_VMEM),
         cost_estimate=cost(0, 6 * 2**20),
         name="inner",
     )(preact, upstream, activations)
@@ -399,9 +400,21 @@
 
 
 def pair_inner_kernel(*refs):
-    first_ref, last_ref = refs[3:5]
-    g_ref, x_ref, side_ref = refs[5:8]
-    read_inner(*refs[:3], g_ref, x_ref, *refs[8:])
+    first_ref, last_ref, m_ref = refs[3:6]
+    g_ref, x_ref, side_ref, sent_ref = refs[6:10]
+    tile_ref, tile_sems = refs[15:]
+    share = m_ref[...]
+    height = tile_ref.shape[0] - share.shape[0]
+    if height:
+        share = jnp.concatenate([share, jnp.zeros((height, share.shape[1]), F32)], axis=0)
+    tile_ref[...] = share.astype(BF16)
+    copies = [
+        pltpu.make_async_copy(tile_ref, sent_ref.at[device], tile_sems.at[device])
+        for device in range(sent_ref.shape[0])
+    ]
+    for copy in copies:
+        copy.start()
+    read_inner(*refs[:3], g_ref, x_ref, *refs[10:15])
     size_z = side_ref.shape[-1]
     size_x, channels, plane = x_ref.shape
     size_y = plane // size_z
@@ -413,22 +426,28 @@
     side_ref[size_x + 1] = high.astype(BF16)
     low, high = z_tiles([x_ref[x] for x in range(size_x)], size_y, size_z, range(size_x))
     side_ref[size_x + 2] = (low + pltpu.roll(high, size_x * size_y, 1)).astype(BF16)
-
-
-def pair_inner(preact, upstream, activations, first, last):
+    for copy in copies:
+        copy.wait()
+
+
+def pair_inner(preact, upstream, activations, first, last, share, sent_shape):
     shape = preact.shape
     channels, size_x, _, size_z = shape
     return pl.pallas_call(
         pair_inner_kernel,
-        in_specs=[HBM] * 3 + [VMEM] * 2,
-        out_specs=[VMEM] * 3,
+        in_specs=[HBM] * 3 + [VMEM] * 3,
+        out_specs=[VMEM] * 3 + [HBM],
         out_shape=inner_outputs(*shape)
-        + [jax.ShapeDtypeStruct((size_x + 3, channels, size_z), BF16)],
-        scratch_shapes=inner_scratch(*shape),
-        compiler_params=params(ALL_VMEM - 3_600_000),
+        + [
+            jax.ShapeDtypeStruct((size_x + 3, channels, size_z), BF16),
+            jax.ShapeDtypeStruct(sent_shape, BF16),
+        ],
+        scratch_shapes=inner_scratch(*shape)
+        + [pltpu.VMEM(sent_shape[1:], BF16), pltpu.SemaphoreType.DMA((sent_shape[0],))],
+        compiler_params=params(INNER_VMEM),
         cost_estimate=cost(0, 6 * 2**20),
         name="inner",
-    )(preact, upstream, activations, first, last)
+    )(preact, upstream, activations, first, last, share)
 
 
 def side_kernel(xlo_ref, xhi_ref, own_ref, sent_ref):
@@ -457,21 +476,33 @@
     )(*x_halos, own)
 
 
-def join_kernel(own_ref, other_ref, low_ref, high_ref):
+def both_columns(is_first, own, other, number, area):
+    first = jnp.where(is_first, own, other).astype(F32)
+    second = jnp.where(is_first, other, own).astype(F32)
+    lane = lax.broadcasted_iota(jnp.int32, first.shape, 1)
+    return jnp.where(
+        lane < area,
+        pltpu.roll(first, -number * area % LANES, 1),
+        pltpu.roll(second, (1 - number) * area % LANES, 1),
+    )
+
+
+def join_kernel(area, own_ref, other_ref, low_ref, high_ref):
     at = own_ref.shape[0] - 3
     me = lax.axis_index("gy")
     for k, out_ref in enumerate((low_ref, high_ref)):
         out_ref[me] = own_ref[at + k]
         out_ref[1 - me] = other_ref[at + k]
-
-
-def join(own, other):
-    tiles = jax.ShapeDtypeStruct((2, *own.shape[1:]), BF16)
-    return pl.pallas_call(
-        join_kernel,
+    own, other = own_ref[at + 2].astype(F32), other_ref[at + 2].astype(F32)
+    high_ref[2] = both_columns(me == 0, own, other, 1, area).astype(BF16)
+
+
+def join(own, other, area):
+    return pl.pallas_call(
+        functools.partial(join_kernel, area),
         in_specs=[VMEM] * 2,
         out_specs=[VMEM] * 2,
-        out_shape=[tiles, tiles],
+        out_shape=[jax.ShapeDtypeStruct((n, *own.shape[1:]), BF16) for n in (2, 3)],
         compiler_params=params(),
         cost_estimate=cost(0, 2**17),
         name="join",
@@ -510,32 +541,27 @@
     )(*sources, planes_x)
 
 
-def edge_kernel(span, sizes, own_ref, other_ref, zlo_ref, zhi_ref, edge_ref):
+def edge_kernel(span, sizes, own_ref, other_ref, ztiles_ref, below_ref, edge_ref):
     size_x, size_y = sizes
-    channels = zlo_ref.shape[1]
+    channels = below_ref.shape[1]
     count = channels // 2
     area = size_x * size_y
     is_first = lax.axis_index("gy") == 0
     at = own_ref.shape[0] - 1
     own, other = own_ref[at].astype(F32), other_ref[at].astype(F32)
-    inputs = (jnp.where(is_first, own, other), jnp.where(is_first, other, own))
+    columns = (both_columns(is_first, own, other, 0, area), below_ref[2].astype(F32))
     lane = lax.broadcasted_iota(jnp.int32, (channels, LANES), 1)
     row = lane % size_y
     few = lax.broadcasted_iota(jnp.int32, (count, LANES), 1)
-    for number, tile_ref in enumerate((zlo_ref, zhi_ref)):
-        value = jnp.where(
-            lane < area,
-            pltpu.roll(inputs[0], -number * area % LANES, 1),
-            pltpu.roll(inputs[1], (1 - number) * area % LANES, 1),
-        )
+    for number, (tile_ref, value) in enumerate(zip((below_ref, ztiles_ref), columns)):
         jump = area - size_y + 1
-        below = jnp.where(lane >= area, pltpu.roll(value, jump, 1), 0.0)
-        above = jnp.where(lane < area, pltpu.roll(value, LANES - jump, 1), 0.0)
+        before = jnp.where(lane >= area, pltpu.roll(value, jump, 1), 0.0)
+        after = jnp.where(lane < area, pltpu.roll(value, LANES - jump, 1), 0.0)
         right = jnp.concatenate(
             [
-                jnp.where(row > 0, pltpu.roll(value, 1, 1), below),
+                jnp.where(row > 0, pltpu.roll(value, 1, 1), before),
                 value,
-                jnp.where(row < size_y - 1, pltpu.roll(value, LANES - 1, 1), above),
+                jnp.where(row < size_y - 1, pltpu.roll(value, LANES - 1, 1), after),
             ],
             axis=0,
         )
@@ -564,7 +590,7 @@
         edge_ref[number] = jnp.concatenate([product, spare], axis=1)
 
 
-def z_edges(own, other, z_halos, span, sizes, width):
+def z_edges(own, other, ztiles, below, span, sizes, width):
     channels = own.shape[1]
     return pl.pallas_call(
         functools.partial(edge_kernel, span, sizes),
@@ -574,7 +600,7 @@
         compiler_params=params(),
         cost_estimate=cost(2**27, 2**20),
         name="edges",
-    )(own, other, *z_halos)
+    )(own, other, ztiles, below)
 
 
 def finish_kernel(scale, rows, channels, mine_ref, other_ref, edge_ref, part_ref, flat, lines, chunks):
@@ -707,25 +733,32 @@
     tall = -(-used // 16) * 16
     first, last = faces(preact, upstream)
     x_halos = (shifted(last, {"gx": 1}), shifted(first, {"gx": -1}))
-    inner, planes_x, own = pair_inner(preact, upstream, activations, first, last)
-    sent = jnp.pad(master.astype(BF16).reshape(used, LANES), ((0, tall - used), (0, 0)))
-    kernel = lax.all_to_all(
-        jnp.broadcast_to(sent[None], (devices, tall, LANES)), AXES, 0, 0, tiled=True
+    inner, planes_x, own, sent = pair_inner(
+        preact,
+        upstream,
+        activations,
+        first,
+        last,
+        master.reshape(used, LANES),
+        (devices, tall, LANES),
     )
+    kernel = lax.all_to_all(sent, AXES, 0, 0, tiled=True)
     planes = (x_halos[0], first, inner, last, x_halos[1])
     own = side(x_halos, own)
     other = shifted(own, {"gy": "swap"})
-    zlo, zhi = join(own, other)
-    z_halos = (shifted(zhi, {"gz": 1}), shifted(zlo, {"gz": -1}))
+    zlo, zhi = join(own, other, size_x * size_y)
+    below = shifted(zhi, {"gz": 1})
     sources = (*planes, other, other)
     mine, theirs = pair_wgrad(sources, planes_x, shape, span)
-    theirs, *z_halos = lax.optimization_barrier((theirs, *z_halos))
+    theirs, below = lax.optimization_barrier((theirs, below))
     theirs = shifted(theirs, {"gy": "swap"})
-    edge = z_edges(own, other, z_halos, span, (size_x, size_y), mine.shape[1])
+    zlo, below = lax.optimization_barrier((zlo, below))
+    above = shifted(zlo, {"gz": -1})
+    edge = z_edges(own, other, zlo, below, span, (size_x, size_y), mine.shape[1])
     part = finish(mine, theirs, edge, scale, rows, channels, (devices // 2, tall, LANES))
     part, kernel = lax.optimization_barrier((part, kernel))
     parts = lax.all_to_all(part, ("gx", "gz"), 0, 0, tiled=True)
-    grad_input = pair_dgrad((*sources, *z_halos), kernel, shape, rows)
+    grad_input = pair_dgrad((*sources, below, above), kernel, shape, rows)
     return grad_input, *adam(parts, master, first_moment, second_moment)
 
 

time: 53.2 us -> 48.6 us (0.914)
  local copies, waits for them, and re-layouts: 3.14 us -> 0.02 us
  Pallas kernels: 18.5 us -> 16.8 us
  starting transfers between devices: 24.7 us -> 25.3 us
    unnamed x18 -> x6, local copies, waits for them, and re-layouts: 2.39 us -> 0.02 us
    pallas_call x2, Pallas kernels: 4.98 us -> 3.89 us  [the longest x1 3.8 us: pair_inner(): pl.pallas_call(pair_inner_kernel, in_specs=[HBM] * 3 + [VMEM] * 3, out_sp...]
    all_to_all x1, starting transfers between devices: 7.72 us -> 8.78 us  [pair_program(): parts = lax.all_to_all(part, ('gx', 'gz'), 0, 0, tiled=True)]
    broadcast_in_dim x1 -> x0, local copies, waits for them, and re-layouts: 0.74 us -> none  [pair_program(): jnp.broadcast_to(sent[None], (devices, tall, LANES))]
    pallas_call x1, Pallas kernels: 1.9 us -> 1.26 us  [faces(): pl.pallas_call(face_kernel, in_specs=[HBM, HBM], out_specs=[VMEM] * 2, ou...]
  transfers between devices with their start and end apart: 8 -> 8, of which waited for: 3 -> 2; matrix products, arithmetic and copies ran while one was open for 1% -> 0% of each run, Pallas kernels for 30% -> 30%
where the time goes in v2:
time: 48.6 us; the launch traced here: 48.2 us
  starting transfers between devices  25.3 us (52%)
  Pallas kernels  16.8 us (35%)
  waiting for transfers between devices  5.35 us (11%)
  between operations  0.8 us (2%)
    ppermute x6, starting transfers between devices, shifted(): return lax.ppermute(value, names if len(names) > 1 else names[0], pairs)  11.2 us
    all_to_all x1, starting transfers between devices, pair_program(): parts = lax.all_to_all(part, ('gx', 'gz'), 0, 0, tiled=True)  8.78 us
    all_to_all x1, starting transfers between devices, pair_program(): kernel = lax.all_to_all(sent, AXES, 0, 0, tiled=True)  5.27 us
    pallas_call x1, Pallas kernels, pair_dgrad(): pl.pallas_call(functools.partial(pair_dgrad_kernel, rows), in_specs=[VMEM...  5.25 us
    pallas_call x1, Pallas kernels, pair_inner(): pl.pallas_call(pair_inner_kernel, in_specs=[HBM] * 3 + [VMEM] * 3, out_sp...  3.8 us
    pallas_call x1, Pallas kernels, pair_wgrad(): pl.pallas_call(functools.partial(pair_wgrad_kernel, span), in_specs=[VMEM...  3.6 us
    all_to_all x1, waiting for transfers between devices, pair_program(): parts = lax.all_to_all(part, ('gx', 'gz'), 0, 0, tiled=True)  2.98 us
    ppermute x6, waiting for transfers between devices, shifted(): return lax.ppermute(value, names if len(names) > 1 else names[0], pairs)  2.37 us
  transfers between devices with their start and end apart: 8, of which 2 were waited for; matrix products, arithmetic and copies ran while one was open for 0% of the time, Pallas kernels for 30%

profile of v2, /device:TPU:0, one launch (start us, length us, event | category | flops | bytes accessed | tf_op | source)
XLA Modules:
  0.0 48.2 jit_solution(11204623854204105842)
XLA Ops:
  0.6 0.0 copy-start
  0.6 1.3 %faces.1 = (bf16[64,1024]{1,0:T(8,128)(2,1)S(1)}, bf16[64,1024]{1,0:T(8,128)(2,1)S(1)}) custom-call(bf16[64,8,8,128]{3,2,1,0:T(8,128)(2,1)} %refs_0_.1, bf16[64,8,8,128]{3,2,1,0:T(8,128)(2,1)} %refs_1_.1), custom_call_target="tpu_custom_call" | custom-call | bytes 1048576 | tf_op jit(solution)/shard_map/faces/pallas_call | solution.py:65
  1.9 4.8 %collective-permute-start = (bf16[64,1024]{1,0:T(8,128)(2,1)S(1)}, bf16[64,1024]{1,0:T(8,128)(2,1)S(1)}, u32[]{:S(2)}, u32[]{:S(2)}) collective-permute-start(bf16[64,1024]{1,0:T(8,128)(2,1)S(1)} %get-tuple-element.25.refs_4_.refs_3_), channel_id=1, source_target_pairs={{0,8},{8,16},{16,24},{1,9},{9,17},{17,25},{2,10},{10,18},{18,26},{... | collective-permute-start | bytes 393224 | tf_op jit(solution)/shard_map/ppermute | solution.py:908
  6.8 1.3 %collective-permute-start.1 = (bf16[64,1024]{1,0:T(8,128)(2,1)S(1)}, bf16[64,1024]{1,0:T(8,128)(2,1)S(1)}, u32[]{:S(2)}, u32[]{:S(2)}) collective-permute-start(bf16[64,1024]{1,0:T(8,128)(2,1)S(1)} %get-tuple-element.26.refs_3_.refs_1_), channel_id=1, source_target_pairs={{8,0},{16,8},{24,16},{9,1},{17,9},{25,17},{10,2},{18,10},{26,18},{... | collective-permute-start | bytes 393224 | tf_op jit(solution)/shard_map/ppermute | solution.py:908
  8.1 0.0 copy-done
  8.1 3.8 %inner.1 = (bf16[6,64,1024]{2,1,0:T(8,128)(2,1)S(1)}, bf16[8,64,1024]{2,1,0:T(8,128)(2,1)S(1)}, bf16[11,64,128]{2,1,0:T(8,128)(2,1)S(1)}, bf16[32,32,128]{2,1,0:T(8,128)(2,1)}) custom-call(bf16[64,8,8,128]{3,2,1,0:T(8,128)(2,1)} %refs_0_.1, bf16[64,8,8,128]{3,2,1,0:T(8,128)(2,1)} %refs_1_.1, bf16[64,8,8,128]{3,2,1,0:T(8,128)(2,1)} %refs_2_.1, ...), custom_call_target="tpu_custom_call" | custom-call | bytes 6291456 | tf_op jit(solution)/shard_map/inner/pallas_call | solution.py:436
  11.9 0.0 collective-permute-done.xlo_ref.refs_0_
  11.9 2.4 %collective-permute-done.1.xhi_ref.refs_4_ = bf16[64,1024]{1,0:T(8,128)(2,1)S(1)} collective-permute-done((bf16[64,1024]{1,0:T(8,128)(2,1)S(1)}, bf16[64,1024]{1,0:T(8,128)(2,1)S(1)}, u32[]{:S(2)}, u32[]{:S(2)}) %collective-permute-start.1) | collective-permute-done | bytes 131104 | tf_op jit(solution)/shard_map/ppermute | solution.py:908
  14.3 0.3 side.1.own_ref
  14.6 0.1 collective-permute-start.2
  14.7 5.3 %all-to-all-start = ((bf16[32,32,128]{2,1,0:T(8,128)(2,1)}), bf16[32,32,128]{2,1,0:T(8,128)(2,1)S(1)}, u32[]{:S(2)}, u32[]{:S(2)}) async-start(bf16[32,32,128]{2,1,0:T(8,128)(2,1)} %get-tuple-element.38), calls=%async_computation | async-start | bytes 524288 | tf_op jit(solution)/shard_map/all_to_all | solution.py:745
  19.9 0.0 collective-permute-done.2.other_ref.refs_5_.refs_6_
  19.9 0.1 join.1
  20.0 3.7 %collective-permute-start.3 = (bf16[3,64,128]{2,1,0:T(8,128)(2,1)S(1)}, bf16[3,64,128]{2,1,0:T(8,128)(2,1)S(1)}, u32[]{:S(2)}, u32[]{:S(2)}) collective-permute-start(bf16[3,64,128]{2,1,0:T(8,128)(2,1)S(1)} %get-tuple-element.32), channel_id=1, source_target_pairs={{0,1},{1,2},{2,3},{4,5},{5,6},{6,7},{8,9},{9,10},{10,11},{12,13},{... | collective-permute-start | bytes 147464 | tf_op jit(solution)/shard_map/ppermute | solution.py:908
  23.7 3.6 %wgrad.1 = (f32[288,256]{1,0:T(8,128)S(1)}, f32[288,256]{1,0:T(8,128)S(1)}) custom-call(bf16[64,1024]{1,0:T(8,128)(2,1)S(1)} %collective-permute-done.xlo_ref.refs_0_, bf16[64,1024]{1,0:T(8,128)(2,1)S(1)} %get-tuple-element.26.refs_3_.refs_1_, bf16[6,64,1024]{2,1,0:T(8,128)(2,1)S(1)} %get-tuple-element.27.refs_2_, ...), custom_call_target="tpu_custom_call" | custom-call | flops 2264924160 | bytes 4194304 | tf_op jit(solution)/shard_map/wgrad/pallas_call | solution.py:532
  27.3 0.0 collective-permute-done.3.below_ref.refs_7_
  27.3 0.1 collective-permute-start.5
  27.4 1.3 %collective-permute-start.4 = (bf16[2,64,128]{2,1,0:T(8,128)(2,1)S(1)}, bf16[2,64,128]{2,1,0:T(8,128)(2,1)S(1)}, u32[]{:S(2)}, u32[]{:S(2)}) collective-permute-start(bf16[2,64,128]{2,1,0:T(8,128)(2,1)S(1)} %get-tuple-element.35.ztiles_ref), channel_id=1, source_target_pairs={{1,0},{2,1},{3,2},{5,4},{6,5},{7,6},{9,8},{10,9},{11,10},{13,12},{... | collective-permute-start | bytes 98312 | tf_op jit(solution)/shard_map/ppermute | solution.py:908
  28.7 0.3 edges.1.edge_ref
  29.0 0.0 collective-permute-done.5.other_ref
  29.1 1.4 %finish.1 = bf16[16,32,128]{2,1,0:T(8,128)(2,1)} custom-call(f32[288,256]{1,0:T(8,128)S(1)} %get-tuple-element.36.mine_ref, f32[288,256]{1,0:T(8,128)S(1)} %collective-permute-done.5.other_ref, f32[2,96,256]{2,1,0:T(8,128)S(1)} %edges.1.edge_ref), custom_call_target="tpu_custom_call" | custom-call | flops 16777216 | bytes 1048576 | tf_op jit(solution)/shard_map/finish/pallas_call | solution.py:634
  30.5 0.0 all-to-all-done.refs_9_
  30.5 8.8 %all-to-all-start.1 = ((bf16[16,32,128]{2,1,0:T(8,128)(2,1)}), bf16[16,32,128]{2,1,0:T(8,128)(2,1)S(1)}, u32[]{:S(2)}, u32[]{:S(2)}) async-start(bf16[16,32,128]{2,1,0:T(8,128)(2,1)} %finish.1), calls=%async_computation.1 | async-start | bytes 262144 | tf_op jit(solution)/shard_map/all_to_all | solution.py:760
  39.3 0.0 copy-start.1
  39.3 0.0 copy-start.2
  39.3 0.0 collective-permute-done.4.refs_8_
  39.3 5.3 %dgrad.1 = bf16[64,8,8,128]{3,2,1,0:T(8,128)(2,1)} custom-call(bf16[64,1024]{1,0:T(8,128)(2,1)S(1)} %collective-permute-done.xlo_ref.refs_0_, bf16[64,1024]{1,0:T(8,128)(2,1)S(1)} %get-tuple-element.26.refs_3_.refs_1_, bf16[6,64,1024]{2,1,0:T(8,128)(2,1)S(1)} %get-tuple-element.27.refs_2_, bf16[64,1024]{1,0:T(8,128)(2,1)S(1)} %get-tuple-element.25.refs_4_.refs_3_, ...), custom_call_target="tpu_custom_call" | custom-call | flops 2415919104 | bytes 4194304 | tf_op jit(solution)/shard_map/dgrad/pallas_call | solution.py:710
  44.6 3.0 %all-to-all-done.1.parts_ref = bf16[16,32,128]{2,1,0:T(8,128)(2,1)S(1)} async-done(((bf16[16,32,128]{2,1,0:T(8,128)(2,1)}), bf16[16,32,128]{2,1,0:T(8,128)(2,1)S(1)}, u32[]{:S(2)}, u32[]{:S(2)}) %all-to-all-start.1) | async-done | bytes 131104 | tf_op jit(solution)/shard_map/all_to_all | solution.py:760
  47.6 0.0 copy-done.1
  47.6 0.0 copy-done.2
  47.6 0.7 %adam.1 = (f32[27,128]{1,0:T(8,128)}, f32[27,128]{1,0:T(8,128)}, f32[27,128]{1,0:T(8,128)}, f32[27,128]{1,0:T(8,128)}) custom-call(bf16[16,32,128]{2,1,0:T(8,128)(2,1)S(1)} %all-to-all-done.1.parts_ref, f32[27,128]{1,0:T(8,128)S(1)} %bitcast.8, f32[27,128]{1,0:T(8,128)S(1)} %bitcast.9, f32[27,128]{1,0:T(8,128)S(1)} %bitcast.10), custom_call_target="tpu_custom_call" | custom-call | flops 262144 | bytes 262144 | tf_op jit(solution)/shard_map/adam/pallas_call | solution.py:673
Async XLA Ops:
  0.6 7.4 %copy-start = (f32[3456]{0:T(1024)S(1)}, f32[3456]{0:T(1024)}, u32[]{:S(2)}) copy-start(f32[3456]{0:T(1024)} %param.9) | copy-start | bytes 41476
  1.9 10.0 %collective-permute-start = (bf16[64,1024]{1,0:T(8,128)(2,1)S(1)}, bf16[64,1024]{1,0:T(8,128)(2,1)S(1)}, u32[]{:S(2)}, u32[]{:S(2)}) collective-permute-start(bf16[64,1024]{1,0:T(8,128)(2,1)S(1)} %get-tuple-element.25.refs_4_.refs_3_), channel_id=1, source_target_pairs={{0,8},{8,16},{16,24},{1,9},{9,17},{17,25},{2,10},{10,18},{18,26},{... | collective-permute-start | bytes 393224 | tf_op jit(solution)/shard_map/ppermute | solution.py:908
  6.8 7.5 %collective-permute-start.1 = (bf16[64,1024]{1,0:T(8,128)(2,1)S(1)}, bf16[64,1024]{1,0:T(8,128)(2,1)S(1)}, u32[]{:S(2)}, u32[]{:S(2)}) collective-permute-start(bf16[64,1024]{1,0:T(8,128)(2,1)S(1)} %get-tuple-element.26.refs_3_.refs_1_), channel_id=1, source_target_pairs={{8,0},{16,8},{24,16},{9,1},{17,9},{25,17},{10,2},{18,10},{26,18},{... | collective-permute-start | bytes 393224 | tf_op jit(solution)/shard_map/ppermute | solution.py:908
  14.6 5.4 %collective-permute-start.2 = (bf16[13,64,128]{2,1,0:T(8,128)(2,1)S(1)}, bf16[13,64,128]{2,1,0:T(8,128)(2,1)S(1)}, u32[]{:S(2)}, u32[]{:S(2)}) collective-permute-start(bf16[13,64,128]{2,1,0:T(8,128)(2,1)S(1)} %side.1.own_ref), channel_id=1, source_target_pairs={{0,4},{4,0},{1,5},{5,1},{2,6},{6,2},{3,7},{7,3},{8,12},{12,8},{9,1... | collective-permute-start | bytes 638984 | tf_op jit(solution)/shard_map/ppermute | solution.py:908
  14.7 15.8 %all-to-all-start = ((bf16[32,32,128]{2,1,0:T(8,128)(2,1)}), bf16[32,32,128]{2,1,0:T(8,128)(2,1)S(1)}, u32[]{:S(2)}, u32[]{:S(2)}) async-start(bf16[32,32,128]{2,1,0:T(8,128)(2,1)} %get-tuple-element.38), calls=%async_computation | async-start | bytes 524288 | tf_op jit(solution)/shard_map/all_to_all | solution.py:745
  20.0 7.3 %collective-permute-start.3 = (bf16[3,64,128]{2,1,0:T(8,128)(2,1)S(1)}, bf16[3,64,128]{2,1,0:T(8,128)(2,1)S(1)}, u32[]{:S(2)}, u32[]{:S(2)}) collective-permute-start(bf16[3,64,128]{2,1,0:T(8,128)(2,1)S(1)} %get-tuple-element.32), channel_id=1, source_target_pairs={{0,1},{1,2},{2,3},{4,5},{5,6},{6,7},{8,9},{9,10},{10,11},{12,13},{... | collective-permute-start | bytes 147464 | tf_op jit(solution)/shard_map/ppermute | solution.py:908
  27.3 1.7 %collective-permute-start.5 = (f32[288,256]{1,0:T(8,128)S(1)}, f32[288,256]{1,0:T(8,128)S(1)}, u32[]{:S(2)}, u32[]{:S(2)}) collective-permute-start(f32[288,256]{1,0:T(8,128)S(1)} %get-tuple-element.37), channel_id=1, source_target_pairs={{0,4},{4,0},{1,5},{5,1},{2,6},{6,2},{3,7},{7,3},{8,12},{12,8},{9,1... | collective-permute-start | bytes 884744 | tf_op jit(solution)/shard_map/ppermute | solution.py:908
  27.4 11.9 %collective-permute-start.4 = (bf16[2,64,128]{2,1,0:T(8,128)(2,1)S(1)}, bf16[2,64,128]{2,1,0:T(8,128)(2,1)S(1)}, u32[]{:S(2)}, u32[]{:S(2)}) collective-permute-start(bf16[2,64,128]{2,1,0:T(8,128)(2,1)S(1)} %get-tuple-element.35.ztiles_ref), channel_id=1, source_target_pairs={{1,0},{2,1},{3,2},{5,4},{6,5},{7,6},{9,8},{10,9},{11,10},{13,12},{... | collective-permute-start | bytes 98312 | tf_op jit(solution)/shard_map/ppermute | solution.py:908
  30.5 17.1 %all-to-all-start.1 = ((bf16[16,32,128]{2,1,0:T(8,128)(2,1)}), bf16[16,32,128]{2,1,0:T(8,128)(2,1)S(1)}, u32[]{:S(2)}, u32[]{:S(2)}) async-start(bf16[16,32,128]{2,1,0:T(8,128)(2,1)} %finish.1), calls=%async_computation.1 | async-start | bytes 262144 | tf_op jit(solution)/shard_map/all_to_all | solution.py:760
  39.3 8.3 %copy-start.1 = (f32[3456]{0:T(1024)S(1)}, f32[3456]{0:T(1024)}, u32[]{:S(2)}) copy-start(f32[3456]{0:T(1024)} %param.10) | copy-start | bytes 41476
  39.3 8.3 %copy-start.2 = (f32[3456]{0:T(1024)S(1)}, f32[3456]{0:T(1024)}, u32[]{:S(2)}) copy-start(f32[3456]{0:T(1024)} %param.11) | copy-start | bytes 41476

commit v3 on v2

--- a/solution.py
+++ b/solution.py
@@ -37,7 +37,8 @@
     return jnp.where(p > 0, u, jnp.zeros_like(u))
 
 
-def face_kernel(p_ref, u_ref, low_ref, high_ref, p_buf, u_buf, tile, sems):
+def face_kernel(p_ref, u_ref, m_ref, low_ref, high_ref, sent_ref, *scratch):
+    p_buf, u_buf, tile, sems, share_ref, share_sems, m_buf = scratch
     size_x, size_z = p_ref.shape[1], p_ref.shape[3]
     copies = []
     for k, x in enumerate((0, size_x - 1)):
@@ -48,6 +49,20 @@
         for copy in pair:
             copy.start()
         copies.append(pair)
+    read = pltpu.make_async_copy(m_ref, m_buf, sems.at[4])
+    read.start()
+    read.wait()
+    share = m_buf[...]
+    height = share_ref.shape[0] - share.shape[0]
+    if height:
+        share = jnp.concatenate([share, jnp.zeros((height, share.shape[1]), F32)], axis=0)
+    share_ref[...] = share.astype(BF16)
+    sends = [
+        pltpu.make_async_copy(share_ref, sent_ref.at[device], share_sems.at[device])
+        for device in range(sent_ref.shape[0])
+    ]
+    for copy in sends:
+        copy.start()
     for k, out_ref in enumerate((low_ref, high_ref)):
         for copy in copies[k]:
             copy.wait()
@@ -56,27 +71,32 @@
             out_ref[:, y * size_z : (y + 1) * size_z] = value
 
         to_planes(masked(p_buf[k], u_buf[k]), tile.at[k], write)
-
-
-def faces(preact, upstream):
+    for copy in sends:
+        copy.wait()
+
+
+def faces(preact, upstream, share, sent_shape):
     channels, size_x, size_y, size_z = preact.shape
     face = jax.ShapeDtypeStruct((channels, size_y * size_z), BF16)
     buffer = pltpu.VMEM((2, channels, size_y, size_z), BF16)
     return pl.pallas_call(
         face_kernel,
-        in_specs=[HBM, HBM],
-        out_specs=[VMEM] * 2,
-        out_shape=[face, face],
+        in_specs=[HBM, HBM, HBM],
+        out_specs=[VMEM, VMEM, HBM],
+        out_shape=[face, face, jax.ShapeDtypeStruct(sent_shape, BF16)],
         scratch_shapes=[
             buffer,
             buffer,
             pltpu.VMEM((2, channels * size_y, size_z), F32),
-            pltpu.SemaphoreType.DMA((4,)),
+            pltpu.SemaphoreType.DMA((5,)),
+            pltpu.VMEM(sent_shape[1:], BF16),
+            pltpu.SemaphoreType.DMA((sent_shape[0],)),
+            pltpu.VMEM(share.shape, F32),
         ],
         compiler_params=params(FACES_VMEM),
         cost_estimate=cost(0, 2**20),
         name="faces",
-    )(preact, upstream)
+    )(preact, upstream, share)
 
 
 def read_inner(p_ref, u_ref, a_ref, g_ref, x_ref, p_buf, u_buf, a_buf, tile, sems):
@@ -400,21 +420,9 @@
 
 
 def pair_inner_kernel(*refs):
-    first_ref, last_ref, m_ref = refs[3:6]
-    g_ref, x_ref, side_ref, sent_ref = refs[6:10]
-    tile_ref, tile_sems = refs[15:]
-    share = m_ref[...]
-    height = tile_ref.shape[0] - share.shape[0]
-    if height:
-        share = jnp.concatenate([share, jnp.zeros((height, share.shape[1]), F32)], axis=0)
-    tile_ref[...] = share.astype(BF16)
-    copies = [
-        pltpu.make_async_copy(tile_ref, sent_ref.at[device], tile_sems.at[device])
-        for device in range(sent_ref.shape[0])
-    ]
-    for copy in copies:
-        copy.start()
-    read_inner(*refs[:3], g_ref, x_ref, *refs[10:15])
+    first_ref, last_ref = refs[3:5]
+    g_ref, x_ref, side_ref = refs[5:8]
+    read_inner(*refs[:3], g_ref, x_ref, *refs[8:])
     size_z = side_ref.shape[-1]
     size_x, channels, plane = x_ref.shape
     size_y = plane // size_z
@@ -426,28 +434,22 @@
     side_ref[size_x + 1] = high.astype(BF16)
     low, high = z_tiles([x_ref[x] for x in range(size_x)], size_y, size_z, range(size_x))
     side_ref[size_x + 2] = (low + pltpu.roll(high, size_x * size_y, 1)).astype(BF16)
-    for copy in copies:
-        copy.wait()
-
-
-def pair_inner(preact, upstream, activations, first, last, share, sent_shape):
+
+
+def pair_inner(preact, upstream, activations, first, last):
     shape = preact.shape
     channels, size_x, _, size_z = shape
     return pl.pallas_call(
         pair_inner_kernel,
-        in_specs=[HBM] * 3 + [VMEM] * 3,
-        out_specs=[VMEM] * 3 + [HBM],
+        in_specs=[HBM] * 3 + [VMEM] * 2,
+        out_specs=[VMEM] * 3,
         out_shape=inner_outputs(*shape)
-        + [
-            jax.ShapeDtypeStruct((size_x + 3, channels, size_z), BF16),
-            jax.ShapeDtypeStruct(sent_shape, BF16),
-        ],
-        scratch_shapes=inner_scratch(*shape)
-        + [pltpu.VMEM(sent_shape[1:], BF16), pltpu.SemaphoreType.DMA((sent_shape[0],))],
+        + [jax.ShapeDtypeStruct((size_x + 3, channels, size_z), BF16)],
+        scratch_shapes=inner_scratch(*shape),
         compiler_params=params(INNER_VMEM),
         cost_estimate=cost(0, 6 * 2**20),
         name="inner",
-    )(preact, upstream, activations, first, last, share)
+    )(preact, upstream, activations, first, last)
 
 
 def side_kernel(xlo_ref, xhi_ref, own_ref, sent_ref):
@@ -731,22 +733,17 @@
     span = lax.axis_size("gz") * rows
     used = master.shape[0] // LANES
     tall = -(-used // 16) * 16
-    first, last = faces(preact, upstream)
-    x_halos = (shifted(last, {"gx": 1}), shifted(first, {"gx": -1}))
-    inner, planes_x, own, sent = pair_inner(
-        preact,
-        upstream,
-        activations,
-        first,
-        last,
-        master.reshape(used, LANES),
-        (devices, tall, LANES),
+    first, last, sent = faces(
+        preact, upstream, master.reshape(used, LANES), (devices, tall, LANES)
     )
     kernel = lax.all_to_all(sent, AXES, 0, 0, tiled=True)
+    x_halos = (shifted(last, {"gx": 1}), shifted(first, {"gx": -1}))
+    inner, planes_x, own = pair_inner(preact, upstream, activations, first, last)
     planes = (x_halos[0], first, inner, last, x_halos[1])
     own = side(x_halos, own)
     other = shifted(own, {"gy": "swap"})
     zlo, zhi = join(own, other, size_x * size_y)
+    zhi, kernel = lax.optimization_barrier((zhi, kernel))
     below = shifted(zhi, {"gz": 1})
     sources = (*planes, other, other)
     mine, theirs = pair_wgrad(sources, planes_x, shape, span)
@@ -867,10 +864,9 @@
     channels, _, _, size_z = shape
     devices = math.prod(lax.axis_size(a) for a in AXES)
     share = master.shape[0]
-    first, last = faces(preact, upstream)
+    first, last, sent = faces(preact, upstream, master.reshape(1, share), (devices, 1, share))
     x_halos = (shifted(last, {"gx": 1}), shifted(first, {"gx": -1}))
     inner, planes_x = inner_planes(preact, upstream, activations)
-    sent = jnp.broadcast_to(master.astype(BF16).reshape(1, 1, share), (devices, 1, share))
     kernel = lax.all_to_all(sent, AXES, 0, 0, tiled=True).reshape(channels, 27 * channels)
     planes = (x_halos[0], first, inner, last, x_halos[1])
     y_sent = y_faces(planes, size_z)

time: 48.6 us -> 52 us (1.070)
  local copies, waits for them, and re-layouts: 0.02 us -> 2.74 us
  waiting for transfers between devices: 5.35 us -> 7.74 us
  starting transfers between devices: 25.3 us -> 23.5 us
    unnamed x6 -> x16, local copies, waits for them, and re-layouts: 0.02 us -> 2.74 us
    ppermute x6, waiting for transfers between devices: 2.37 us -> 4.81 us  [shifted(): return lax.ppermute(value, names if len(names) > 1 else names[0], pairs)]
    all_to_all x1, starting transfers between devices: 8.78 us -> 6.36 us  [pair_program(): parts = lax.all_to_all(part, ('gx', 'gz'), 0, 0, tiled=True)]
    all_to_all x1, starting transfers between devices: 5.27 us -> 7.3 us  [pair_program(): kernel = lax.all_to_all(sent, AXES, 0, 0, tiled=True)]
    ppermute x6, starting transfers between devices: 11.2 us -> 9.82 us  [shifted(): return lax.ppermute(value, names if len(names) > 1 else names[0], pairs)]
  transfers between devices with their start and end apart: 8 -> 8, of which waited for: 2 -> 3; matrix products, arithmetic and copies ran while one was open for 0% -> 0% of each run, Pallas kernels for 30% -> 28%
where the time goes in v3:
time: 52 us; the launch traced here: 51.5 us
  starting transfers between devices  23.5 us (45%)
  Pallas kernels  16.7 us (32%)
  waiting for transfers between devices  7.74 us (15%)
  local copies, waits for them, and re-layouts  2.74 us (5%)
  between operations  0.83 us (2%)
    ppermute x6, starting transfers between devices, shifted(): return lax.ppermute(value, names if len(names) > 1 else names[0], pairs)  9.82 us
    all_to_all x1, starting transfers between devices, pair_program(): kernel = lax.all_to_all(sent, AXES, 0, 0, tiled=True)  7.3 us
    all_to_all x1, starting transfers between devices, pair_program(): parts = lax.all_to_all(part, ('gx', 'gz'), 0, 0, tiled=True)  6.36 us
    pallas_call x1, Pallas kernels, pair_dgrad(): pl.pallas_call(functools.partial(pair_dgrad_kernel, rows), in_specs=[VMEM...  5.25 us
    ppermute x6, waiting for transfers between devices, shifted(): return lax.ppermute(value, names if len(names) > 1 else names[0], pairs)  4.81 us
    pallas_call x1, Pallas kernels, pair_wgrad(): pl.pallas_call(functools.partial(pair_wgrad_kernel, span), in_specs=[VMEM...  3.6 us
    pallas_call x1, Pallas kernels, pair_inner(): pl.pallas_call(pair_inner_kernel, in_specs=[HBM] * 3 + [VMEM] * 2, out_sp...  3.3 us
    all_to_all x1, waiting for transfers between devices, pair_program(): parts = lax.all_to_all(part, ('gx', 'gz'), 0, 0, tiled=True)  2.93 us
  transfers between devices with their start and end apart: 8, of which 3 were waited for; matrix products, arithmetic and copies ran while one was open for 0% of the time, Pallas kernels for 28%

profile of v3, /device:TPU:0, one launch (start us, length us, event | category | flops | bytes accessed | tf_op | source)
XLA Modules:
  0.0 51.5 jit_solution(8540462421804954572)
XLA Ops:
  0.6 0.0 copy-start.1
  0.6 0.7 %copy-done.1 = f32[3456]{0:T(1024)S(1)} copy-done((f32[3456]{0:T(1024)S(1)}, f32[3456]{0:T(1024)}, u32[]{:S(2)}) %copy-start.1) | copy-done | bytes 13848
  1.4 1.8 %faces.1 = (bf16[64,1024]{1,0:T(8,128)(2,1)S(1)}, bf16[64,1024]{1,0:T(8,128)(2,1)S(1)}, bf16[32,32,128]{2,1,0:T(8,128)(2,1)}) custom-call(bf16[64,8,8,128]{3,2,1,0:T(8,128)(2,1)} %refs_0_.1, bf16[64,8,8,128]{3,2,1,0:T(8,128)(2,1)} %refs_1_.1, f32[27,128]{1,0:T(8,128)S(1)} %bitcast.7), custom_call_target="tpu_custom_call" | custom-call | bytes 1048576 | tf_op jit(solution)/shard_map/faces/pallas_call | solution.py:82
  3.1 7.3 %all-to-all-start = ((bf16[32,32,128]{2,1,0:T(8,128)(2,1)}), bf16[32,32,128]{2,1,0:T(8,128)(2,1)S(1)}, u32[]{:S(2)}, u32[]{:S(2)}) async-start(bf16[32,32,128]{2,1,0:T(8,128)(2,1)} %get-tuple-element.35), calls=%async_computation | async-start | bytes 524288 | tf_op jit(solution)/shard_map/all_to_all | solution.py:739
  10.4 3.7 %collective-permute-start = (bf16[64,1024]{1,0:T(8,128)(2,1)S(1)}, bf16[64,1024]{1,0:T(8,128)(2,1)S(1)}, u32[]{:S(2)}, u32[]{:S(2)}) collective-permute-start(bf16[64,1024]{1,0:T(8,128)(2,1)S(1)} %get-tuple-element.27.refs_4_.refs_3_), channel_id=1, source_target_pairs={{0,8},{8,16},{16,24},{1,9},{9,17},{17,25},{2,10},{10,18},{18,26},{... | collective-permute-start | bytes 393224 | tf_op jit(solution)/shard_map/ppermute | solution.py:904
  14.1 1.3 %collective-permute-start.1 = (bf16[64,1024]{1,0:T(8,128)(2,1)S(1)}, bf16[64,1024]{1,0:T(8,128)(2,1)S(1)}, u32[]{:S(2)}, u32[]{:S(2)}) collective-permute-start(bf16[64,1024]{1,0:T(8,128)(2,1)S(1)} %get-tuple-element.28.refs_3_.refs_1_), channel_id=1, source_target_pairs={{8,0},{16,8},{24,16},{9,1},{17,9},{25,17},{10,2},{18,10},{26,18},{... | collective-permute-start | bytes 393224 | tf_op jit(solution)/shard_map/ppermute | solution.py:904
  15.4 3.3 %inner.1 = (bf16[6,64,1024]{2,1,0:T(8,128)(2,1)S(1)}, bf16[8,64,1024]{2,1,0:T(8,128)(2,1)S(1)}, bf16[11,64,128]{2,1,0:T(8,128)(2,1)S(1)}) custom-call(bf16[64,8,8,128]{3,2,1,0:T(8,128)(2,1)S(1)} %copy-done, bf16[64,8,8,128]{3,2,1,0:T(8,128)(2,1)} %refs_1_.1, bf16[64,8,8,128]{3,2,1,0:T(8,128)(2,1)} %refs_2_.1, ...), custom_call_target="tpu_custom_call" | custom-call | bytes 6291456 | tf_op jit(solution)/shard_map/inner/pallas_call | solution.py:442
  18.7 0.0 copy-start.5
  18.7 0.9 %copy-done.5 = bf16[6,64,1024]{2,1,0:T(8,128)(2,1)} copy-done((bf16[6,64,1024]{2,1,0:T(8,128)(2,1)}, bf16[6,64,1024]{2,1,0:T(8,128)(2,1)S(1)}, u32[]{:S(2)}) %copy-start.5) | copy-done | bytes 786456
  19.6 3.3 %collective-permute-done.1.xhi_ref.refs_4_ = bf16[64,1024]{1,0:T(8,128)(2,1)S(1)} collective-permute-done((bf16[64,1024]{1,0:T(8,128)(2,1)S(1)}, bf16[64,1024]{1,0:T(8,128)(2,1)S(1)}, u32[]{:S(2)}, u32[]{:S(2)}) %collective-permute-start.1) | collective-permute-done | bytes 131104 | tf_op jit(solution)/shard_map/ppermute | solution.py:904
  23.0 0.3 side.1.own_ref
  23.3 0.1 collective-permute-start.2
  23.4 1.5 %collective-permute-done.2.other_ref.refs_5_.refs_6_ = bf16[13,64,128]{2,1,0:T(8,128)(2,1)S(1)} collective-permute-done((bf16[13,64,128]{2,1,0:T(8,128)(2,1)S(1)}, bf16[13,64,128]{2,1,0:T(8,128)(2,1)S(1)}, u32[]{:S(2)}, u32[]{:S(2)}) %collective-permute-start.2) | collective-permute-done | bytes 213024 | tf_op jit(solution)/shard_map/ppermute | solution.py:904
  24.8 0.1 join.1
  24.9 3.3 %collective-permute-start.3 = (bf16[3,64,128]{2,1,0:T(8,128)(2,1)S(1)}, bf16[3,64,128]{2,1,0:T(8,128)(2,1)S(1)}, u32[]{:S(2)}, u32[]{:S(2)}) collective-permute-start(bf16[3,64,128]{2,1,0:T(8,128)(2,1)S(1)} %get-tuple-element.36), channel_id=1, source_target_pairs={{0,1},{1,2},{2,3},{4,5},{5,6},{6,7},{8,9},{9,10},{10,11},{12,13},{... | collective-permute-start | bytes 147464 | tf_op jit(solution)/shard_map/ppermute | solution.py:904
  28.2 0.0 copy-start.6
  28.2 1.1 %copy-done.6 = bf16[6,64,1024]{2,1,0:T(8,128)(2,1)S(1)} copy-done((bf16[6,64,1024]{2,1,0:T(8,128)(2,1)S(1)}, bf16[6,64,1024]{2,1,0:T(8,128)(2,1)}, u32[]{:S(2)}) %copy-start.6) | copy-done | bytes 786456
  29.3 3.6 %wgrad.1 = (f32[288,256]{1,0:T(8,128)S(1)}, f32[288,256]{1,0:T(8,128)S(1)}) custom-call(bf16[64,1024]{1,0:T(8,128)(2,1)S(1)} %collective-permute-done.xlo_ref.refs_0_, bf16[64,1024]{1,0:T(8,128)(2,1)S(1)} %get-tuple-element.28.refs_3_.refs_1_, bf16[6,64,1024]{2,1,0:T(8,128)(2,1)S(1)} %copy-done.6, bf16[64,1024]{1,0:T(8,128)(2,1)S(1)} %get-tuple-element.27.refs_4_.refs_3_, ...), custom_call_target="tpu_custom_call" | custom-call | flops 2264924160 | bytes 4194304 | tf_op jit(solution)/shard_map/wgrad/pallas_call | solution.py:534
  32.9 0.1 collective-permute-start.5
  33.0 0.0 copy-start.7
  33.0 1.4 %collective-permute-start.4 = (bf16[2,64,128]{2,1,0:T(8,128)(2,1)S(1)}, bf16[2,64,128]{2,1,0:T(8,128)(2,1)S(1)}, u32[]{:S(2)}, u32[]{:S(2)}) collective-permute-start(bf16[2,64,128]{2,1,0:T(8,128)(2,1)S(1)} %get-tuple-element.39.ztiles_ref), channel_id=1, source_target_pairs={{1,0},{2,1},{3,2},{5,4},{6,5},{7,6},{9,8},{10,9},{11,10},{13,12},{... | collective-permute-start | bytes 98312 | tf_op jit(solution)/shard_map/ppermute | solution.py:904
  34.5 0.3 edges.1.edge_ref
  34.8 0.0 collective-permute-done.5.other_ref
  34.8 1.4 %finish.1 = bf16[16,32,128]{2,1,0:T(8,128)(2,1)} custom-call(f32[288,256]{1,0:T(8,128)S(1)} %get-tuple-element.40.mine_ref, f32[288,256]{1,0:T(8,128)S(1)} %collective-permute-done.5.other_ref, f32[2,96,256]{2,1,0:T(8,128)S(1)} %edges.1.edge_ref), custom_call_target="tpu_custom_call" | custom-call | flops 16777216 | bytes 1048576 | tf_op jit(solution)/shard_map/finish/pallas_call | solution.py:636
  36.3 6.4 %all-to-all-start.1 = ((bf16[16,32,128]{2,1,0:T(8,128)(2,1)}), bf16[16,32,128]{2,1,0:T(8,128)(2,1)S(1)}, u32[]{:S(2)}, u32[]{:S(2)}) async-start(bf16[16,32,128]{2,1,0:T(8,128)(2,1)} %finish.1), calls=%async_computation.1 | async-start | bytes 262144 | tf_op jit(solution)/shard_map/all_to_all | solution.py:757
  42.6 0.0 copy-start.2
  42.6 0.0 copy-start.3
  42.7 0.0 copy-start.4
  42.7 0.0 collective-permute-done.4.refs_8_
  42.7 5.3 %dgrad.1 = bf16[64,8,8,128]{3,2,1,0:T(8,128)(2,1)} custom-call(bf16[64,1024]{1,0:T(8,128)(2,1)S(1)} %collective-permute-done.xlo_ref.refs_0_, bf16[64,1024]{1,0:T(8,128)(2,1)S(1)} %get-tuple-element.28.refs_3_.refs_1_, bf16[6,64,1024]{2,1,0:T(8,128)(2,1)S(1)} %copy-done.7, bf16[64,1024]{1,0:T(8,128)(2,1)S(1)} %get-tuple-element.27.refs_4_.refs_3_, ...), custom_call_target="tpu_custom_call" | custom-call | flops 2415919104 | bytes 4194304 | tf_op jit(solution)/shard_map/dgrad/pallas_call | solution.py:712
  47.9 2.9 %all-to-all-done.1.parts_ref = bf16[16,32,128]{2,1,0:T(8,128)(2,1)S(1)} async-done(((bf16[16,32,128]{2,1,0:T(8,128)(2,1)}), bf16[16,32,128]{2,1,0:T(8,128)(2,1)S(1)}, u32[]{:S(2)}, u32[]{:S(2)}) %all-to-all-start.1) | async-done | bytes 131104 | tf_op jit(solution)/shard_map/all_to_all | solution.py:757
  50.9 0.7 %adam.1 = (f32[27,128]{1,0:T(8,128)}, f32[27,128]{1,0:T(8,128)}, f32[27,128]{1,0:T(8,128)}, f32[27,128]{1,0:T(8,128)}) custom-call(bf16[16,32,128]{2,1,0:T(8,128)(2,1)S(1)} %all-to-all-done.1.parts_ref, f32[27,128]{1,0:T(8,128)S(1)} %bitcast.8, f32[27,128]{1,0:T(8,128)S(1)} %bitcast.9, f32[27,128]{1,0:T(8,128)S(1)} %bitcast.10), custom_call_target="tpu_custom_call" | custom-call | flops 262144 | bytes 262144 | tf_op jit(solution)/shard_map/adam/pallas_call | solution.py:675
  (9 shorter events, 0.0 us)
Async XLA Ops:
  0.6 0.7 %copy-start.1 = (f32[3456]{0:T(1024)S(1)}, f32[3456]{0:T(1024)}, u32[]{:S(2)}) copy-start(f32[3456]{0:T(1024)} %param.9) | copy-start | bytes 41476
  1.4 14.1 %copy-start = (bf16[64,8,8,128]{3,2,1,0:T(8,128)(2,1)S(1)}, bf16[64,8,8,128]{3,2,1,0:T(8,128)(2,1)}, u32[]{:S(2)}) copy-start(bf16[64,8,8,128]{3,2,1,0:T(8,128)(2,1)} %refs_0_.1) | copy-start | bytes 3145732
  3.1 21.8 %all-to-all-start = ((bf16[32,32,128]{2,1,0:T(8,128)(2,1)}), bf16[32,32,128]{2,1,0:T(8,128)(2,1)S(1)}, u32[]{:S(2)}, u32[]{:S(2)}) async-start(bf16[32,32,128]{2,1,0:T(8,128)(2,1)} %get-tuple-element.35), calls=%async_computation | async-start | bytes 524288 | tf_op jit(solution)/shard_map/all_to_all | solution.py:739
  10.4 9.2 %collective-permute-start = (bf16[64,1024]{1,0:T(8,128)(2,1)S(1)}, bf16[64,1024]{1,0:T(8,128)(2,1)S(1)}, u32[]{:S(2)}, u32[]{:S(2)}) collective-permute-start(bf16[64,1024]{1,0:T(8,128)(2,1)S(1)} %get-tuple-element.27.refs_4_.refs_3_), channel_id=1, source_target_pairs={{0,8},{8,16},{16,24},{1,9},{9,17},{17,25},{2,10},{10,18},{18,26},{... | collective-permute-start | bytes 393224 | tf_op jit(solution)/shard_map/ppermute | solution.py:904
  14.1 8.8 %collective-permute-start.1 = (bf16[64,1024]{1,0:T(8,128)(2,1)S(1)}, bf16[64,1024]{1,0:T(8,128)(2,1)S(1)}, u32[]{:S(2)}, u32[]{:S(2)}) collective-permute-start(bf16[64,1024]{1,0:T(8,128)(2,1)S(1)} %get-tuple-element.28.refs_3_.refs_1_), channel_id=1, source_target_pairs={{8,0},{16,8},{24,16},{9,1},{17,9},{25,17},{10,2},{18,10},{26,18},{... | collective-permute-start | bytes 393224 | tf_op jit(solution)/shard_map/ppermute | solution.py:904
  18.7 0.9 %copy-start.5 = (bf16[6,64,1024]{2,1,0:T(8,128)(2,1)}, bf16[6,64,1024]{2,1,0:T(8,128)(2,1)S(1)}, u32[]{:S(2)}) copy-start(bf16[6,64,1024]{2,1,0:T(8,128)(2,1)S(1)} %get-tuple-element.29.refs_2_) | copy-start | bytes 2359300
  23.3 1.5 %collective-permute-start.2 = (bf16[13,64,128]{2,1,0:T(8,128)(2,1)S(1)}, bf16[13,64,128]{2,1,0:T(8,128)(2,1)S(1)}, u32[]{:S(2)}, u32[]{:S(2)}) collective-permute-start(bf16[13,64,128]{2,1,0:T(8,128)(2,1)S(1)} %side.1.own_ref), channel_id=1, source_target_pairs={{0,4},{4,0},{1,5},{5,1},{2,6},{6,2},{3,7},{7,3},{8,12},{12,8},{9,1... | collective-permute-start | bytes 638984 | tf_op jit(solution)/shard_map/ppermute | solution.py:904
  24.9 8.0 %collective-permute-start.3 = (bf16[3,64,128]{2,1,0:T(8,128)(2,1)S(1)}, bf16[3,64,128]{2,1,0:T(8,128)(2,1)S(1)}, u32[]{:S(2)}, u32[]{:S(2)}) collective-permute-start(bf16[3,64,128]{2,1,0:T(8,128)(2,1)S(1)} %get-tuple-element.36), channel_id=1, source_target_pairs={{0,1},{1,2},{2,3},{4,5},{5,6},{6,7},{8,9},{9,10},{10,11},{12,13},{... | collective-permute-start | bytes 147464 | tf_op jit(solution)/shard_map/ppermute | solution.py:904
  28.2 1.1 %copy-start.6 = (bf16[6,64,1024]{2,1,0:T(8,128)(2,1)S(1)}, bf16[6,64,1024]{2,1,0:T(8,128)(2,1)}, u32[]{:S(2)}) copy-start(bf16[6,64,1024]{2,1,0:T(8,128)(2,1)} %copy-done.5) | copy-start | bytes 2359300
  32.9 1.9 %collective-permute-start.5 = (f32[288,256]{1,0:T(8,128)S(1)}, f32[288,256]{1,0:T(8,128)S(1)}, u32[]{:S(2)}, u32[]{:S(2)}) collective-permute-start(f32[288,256]{1,0:T(8,128)S(1)} %get-tuple-element.41), channel_id=1, source_target_pairs={{0,4},{4,0},{1,5},{5,1},{2,6},{6,2},{3,7},{7,3},{8,12},{12,8},{9,1... | collective-permute-start | bytes 884744 | tf_op jit(solution)/shard_map/ppermute | solution.py:904
  33.0 9.7 %copy-start.7 = (bf16[6,64,1024]{2,1,0:T(8,128)(2,1)S(1)}, bf16[6,64,1024]{2,1,0:T(8,128)(2,1)}, u32[]{:S(2)}) copy-start(bf16[6,64,1024]{2,1,0:T(8,128)(2,1)} %copy-done.5) | copy-start | bytes 2359300
  33.0 9.6 %collective-permute-start.4 = (bf16[2,64,128]{2,1,0:T(8,128)(2,1)S(1)}, bf16[2,64,128]{2,1,0:T(8,128)(2,1)S(1)}, u32[]{:S(2)}, u32[]{:S(2)}) collective-permute-start(bf16[2,64,128]{2,1,0:T(8,128)(2,1)S(1)} %get-tuple-element.39.ztiles_ref), channel_id=1, source_target_pairs={{1,0},{2,1},{3,2},{5,4},{6,5},{7,6},{9,8},{10,9},{11,10},{13,12},{... | collective-permute-start | bytes 98312 | tf_op jit(solution)/shard_map/ppermute | solution.py:904
  36.3 14.6 %all-to-all-start.1 = ((bf16[16,32,128]{2,1,0:T(8,128)(2,1)}), bf16[16,32,128]{2,1,0:T(8,128)(2,1)S(1)}, u32[]{:S(2)}, u32[]{:S(2)}) async-start(bf16[16,32,128]{2,1,0:T(8,128)(2,1)} %finish.1), calls=%async_computation.1 | async-start | bytes 262144 | tf_op jit(solution)/shard_map/all_to_all | solution.py:757
  42.6 8.2 %copy-start.2 = (f32[3456]{0:T(1024)S(1)}, f32[3456]{0:T(1024)}, u32[]{:S(2)}) copy-start(f32[3456]{0:T(1024)} %param.9) | copy-start | bytes 41476
  42.6 8.2 %copy-start.3 = (f32[3456]{0:T(1024)S(1)}, f32[3456]{0:T(1024)}, u32[]{:S(2)}) copy-start(f32[3456]{0:T(1024)} %param.10) | copy-start | bytes 41476
  42.7 8.2 %copy-start.4 = (f32[3456]{0:T(1024)S(1)}, f32[3456]{0:T(1024)}, u32[]{:S(2)}) copy-start(f32[3456]{0:T(1024)} %param.11) | copy-start | bytes 41476

commit v4 on v2

--- a/solution.py
+++ b/solution.py
@@ -14,7 +14,7 @@
 HBM = pl.BlockSpec(memory_space=pltpu.HBM)
 F32 = jnp.float32
 BF16 = jnp.bfloat16
-FACES_VMEM = 56_200_000
+FACES_VMEM = 55_900_000
 INNER_VMEM = 53_000_000
 
 
@@ -37,7 +37,9 @@
     return jnp.where(p > 0, u, jnp.zeros_like(u))
 
 
-def face_kernel(p_ref, u_ref, low_ref, high_ref, p_buf, u_buf, tile, sems):
+def face_kernel(axis, p_ref, u_ref, *refs):
+    p_buf, u_buf, tile, sems = refs[-4:]
+    out_refs, swap_refs = refs[:2], refs[2:-4]
     size_x, size_z = p_ref.shape[1], p_ref.shape[3]
     copies = []
     for k, x in enumerate((0, size_x - 1)):
@@ -48,7 +50,7 @@
         for copy in pair:
             copy.start()
         copies.append(pair)
-    for k, out_ref in enumerate((low_ref, high_ref)):
+    for k, out_ref in enumerate(out_refs):
         for copy in copies[k]:
             copy.wait()
 
@@ -56,17 +58,30 @@
             out_ref[:, y * size_z : (y + 1) * size_z] = value
 
         to_planes(masked(p_buf[k], u_buf[k]), tile.at[k], write)
-
-
-def faces(preact, upstream):
+    if axis is not None:
+        odd = lax.rem(lax.axis_index(axis), 2) == 1
+
+        @pl.when(odd)
+        def _():
+            for swap_ref, out_ref in zip(swap_refs, out_refs):
+                swap_ref[...] = out_ref[...]
+
+        @pl.when(jnp.logical_not(odd))
+        def _():
+            for swap_ref, out_ref in zip(swap_refs, out_refs[::-1]):
+                swap_ref[...] = out_ref[...]
+
+
+def faces(preact, upstream, axis=None):
     channels, size_x, size_y, size_z = preact.shape
     face = jax.ShapeDtypeStruct((channels, size_y * size_z), BF16)
     buffer = pltpu.VMEM((2, channels, size_y, size_z), BF16)
-    return pl.pallas_call(
-        face_kernel,
+    count = 2 if axis is None else 4
+    return pl.pallas_call(
+        functools.partial(face_kernel, axis),
         in_specs=[HBM, HBM],
-        out_specs=[VMEM] * 2,
-        out_shape=[face, face],
+        out_specs=[VMEM] * count,
+        out_shape=[face] * count,
         scratch_shapes=[
             buffer,
             buffer,
@@ -450,30 +465,41 @@
     )(preact, upstream, activations, first, last, share)
 
 
-def side_kernel(xlo_ref, xhi_ref, own_ref, sent_ref):
+def side_kernel(odd_ref, even_ref, own_ref, sent_ref, xlo_ref, xhi_ref):
     size_x = own_ref.shape[0] - 3
     size_z = own_ref.shape[-1]
     size_y = xlo_ref.shape[-1] // size_z
-    sent_ref[0] = row_for_other(xlo_ref, size_z)
+    odd = lax.rem(lax.axis_index("gx"), 2) == 1
+    first, second = even_ref[...].astype(F32), odd_ref[...].astype(F32)
+    low = jnp.where(odd, first, second).astype(BF16)
+    high = jnp.where(odd, second, first).astype(BF16)
+    xlo_ref[...] = low
+    xhi_ref[...] = high
+    sent_ref[0] = row_for_other(low, size_z)
     for x in range(size_x):
         sent_ref[x + 1] = own_ref[x]
-    sent_ref[size_x + 1] = row_for_other(xhi_ref, size_z)
-    tiles = z_tiles([xlo_ref[...], xhi_ref[...]], size_y, size_z, (0, size_x + 1))
+    sent_ref[size_x + 1] = row_for_other(high, size_z)
+    tiles = z_tiles([low, high], size_y, size_z, (0, size_x + 1))
     for k in range(2):
         sent_ref[size_x + 2 + k] = (own_ref[size_x + k].astype(F32) + tiles[k]).astype(BF16)
     sent_ref[size_x + 4] = own_ref[size_x + 2]
 
 
-def side(x_halos, own):
+def side(halves, own):
+    plane = jax.ShapeDtypeStruct(halves[0].shape, BF16)
     return pl.pallas_call(
         side_kernel,
         in_specs=[VMEM] * 3,
-        out_specs=VMEM,
-        out_shape=jax.ShapeDtypeStruct((own.shape[0] + 2, *own.shape[1:]), BF16),
+        out_specs=[VMEM] * 3,
+        out_shape=[
+            jax.ShapeDtypeStruct((own.shape[0] + 2, *own.shape[1:]), BF16),
+            plane,
+            plane,
+        ],
         compiler_params=params(),
         cost_estimate=cost(2**25, 2**19),
         name="side",
-    )(*x_halos, own)
+    )(*halves, own)
 
 
 def both_columns(is_first, own, other, number, area):
@@ -682,11 +708,10 @@
     return tuple(out.reshape(share) for out in outs)
 
 
-def pair_dgrad_kernel(rows, *refs):
-    w_ref, out_ref, g3, turned, weights, tile, chunks, lines = refs[9:]
-    channels, size_x, size_y, size_z = out_ref.shape
+def spread_kernel(rows, w_ref, weights_ref, turned, chunks, lines):
+    count, height, width = w_ref.shape
+    channels = rows * count
     taps = 27 * channels
-    count, height, width = w_ref.shape
     chunks[...] = w_ref[...].astype(F32).reshape(chunks.shape)
     line = jnp.concatenate(
         [chunks[pl.ds(k, count, stride=height), :] for k in range(rows * taps // width)], axis=1
@@ -700,27 +725,45 @@
                 :, k * LANES : (k + 1) * LANES
             ]
     whole = [lines[k * channels : (k + 1) * channels, :] for k in range(pieces)]
-    spread_weights(jnp.concatenate(whole, axis=1)[:, :taps], turned, weights)
+    spread_weights(jnp.concatenate(whole, axis=1)[:, :taps], turned, weights_ref)
+
+
+def spread(kernel, channels, rows):
+    return pl.pallas_call(
+        functools.partial(spread_kernel, rows),
+        in_specs=[VMEM],
+        out_specs=VMEM,
+        out_shape=jax.ShapeDtypeStruct((3, 2 * channels, 12 * channels), BF16),
+        scratch_shapes=[
+            flat_scratch(channels),
+            pltpu.VMEM((kernel.shape[0] * kernel.shape[1], kernel.shape[2]), F32),
+            pltpu.VMEM((-(-27 * channels // LANES) * channels, LANES), F32),
+        ],
+        compiler_params=params(),
+        cost_estimate=cost(2**20, 2**21),
+        name="spread",
+    )(kernel)
+
+
+def pair_dgrad_kernel(*refs):
+    weights_ref, out_ref, g3, tile = refs[9:]
+    _, size_x, size_y, size_z = out_ref.shape
     halo = pair_z_halo(refs[7], refs[8], size_x + 2, size_y, size_z)
-    input_products(refs, halo, g3, weights, tile, out_ref)
-
-
-def pair_dgrad(sources, kernel, shape, rows):
-    channels = shape[0]
-    return pl.pallas_call(
-        functools.partial(pair_dgrad_kernel, rows),
+    input_products(refs, halo, g3, weights_ref, tile, out_ref)
+
+
+def pair_dgrad(sources, weights, shape):
+    channels, _, size_y, size_z = shape
+    return pl.pallas_call(
+        pair_dgrad_kernel,
         in_specs=[VMEM] * 10,
         out_specs=VMEM,
         out_shape=jax.ShapeDtypeStruct(shape, BF16),
-        scratch_shapes=dgrad_scratch(*shape)
-        + [
-            pltpu.VMEM((kernel.shape[0] * kernel.shape[1], kernel.shape[2]), F32),
-            pltpu.VMEM((-(-27 * channels // LANES) * channels, LANES), F32),
-        ],
+        scratch_shapes=[g3_scratch(*shape), pltpu.VMEM((2, channels * size_y, size_z), F32)],
         compiler_params=params(32 * 2**20),
         cost_estimate=dgrad_cost(*shape),
         name="dgrad",
-    )(*sources, kernel)
+    )(*sources, weights)
 
 
 def pair_program(activations, preact, upstream, master, first_moment, second_moment, scale):
@@ -731,8 +774,9 @@
     span = lax.axis_size("gz") * rows
     used = master.shape[0] // LANES
     tall = -(-used // 16) * 16
-    first, last = faces(preact, upstream)
-    x_halos = (shifted(last, {"gx": 1}), shifted(first, {"gx": -1}))
+    first, last, *swaps = faces(preact, upstream, "gx")
+    odd_halves = swapped(swaps[1], "gx", 1)
+    even_halves = swapped(swaps[0], "gx", 0)
     inner, planes_x, own, sent = pair_inner(
         preact,
         upstream,
@@ -743,8 +787,8 @@
         (devices, tall, LANES),
     )
     kernel = lax.all_to_all(sent, AXES, 0, 0, tiled=True)
-    planes = (x_halos[0], first, inner, last, x_halos[1])
-    own = side(x_halos, own)
+    own, xlo, xhi = side((odd_halves, even_halves), own)
+    planes = (xlo, first, inner, last, xhi)
     other = shifted(own, {"gy": "swap"})
     zlo, zhi = join(own, other, size_x * size_y)
     below = shifted(zhi, {"gz": 1})
@@ -752,13 +796,13 @@
     mine, theirs = pair_wgrad(sources, planes_x, shape, span)
     theirs, below = lax.optimization_barrier((theirs, below))
     theirs = shifted(theirs, {"gy": "swap"})
-    zlo, below = lax.optimization_barrier((zlo, below))
-    above = shifted(zlo, {"gz": -1})
     edge = z_edges(own, other, zlo, below, span, (size_x, size_y), mine.shape[1])
     part = finish(mine, theirs, edge, scale, rows, channels, (devices // 2, tall, LANES))
-    part, kernel = lax.optimization_barrier((part, kernel))
+    part, kernel, zlo = lax.optimization_barrier((part, kernel, zlo))
     parts = lax.all_to_all(part, ("gx", "gz"), 0, 0, tiled=True)
-    grad_input = pair_dgrad((*sources, below, above), kernel, shape, rows)
+    above = shifted(zlo, {"gz": -1})
+    weights = spread(kernel, channels, rows)
+    grad_input = pair_dgrad((*sources, below, above), weights, shape)
     return grad_input, *adam(parts, master, first_moment, second_moment)
 
 
@@ -908,6 +952,13 @@
     return lax.ppermute(value, names if len(names) > 1 else names[0], pairs)
 
 
+def swapped(value, axis, start):
+    pairs = []
+    for low in range(start, lax.axis_size(axis) - 1, 2):
+        pairs += [(low, low + 1), (low + 1, low)]
+    return lax.ppermute(value, axis, pairs)
+
+
 def local(activations, preact, upstream, master, first_moment, second_moment):
     channels, size_x, size_y, size_z = activations.shape
     devices = math.prod(lax.axis_size(a) for a in AXES)

time: 48.6 us -> 49.1 us (1.010)
  Pallas kernels: 16.8 us -> 17.6 us
    ppermute x0 -> x2, starting transfers between devices: none -> 6.4 us  [swapped(): return lax.ppermute(value, axis, pairs)]
    ppermute x6 -> x4, starting transfers between devices: 11.2 us -> 5.09 us  [shifted(): return lax.ppermute(value, names if len(names) > 1 else names[0], pairs)]
    ppermute x0 -> x2, waiting for transfers between devices: none -> 2.12 us  [swapped(): return lax.ppermute(value, axis, pairs)]
    all_to_all x1, waiting for transfers between devices: 2.98 us -> 1.78 us  [pair_program(): parts = lax.all_to_all(part, ('gx', 'gz'), 0, 0, tiled=True)]
    ppermute x6 -> x4, waiting for transfers between devices: 2.37 us -> 1.23 us  [shifted(): return lax.ppermute(value, names if len(names) > 1 else names[0], pairs)]
    pallas_call x3 -> x4, Pallas kernels: 6.83 us -> 7.63 us  [the longest x1 5.28 us: pair_dgrad(): pl.pallas_call(pair_dgrad_kernel, in_specs=[VMEM] * 10, out_specs=VMEM, o...]
  transfers between devices with their start and end apart: 8 -> 8, of which waited for: 2 -> 3; matrix products, arithmetic and copies ran while one was open for 0% -> 0% of each run, Pallas kernels for 30% -> 31%
where the time goes in v4:
time: 49.1 us; the launch traced here: 48.8 us
  starting transfers between devices  25.2 us (51%)
  Pallas kernels  17.6 us (36%)
  waiting for transfers between devices  5.13 us (10%)
  between operations  0.79 us (2%)
    all_to_all x1, starting transfers between devices, pair_program(): parts = lax.all_to_all(part, ('gx', 'gz'), 0, 0, tiled=True)  8.82 us
    ppermute x2, starting transfers between devices, swapped(): return lax.ppermute(value, axis, pairs)  6.4 us
    pallas_call x1, Pallas kernels, pair_dgrad(): pl.pallas_call(pair_dgrad_kernel, in_specs=[VMEM] * 10, out_specs=VMEM, o...  5.28 us
    ppermute x4, starting transfers between devices, shifted(): return lax.ppermute(value, names if len(names) > 1 else names[0], pairs)  5.09 us
    all_to_all x1, starting transfers between devices, pair_program(): kernel = lax.all_to_all(sent, AXES, 0, 0, tiled=True)  4.94 us
    pallas_call x1, Pallas kernels, pair_inner(): pl.pallas_call(pair_inner_kernel, in_specs=[HBM] * 3 + [VMEM] * 3, out_sp...  3.79 us
    pallas_call x1, Pallas kernels, pair_wgrad(): pl.pallas_call(functools.partial(pair_wgrad_kernel, span), in_specs=[VMEM...  3.6 us
    ppermute x2, waiting for transfers between devices, swapped(): return lax.ppermute(value, axis, pairs)  2.12 us
  transfers between devices with their start and end apart: 8, of which 3 were waited for; matrix products, arithmetic and copies ran while one was open for 0% of the time, Pallas kernels for 31%

profile of v4, /device:TPU:0, one launch (start us, length us, event | category | flops | bytes accessed | tf_op | source)
XLA Modules:
  0.0 48.8 jit_solution(6176997694601304842)
XLA Ops:
  0.6 0.0 copy-start
  0.6 1.3 %faces.1 = (bf16[64,1024]{1,0:T(8,128)(2,1)S(1)}, bf16[64,1024]{1,0:T(8,128)(2,1)S(1)}, bf16[64,1024]{1,0:T(8,128)(2,1)S(1)}, bf16[64,1024]{1,0:T(8,128)(2,1)S(1)}) custom-call(bf16[64,8,8,128]{3,2,1,0:T(8,128)(2,1)} %refs_0_.1, bf16[64,8,8,128]{3,2,1,0:T(8,128)(2,1)} %refs_1_.1), custom_call_target="tpu_custom_call" | custom-call | bytes 1048576 | tf_op jit(solution)/shard_map/faces/pallas_call | solution.py:80
  1.9 0.7 %collective-permute-start = (bf16[64,1024]{1,0:T(8,128)(2,1)S(1)}, bf16[64,1024]{1,0:T(8,128)(2,1)S(1)}, u32[]{:S(2)}, u32[]{:S(2)}) collective-permute-start(bf16[64,1024]{1,0:T(8,128)(2,1)S(1)} %get-tuple-element.29), channel_id=1, source_target_pairs={{8,16},{16,8},{9,17},{17,9},{10,18},{18,10},{11,19},{19,11},{12,20... | collective-permute-start | bytes 393224 | tf_op jit(solution)/shard_map/ppermute | solution.py:959
  2.6 5.7 %collective-permute-start.1 = (bf16[64,1024]{1,0:T(8,128)(2,1)S(1)}, bf16[64,1024]{1,0:T(8,128)(2,1)S(1)}, u32[]{:S(2)}, u32[]{:S(2)}) collective-permute-start(bf16[64,1024]{1,0:T(8,128)(2,1)S(1)} %get-tuple-element.30), channel_id=1, source_target_pairs={{0,8},{8,0},{16,24},{24,16},{1,9},{9,1},{17,25},{25,17},{2,10},{10... | collective-permute-start | bytes 393224 | tf_op jit(solution)/shard_map/ppermute | solution.py:959
  8.3 0.0 copy-done
  8.3 3.8 %inner.1 = (bf16[6,64,1024]{2,1,0:T(8,128)(2,1)S(1)}, bf16[8,64,1024]{2,1,0:T(8,128)(2,1)S(1)}, bf16[11,64,128]{2,1,0:T(8,128)(2,1)S(1)}, bf16[32,32,128]{2,1,0:T(8,128)(2,1)}) custom-call(bf16[64,8,8,128]{3,2,1,0:T(8,128)(2,1)} %refs_0_.1, bf16[64,8,8,128]{3,2,1,0:T(8,128)(2,1)} %refs_1_.1, bf16[64,8,8,128]{3,2,1,0:T(8,128)(2,1)} %refs_2_.1, ...), custom_call_target="tpu_custom_call" | custom-call | bytes 6291456 | tf_op jit(solution)/shard_map/inner/pallas_call | solution.py:451
  12.1 0.0 collective-permute-done.odd_ref
  12.2 2.1 %collective-permute-done.1.even_ref = bf16[64,1024]{1,0:T(8,128)(2,1)S(1)} collective-permute-done((bf16[64,1024]{1,0:T(8,128)(2,1)S(1)}, bf16[64,1024]{1,0:T(8,128)(2,1)S(1)}, u32[]{:S(2)}, u32[]{:S(2)}) %collective-permute-start.1) | collective-permute-done | bytes 131104 | tf_op jit(solution)/shard_map/ppermute | solution.py:959
  14.3 0.4 side.1
  14.7 0.1 collective-permute-start.2
  14.7 4.9 %all-to-all-start = ((bf16[32,32,128]{2,1,0:T(8,128)(2,1)}), bf16[32,32,128]{2,1,0:T(8,128)(2,1)S(1)}, u32[]{:S(2)}, u32[]{:S(2)}) async-start(bf16[32,32,128]{2,1,0:T(8,128)(2,1)} %get-tuple-element.45), calls=%async_computation | async-start | bytes 524288 | tf_op jit(solution)/shard_map/all_to_all | solution.py:789
  19.7 0.0 collective-permute-done.2.refs_5_.refs_6_.other_ref
  19.7 0.1 join.1
  19.8 3.7 %collective-permute-start.3 = (bf16[3,64,128]{2,1,0:T(8,128)(2,1)S(1)}, bf16[3,64,128]{2,1,0:T(8,128)(2,1)S(1)}, u32[]{:S(2)}, u32[]{:S(2)}) collective-permute-start(bf16[3,64,128]{2,1,0:T(8,128)(2,1)S(1)} %get-tuple-element.40), channel_id=1, source_target_pairs={{0,1},{1,2},{2,3},{4,5},{5,6},{6,7},{8,9},{9,10},{10,11},{12,13},{... | collective-permute-start | bytes 147464 | tf_op jit(solution)/shard_map/ppermute | solution.py:952
  23.4 3.6 %wgrad.1 = (f32[288,256]{1,0:T(8,128)S(1)}, f32[288,256]{1,0:T(8,128)S(1)}) custom-call(bf16[64,1024]{1,0:T(8,128)(2,1)S(1)} %get-tuple-element.34.refs_0_, bf16[64,1024]{1,0:T(8,128)(2,1)S(1)} %get-tuple-element.31.refs_3_.refs_1_, bf16[6,64,1024]{2,1,0:T(8,128)(2,1)S(1)} %get-tuple-element.35.refs_2_, ...), custom_call_target="tpu_custom_call" | custom-call | flops 2264924160 | bytes 4194304 | tf_op jit(solution)/shard_map/wgrad/pallas_call | solution.py:558
  27.1 0.0 collective-permute-done.3.below_ref.refs_7_
  27.1 0.1 collective-permute-start.4
  27.1 0.3 edges.1.edge_ref
  27.5 1.2 %collective-permute-done.4.other_ref = f32[288,256]{1,0:T(8,128)S(1)} collective-permute-done((f32[288,256]{1,0:T(8,128)S(1)}, f32[288,256]{1,0:T(8,128)S(1)}, u32[]{:S(2)}, u32[]{:S(2)}) %collective-permute-start.4) | collective-permute-done | bytes 294944 | tf_op jit(solution)/shard_map/ppermute | solution.py:952
  28.7 1.5 %finish.1 = bf16[16,32,128]{2,1,0:T(8,128)(2,1)} custom-call(f32[288,256]{1,0:T(8,128)S(1)} %get-tuple-element.42.mine_ref, f32[288,256]{1,0:T(8,128)S(1)} %collective-permute-done.4.other_ref, f32[2,96,256]{2,1,0:T(8,128)S(1)} %edges.1.edge_ref), custom_call_target="tpu_custom_call" | custom-call | flops 16777216 | bytes 1048576 | tf_op jit(solution)/shard_map/finish/pallas_call | solution.py:660
  30.2 0.0 all-to-all-done.w_ref
  30.2 1.3 %collective-permute-start.5 = (bf16[2,64,128]{2,1,0:T(8,128)(2,1)S(1)}, bf16[2,64,128]{2,1,0:T(8,128)(2,1)S(1)}, u32[]{:S(2)}, u32[]{:S(2)}) collective-permute-start(bf16[2,64,128]{2,1,0:T(8,128)(2,1)S(1)} %get-tuple-element.46.ztiles_ref), channel_id=1, source_target_pairs={{1,0},{2,1},{3,2},{5,4},{6,5},{7,6},{9,8},{10,9},{11,10},{13,12},{... | collective-permute-start | bytes 98312 | tf_op jit(solution)/shard_map/ppermute | solution.py:952
  31.5 8.8 %all-to-all-start.1 = ((bf16[16,32,128]{2,1,0:T(8,128)(2,1)}), bf16[16,32,128]{2,1,0:T(8,128)(2,1)S(1)}, u32[]{:S(2)}, u32[]{:S(2)}) async-start(bf16[16,32,128]{2,1,0:T(8,128)(2,1)} %finish.1), calls=%async_computation.1 | async-start | bytes 262144 | tf_op jit(solution)/shard_map/all_to_all | solution.py:802
  40.3 0.7 %spread.1.refs_9_ = bf16[3,128,768]{2,1,0:T(8,128)(2,1)S(1)} custom-call(bf16[32,32,128]{2,1,0:T(8,128)(2,1)S(1)} %all-to-all-done.w_ref), custom_call_target="tpu_custom_call" | custom-call | flops 1048576 | bytes 2097152 | tf_op jit(solution)/shard_map/spread/pallas_call | solution.py:732
  41.0 0.0 copy-start.1
  41.0 0.0 copy-start.2
  41.0 0.0 collective-permute-done.5.refs_8_
  41.0 5.3 %dgrad.1 = bf16[64,8,8,128]{3,2,1,0:T(8,128)(2,1)} custom-call(bf16[64,1024]{1,0:T(8,128)(2,1)S(1)} %get-tuple-element.34.refs_0_, bf16[64,1024]{1,0:T(8,128)(2,1)S(1)} %get-tuple-element.31.refs_3_.refs_1_, bf16[6,64,1024]{2,1,0:T(8,128)(2,1)S(1)} %get-tuple-element.35.refs_2_, bf16[64,1024]{1,0:T(8,128)(2,1)S(1)} %get-tuple-element.32.refs_4_.refs_3_, ...), custom_call_target="tpu_custom_call" | custom-call | flops 2415919104 | bytes 4194304 | tf_op jit(solution)/shard_map/dgrad/pallas_call | solution.py:757
  46.3 1.8 %all-to-all-done.1.parts_ref = bf16[16,32,128]{2,1,0:T(8,128)(2,1)S(1)} async-done(((bf16[16,32,128]{2,1,0:T(8,128)(2,1)}), bf16[16,32,128]{2,1,0:T(8,128)(2,1)S(1)}, u32[]{:S(2)}, u32[]{:S(2)}) %all-to-all-start.1) | async-done | bytes 131104 | tf_op jit(solution)/shard_map/all_to_all | solution.py:802
  48.1 0.0 copy-done.1
  48.1 0.0 copy-done.2
  48.1 0.7 %adam.1 = (f32[27,128]{1,0:T(8,128)}, f32[27,128]{1,0:T(8,128)}, f32[27,128]{1,0:T(8,128)}, f32[27,128]{1,0:T(8,128)}) custom-call(bf16[16,32,128]{2,1,0:T(8,128)(2,1)S(1)} %all-to-all-done.1.parts_ref, f32[27,128]{1,0:T(8,128)S(1)} %bitcast.8, f32[27,128]{1,0:T(8,128)S(1)} %bitcast.9, f32[27,128]{1,0:T(8,128)S(1)} %bitcast.10), custom_call_target="tpu_custom_call" | custom-call | flops 262144 | bytes 262144 | tf_op jit(solution)/shard_map/adam/pallas_call | solution.py:699
Async XLA Ops:
  0.6 7.7 %copy-start = (f32[3456]{0:T(1024)S(1)}, f32[3456]{0:T(1024)}, u32[]{:S(2)}) copy-start(f32[3456]{0:T(1024)} %param.9) | copy-start | bytes 41476
  1.9 10.2 %collective-permute-start = (bf16[64,1024]{1,0:T(8,128)(2,1)S(1)}, bf16[64,1024]{1,0:T(8,128)(2,1)S(1)}, u32[]{:S(2)}, u32[]{:S(2)}) collective-permute-start(bf16[64,1024]{1,0:T(8,128)(2,1)S(1)} %get-tuple-element.29), channel_id=1, source_target_pairs={{8,16},{16,8},{9,17},{17,9},{10,18},{18,10},{11,19},{19,11},{12,20... | collective-permute-start | bytes 393224 | tf_op jit(solution)/shard_map/ppermute | solution.py:959
  2.6 11.7 %collective-permute-start.1 = (bf16[64,1024]{1,0:T(8,128)(2,1)S(1)}, bf16[64,1024]{1,0:T(8,128)(2,1)S(1)}, u32[]{:S(2)}, u32[]{:S(2)}) collective-permute-start(bf16[64,1024]{1,0:T(8,128)(2,1)S(1)} %get-tuple-element.30), channel_id=1, source_target_pairs={{0,8},{8,0},{16,24},{24,16},{1,9},{9,1},{17,25},{25,17},{2,10},{10... | collective-permute-start | bytes 393224 | tf_op jit(solution)/shard_map/ppermute | solution.py:959
  14.7 5.0 %collective-permute-start.2 = (bf16[13,64,128]{2,1,0:T(8,128)(2,1)S(1)}, bf16[13,64,128]{2,1,0:T(8,128)(2,1)S(1)}, u32[]{:S(2)}, u32[]{:S(2)}) collective-permute-start(bf16[13,64,128]{2,1,0:T(8,128)(2,1)S(1)} %get-tuple-element.37.own_ref), channel_id=1, source_target_pairs={{0,4},{4,0},{1,5},{5,1},{2,6},{6,2},{3,7},{7,3},{8,12},{12,8},{9,1... | collective-permute-start | bytes 638984 | tf_op jit(solution)/shard_map/ppermute | solution.py:952
  14.7 15.4 %all-to-all-start = ((bf16[32,32,128]{2,1,0:T(8,128)(2,1)}), bf16[32,32,128]{2,1,0:T(8,128)(2,1)S(1)}, u32[]{:S(2)}, u32[]{:S(2)}) async-start(bf16[32,32,128]{2,1,0:T(8,128)(2,1)} %get-tuple-element.45), calls=%async_computation | async-start | bytes 524288 | tf_op jit(solution)/shard_map/all_to_all | solution.py:789
  19.8 7.3 %collective-permute-start.3 = (bf16[3,64,128]{2,1,0:T(8,128)(2,1)S(1)}, bf16[3,64,128]{2,1,0:T(8,128)(2,1)S(1)}, u32[]{:S(2)}, u32[]{:S(2)}) collective-permute-start(bf16[3,64,128]{2,1,0:T(8,128)(2,1)S(1)} %get-tuple-element.40), channel_id=1, source_target_pairs={{0,1},{1,2},{2,3},{4,5},{5,6},{6,7},{8,9},{9,10},{10,11},{12,13},{... | collective-permute-start | bytes 147464 | tf_op jit(solution)/shard_map/ppermute | solution.py:952
  27.1 1.6 %collective-permute-start.4 = (f32[288,256]{1,0:T(8,128)S(1)}, f32[288,256]{1,0:T(8,128)S(1)}, u32[]{:S(2)}, u32[]{:S(2)}) collective-permute-start(f32[288,256]{1,0:T(8,128)S(1)} %get-tuple-element.43), channel_id=1, source_target_pairs={{0,4},{4,0},{1,5},{5,1},{2,6},{6,2},{3,7},{7,3},{8,12},{12,8},{9,1... | collective-permute-start | bytes 884744 | tf_op jit(solution)/shard_map/ppermute | solution.py:952
  30.2 10.8 %collective-permute-start.5 = (bf16[2,64,128]{2,1,0:T(8,128)(2,1)S(1)}, bf16[2,64,128]{2,1,0:T(8,128)(2,1)S(1)}, u32[]{:S(2)}, u32[]{:S(2)}) collective-permute-start(bf16[2,64,128]{2,1,0:T(8,128)(2,1)S(1)} %get-tuple-element.46.ztiles_ref), channel_id=1, source_target_pairs={{1,0},{2,1},{3,2},{5,4},{6,5},{7,6},{9,8},{10,9},{11,10},{13,12},{... | collective-permute-start | bytes 98312 | tf_op jit(solution)/shard_map/ppermute | solution.py:952
  31.5 16.6 %all-to-all-start.1 = ((bf16[16,32,128]{2,1,0:T(8,128)(2,1)}), bf16[16,32,128]{2,1,0:T(8,128)(2,1)S(1)}, u32[]{:S(2)}, u32[]{:S(2)}) async-start(bf16[16,32,128]{2,1,0:T(8,128)(2,1)} %finish.1), calls=%async_computation.1 | async-start | bytes 262144 | tf_op jit(solution)/shard_map/all_to_all | solution.py:802
  41.0 7.1 %copy-start.1 = (f32[3456]{0:T(1024)S(1)}, f32[3456]{0:T(1024)}, u32[]{:S(2)}) copy-start(f32[3456]{0:T(1024)} %param.10) | copy-start | bytes 41476
  41.0 7.1 %copy-start.2 = (f32[3456]{0:T(1024)S(1)}, f32[3456]{0:T(1024)}, u32[]{:S(2)}) copy-start(f32[3456]{0:T(1024)} %param.11) | copy-start | bytes 41476

commit v5 on v4

--- a/solution.py
+++ b/solution.py
@@ -26,18 +26,21 @@
     return pl.CostEstimate(flops=flops, bytes_accessed=moved, transcendentals=0)
 
 
-def to_planes(value, tile, write):
+def to_planes(value, tile, write, rows=1):
     channels, size_y, size_z = value.shape
+    count = channels // rows
     tile[...] = value.astype(F32).reshape(channels * size_y, size_z)
     for y in range(size_y):
-        write(y, tile[pl.ds(y, channels, stride=size_y), :].astype(BF16))
+        for r in range(rows):
+            picked = tile[pl.ds(r * size_y + y, count, stride=rows * size_y), :]
+            write(slice(r * count, (r + 1) * count), y, picked.astype(BF16))
 
 
 def masked(p, u):
     return jnp.where(p > 0, u, jnp.zeros_like(u))
 
 
-def face_kernel(axis, p_ref, u_ref, *refs):
+def face_kernel(axis, rows, p_ref, u_ref, *refs):
     p_buf, u_buf, tile, sems = refs[-4:]
     out_refs, swap_refs = refs[:2], refs[2:-4]
     size_x, size_z = p_ref.shape[1], p_ref.shape[3]
@@ -54,12 +57,12 @@
         for copy in copies[k]:
             copy.wait()
 
-        def write(y, value):
-            out_ref[:, y * size_z : (y + 1) * size_z] = value
-
-        to_planes(masked(p_buf[k], u_buf[k]), tile.at[k], write)
+        def write(at, y, value):
+            out_ref[at, y * size_z : (y + 1) * size_z] = value
+
+        to_planes(masked(p_buf[k], u_buf[k]), tile.at[k], write, rows)
     if axis is not None:
-        odd = lax.rem(lax.axis_index(axis), 2) == 1
+        odd = is_odd(axis)
 
         @pl.when(odd)
         def _():
@@ -72,13 +75,13 @@
                 swap_ref[...] = out_ref[...]
 
 
-def faces(preact, upstream, axis=None):
+def faces(preact, upstream, axis=None, rows=1):
     channels, size_x, size_y, size_z = preact.shape
     face = jax.ShapeDtypeStruct((channels, size_y * size_z), BF16)
     buffer = pltpu.VMEM((2, channels, size_y, size_z), BF16)
     count = 2 if axis is None else 4
     return pl.pallas_call(
-        functools.partial(face_kernel, axis),
+        functools.partial(face_kernel, axis, rows),
         in_specs=[HBM, HBM],
         out_specs=[VMEM] * count,
         out_shape=[face] * count,
@@ -94,7 +97,7 @@
     )(preact, upstream)
 
 
-def read_inner(p_ref, u_ref, a_ref, g_ref, x_ref, p_buf, u_buf, a_buf, tile, sems):
+def read_inner(rows, p_ref, u_ref, a_ref, g_ref, x_ref, p_buf, u_buf, a_buf, tile, sems):
     channels, size_x, size_y, size_z = a_ref.shape
     inner = size_x - 2
     copies = []
@@ -116,21 +119,21 @@
         for copy in copies[x]:
             copy.wait()
 
-        def write(y, value):
-            g_ref[x, :, y * size_z : (y + 1) * size_z] = value
-
-        to_planes(masked(p_buf[x], u_buf[x]), tile.at[x % 2], write)
+        def write(at, y, value):
+            g_ref[x, at, y * size_z : (y + 1) * size_z] = value
+
+        to_planes(masked(p_buf[x], u_buf[x]), tile.at[x % 2], write, rows)
     for x in range(size_x):
         copies[inner + x][0].wait()
 
-        def write(y, value):
-            x_ref[x, :, y * size_z : (y + 1) * size_z] = value
+        def write(at, y, value):
+            x_ref[x, at, y * size_z : (y + 1) * size_z] = value
 
         to_planes(a_buf[x], tile.at[x % 2], write)
 
 
 def inner_kernel(*refs):
-    read_inner(*refs)
+    read_inner(1, *refs)
 
 
 def inner_outputs(channels, size_x, size_y, size_z):
@@ -225,11 +228,11 @@
     return put_columns(columns, lambda number: number, rows_y, size_z)
 
 
-def pair_z_halo(low_ref, high_ref, planes, size_y, size_z):
-    me = lax.axis_index("gy")
+def pair_z_halo(even_ref, odd_ref, planes, size_y, size_z):
+    me, odd = lax.axis_index("gy"), is_odd("gz")
     sides = []
-    for ref in (low_ref, high_ref):
-        first, second = ref[0].astype(F32), ref[1].astype(F32)
+    for low, high in ((even_ref, odd_ref), (odd_ref, even_ref)):
+        first, second = (either(odd, low[k], high[k]) for k in range(2))
         lane = lax.broadcasted_iota(jnp.int32, first.shape, 1)
         own = jnp.where(me == 0, first, second)
         before = jnp.where(me == 0, 0.0, first)
@@ -414,10 +417,10 @@
     return jnp.where(lax.axis_index("gy") == 0, high, low).astype(BF16)
 
 
-def pair_inner_kernel(*refs):
+def pair_inner_kernel(rows, *refs):
     first_ref, last_ref, m_ref = refs[3:6]
-    g_ref, x_ref, side_ref, sent_ref = refs[6:10]
-    tile_ref, tile_sems = refs[15:]
+    g_ref, x_ref, side_ref, columns_ref, sent_ref = refs[6:11]
+    tile_ref, tile_sems = refs[16:]
     share = m_ref[...]
     height = tile_ref.shape[0] - share.shape[0]
     if height:
@@ -429,7 +432,7 @@
     ]
     for copy in copies:
         copy.start()
-    read_inner(*refs[:3], g_ref, x_ref, *refs[10:15])
+    read_inner(rows, *refs[:3], g_ref, x_ref, *refs[11:16])
     size_z = side_ref.shape[-1]
     size_x, channels, plane = x_ref.shape
     size_y = plane // size_z
@@ -440,21 +443,22 @@
     side_ref[size_x] = low.astype(BF16)
     side_ref[size_x + 1] = high.astype(BF16)
     low, high = z_tiles([x_ref[x] for x in range(size_x)], size_y, size_z, range(size_x))
-    side_ref[size_x + 2] = (low + pltpu.roll(high, size_x * size_y, 1)).astype(BF16)
+    columns_ref[...] = (low + pltpu.roll(high, size_x * size_y, 1)).astype(BF16)
     for copy in copies:
         copy.wait()
 
 
-def pair_inner(preact, upstream, activations, first, last, share, sent_shape):
+def pair_inner(preact, upstream, activations, first, last, share, sent_shape, rows):
     shape = preact.shape
     channels, size_x, _, size_z = shape
     return pl.pallas_call(
-        pair_inner_kernel,
+        functools.partial(pair_inner_kernel, rows),
         in_specs=[HBM] * 3 + [VMEM] * 3,
-        out_specs=[VMEM] * 3 + [HBM],
+        out_specs=[VMEM] * 4 + [HBM],
         out_shape=inner_outputs(*shape)
         + [
-            jax.ShapeDtypeStruct((size_x + 3, channels, size_z), BF16),
+            jax.ShapeDtypeStruct((size_x + 2, channels, size_z), BF16),
+            jax.ShapeDtypeStruct((channels, LANES), BF16),
             jax.ShapeDtypeStruct(sent_shape, BF16),
         ],
         scratch_shapes=inner_scratch(*shape)
@@ -465,14 +469,21 @@
     )(preact, upstream, activations, first, last, share)
 
 
+def is_odd(axis):
+    return lax.rem(lax.axis_index(axis), 2) == 1
+
+
+def either(condition, first, second):
+    return jnp.where(condition, first.astype(F32), second.astype(F32))
+
+
 def side_kernel(odd_ref, even_ref, own_ref, sent_ref, xlo_ref, xhi_ref):
-    size_x = own_ref.shape[0] - 3
+    size_x = own_ref.shape[0] - 2
     size_z = own_ref.shape[-1]
     size_y = xlo_ref.shape[-1] // size_z
-    odd = lax.rem(lax.axis_index("gx"), 2) == 1
-    first, second = even_ref[...].astype(F32), odd_ref[...].astype(F32)
-    low = jnp.where(odd, first, second).astype(BF16)
-    high = jnp.where(odd, second, first).astype(BF16)
+    odd = is_odd("gx")
+    low = either(odd, even_ref[...], odd_ref[...]).astype(BF16)
+    high = either(odd, odd_ref[...], even_ref[...]).astype(BF16)
     xlo_ref[...] = low
     xhi_ref[...] = high
     sent_ref[0] = row_for_other(low, size_z)
@@ -482,7 +493,6 @@
     tiles = z_tiles([low, high], size_y, size_z, (0, size_x + 1))
     for k in range(2):
         sent_ref[size_x + 2 + k] = (own_ref[size_x + k].astype(F32) + tiles[k]).astype(BF16)
-    sent_ref[size_x + 4] = own_ref[size_x + 2]
 
 
 def side(halves, own):
@@ -502,85 +512,86 @@
     )(*halves, own)
 
 
-def both_columns(is_first, own, other, number, area):
-    first = jnp.where(is_first, own, other).astype(F32)
-    second = jnp.where(is_first, other, own).astype(F32)
-    lane = lax.broadcasted_iota(jnp.int32, first.shape, 1)
-    return jnp.where(
-        lane < area,
-        pltpu.roll(first, -number * area % LANES, 1),
-        pltpu.roll(second, (1 - number) * area % LANES, 1),
-    )
-
-
-def join_kernel(area, own_ref, other_ref, low_ref, high_ref):
-    at = own_ref.shape[0] - 3
+def own_columns(columns, number, area):
     me = lax.axis_index("gy")
-    for k, out_ref in enumerate((low_ref, high_ref)):
-        out_ref[me] = own_ref[at + k]
-        out_ref[1 - me] = other_ref[at + k]
-    own, other = own_ref[at + 2].astype(F32), other_ref[at + 2].astype(F32)
-    high_ref[2] = both_columns(me == 0, own, other, 1, area).astype(BF16)
-
-
-def join(own, other, area):
+    value = columns.astype(F32)
+    lane = lax.broadcasted_iota(jnp.int32, value.shape, 1)
+    first = pltpu.roll(value, -number * area % LANES, 1)
+    second = pltpu.roll(value, (1 - number) * area % LANES, 1)
+    first = jnp.where(lane < area, first, 0.0)
+    second = jnp.where((lane >= area) & (lane < 2 * area), second, 0.0)
+    return jnp.where(me == 0, first, second)
+
+
+def join_kernel(area, own_ref, other_ref, columns_ref, even_ref, odd_ref):
+    at = own_ref.shape[0] - 2
+    me = lax.axis_index("gy")
+    last = own_columns(columns_ref[...], 1, area).astype(BF16)
+
+    def fill(up_ref, down_ref):
+        for k, out_ref in enumerate((down_ref, up_ref)):
+            out_ref[me] = own_ref[at + k]
+            out_ref[1 - me] = other_ref[at + k]
+        up_ref[2] = last
+        down_ref[2] = last
+
+    odd = is_odd("gz")
+
+    @pl.when(odd)
+    def _():
+        fill(odd_ref, even_ref)
+
+    @pl.when(jnp.logical_not(odd))
+    def _():
+        fill(even_ref, odd_ref)
+
+
+def join(own, other, columns, area):
     return pl.pallas_call(
         functools.partial(join_kernel, area),
-        in_specs=[VMEM] * 2,
+        in_specs=[VMEM] * 3,
         out_specs=[VMEM] * 2,
-        out_shape=[jax.ShapeDtypeStruct((n, *own.shape[1:]), BF16) for n in (2, 3)],
+        out_shape=[jax.ShapeDtypeStruct((3, *own.shape[1:]), BF16)] * 2,
         compiler_params=params(),
         cost_estimate=cost(0, 2**17),
         name="join",
-    )(own, other)
-
-
-def pair_wgrad_kernel(span, *refs):
-    x_ref, mine_ref, theirs_ref, g3, x3, acc = refs[7:]
-    channels = x_ref.shape[1]
-    weight_products(refs, None, x_ref, g3, x3, acc)
-    is_first = lax.axis_index("gy") == 0
-    width = 3 * channels
-    halves = []
-    for half in range(2):
-        at = range(half * span, 9 * channels, 2 * span)
-        halves.append(jnp.concatenate([acc[start : start + span, :] for start in at], axis=0))
-    spare = jnp.zeros((halves[0].shape[0], mine_ref.shape[1] - width), F32)
-    for ref, order in ((mine_ref, halves), (theirs_ref, halves[::-1])):
-        picked = jnp.where(is_first, order[0], order[1])
-        ref[...] = jnp.concatenate([picked, spare], axis=1)
-
-
-def pair_wgrad(sources, planes_x, shape, span):
+    )(own, other, columns)
+
+
+def pair_wgrad_kernel(*refs):
+    x_ref, acc_ref, g3, x3 = refs[7:]
+    weight_products(refs, None, x_ref, g3, x3, acc_ref)
+
+
+def pair_wgrad(sources, planes_x, shape):
     channels = shape[0]
-    width = -(-3 * channels // LANES) * LANES
-    part = jax.ShapeDtypeStruct((9 * channels // 2, width), F32)
-    return pl.pallas_call(
-        functools.partial(pair_wgrad_kernel, span),
+    return pl.pallas_call(
+        pair_wgrad_kernel,
         in_specs=[VMEM] * 8,
-        out_specs=[VMEM] * 2,
-        out_shape=[part, part],
-        scratch_shapes=[g3_scratch(*shape), x3_scratch(*shape), acc_scratch(channels)],
+        out_specs=VMEM,
+        out_shape=jax.ShapeDtypeStruct((9 * channels, 3 * channels), F32),
+        scratch_shapes=[g3_scratch(*shape), x3_scratch(*shape)],
         compiler_params=params(32 * 2**20),
         cost_estimate=wgrad_cost(*shape),
         name="wgrad",
     )(*sources, planes_x)
 
 
-def edge_kernel(span, sizes, own_ref, other_ref, ztiles_ref, below_ref, edge_ref):
+def finish_kernel(scale, rows, sizes, *refs):
+    acc_ref, columns_ref, even_ref, odd_ref, from_odd_ref, from_even_ref = refs[:6]
+    part_ref, flat, chunks = refs[6:]
     size_x, size_y = sizes
-    channels = below_ref.shape[1]
-    count = channels // 2
+    channels = columns_ref.shape[0]
     area = size_x * size_y
-    is_first = lax.axis_index("gy") == 0
-    at = own_ref.shape[0] - 1
-    own, other = own_ref[at].astype(F32), other_ref[at].astype(F32)
-    columns = (both_columns(is_first, own, other, 0, area), below_ref[2].astype(F32))
+    odd = is_odd("gz")
     lane = lax.broadcasted_iota(jnp.int32, (channels, LANES), 1)
     row = lane % size_y
-    few = lax.broadcasted_iota(jnp.int32, (count, LANES), 1)
-    for number, (tile_ref, value) in enumerate(zip((below_ref, ztiles_ref), columns)):
-        jump = area - size_y + 1
+    jump = area - size_y + 1
+    below = [either(odd, from_even_ref[k], from_odd_ref[k]) for k in range(3)]
+    own = [either(odd, even_ref[k], odd_ref[k]) for k in range(2)]
+    pairs = ((below[:2], own_columns(columns_ref[...], 0, area)), (own, below[2]))
+    edges = []
+    for tiles, value in pairs:
         before = jnp.where(lane >= area, pltpu.roll(value, jump, 1), 0.0)
         after = jnp.where(lane < area, pltpu.roll(value, LANES - jump, 1), 0.0)
         right = jnp.concatenate(
@@ -591,86 +602,52 @@
             ],
             axis=0,
         )
-        tiles = []
-        for device in range(2):
-            tile = tile_ref[device].astype(F32)
-            halves = [
-                jnp.concatenate(
-                    [tile[s : s + span] for s in range(half * span, channels, 2 * span)], axis=0
-                )
-                for half in range(2)
-            ]
-            tiles.append(jnp.where(is_first, halves[0], halves[1]))
         left = []
         for a in range(3):
             first = pltpu.roll(tiles[0], -a * size_y % LANES, 1)
             second = pltpu.roll(tiles[1], (area - a * size_y) % LANES, 1)
-            left.append(jnp.where(few < area, first, jnp.where(few < 2 * area, second, 0.0)))
-        product = lax.dot_general(
-            jnp.concatenate(left, axis=0).astype(BF16),
-            right.astype(BF16),
-            (((1,), (1,)), ((), ())),
-            preferred_element_type=F32,
+            left.append(jnp.where(lane < area, first, jnp.where(lane < 2 * area, second, 0.0)))
+        edges.append(
+            lax.dot_general(
+                jnp.concatenate(left, axis=0).astype(BF16),
+                right.astype(BF16),
+                (((1,), (1,)), ((), ())),
+                preferred_element_type=F32,
+            )
         )
-        spare = jnp.zeros((3 * count, edge_ref.shape[2] - 3 * channels), F32)
-        edge_ref[number] = jnp.concatenate([product, spare], axis=1)
-
-
-def z_edges(own, other, ztiles, below, span, sizes, width):
-    channels = own.shape[1]
-    return pl.pallas_call(
-        functools.partial(edge_kernel, span, sizes),
-        in_specs=[VMEM] * 4,
-        out_specs=VMEM,
-        out_shape=jax.ShapeDtypeStruct((2, 3 * channels // 2, width), F32),
-        compiler_params=params(),
-        cost_estimate=cost(2**27, 2**20),
-        name="edges",
-    )(own, other, ztiles, below)
-
-
-def finish_kernel(scale, rows, channels, mine_ref, other_ref, edge_ref, part_ref, flat, lines, chunks):
-    count = channels // 2
-    taps = 27 * channels
-    total = mine_ref[...] + other_ref[...]
     blocks = []
     for a in range(3):
         for c in range(3):
-            block = total[(3 * a + c) * count : (3 * a + c + 1) * count]
+            block = acc_ref[(3 * a + c) * channels : (3 * a + c + 1) * channels, :]
             if c != 1:
-                block = block + edge_ref[c // 2, a * count : (a + 1) * count, :]
+                block = block + edges[c // 2][a * channels : (a + 1) * channels]
             blocks.append(block)
-    whole = to_flat(jnp.concatenate(blocks, axis=0) * scale, count, channels, flat)
-    pieces = whole.shape[1] // LANES
-    for k in range(pieces):
-        lines[k * count : (k + 1) * count, :] = whole[:, k * LANES : (k + 1) * LANES]
-    number, tall, width = part_ref.shape
-    parts = []
-    for r in range(rows):
-        found = [lines[pl.ds(k * count + r, number, stride=rows), :] for k in range(pieces)]
-        parts.append(jnp.concatenate(found, axis=1)[:, :taps])
-    line = jnp.concatenate(parts, axis=1)
+    whole = to_flat(jnp.concatenate(blocks, axis=0) * scale, channels, channels, flat)
+    count, height, width = part_ref.shape
+    line = jnp.concatenate(
+        [whole[r * count : (r + 1) * count, : 27 * channels] for r in range(rows)], axis=1
+    )
     chunks[...] = jnp.zeros_like(chunks)
     for k in range(line.shape[1] // width):
-        chunks[pl.ds(k, number, stride=tall), :] = line[:, k * width : (k + 1) * width]
+        chunks[pl.ds(k, count, stride=height), :] = line[:, k * width : (k + 1) * width]
     part_ref[...] = chunks[...].reshape(part_ref.shape).astype(BF16)
 
 
-def finish(mine, other, edge, scale, rows, channels, part_shape):
-    return pl.pallas_call(
-        functools.partial(finish_kernel, scale, rows, channels),
-        in_specs=[VMEM] * 3,
+def finish(acc, columns, sent, received, scale, rows, sizes, part_shape):
+    channels = columns.shape[0]
+    return pl.pallas_call(
+        functools.partial(finish_kernel, scale, rows, sizes),
+        in_specs=[VMEM] * 6,
         out_specs=VMEM,
         out_shape=jax.ShapeDtypeStruct(part_shape, BF16),
         scratch_shapes=[
             flat_scratch(channels),
-            pltpu.VMEM((-(-27 * channels // LANES) * channels // 2, LANES), F32),
             pltpu.VMEM((part_shape[0] * part_shape[1], part_shape[2]), F32),
         ],
         compiler_params=params(),
-        cost_estimate=cost(2**24, 2**20),
+        cost_estimate=cost(2**27, 2**21),
         name="finish",
-    )(mine, other, edge)
+    )(acc, columns, *sent, *received[::-1])
 
 
 def adam_step(master, first, second, weight_grad):
@@ -708,24 +685,15 @@
     return tuple(out.reshape(share) for out in outs)
 
 
-def spread_kernel(rows, w_ref, weights_ref, turned, chunks, lines):
+def spread_kernel(rows, w_ref, weights_ref, turned, chunks):
     count, height, width = w_ref.shape
-    channels = rows * count
-    taps = 27 * channels
+    taps = 27 * rows * count
     chunks[...] = w_ref[...].astype(F32).reshape(chunks.shape)
     line = jnp.concatenate(
         [chunks[pl.ds(k, count, stride=height), :] for k in range(rows * taps // width)], axis=1
     )
-    pieces = lines.shape[0] // channels
-    spare = jnp.zeros((count, pieces * LANES - taps), F32)
-    for r in range(rows):
-        found = jnp.concatenate([line[:, r * taps : (r + 1) * taps], spare], axis=1)
-        for k in range(pieces):
-            lines[pl.ds(k * channels + r, count, stride=rows), :] = found[
-                :, k * LANES : (k + 1) * LANES
-            ]
-    whole = [lines[k * channels : (k + 1) * channels, :] for k in range(pieces)]
-    spread_weights(jnp.concatenate(whole, axis=1)[:, :taps], turned, weights_ref)
+    whole = jnp.concatenate([line[:, r * taps : (r + 1) * taps] for r in range(rows)], axis=0)
+    spread_weights(whole, turned, weights_ref)
 
 
 def spread(kernel, channels, rows):
@@ -737,7 +705,6 @@
         scratch_shapes=[
             flat_scratch(channels),
             pltpu.VMEM((kernel.shape[0] * kernel.shape[1], kernel.shape[2]), F32),
-            pltpu.VMEM((-(-27 * channels // LANES) * channels, LANES), F32),
         ],
         compiler_params=params(),
         cost_estimate=cost(2**20, 2**21),
@@ -771,38 +738,29 @@
     channels, size_x, size_y, _ = shape
     devices = math.prod(lax.axis_size(a) for a in AXES)
     rows = channels // devices
-    span = lax.axis_size("gz") * rows
     used = master.shape[0] // LANES
-    tall = -(-used // 16) * 16
-    first, last, *swaps = faces(preact, upstream, "gx")
+    block = (devices, -(-used // 16) * 16, LANES)
+    first, last, *swaps = faces(preact, upstream, "gx", rows)
     odd_halves = swapped(swaps[1], "gx", 1)
     even_halves = swapped(swaps[0], "gx", 0)
-    inner, planes_x, own, sent = pair_inner(
-        preact,
-        upstream,
-        activations,
-        first,
-        last,
-        master.reshape(used, LANES),
-        (devices, tall, LANES),
+    inner, planes_x, own, columns, sent = pair_inner(
+        preact, upstream, activations, first, last, master.reshape(used, LANES), block, rows
     )
     kernel = lax.all_to_all(sent, AXES, 0, 0, tiled=True)
     own, xlo, xhi = side((odd_halves, even_halves), own)
     planes = (xlo, first, inner, last, xhi)
     other = shifted(own, {"gy": "swap"})
-    zlo, zhi = join(own, other, size_x * size_y)
-    below = shifted(zhi, {"gz": 1})
+    z_sent = join(own, other, columns, size_x * size_y)
+    from_odd = swapped(z_sent[1], "gz", 1)
+    from_even = swapped(z_sent[0], "gz", 0)
     sources = (*planes, other, other)
-    mine, theirs = pair_wgrad(sources, planes_x, shape, span)
-    theirs, below = lax.optimization_barrier((theirs, below))
-    theirs = shifted(theirs, {"gy": "swap"})
-    edge = z_edges(own, other, zlo, below, span, (size_x, size_y), mine.shape[1])
-    part = finish(mine, theirs, edge, scale, rows, channels, (devices // 2, tall, LANES))
-    part, kernel, zlo = lax.optimization_barrier((part, kernel, zlo))
-    parts = lax.all_to_all(part, ("gx", "gz"), 0, 0, tiled=True)
-    above = shifted(zlo, {"gz": -1})
+    acc = pair_wgrad(sources, planes_x, shape)
+    z_received = (from_even, from_odd)
+    part = finish(acc, columns, z_sent, z_received, scale, rows, (size_x, size_y), block)
+    part, kernel = lax.optimization_barrier((part, kernel))
+    parts = lax.all_to_all(part, AXES, 0, 0, tiled=True)
     weights = spread(kernel, channels, rows)
-    grad_input = pair_dgrad((*sources, below, above), weights, shape)
+    grad_input = pair_dgrad((*sources, *z_received), weights, shape)
     return grad_input, *adam(parts, master, first_moment, second_moment)
 
 
@@ -968,7 +926,7 @@
         lax.axis_size("gy") == 2
         and channels % devices == 0
         and share % LANES == 0
-        and channels // devices * lax.axis_size("gz") % 8 == 0
+        and channels // (channels // devices) % 16 == 0
         and 2 * size_x * size_y <= LANES
         and (size_x + 2) * size_y <= LANES
     )

time: 49.1 us -> 44.9 us (0.914)
  starting transfers between devices: 25.2 us -> 20.4 us
    ppermute x4 -> x1, starting transfers between devices: 5.09 us -> 0.32 us  [shifted(): return lax.ppermute(value, names if len(names) > 1 else names[0], pairs)]
    ppermute x2 -> x4, starting transfers between devices: 6.4 us -> 8.83 us  [swapped(): return lax.ppermute(value, axis, pairs)]
    all_to_all x1, starting transfers between devices: 8.82 us -> 6.42 us  [pair_program(): parts = lax.all_to_all(part, AXES, 0, 0, tiled=True)]
    all_to_all x1, waiting for transfers between devices: 1.78 us -> 4.02 us  [pair_program(): parts = lax.all_to_all(part, AXES, 0, 0, tiled=True)]
    ppermute x2 -> x4, waiting for transfers between devices: 2.12 us -> 0.01 us  [swapped(): return lax.ppermute(value, axis, pairs)]
    pallas_call x6 -> x5, Pallas kernels: 10.6 us -> 11 us  [the longest x1 4 us: pair_inner(): pl.pallas_call(functools.partial(pair_inner_kernel, rows), in_specs=[HBM]...]
    ppermute x4 -> x1, waiting for transfers between devices: 1.23 us -> 1.19 us  [shifted(): return lax.ppermute(value, names if len(names) > 1 else names[0], pairs)]
  transfers between devices with their start and end apart: 8 -> 7, of which waited for: 3 -> 3; matrix products, arithmetic and copies ran while one was open for 0% -> 0% of each run, Pallas kernels for 31% -> 36%
where the time goes in v5:
time: 44.9 us; the launch traced here: 44.6 us
  starting transfers between devices  20.4 us (45%)
  Pallas kernels  18 us (40%)
  waiting for transfers between devices  5.41 us (12%)
  between operations  0.76 us (2%)
    ppermute x4, starting transfers between devices, swapped(): return lax.ppermute(value, axis, pairs)  8.83 us
    all_to_all x1, starting transfers between devices, pair_program(): parts = lax.all_to_all(part, AXES, 0, 0, tiled=True)  6.42 us
    pallas_call x1, Pallas kernels, pair_dgrad(): pl.pallas_call(pair_dgrad_kernel, in_specs=[VMEM] * 10, out_specs=VMEM, o...  5.29 us
    all_to_all x1, starting transfers between devices, pair_program(): kernel = lax.all_to_all(sent, AXES, 0, 0, tiled=True)  4.84 us
    all_to_all x1, waiting for transfers between devices, pair_program(): parts = lax.all_to_all(part, AXES, 0, 0, tiled=True)  4.02 us
    pallas_call x1, Pallas kernels, pair_inner(): pl.pallas_call(functools.partial(pair_inner_kernel, rows), in_specs=[HBM]...  4 us
    pallas_call x1, Pallas kernels, pair_wgrad(): pl.pallas_call(pair_wgrad_kernel, in_specs=[VMEM] * 8, out_specs=VMEM, ou...  3.6 us
    pallas_call x1, Pallas kernels, finish(): pl.pallas_call(functools.partial(finish_kernel, scale, rows, sizes), in_s...  1.94 us
  transfers between devices with their start and end apart: 7, of which 3 were waited for; matrix products, arithmetic and copies ran while one was open for 0% of the time, Pallas kernels for 36%

profile of v5, /device:TPU:0, one launch (start us, length us, event | category | flops | bytes accessed | tf_op | source)
XLA Modules:
  0.0 44.6 jit_solution(3721660740646166524)
XLA Ops:
  0.6 0.0 copy-start
  0.6 1.3 %faces.1 = (bf16[64,1024]{1,0:T(8,128)(2,1)S(1)}, bf16[64,1024]{1,0:T(8,128)(2,1)S(1)}, bf16[64,1024]{1,0:T(8,128)(2,1)S(1)}, bf16[64,1024]{1,0:T(8,128)(2,1)S(1)}) custom-call(bf16[64,8,8,128]{3,2,1,0:T(8,128)(2,1)} %refs_0_.1, bf16[64,8,8,128]{3,2,1,0:T(8,128)(2,1)} %refs_1_.1), custom_call_target="tpu_custom_call" | custom-call | bytes 1048576 | tf_op jit(solution)/shard_map/faces/pallas_call | solution.py:83
  2.0 0.7 %collective-permute-start = (bf16[64,1024]{1,0:T(8,128)(2,1)S(1)}, bf16[64,1024]{1,0:T(8,128)(2,1)S(1)}, u32[]{:S(2)}, u32[]{:S(2)}) collective-permute-start(bf16[64,1024]{1,0:T(8,128)(2,1)S(1)} %get-tuple-element.25), channel_id=1, source_target_pairs={{8,16},{16,8},{9,17},{17,9},{10,18},{18,10},{11,19},{19,11},{12,20... | collective-permute-start | bytes 393224 | tf_op jit(solution)/shard_map/ppermute | solution.py:917
  2.7 5.7 %collective-permute-start.1 = (bf16[64,1024]{1,0:T(8,128)(2,1)S(1)}, bf16[64,1024]{1,0:T(8,128)(2,1)S(1)}, u32[]{:S(2)}, u32[]{:S(2)}) collective-permute-start(bf16[64,1024]{1,0:T(8,128)(2,1)S(1)} %get-tuple-element.26), channel_id=1, source_target_pairs={{0,8},{8,0},{16,24},{24,16},{1,9},{9,1},{17,25},{25,17},{2,10},{10... | collective-permute-start | bytes 393224 | tf_op jit(solution)/shard_map/ppermute | solution.py:917
  8.4 0.0 copy-done
  8.4 4.0 %inner.1 = (bf16[6,64,1024]{2,1,0:T(8,128)(2,1)S(1)}, bf16[8,64,1024]{2,1,0:T(8,128)(2,1)S(1)}, bf16[10,64,128]{2,1,0:T(8,128)(2,1)S(1)}, bf16[64,128]{1,0:T(8,128)(2,1)S(1)}, bf16[32,32,128]{2,1,0:T(8,128)(2,1)}) custom-call(bf16[64,8,8,128]{3,2,1,0:T(8,128)(2,1)} %refs_0_.1, bf16[64,8,8,128]{3,2,1,0:T(8,128)(2,1)} %refs_1_.1, ...), custom_call_target="tpu_custom_call" | custom-call | bytes 6291456 | tf_op jit(solution)/shard_map/inner/pallas_call | solution.py:454
  12.4 4.8 %all-to-all-start = ((bf16[32,32,128]{2,1,0:T(8,128)(2,1)}), bf16[32,32,128]{2,1,0:T(8,128)(2,1)S(1)}, u32[]{:S(2)}, u32[]{:S(2)}) async-start(bf16[32,32,128]{2,1,0:T(8,128)(2,1)} %get-tuple-element.38), calls=%async_computation | async-start | bytes 524288 | tf_op jit(solution)/shard_map/all_to_all | solution.py:749
  17.3 0.0 collective-permute-done.odd_ref
  17.3 0.0 collective-permute-done.1.even_ref
  17.3 0.4 side.1
  17.7 0.3 collective-permute-start.2
  18.0 1.2 %collective-permute-done.2.other_ref.refs_5_.refs_6_ = bf16[12,64,128]{2,1,0:T(8,128)(2,1)S(1)} collective-permute-done((bf16[12,64,128]{2,1,0:T(8,128)(2,1)S(1)}, bf16[12,64,128]{2,1,0:T(8,128)(2,1)S(1)}, u32[]{:S(2)}, u32[]{:S(2)}) %collective-permute-start.2) | collective-permute-done | bytes 196640 | tf_op jit(solution)/shard_map/ppermute | solution.py:910
  19.2 0.1 join.1
  19.3 1.8 %collective-permute-start.3 = (bf16[3,64,128]{2,1,0:T(8,128)(2,1)S(1)}, bf16[3,64,128]{2,1,0:T(8,128)(2,1)S(1)}, u32[]{:S(2)}, u32[]{:S(2)}) collective-permute-start(bf16[3,64,128]{2,1,0:T(8,128)(2,1)S(1)} %get-tuple-element.35.refs_2_), channel_id=1, source_target_pairs={{0,1},{1,0},{2,3},{3,2},{4,5},{5,4},{6,7},{7,6},{8,9},{9,8},{10,11... | collective-permute-start | bytes 147464 | tf_op jit(solution)/shard_map/ppermute | solution.py:917
  21.0 0.7 %collective-permute-start.4 = (bf16[3,64,128]{2,1,0:T(8,128)(2,1)S(1)}, bf16[3,64,128]{2,1,0:T(8,128)(2,1)S(1)}, u32[]{:S(2)}, u32[]{:S(2)}) collective-permute-start(bf16[3,64,128]{2,1,0:T(8,128)(2,1)S(1)} %get-tuple-element.36.refs_3_), channel_id=1, source_target_pairs={{1,2},{2,1},{5,6},{6,5},{9,10},{10,9},{13,14},{14,13},{17,18},{18,... | collective-permute-start | bytes 147464 | tf_op jit(solution)/shard_map/ppermute | solution.py:917
  21.7 3.6 %wgrad.1.refs_0_ = f32[576,192]{1,0:T(8,128)S(1)} custom-call(bf16[64,1024]{1,0:T(8,128)(2,1)S(1)} %get-tuple-element.30.refs_0_, bf16[64,1024]{1,0:T(8,128)(2,1)S(1)} %get-tuple-element.27.refs_3_.refs_1_, bf16[6,64,1024]{2,1,0:T(8,128)(2,1)S(1)} %get-tuple-element.31.refs_2_, bf16[64,1024]{1,0:T(8,128)(2,1)S(1)} %get-tuple-element.28.refs_4_.refs_3_, ...), custom_call_target="tpu_custom_call" | custom-call | flops 2264924160 | bytes 4194304 | tf_op jit(solution)/shard_map/wgrad/pallas_call | solution.py:568
  25.3 0.0 collective-permute-done.3.refs_5_.refs_7_
  25.3 0.0 collective-permute-done.4.refs_4_.refs_8_
  25.3 1.9 %finish.1 = bf16[32,32,128]{2,1,0:T(8,128)(2,1)} custom-call(f32[576,192]{1,0:T(8,128)S(1)} %wgrad.1.refs_0_, bf16[64,128]{1,0:T(8,128)(2,1)S(1)} %get-tuple-element.34.columns_ref.refs_1_, bf16[3,64,128]{2,1,0:T(8,128)(2,1)S(1)} %get-tuple-element.35.refs_2_, bf16[3,64,128]{2,1,0:T(8,128)(2,1)S(1)} %get-tuple-element.36.refs_3_, ...), custom_call_target="tpu_custom_call" | custom-call | flops 134217728 | bytes 2097152 | tf_op jit(solution)/shard_map/finish/pallas_call | solution.py:638
  27.3 0.2 all-to-all-done.w_ref
  27.5 6.4 %all-to-all-start.1 = ((bf16[32,32,128]{2,1,0:T(8,128)(2,1)}), bf16[32,32,128]{2,1,0:T(8,128)(2,1)S(1)}, u32[]{:S(2)}, u32[]{:S(2)}) async-start(bf16[32,32,128]{2,1,0:T(8,128)(2,1)} %finish.1), calls=%async_computation.1 | async-start | bytes 524288 | tf_op jit(solution)/shard_map/all_to_all | solution.py:761
  33.9 0.7 %spread.1.refs_9_ = bf16[3,128,768]{2,1,0:T(8,128)(2,1)S(1)} custom-call(bf16[32,32,128]{2,1,0:T(8,128)(2,1)S(1)} %all-to-all-done.w_ref), custom_call_target="tpu_custom_call" | custom-call | flops 1048576 | bytes 2097152 | tf_op jit(solution)/shard_map/spread/pallas_call | solution.py:700
  34.6 0.0 copy-start.1
  34.6 0.0 copy-start.2
  34.6 5.3 %dgrad.1 = bf16[64,8,8,128]{3,2,1,0:T(8,128)(2,1)} custom-call(bf16[64,1024]{1,0:T(8,128)(2,1)S(1)} %get-tuple-element.30.refs_0_, bf16[64,1024]{1,0:T(8,128)(2,1)S(1)} %get-tuple-element.27.refs_3_.refs_1_, bf16[6,64,1024]{2,1,0:T(8,128)(2,1)S(1)} %get-tuple-element.31.refs_2_, bf16[64,1024]{1,0:T(8,128)(2,1)S(1)} %get-tuple-element.28.refs_4_.refs_3_, ...), custom_call_target="tpu_custom_call" | custom-call | flops 2415919104 | bytes 4194304 | tf_op jit(solution)/shard_map/dgrad/pallas_call | solution.py:724
  39.9 4.0 %all-to-all-done.1.parts_ref = bf16[32,32,128]{2,1,0:T(8,128)(2,1)S(1)} async-done(((bf16[32,32,128]{2,1,0:T(8,128)(2,1)}), bf16[32,32,128]{2,1,0:T(8,128)(2,1)S(1)}, u32[]{:S(2)}, u32[]{:S(2)}) %all-to-all-start.1) | async-done | bytes 262176 | tf_op jit(solution)/shard_map/all_to_all | solution.py:761
  43.9 0.0 copy-done.1
  43.9 0.0 copy-done.2
  43.9 0.7 %adam.1 = (f32[27,128]{1,0:T(8,128)}, f32[27,128]{1,0:T(8,128)}, f32[27,128]{1,0:T(8,128)}, f32[27,128]{1,0:T(8,128)}) custom-call(bf16[32,32,128]{2,1,0:T(8,128)(2,1)S(1)} %all-to-all-done.1.parts_ref, f32[27,128]{1,0:T(8,128)S(1)} %bitcast.8, f32[27,128]{1,0:T(8,128)S(1)} %bitcast.9, f32[27,128]{1,0:T(8,128)S(1)} %bitcast.10), custom_call_target="tpu_custom_call" | custom-call | flops 262144 | bytes 262144 | tf_op jit(solution)/shard_map/adam/pallas_call | solution.py:676
Async XLA Ops:
  0.6 7.8 %copy-start = (f32[3456]{0:T(1024)S(1)}, f32[3456]{0:T(1024)}, u32[]{:S(2)}) copy-start(f32[3456]{0:T(1024)} %param.9) | copy-start | bytes 41476
  2.0 15.3 %collective-permute-start = (bf16[64,1024]{1,0:T(8,128)(2,1)S(1)}, bf16[64,1024]{1,0:T(8,128)(2,1)S(1)}, u32[]{:S(2)}, u32[]{:S(2)}) collective-permute-start(bf16[64,1024]{1,0:T(8,128)(2,1)S(1)} %get-tuple-element.25), channel_id=1, source_target_pairs={{8,16},{16,8},{9,17},{17,9},{10,18},{18,10},{11,19},{19,11},{12,20... | collective-permute-start | bytes 393224 | tf_op jit(solution)/shard_map/ppermute | solution.py:917
  2.7 14.6 %collective-permute-start.1 = (bf16[64,1024]{1,0:T(8,128)(2,1)S(1)}, bf16[64,1024]{1,0:T(8,128)(2,1)S(1)}, u32[]{:S(2)}, u32[]{:S(2)}) collective-permute-start(bf16[64,1024]{1,0:T(8,128)(2,1)S(1)} %get-tuple-element.26), channel_id=1, source_target_pairs={{0,8},{8,0},{16,24},{24,16},{1,9},{9,1},{17,25},{25,17},{2,10},{10... | collective-permute-start | bytes 393224 | tf_op jit(solution)/shard_map/ppermute | solution.py:917
  12.4 15.0 %all-to-all-start = ((bf16[32,32,128]{2,1,0:T(8,128)(2,1)}), bf16[32,32,128]{2,1,0:T(8,128)(2,1)S(1)}, u32[]{:S(2)}, u32[]{:S(2)}) async-start(bf16[32,32,128]{2,1,0:T(8,128)(2,1)} %get-tuple-element.38), calls=%async_computation | async-start | bytes 524288 | tf_op jit(solution)/shard_map/all_to_all | solution.py:749
  17.7 1.5 %collective-permute-start.2 = (bf16[12,64,128]{2,1,0:T(8,128)(2,1)S(1)}, bf16[12,64,128]{2,1,0:T(8,128)(2,1)S(1)}, u32[]{:S(2)}, u32[]{:S(2)}) collective-permute-start(bf16[12,64,128]{2,1,0:T(8,128)(2,1)S(1)} %get-tuple-element.33.own_ref), channel_id=1, source_target_pairs={{0,4},{4,0},{1,5},{5,1},{2,6},{6,2},{3,7},{7,3},{8,12},{12,8},{9,1... | collective-permute-start | bytes 589832 | tf_op jit(solution)/shard_map/ppermute | solution.py:910
  19.3 6.0 %collective-permute-start.3 = (bf16[3,64,128]{2,1,0:T(8,128)(2,1)S(1)}, bf16[3,64,128]{2,1,0:T(8,128)(2,1)S(1)}, u32[]{:S(2)}, u32[]{:S(2)}) collective-permute-start(bf16[3,64,128]{2,1,0:T(8,128)(2,1)S(1)} %get-tuple-element.35.refs_2_), channel_id=1, source_target_pairs={{0,1},{1,0},{2,3},{3,2},{4,5},{5,4},{6,7},{7,6},{8,9},{9,8},{10,11... | collective-permute-start | bytes 147464 | tf_op jit(solution)/shard_map/ppermute | solution.py:917
  21.0 4.3 %collective-permute-start.4 = (bf16[3,64,128]{2,1,0:T(8,128)(2,1)S(1)}, bf16[3,64,128]{2,1,0:T(8,128)(2,1)S(1)}, u32[]{:S(2)}, u32[]{:S(2)}) collective-permute-start(bf16[3,64,128]{2,1,0:T(8,128)(2,1)S(1)} %get-tuple-element.36.refs_3_), channel_id=1, source_target_pairs={{1,2},{2,1},{5,6},{6,5},{9,10},{10,9},{13,14},{14,13},{17,18},{18,... | collective-permute-start | bytes 147464 | tf_op jit(solution)/shard_map/ppermute | solution.py:917
  27.5 16.4 %all-to-all-start.1 = ((bf16[32,32,128]{2,1,0:T(8,128)(2,1)}), bf16[32,32,128]{2,1,0:T(8,128)(2,1)S(1)}, u32[]{:S(2)}, u32[]{:S(2)}) async-start(bf16[32,32,128]{2,1,0:T(8,128)(2,1)} %finish.1), calls=%async_computation.1 | async-start | bytes 524288 | tf_op jit(solution)/shard_map/all_to_all | solution.py:761
  34.6 9.3 %copy-start.1 = (f32[3456]{0:T(1024)S(1)}, f32[3456]{0:T(1024)}, u32[]{:S(2)}) copy-start(f32[3456]{0:T(1024)} %param.10) | copy-start | bytes 41476
  34.6 9.3 %copy-start.2 = (f32[3456]{0:T(1024)S(1)}, f32[3456]{0:T(1024)}, u32[]{:S(2)}) copy-start(f32[3456]{0:T(1024)} %param.11) | copy-start | bytes 41476

commit v6 on v5

--- a/solution.py
+++ b/solution.py
@@ -15,7 +15,7 @@
 F32 = jnp.float32
 BF16 = jnp.bfloat16
 FACES_VMEM = 55_900_000
-INNER_VMEM = 53_000_000
+INNER_VMEM = 54_800_000
 
 
 def params(limit=24 * 2**20):
@@ -97,24 +97,18 @@
     )(preact, upstream)
 
 
-def read_inner(rows, p_ref, u_ref, a_ref, g_ref, x_ref, p_buf, u_buf, a_buf, tile, sems):
-    channels, size_x, size_y, size_z = a_ref.shape
+def read_inner(rows, p_ref, u_ref, g_ref, p_buf, u_buf, tile, sems):
+    size_x, size_z = p_ref.shape[1], p_ref.shape[3]
     inner = size_x - 2
     copies = []
     for x in range(inner):
-        copies.append(
-            (
-                pltpu.make_async_copy(p_ref.at[:, x + 1], p_buf.at[x], sems.at[x]),
-                pltpu.make_async_copy(u_ref.at[:, x + 1], u_buf.at[x], sems.at[inner + x]),
-            )
+        pair = (
+            pltpu.make_async_copy(p_ref.at[:, x + 1], p_buf.at[x], sems.at[x]),
+            pltpu.make_async_copy(u_ref.at[:, x + 1], u_buf.at[x], sems.at[inner + x]),
         )
-    for x in range(size_x):
-        copies.append(
-            (pltpu.make_async_copy(a_ref.at[:, x], a_buf.at[x], sems.at[2 * inner + x]),)
-        )
-    for group in copies:
-        for copy in group:
+        for copy in pair:
             copy.start()
+        copies.append(pair)
     for x in range(inner):
         for copy in copies[x]:
             copy.wait()
@@ -123,49 +117,68 @@
             g_ref[x, at, y * size_z : (y + 1) * size_z] = value
 
         to_planes(masked(p_buf[x], u_buf[x]), tile.at[x % 2], write, rows)
-    for x in range(size_x):
-        copies[inner + x][0].wait()
-
-        def write(at, y, value):
-            x_ref[x, at, y * size_z : (y + 1) * size_z] = value
-
-        to_planes(a_buf[x], tile.at[x % 2], write)
 
 
 def inner_kernel(*refs):
     read_inner(1, *refs)
 
 
-def inner_outputs(channels, size_x, size_y, size_z):
-    plane = size_y * size_z
-    return [
-        jax.ShapeDtypeStruct((size_x - 2, channels, plane), BF16),
-        jax.ShapeDtypeStruct((size_x, channels, plane), BF16),
-    ]
+def inner_output(channels, size_x, size_y, size_z):
+    return jax.ShapeDtypeStruct((size_x - 2, channels, size_y * size_z), BF16)
 
 
 def inner_scratch(channels, size_x, size_y, size_z):
     return [
         pltpu.VMEM((size_x - 2, channels, size_y, size_z), BF16),
         pltpu.VMEM((size_x - 2, channels, size_y, size_z), BF16),
-        pltpu.VMEM((size_x, channels, size_y, size_z), BF16),
         pltpu.VMEM((2, channels * size_y, size_z), F32),
-        pltpu.SemaphoreType.DMA((3 * size_x - 4,)),
+        pltpu.SemaphoreType.DMA((2 * size_x - 4,)),
     ]
 
 
-def inner_planes(preact, upstream, activations):
+def inner_planes(preact, upstream):
     shape = preact.shape
     return pl.pallas_call(
         inner_kernel,
-        in_specs=[HBM] * 3,
-        out_specs=[VMEM] * 2,
-        out_shape=inner_outputs(*shape),
+        in_specs=[HBM] * 2,
+        out_specs=VMEM,
+        out_shape=inner_output(*shape),
         scratch_shapes=inner_scratch(*shape),
         compiler_params=params(INNER_VMEM),
-        cost_estimate=cost(0, 6 * 2**20),
+        cost_estimate=cost(0, 4 * 2**20),
         name="inner",
-    )(preact, upstream, activations)
+    )(preact, upstream)
+
+
+def input_kernel(a_ref, x_ref, *refs):
+    tile = refs[-1]
+    channels, size_x, size_y, size_z = a_ref.shape
+    for x in range(size_x):
+
+        def write(at, y, value):
+            x_ref[x, at, y * size_z : (y + 1) * size_z] = value
+
+        to_planes(a_ref[:, x], tile.at[x % 2], write)
+    if len(refs) > 1:
+        low, high = z_tiles([x_ref[x] for x in range(size_x)], size_y, size_z, range(size_x))
+        refs[0][...] = (low + pltpu.roll(high, size_x * size_y, 1)).astype(BF16)
+
+
+def input_planes(activations, with_columns):
+    channels, size_x, size_y, size_z = activations.shape
+    outs = [jax.ShapeDtypeStruct((size_x, channels, size_y * size_z), BF16)]
+    if with_columns:
+        outs.append(jax.ShapeDtypeStruct((channels, LANES), BF16))
+    return pl.pallas_call(
+        input_kernel,
+        in_specs=[VMEM],
+        out_specs=[VMEM] * len(outs),
+        out_shape=outs,
+        scratch_shapes=[pltpu.VMEM((2, channels * size_y, size_z), F32)],
+        compiler_params=params(),
+        cost_estimate=cost(0, 2 * 2**20),
+        name="inputs",
+    )(activations)
 
 
 def body_of(refs, index):
@@ -215,7 +228,7 @@
     rows = [jnp.concatenate(pair, axis=1) for pair in columns]
     return jnp.dot(
         jnp.concatenate(rows, axis=0).astype(BF16), put, preferred_element_type=F32
-    )
+    ).astype(BF16)
 
 
 def z_halo(low_ref, high_ref, planes, rows_y, size_z):
@@ -228,7 +241,7 @@
     return put_columns(columns, lambda number: number, rows_y, size_z)
 
 
-def pair_z_halo(even_ref, odd_ref, planes, size_y, size_z):
+def pair_z_halo(odd_ref, even_ref, planes, size_y, size_z):
     me, odd = lax.axis_index("gy"), is_odd("gz")
     sides = []
     for low, high in ((even_ref, odd_ref), (odd_ref, even_ref)):
@@ -265,22 +278,26 @@
     rows_y = plane // size_z + 2
     base = 3 * channels * index
     lane = lax.broadcasted_iota(jnp.int32, (channels, size_z), 1)
+    is_first, is_last = lane == 0, lane == size_z - 1
     low, high = y_halo(refs[5:7], index)
     body = body_of(refs[:5], index)
     for row in range(rows_y):
         cols = slice(row * size_z, (row + 1) * size_z)
         if row == 0:
-            wide = low
+            value = low.astype(BF16)
         elif row == rows_y - 1:
-            wide = high
+            value = high.astype(BF16)
         else:
-            wide = body[:, (row - 1) * size_z : row * size_z].astype(F32)
-        edge = 0.0 if halo is None else halo[index * channels : (index + 1) * channels, cols]
-        before = jnp.where(lane == 0, edge, pltpu.roll(wide, 1, 1))
-        after = jnp.where(lane == size_z - 1, edge, pltpu.roll(wide, size_z - 1, 1))
-        g3[base : base + channels, cols] = before.astype(BF16)
-        g3[base + channels : base + 2 * channels, cols] = wide.astype(BF16)
-        g3[base + 2 * channels : base + 3 * channels, cols] = after.astype(BF16)
+            value = body[:, (row - 1) * size_z : row * size_z]
+        if halo is None:
+            edge = jnp.zeros_like(value)
+        else:
+            edge = halo[index * channels : (index + 1) * channels, cols]
+        before = jnp.where(is_first, edge, pltpu.roll(value, 1, 1))
+        after = jnp.where(is_last, edge, pltpu.roll(value, size_z - 1, 1))
+        g3[base : base + channels, cols] = before
+        g3[base + channels : base + 2 * channels, cols] = value
+        g3[base + 2 * channels : base + 3 * channels, cols] = after
 
 
 def weight_products(refs, halo, x_ref, g3, x3, acc):
@@ -418,9 +435,8 @@
 
 
 def pair_inner_kernel(rows, *refs):
-    first_ref, last_ref, m_ref = refs[3:6]
-    g_ref, x_ref, side_ref, columns_ref, sent_ref = refs[6:11]
-    tile_ref, tile_sems = refs[16:]
+    first_ref, last_ref, m_ref, g_ref, side_ref, sent_ref = refs[2:8]
+    tile_ref, tile_sems = refs[12:]
     share = m_ref[...]
     height = tile_ref.shape[0] - share.shape[0]
     if height:
@@ -432,41 +448,40 @@
     ]
     for copy in copies:
         copy.start()
-    read_inner(rows, *refs[:3], g_ref, x_ref, *refs[11:16])
+    read_inner(rows, *refs[:2], g_ref, *refs[8:12])
     size_z = side_ref.shape[-1]
-    size_x, channels, plane = x_ref.shape
-    size_y = plane // size_z
-    bodies = [first_ref] + [g_ref.at[x] for x in range(size_x - 2)] + [last_ref]
+    inner, _, plane = g_ref.shape
+    size_x = inner + 2
+    bodies = [first_ref] + [g_ref.at[x] for x in range(inner)] + [last_ref]
     for x, body in enumerate(bodies):
         side_ref[x] = row_for_other(body, size_z)
-    low, high = z_tiles([body[...] for body in bodies], size_y, size_z, range(1, size_x + 1))
+    low, high = z_tiles(
+        [body[...] for body in bodies], plane // size_z, size_z, range(1, size_x + 1)
+    )
     side_ref[size_x] = low.astype(BF16)
     side_ref[size_x + 1] = high.astype(BF16)
-    low, high = z_tiles([x_ref[x] for x in range(size_x)], size_y, size_z, range(size_x))
-    columns_ref[...] = (low + pltpu.roll(high, size_x * size_y, 1)).astype(BF16)
     for copy in copies:
         copy.wait()
 
 
-def pair_inner(preact, upstream, activations, first, last, share, sent_shape, rows):
+def pair_inner(preact, upstream, first, last, share, sent_shape, rows):
     shape = preact.shape
     channels, size_x, _, size_z = shape
     return pl.pallas_call(
         functools.partial(pair_inner_kernel, rows),
-        in_specs=[HBM] * 3 + [VMEM] * 3,
-        out_specs=[VMEM] * 4 + [HBM],
-        out_shape=inner_outputs(*shape)
-        + [
+        in_specs=[HBM] * 2 + [VMEM] * 3,
+        out_specs=[VMEM] * 2 + [HBM],
+        out_shape=[
+            inner_output(*shape),
             jax.ShapeDtypeStruct((size_x + 2, channels, size_z), BF16),
-            jax.ShapeDtypeStruct((channels, LANES), BF16),
             jax.ShapeDtypeStruct(sent_shape, BF16),
         ],
         scratch_shapes=inner_scratch(*shape)
         + [pltpu.VMEM(sent_shape[1:], BF16), pltpu.SemaphoreType.DMA((sent_shape[0],))],
         compiler_params=params(INNER_VMEM),
-        cost_estimate=cost(0, 6 * 2**20),
+        cost_estimate=cost(0, 4 * 2**20),
         name="inner",
-    )(preact, upstream, activations, first, last, share)
+    )(preact, upstream, first, last, share)
 
 
 def is_odd(axis):
@@ -647,7 +662,7 @@
         compiler_params=params(),
         cost_estimate=cost(2**27, 2**21),
         name="finish",
-    )(acc, columns, *sent, *received[::-1])
+    )(acc, columns, *sent, *received)
 
 
 def adam_step(master, first, second, weight_grad):
@@ -743,19 +758,21 @@
     first, last, *swaps = faces(preact, upstream, "gx", rows)
     odd_halves = swapped(swaps[1], "gx", 1)
     even_halves = swapped(swaps[0], "gx", 0)
-    inner, planes_x, own, columns, sent = pair_inner(
-        preact, upstream, activations, first, last, master.reshape(used, LANES), block, rows
+    inner, own, sent = pair_inner(
+        preact, upstream, first, last, master.reshape(used, LANES), block, rows
     )
     kernel = lax.all_to_all(sent, AXES, 0, 0, tiled=True)
     own, xlo, xhi = side((odd_halves, even_halves), own)
     planes = (xlo, first, inner, last, xhi)
+    own, activations = lax.optimization_barrier((own, activations))
     other = shifted(own, {"gy": "swap"})
+    planes_x, columns = input_planes(activations, True)
     z_sent = join(own, other, columns, size_x * size_y)
     from_odd = swapped(z_sent[1], "gz", 1)
     from_even = swapped(z_sent[0], "gz", 0)
     sources = (*planes, other, other)
     acc = pair_wgrad(sources, planes_x, shape)
-    z_received = (from_even, from_odd)
+    z_received = (from_odd, from_even)
     part = finish(acc, columns, z_sent, z_received, scale, rows, (size_x, size_y), block)
     part, kernel = lax.optimization_barrier((part, kernel))
     parts = lax.all_to_all(part, AXES, 0, 0, tiled=True)
@@ -871,7 +888,8 @@
     share = master.shape[0]
     first, last = faces(preact, upstream)
     x_halos = (shifted(last, {"gx": 1}), shifted(first, {"gx": -1}))
-    inner, planes_x = inner_planes(preact, upstream, activations)
+    inner = inner_planes(preact, upstream)
+    (planes_x,) = input_planes(activations, False)
     sent = jnp.broadcast_to(master.astype(BF16).reshape(1, 1, share), (devices, 1, share))
     kernel = lax.all_to_all(sent, AXES, 0, 0, tiled=True).reshape(channels, 27 * channels)
     planes = (x_halos[0], first, inner, last, x_halos[1])

time: 44.9 us -> 43.8 us (0.976)
  waiting for transfers between devices: 5.41 us -> 4.38 us
    ppermute x4, starting transfers between devices: 8.83 us -> 11.6 us  [swapped(): return lax.ppermute(value, axis, pairs)]
    all_to_all x1, starting transfers between devices: 6.42 us -> 3.78 us  [pair_program(): parts = lax.all_to_all(part, AXES, 0, 0, tiled=True)]
    pallas_call x1, Pallas kernels: 4 us -> 2.92 us  [pair_inner(): pl.pallas_call(functools.partial(pair_inner_kernel, rows), in_specs=[HBM]...]
    ppermute x1, waiting for transfers between devices: 1.19 us -> 0.14 us  [shifted(): return lax.ppermute(value, names if len(names) > 1 else names[0], pairs)]
    pallas_call x0 -> x1, Pallas kernels: none -> 1.05 us  [input_planes(): pl.pallas_call(input_kernel, in_specs=[VMEM], out_specs=[VMEM] * len(outs...]
  transfers between devices with their start and end apart: 7 -> 7, of which waited for: 3 -> 2; matrix products, arithmetic and copies ran while one was open for 0% -> 0% of each run, Pallas kernels for 36% -> 36%
where the time goes in v6:
time: 43.8 us; the launch traced here: 43.5 us
  starting transfers between devices  20.6 us (47%)
  Pallas kernels  17.7 us (40%)
  waiting for transfers between devices  4.38 us (10%)
  between operations  0.77 us (2%)
    ppermute x4, starting transfers between devices, swapped(): return lax.ppermute(value, axis, pairs)  11.6 us
    pallas_call x1, Pallas kernels, pair_dgrad(): pl.pallas_call(pair_dgrad_kernel, in_specs=[VMEM] * 10, out_specs=VMEM, o...  5.08 us
    all_to_all x1, starting transfers between devices, pair_program(): kernel = lax.all_to_all(sent, AXES, 0, 0, tiled=True)  4.84 us
    all_to_all x1, waiting for transfers between devices, pair_program(): parts = lax.all_to_all(part, AXES, 0, 0, tiled=True)  4.23 us
    all_to_all x1, starting transfers between devices, pair_program(): parts = lax.all_to_all(part, AXES, 0, 0, tiled=True)  3.78 us
    pallas_call x1, Pallas kernels, pair_wgrad(): pl.pallas_call(pair_wgrad_kernel, in_specs=[VMEM] * 8, out_specs=VMEM, ou...  3.56 us
    pallas_call x1, Pallas kernels, pair_inner(): pl.pallas_call(functools.partial(pair_inner_kernel, rows), in_specs=[HBM]...  2.92 us
    pallas_call x1, Pallas kernels, finish(): pl.pallas_call(functools.partial(finish_kernel, scale, rows, sizes), in_s...  1.96 us
  transfers between devices with their start and end apart: 7, of which 2 were waited for; matrix products, arithmetic and copies ran while one was open for 0% of the time, Pallas kernels for 36%

profile of v6, /device:TPU:0, one launch (start us, length us, event | category | flops | bytes accessed | tf_op | source)
XLA Modules:
  0.0 43.5 jit_solution(637050809061286230)
XLA Ops:
  0.6 0.0 copy-start.1
  0.6 1.3 %faces.1 = (bf16[64,1024]{1,0:T(8,128)(2,1)S(1)}, bf16[64,1024]{1,0:T(8,128)(2,1)S(1)}, bf16[64,1024]{1,0:T(8,128)(2,1)S(1)}, bf16[64,1024]{1,0:T(8,128)(2,1)S(1)}) custom-call(bf16[64,8,8,128]{3,2,1,0:T(8,128)(2,1)} %refs_0_.1, bf16[64,8,8,128]{3,2,1,0:T(8,128)(2,1)} %refs_1_.1), custom_call_target="tpu_custom_call" | custom-call | bytes 1048576 | tf_op jit(solution)/shard_map/faces/pallas_call | solution.py:83
  2.0 0.7 %collective-permute-start = (bf16[64,1024]{1,0:T(8,128)(2,1)S(1)}, bf16[64,1024]{1,0:T(8,128)(2,1)S(1)}, u32[]{:S(2)}, u32[]{:S(2)}) collective-permute-start(bf16[64,1024]{1,0:T(8,128)(2,1)S(1)} %get-tuple-element.27), channel_id=1, source_target_pairs={{8,16},{16,8},{9,17},{17,9},{10,18},{18,10},{11,19},{19,11},{12,20... | collective-permute-start | bytes 393224 | tf_op jit(solution)/shard_map/ppermute | solution.py:935
  2.7 5.7 %collective-permute-start.1 = (bf16[64,1024]{1,0:T(8,128)(2,1)S(1)}, bf16[64,1024]{1,0:T(8,128)(2,1)S(1)}, u32[]{:S(2)}, u32[]{:S(2)}) collective-permute-start(bf16[64,1024]{1,0:T(8,128)(2,1)S(1)} %get-tuple-element.28), channel_id=1, source_target_pairs={{0,8},{8,0},{16,24},{24,16},{1,9},{9,1},{17,25},{25,17},{2,10},{10... | collective-permute-start | bytes 393224 | tf_op jit(solution)/shard_map/ppermute | solution.py:935
  8.4 0.0 copy-done.1
  8.4 0.0 copy-start
  8.4 2.9 %inner.1 = (bf16[6,64,1024]{2,1,0:T(8,128)(2,1)S(1)}, bf16[10,64,128]{2,1,0:T(8,128)(2,1)S(1)}, bf16[32,32,128]{2,1,0:T(8,128)(2,1)}) custom-call(bf16[64,8,8,128]{3,2,1,0:T(8,128)(2,1)} %refs_0_.1, bf16[64,8,8,128]{3,2,1,0:T(8,128)(2,1)} %refs_1_.1, bf16[64,1024]{1,0:T(8,128)(2,1)S(1)} %get-tuple-element.29.refs_2_.refs_1_, ...), custom_call_target="tpu_custom_call" | custom-call | bytes 4194304 | tf_op jit(solution)/shard_map/inner/pallas_call | solution.py:470
  11.3 4.8 %all-to-all-start = ((bf16[32,32,128]{2,1,0:T(8,128)(2,1)}), bf16[32,32,128]{2,1,0:T(8,128)(2,1)S(1)}, u32[]{:S(2)}, u32[]{:S(2)}) async-start(bf16[32,32,128]{2,1,0:T(8,128)(2,1)} %get-tuple-element.42), calls=%async_computation | async-start | bytes 524288 | tf_op jit(solution)/shard_map/all_to_all | solution.py:764
  16.2 0.0 collective-permute-done.odd_ref
  16.2 0.0 collective-permute-done.1.even_ref
  16.2 0.4 side.1
  16.6 0.3 collective-permute-start.2
  16.9 0.0 copy-done
  16.9 1.0 %inputs.1 = (bf16[8,64,1024]{2,1,0:T(8,128)(2,1)S(1)}, bf16[64,128]{1,0:T(8,128)(2,1)S(1)}) custom-call(bf16[64,8,8,128]{3,2,1,0:T(8,128)(2,1)S(1)} %copy-done), custom_call_target="tpu_custom_call" | custom-call | bytes 2097152 | tf_op jit(solution)/shard_map/inputs/pallas_call | solution.py:172
  18.0 0.1 collective-permute-done.2.other_ref.refs_5_.refs_6_
  18.1 0.1 join.1
  18.2 0.7 %collective-permute-start.3 = (bf16[3,64,128]{2,1,0:T(8,128)(2,1)S(1)}, bf16[3,64,128]{2,1,0:T(8,128)(2,1)S(1)}, u32[]{:S(2)}, u32[]{:S(2)}) collective-permute-start(bf16[3,64,128]{2,1,0:T(8,128)(2,1)S(1)} %get-tuple-element.39.refs_3_), channel_id=1, source_target_pairs={{1,2},{2,1},{5,6},{6,5},{9,10},{10,9},{13,14},{14,13},{17,18},{18,... | collective-permute-start | bytes 147464 | tf_op jit(solution)/shard_map/ppermute | solution.py:935
  18.9 4.5 %collective-permute-start.4 = (bf16[3,64,128]{2,1,0:T(8,128)(2,1)S(1)}, bf16[3,64,128]{2,1,0:T(8,128)(2,1)S(1)}, u32[]{:S(2)}, u32[]{:S(2)}) collective-permute-start(bf16[3,64,128]{2,1,0:T(8,128)(2,1)S(1)} %get-tuple-element.40.refs_2_), channel_id=1, source_target_pairs={{0,1},{1,0},{2,3},{3,2},{4,5},{5,4},{6,7},{7,6},{8,9},{9,8},{10,11... | collective-permute-start | bytes 147464 | tf_op jit(solution)/shard_map/ppermute | solution.py:935
  23.4 3.6 %wgrad.1.refs_0_ = f32[576,192]{1,0:T(8,128)S(1)} custom-call(bf16[64,1024]{1,0:T(8,128)(2,1)S(1)} %get-tuple-element.32.refs_0_, bf16[64,1024]{1,0:T(8,128)(2,1)S(1)} %get-tuple-element.29.refs_2_.refs_1_, bf16[6,64,1024]{2,1,0:T(8,128)(2,1)S(1)} %get-tuple-element.33.refs_2_, bf16[64,1024]{1,0:T(8,128)(2,1)S(1)} %get-tuple-element.30.refs_3_, ...), custom_call_target="tpu_custom_call" | custom-call | flops 2264924160 | bytes 4194304 | tf_op jit(solution)/shard_map/wgrad/pallas_call | solution.py:583
  27.0 0.0 collective-permute-done.3.refs_4_.refs_7_
  27.0 0.0 collective-permute-done.4.refs_5_.refs_8_
  27.0 2.0 %finish.1 = bf16[32,32,128]{2,1,0:T(8,128)(2,1)} custom-call(f32[576,192]{1,0:T(8,128)S(1)} %wgrad.1.refs_0_, bf16[64,128]{1,0:T(8,128)(2,1)S(1)} %get-tuple-element.38.columns_ref.refs_1_, bf16[3,64,128]{2,1,0:T(8,128)(2,1)S(1)} %get-tuple-element.40.refs_2_, bf16[3,64,128]{2,1,0:T(8,128)(2,1)S(1)} %get-tuple-element.39.refs_3_, ...), custom_call_target="tpu_custom_call" | custom-call | flops 134217728 | bytes 2097152 | tf_op jit(solution)/shard_map/finish/pallas_call | solution.py:653
  28.9 0.0 all-to-all-done.w_ref
  28.9 3.8 %all-to-all-start.1 = ((bf16[32,32,128]{2,1,0:T(8,128)(2,1)}), bf16[32,32,128]{2,1,0:T(8,128)(2,1)S(1)}, u32[]{:S(2)}, u32[]{:S(2)}) async-start(bf16[32,32,128]{2,1,0:T(8,128)(2,1)} %finish.1), calls=%async_computation.1 | async-start | bytes 524288 | tf_op jit(solution)/shard_map/all_to_all | solution.py:778
  32.7 0.7 %spread.1.refs_9_ = bf16[3,128,768]{2,1,0:T(8,128)(2,1)S(1)} custom-call(bf16[32,32,128]{2,1,0:T(8,128)(2,1)S(1)} %all-to-all-done.w_ref), custom_call_target="tpu_custom_call" | custom-call | flops 1048576 | bytes 2097152 | tf_op jit(solution)/shard_map/spread/pallas_call | solution.py:715
  33.4 0.0 copy-start.2
  33.4 0.0 copy-start.3
  33.4 5.1 %dgrad.1 = bf16[64,8,8,128]{3,2,1,0:T(8,128)(2,1)} custom-call(bf16[64,1024]{1,0:T(8,128)(2,1)S(1)} %get-tuple-element.32.refs_0_, bf16[64,1024]{1,0:T(8,128)(2,1)S(1)} %get-tuple-element.29.refs_2_.refs_1_, bf16[6,64,1024]{2,1,0:T(8,128)(2,1)S(1)} %get-tuple-element.33.refs_2_, bf16[64,1024]{1,0:T(8,128)(2,1)S(1)} %get-tuple-element.30.refs_3_, ...), custom_call_target="tpu_custom_call" | custom-call | flops 2415919104 | bytes 4194304 | tf_op jit(solution)/shard_map/dgrad/pallas_call | solution.py:739
  38.5 4.2 %all-to-all-done.1.parts_ref = bf16[32,32,128]{2,1,0:T(8,128)(2,1)S(1)} async-done(((bf16[32,32,128]{2,1,0:T(8,128)(2,1)}), bf16[32,32,128]{2,1,0:T(8,128)(2,1)S(1)}, u32[]{:S(2)}, u32[]{:S(2)}) %all-to-all-start.1) | async-done | bytes 262176 | tf_op jit(solution)/shard_map/all_to_all | solution.py:778
  42.8 0.0 copy-done.2
  42.8 0.0 copy-done.3
  42.8 0.7 %adam.1 = (f32[27,128]{1,0:T(8,128)}, f32[27,128]{1,0:T(8,128)}, f32[27,128]{1,0:T(8,128)}, f32[27,128]{1,0:T(8,128)}) custom-call(bf16[32,32,128]{2,1,0:T(8,128)(2,1)S(1)} %all-to-all-done.1.parts_ref, f32[27,128]{1,0:T(8,128)S(1)} %bitcast.8, f32[27,128]{1,0:T(8,128)S(1)} %bitcast.9, f32[27,128]{1,0:T(8,128)S(1)} %bitcast.10), custom_call_target="tpu_custom_call" | custom-call | flops 262144 | bytes 262144 | tf_op jit(solution)/shard_map/adam/pallas_call | solution.py:691
Async XLA Ops:
  0.6 7.8 %copy-start.1 = (f32[3456]{0:T(1024)S(1)}, f32[3456]{0:T(1024)}, u32[]{:S(2)}) copy-start(f32[3456]{0:T(1024)} %param.9) | copy-start | bytes 41476
  2.0 14.2 %collective-permute-start = (bf16[64,1024]{1,0:T(8,128)(2,1)S(1)}, bf16[64,1024]{1,0:T(8,128)(2,1)S(1)}, u32[]{:S(2)}, u32[]{:S(2)}) collective-permute-start(bf16[64,1024]{1,0:T(8,128)(2,1)S(1)} %get-tuple-element.27), channel_id=1, source_target_pairs={{8,16},{16,8},{9,17},{17,9},{10,18},{18,10},{11,19},{19,11},{12,20... | collective-permute-start | bytes 393224 | tf_op jit(solution)/shard_map/ppermute | solution.py:935
  2.7 13.5 %collective-permute-start.1 = (bf16[64,1024]{1,0:T(8,128)(2,1)S(1)}, bf16[64,1024]{1,0:T(8,128)(2,1)S(1)}, u32[]{:S(2)}, u32[]{:S(2)}) collective-permute-start(bf16[64,1024]{1,0:T(8,128)(2,1)S(1)} %get-tuple-element.28), channel_id=1, source_target_pairs={{0,8},{8,0},{16,24},{24,16},{1,9},{9,1},{17,25},{25,17},{2,10},{10... | collective-permute-start | bytes 393224 | tf_op jit(solution)/shard_map/ppermute | solution.py:935
  8.4 8.5 %copy-start = (bf16[64,8,8,128]{3,2,1,0:T(8,128)(2,1)S(1)}, bf16[64,8,8,128]{3,2,1,0:T(8,128)(2,1)}, u32[]{:S(2)}) copy-start(bf16[64,8,8,128]{3,2,1,0:T(8,128)(2,1)} %a_ref) | copy-start | bytes 3145732
  11.3 17.6 %all-to-all-start = ((bf16[32,32,128]{2,1,0:T(8,128)(2,1)}), bf16[32,32,128]{2,1,0:T(8,128)(2,1)S(1)}, u32[]{:S(2)}, u32[]{:S(2)}) async-start(bf16[32,32,128]{2,1,0:T(8,128)(2,1)} %get-tuple-element.42), calls=%async_computation | async-start | bytes 524288 | tf_op jit(solution)/shard_map/all_to_all | solution.py:764
  16.6 1.5 %collective-permute-start.2 = (bf16[12,64,128]{2,1,0:T(8,128)(2,1)S(1)}, bf16[12,64,128]{2,1,0:T(8,128)(2,1)S(1)}, u32[]{:S(2)}, u32[]{:S(2)}) collective-permute-start(bf16[12,64,128]{2,1,0:T(8,128)(2,1)S(1)} %get-tuple-element.36.own_ref), channel_id=1, source_target_pairs={{0,4},{4,0},{1,5},{5,1},{2,6},{6,2},{3,7},{7,3},{8,12},{12,8},{9,1... | collective-permute-start | bytes 589832 | tf_op jit(solution)/shard_map/ppermute | solution.py:928
  18.2 8.8 %collective-permute-start.3 = (bf16[3,64,128]{2,1,0:T(8,128)(2,1)S(1)}, bf16[3,64,128]{2,1,0:T(8,128)(2,1)S(1)}, u32[]{:S(2)}, u32[]{:S(2)}) collective-permute-start(bf16[3,64,128]{2,1,0:T(8,128)(2,1)S(1)} %get-tuple-element.39.refs_3_), channel_id=1, source_target_pairs={{1,2},{2,1},{5,6},{6,5},{9,10},{10,9},{13,14},{14,13},{17,18},{18,... | collective-permute-start | bytes 147464 | tf_op jit(solution)/shard_map/ppermute | solution.py:935
  18.9 8.1 %collective-permute-start.4 = (bf16[3,64,128]{2,1,0:T(8,128)(2,1)S(1)}, bf16[3,64,128]{2,1,0:T(8,128)(2,1)S(1)}, u32[]{:S(2)}, u32[]{:S(2)}) collective-permute-start(bf16[3,64,128]{2,1,0:T(8,128)(2,1)S(1)} %get-tuple-element.40.refs_2_), channel_id=1, source_target_pairs={{0,1},{1,0},{2,3},{3,2},{4,5},{5,4},{6,7},{7,6},{8,9},{9,8},{10,11... | collective-permute-start | bytes 147464 | tf_op jit(solution)/shard_map/ppermute | solution.py:935
  28.9 13.8 %all-to-all-start.1 = ((bf16[32,32,128]{2,1,0:T(8,128)(2,1)}), bf16[32,32,128]{2,1,0:T(8,128)(2,1)S(1)}, u32[]{:S(2)}, u32[]{:S(2)}) async-start(bf16[32,32,128]{2,1,0:T(8,128)(2,1)} %finish.1), calls=%async_computation.1 | async-start | bytes 524288 | tf_op jit(solution)/shard_map/all_to_all | solution.py:778
  33.4 9.3 %copy-start.2 = (f32[3456]{0:T(1024)S(1)}, f32[3456]{0:T(1024)}, u32[]{:S(2)}) copy-start(f32[3456]{0:T(1024)} %param.10) | copy-start | bytes 41476
  33.4 9.3 %copy-start.3 = (f32[3456]{0:T(1024)S(1)}, f32[3456]{0:T(1024)}, u32[]{:S(2)}) copy-start(f32[3456]{0:T(1024)} %param.11) | copy-start | bytes 41476

commit v7 on v6

--- a/solution.py
+++ b/solution.py
@@ -38,6 +38,16 @@
 
 def masked(p, u):
     return jnp.where(p > 0, u, jnp.zeros_like(u))
+
+
+def choose(condition, out_ref, first_ref, second_ref):
+    @pl.when(condition)
+    def _():
+        out_ref[...] = first_ref[...]
+
+    @pl.when(jnp.logical_not(condition))
+    def _():
+        out_ref[...] = second_ref[...]
 
 
 def face_kernel(axis, rows, p_ref, u_ref, *refs):
@@ -62,24 +72,14 @@
 
         to_planes(masked(p_buf[k], u_buf[k]), tile.at[k], write, rows)
     if axis is not None:
-        odd = is_odd(axis)
-
-        @pl.when(odd)
-        def _():
-            for swap_ref, out_ref in zip(swap_refs, out_refs):
-                swap_ref[...] = out_ref[...]
-
-        @pl.when(jnp.logical_not(odd))
-        def _():
-            for swap_ref, out_ref in zip(swap_refs, out_refs[::-1]):
-                swap_ref[...] = out_ref[...]
+        choose(is_odd(axis), swap_refs[0], out_refs[1], out_refs[0])
 
 
 def faces(preact, upstream, axis=None, rows=1):
     channels, size_x, size_y, size_z = preact.shape
     face = jax.ShapeDtypeStruct((channels, size_y * size_z), BF16)
     buffer = pltpu.VMEM((2, channels, size_y, size_z), BF16)
-    count = 2 if axis is None else 4
+    count = 2 if axis is None else 3
     return pl.pallas_call(
         functools.partial(face_kernel, axis, rows),
         in_specs=[HBM, HBM],
@@ -435,8 +435,9 @@
 
 
 def pair_inner_kernel(rows, *refs):
-    first_ref, last_ref, m_ref, g_ref, side_ref, sent_ref = refs[2:8]
-    tile_ref, tile_sems = refs[12:]
+    first_ref, last_ref, m_ref, g_ref, side_ref, swap_ref, sent_ref = refs[2:9]
+    tile_ref, tile_sems = refs[13:]
+    choose(is_odd("gx"), swap_ref, first_ref, last_ref)
     share = m_ref[...]
     height = tile_ref.shape[0] - share.shape[0]
     if height:
@@ -448,7 +449,7 @@
     ]
     for copy in copies:
         copy.start()
-    read_inner(rows, *refs[:2], g_ref, *refs[8:12])
+    read_inner(rows, *refs[:2], g_ref, *refs[9:13])
     size_z = side_ref.shape[-1]
     inner, _, plane = g_ref.shape
     size_x = inner + 2
@@ -470,10 +471,11 @@
     return pl.pallas_call(
         functools.partial(pair_inner_kernel, rows),
         in_specs=[HBM] * 2 + [VMEM] * 3,
-        out_specs=[VMEM] * 2 + [HBM],
+        out_specs=[VMEM] * 3 + [HBM],
         out_shape=[
             inner_output(*shape),
             jax.ShapeDtypeStruct((size_x + 2, channels, size_z), BF16),
+            jax.ShapeDtypeStruct(first.shape, BF16),
             jax.ShapeDtypeStruct(sent_shape, BF16),
         ],
         scratch_shapes=inner_scratch(*shape)
@@ -505,9 +507,17 @@
     for x in range(size_x):
         sent_ref[x + 1] = own_ref[x]
     sent_ref[size_x + 1] = row_for_other(high, size_z)
-    tiles = z_tiles([low, high], size_y, size_z, (0, size_x + 1))
-    for k in range(2):
-        sent_ref[size_x + 2 + k] = (own_ref[size_x + k].astype(F32) + tiles[k]).astype(BF16)
+    lane = lax.broadcasted_iota(jnp.int32, (low.shape[0], LANES), 1)
+    first, second = own_ref[size_x], own_ref[size_x + 1]
+    for number, plane in ((0, low), (size_x + 1, high)):
+        for y in range(size_y):
+            at = number * size_y + y
+            head = plane[:, y * size_z : y * size_z + LANES]
+            tail = plane[:, (y + 1) * size_z - LANES : (y + 1) * size_z]
+            first = jnp.where(lane == at, pltpu.roll(head, at, 1), first)
+            second = jnp.where(lane == at, pltpu.roll(tail, at + 1, 1), second)
+    sent_ref[size_x + 2] = first
+    sent_ref[size_x + 3] = second
 
 
 def side(halves, own):
@@ -594,7 +604,7 @@
 
 def finish_kernel(scale, rows, sizes, *refs):
     acc_ref, columns_ref, even_ref, odd_ref, from_odd_ref, from_even_ref = refs[:6]
-    part_ref, flat, chunks = refs[6:]
+    part_ref, chunks = refs[6:]
     size_x, size_y = sizes
     channels = columns_ref.shape[0]
     area = size_x * size_y
@@ -630,21 +640,23 @@
                 preferred_element_type=F32,
             )
         )
-    blocks = []
+    count, height, width = part_ref.shape
+    chunks[...] = jnp.zeros_like(chunks)
+    pieces = rows * acc_ref.shape[1] // width
     for a in range(3):
         for c in range(3):
-            block = acc_ref[(3 * a + c) * channels : (3 * a + c + 1) * channels, :]
+            at = 3 * a + c
+            block = acc_ref[at * channels : (at + 1) * channels, :]
             if c != 1:
                 block = block + edges[c // 2][a * channels : (a + 1) * channels]
-            blocks.append(block)
-    whole = to_flat(jnp.concatenate(blocks, axis=0) * scale, channels, channels, flat)
-    count, height, width = part_ref.shape
-    line = jnp.concatenate(
-        [whole[r * count : (r + 1) * count, : 27 * channels] for r in range(rows)], axis=1
-    )
-    chunks[...] = jnp.zeros_like(chunks)
-    for k in range(line.shape[1] // width):
-        chunks[pl.ds(k, count, stride=height), :] = line[:, k * width : (k + 1) * width]
+            block = block * scale
+            line = jnp.concatenate(
+                [block[r * count : (r + 1) * count] for r in range(rows)], axis=1
+            )
+            for k in range(pieces):
+                chunks[pl.ds(at * pieces + k, count, stride=height), :] = line[
+                    :, k * width : (k + 1) * width
+                ]
     part_ref[...] = chunks[...].reshape(part_ref.shape).astype(BF16)
 
 
@@ -655,10 +667,7 @@
         in_specs=[VMEM] * 6,
         out_specs=VMEM,
         out_shape=jax.ShapeDtypeStruct(part_shape, BF16),
-        scratch_shapes=[
-            flat_scratch(channels),
-            pltpu.VMEM((part_shape[0] * part_shape[1], part_shape[2]), F32),
-        ],
+        scratch_shapes=[pltpu.VMEM((part_shape[0] * part_shape[1], part_shape[2]), F32)],
         compiler_params=params(),
         cost_estimate=cost(2**27, 2**21),
         name="finish",
@@ -674,11 +683,49 @@
     return master - 0.05 * update, new_first, new_second
 
 
-def adam_kernel(parts_ref, master_ref, first_ref, second_ref, *out_refs):
-    weight_grad = parts_ref[0].astype(F32)
+def in_flat_order(value, rows, places, spread_rows):
+    taps = 27
+    lane = lax.broadcasted_iota(jnp.int32, (9, LANES), 1)
+    rows[: value.shape[0], :] = value
+    thirds = [rows[pl.ds(k, 9, stride=3), :] for k in range(3)]
+    half = LANES // 2
+    by_y = (
+        jnp.where(lane < half, thirds[0], thirds[1]),
+        jnp.where(lane < half, pltpu.roll(thirds[0], half, 1), pltpu.roll(thirds[2], half, 1)),
+        jnp.where(lane < half, thirds[1], thirds[2]),
+    )
+    places[...] = jnp.zeros_like(places)
+    for b in range(3):
+        spread_rows[b, :9, :] = by_y[b]
+        for block in range(9):
+            tap = (2 - block // 3) * 9 + b * 3 + 2 - block % 3
+            places[tap : tap + 1, :] = spread_rows[b, block : block + 1, :]
+    line = places[...].T
+    number = lax.broadcasted_iota(jnp.int32, (LANES, LANES), 0) * taps
+    column = lax.broadcasted_iota(jnp.int32, (LANES, LANES), 1)
+    for bit in range(7):
+        turn = 1 << bit
+        line = jnp.where((number & turn) != 0, pltpu.roll(line, turn, 1), line)
+    start = number & (LANES - 1)
+    line = jnp.concatenate(
+        [jnp.where(column >= start, line, 0.0), jnp.where(column < start, line, 0.0)], axis=0
+    )
+    target = lax.broadcasted_iota(jnp.int32, (32, 2 * LANES), 0)
+    source = lax.broadcasted_iota(jnp.int32, (32, 2 * LANES), 1)
+    goes = lax.shift_right_logical((source & (LANES - 1)) * taps, 7)
+    goes = goes + jnp.where(source < LANES, 0, 1)
+    pick = jnp.where(goes == target, 1.0, 0.0)
+    return jnp.dot(
+        pick, line, preferred_element_type=F32, precision=lax.Precision.HIGHEST
+    )[:taps]
+
+
+def adam_kernel(parts_ref, master_ref, first_ref, second_ref, *refs):
+    out_refs, scratch = refs[:4], refs[4:]
+    total = parts_ref[0].astype(F32)
     for source in range(1, parts_ref.shape[0]):
-        weight_grad = weight_grad + parts_ref[source].astype(F32)
-    weight_grad = weight_grad[: master_ref.shape[0]]
+        total = total + parts_ref[source].astype(F32)
+    weight_grad = in_flat_order(total, *scratch)
     results = adam_step(master_ref[...], first_ref[...], second_ref[...], weight_grad)
     for out_ref, result in zip(out_refs, (weight_grad, *results)):
         out_ref[...] = result
@@ -693,8 +740,13 @@
         in_specs=[VMEM] * 4,
         out_specs=[VMEM] * 4,
         out_shape=[result] * 4,
+        scratch_shapes=[
+            pltpu.VMEM(parts.shape[1:], F32),
+            pltpu.VMEM((LANES, LANES), F32),
+            pltpu.VMEM((3, 16, LANES), F32),
+        ],
         compiler_params=params(),
-        cost_estimate=cost(2**18, 2**18),
+        cost_estimate=cost(2**22, 2**19),
         name="adam",
     )(parts, *tiled)
     return tuple(out.reshape(share) for out in outs)
@@ -755,12 +807,12 @@
     rows = channels // devices
     used = master.shape[0] // LANES
     block = (devices, -(-used // 16) * 16, LANES)
-    first, last, *swaps = faces(preact, upstream, "gx", rows)
-    odd_halves = swapped(swaps[1], "gx", 1)
-    even_halves = swapped(swaps[0], "gx", 0)
-    inner, own, sent = pair_inner(
+    first, last, odd_sent = faces(preact, upstream, "gx", rows)
+    odd_halves = swapped(odd_sent, "gx", 1)
+    inner, own, even_sent, sent = pair_inner(
         preact, upstream, first, last, master.reshape(used, LANES), block, rows
     )
+    even_halves = swapped(even_sent, "gx", 0)
     kernel = lax.all_to_all(sent, AXES, 0, 0, tiled=True)
     own, xlo, xhi = side((odd_halves, even_halves), own)
     planes = (xlo, first, inner, last, xhi)
@@ -944,7 +996,7 @@
         lax.axis_size("gy") == 2
         and channels % devices == 0
         and share % LANES == 0
-        and channels // (channels // devices) % 16 == 0
+        and channels // devices * channels == LANES
         and 2 * size_x * size_y <= LANES
         and (size_x + 2) * size_y <= LANES
     )

time: 43.8 us -> 43.9 us (level)
    pallas_call x1, Pallas kernels: 0.69 us -> 1.53 us  [adam(): pl.pallas_call(adam_kernel, in_specs=[VMEM] * 4, out_specs=[VMEM] * 4, ou...]
    pallas_call x1, Pallas kernels: 1.96 us -> 1.33 us  [finish(): pl.pallas_call(functools.partial(finish_kernel, scale, rows, sizes), in_s...]
  transfers between devices with their start and end apart: 7 -> 7, of which waited for: 2 -> 2; matrix products, arithmetic and copies ran while one was open for 0% -> 0% of each run, Pallas kernels for 36% -> 34%
where the time goes in v7:
time: 43.9 us; the launch traced here: 43.6 us
  starting transfers between devices  20.6 us (47%)
  Pallas kernels  17.8 us (41%)
  waiting for transfers between devices  4.38 us (10%)
  between operations  0.78 us (2%)
    ppermute x4, starting transfers between devices, swapped(): return lax.ppermute(value, axis, pairs)  11.6 us
    pallas_call x1, Pallas kernels, pair_dgrad(): pl.pallas_call(pair_dgrad_kernel, in_specs=[VMEM] * 10, out_specs=VMEM, o...  5.08 us
    all_to_all x1, starting transfers between devices, pair_program(): kernel = lax.all_to_all(sent, AXES, 0, 0, tiled=True)  4.84 us
    all_to_all x1, waiting for transfers between devices, pair_program(): parts = lax.all_to_all(part, AXES, 0, 0, tiled=True)  4.23 us
    all_to_all x1, starting transfers between devices, pair_program(): parts = lax.all_to_all(part, AXES, 0, 0, tiled=True)  3.78 us
    pallas_call x1, Pallas kernels, pair_wgrad(): pl.pallas_call(pair_wgrad_kernel, in_specs=[VMEM] * 8, out_specs=VMEM, ou...  3.56 us
    pallas_call x1, Pallas kernels, pair_inner(): pl.pallas_call(functools.partial(pair_inner_kernel, rows), in_specs=[HBM]...  2.95 us
    pallas_call x1, Pallas kernels, adam(): pl.pallas_call(adam_kernel, in_specs=[VMEM] * 4, out_specs=[VMEM] * 4, ou...  1.53 us
  transfers between devices with their start and end apart: 7, of which 2 were waited for; matrix products, arithmetic and copies ran while one was open for 0% of the time, Pallas kernels for 34%

profile of v7, /device:TPU:0, one launch (start us, length us, event | category | flops | bytes accessed | tf_op | source)
XLA Modules:
  0.0 43.6 jit_solution(14605850178588341801)
XLA Ops:
  0.6 0.0 copy-start.1
  0.6 1.3 %faces.1 = (bf16[64,1024]{1,0:T(8,128)(2,1)S(1)}, bf16[64,1024]{1,0:T(8,128)(2,1)S(1)}, bf16[64,1024]{1,0:T(8,128)(2,1)S(1)}) custom-call(bf16[64,8,8,128]{3,2,1,0:T(8,128)(2,1)} %refs_0_.1, bf16[64,8,8,128]{3,2,1,0:T(8,128)(2,1)} %refs_1_.1), custom_call_target="tpu_custom_call" | custom-call | bytes 1048576 | tf_op jit(solution)/shard_map/faces/pallas_call | solution.py:83
  2.0 0.7 %collective-permute-start = (bf16[64,1024]{1,0:T(8,128)(2,1)S(1)}, bf16[64,1024]{1,0:T(8,128)(2,1)S(1)}, u32[]{:S(2)}, u32[]{:S(2)}) collective-permute-start(bf16[64,1024]{1,0:T(8,128)(2,1)S(1)} %get-tuple-element.27), channel_id=1, source_target_pairs={{8,16},{16,8},{9,17},{17,9},{10,18},{18,10},{11,19},{19,11},{12,20... | collective-permute-start | bytes 393224 | tf_op jit(solution)/shard_map/ppermute | solution.py:987
  2.7 0.0 copy-done.1
  2.7 0.0 copy-start
  2.7 2.9 %inner.1 = (bf16[6,64,1024]{2,1,0:T(8,128)(2,1)S(1)}, bf16[10,64,128]{2,1,0:T(8,128)(2,1)S(1)}, bf16[64,1024]{1,0:T(8,128)(2,1)S(1)}, bf16[32,32,128]{2,1,0:T(8,128)(2,1)}) custom-call(bf16[64,8,8,128]{3,2,1,0:T(8,128)(2,1)} %refs_0_.1, bf16[64,8,8,128]{3,2,1,0:T(8,128)(2,1)} %refs_1_.1, bf16[64,1024]{1,0:T(8,128)(2,1)S(1)} %get-tuple-element.28.refs_2_.refs_1_, ...), custom_call_target="tpu_custom_call" | custom-call | bytes 4194304 | tf_op jit(solution)/shard_map/inner/pallas_call | solution.py:471
  5.6 5.7 %collective-permute-start.1 = (bf16[64,1024]{1,0:T(8,128)(2,1)S(1)}, bf16[64,1024]{1,0:T(8,128)(2,1)S(1)}, u32[]{:S(2)}, u32[]{:S(2)}) collective-permute-start(bf16[64,1024]{1,0:T(8,128)(2,1)S(1)} %get-tuple-element.30), channel_id=1, source_target_pairs={{0,8},{8,0},{16,24},{24,16},{1,9},{9,1},{17,25},{25,17},{2,10},{10... | collective-permute-start | bytes 393224 | tf_op jit(solution)/shard_map/ppermute | solution.py:987
  11.4 4.8 %all-to-all-start = ((bf16[32,32,128]{2,1,0:T(8,128)(2,1)}), bf16[32,32,128]{2,1,0:T(8,128)(2,1)S(1)}, u32[]{:S(2)}, u32[]{:S(2)}) async-start(bf16[32,32,128]{2,1,0:T(8,128)(2,1)} %get-tuple-element.42), calls=%async_computation | async-start | bytes 524288 | tf_op jit(solution)/shard_map/all_to_all | solution.py:816
  16.2 0.0 collective-permute-done.odd_ref
  16.2 0.0 collective-permute-done.1.even_ref
  16.2 0.2 side.1
  16.5 0.3 collective-permute-start.2
  16.8 0.0 copy-done
  16.8 1.0 %inputs.1 = (bf16[8,64,1024]{2,1,0:T(8,128)(2,1)S(1)}, bf16[64,128]{1,0:T(8,128)(2,1)S(1)}) custom-call(bf16[64,8,8,128]{3,2,1,0:T(8,128)(2,1)S(1)} %copy-done), custom_call_target="tpu_custom_call" | custom-call | bytes 2097152 | tf_op jit(solution)/shard_map/inputs/pallas_call | solution.py:172
  17.8 0.1 collective-permute-done.2.other_ref.refs_5_.refs_6_
  18.0 0.1 join.1
  18.1 0.7 %collective-permute-start.3 = (bf16[3,64,128]{2,1,0:T(8,128)(2,1)S(1)}, bf16[3,64,128]{2,1,0:T(8,128)(2,1)S(1)}, u32[]{:S(2)}, u32[]{:S(2)}) collective-permute-start(bf16[3,64,128]{2,1,0:T(8,128)(2,1)S(1)} %get-tuple-element.39.refs_3_), channel_id=1, source_target_pairs={{1,2},{2,1},{5,6},{6,5},{9,10},{10,9},{13,14},{14,13},{17,18},{18,... | collective-permute-start | bytes 147464 | tf_op jit(solution)/shard_map/ppermute | solution.py:987
  18.7 4.5 %collective-permute-start.4 = (bf16[3,64,128]{2,1,0:T(8,128)(2,1)S(1)}, bf16[3,64,128]{2,1,0:T(8,128)(2,1)S(1)}, u32[]{:S(2)}, u32[]{:S(2)}) collective-permute-start(bf16[3,64,128]{2,1,0:T(8,128)(2,1)S(1)} %get-tuple-element.40.refs_2_), channel_id=1, source_target_pairs={{0,1},{1,0},{2,3},{3,2},{4,5},{5,4},{6,7},{7,6},{8,9},{9,8},{10,11... | collective-permute-start | bytes 147464 | tf_op jit(solution)/shard_map/ppermute | solution.py:987
  23.3 3.6 %wgrad.1.refs_0_ = f32[576,192]{1,0:T(8,128)S(1)} custom-call(bf16[64,1024]{1,0:T(8,128)(2,1)S(1)} %get-tuple-element.32.refs_0_, bf16[64,1024]{1,0:T(8,128)(2,1)S(1)} %get-tuple-element.28.refs_2_.refs_1_, bf16[6,64,1024]{2,1,0:T(8,128)(2,1)S(1)} %get-tuple-element.33.refs_2_, bf16[64,1024]{1,0:T(8,128)(2,1)S(1)} %get-tuple-element.29.refs_3_, ...), custom_call_target="tpu_custom_call" | custom-call | flops 2264924160 | bytes 4194304 | tf_op jit(solution)/shard_map/wgrad/pallas_call | solution.py:593
  26.9 0.0 collective-permute-done.3.refs_4_.refs_7_
  26.9 0.0 collective-permute-done.4.refs_5_.refs_8_
  26.9 1.3 %finish.1 = bf16[32,32,128]{2,1,0:T(8,128)(2,1)} custom-call(f32[576,192]{1,0:T(8,128)S(1)} %wgrad.1.refs_0_, bf16[64,128]{1,0:T(8,128)(2,1)S(1)} %get-tuple-element.38.columns_ref.refs_1_, bf16[3,64,128]{2,1,0:T(8,128)(2,1)S(1)} %get-tuple-element.40.refs_2_, bf16[3,64,128]{2,1,0:T(8,128)(2,1)S(1)} %get-tuple-element.39.refs_3_, ...), custom_call_target="tpu_custom_call" | custom-call | flops 134217728 | bytes 2097152 | tf_op jit(solution)/shard_map/finish/pallas_call | solution.py:665
  28.2 0.0 all-to-all-done.w_ref
  28.2 3.8 %all-to-all-start.1 = ((bf16[32,32,128]{2,1,0:T(8,128)(2,1)}), bf16[32,32,128]{2,1,0:T(8,128)(2,1)S(1)}, u32[]{:S(2)}, u32[]{:S(2)}) async-start(bf16[32,32,128]{2,1,0:T(8,128)(2,1)} %finish.1), calls=%async_computation.1 | async-start | bytes 524288 | tf_op jit(solution)/shard_map/all_to_all | solution.py:830
  32.0 0.7 %spread.1.refs_9_ = bf16[3,128,768]{2,1,0:T(8,128)(2,1)S(1)} custom-call(bf16[32,32,128]{2,1,0:T(8,128)(2,1)S(1)} %all-to-all-done.w_ref), custom_call_target="tpu_custom_call" | custom-call | flops 1048576 | bytes 2097152 | tf_op jit(solution)/shard_map/spread/pallas_call | solution.py:767
  32.7 0.0 copy-start.2
  32.7 0.0 copy-start.3
  32.7 5.1 %dgrad.1 = bf16[64,8,8,128]{3,2,1,0:T(8,128)(2,1)} custom-call(bf16[64,1024]{1,0:T(8,128)(2,1)S(1)} %get-tuple-element.32.refs_0_, bf16[64,1024]{1,0:T(8,128)(2,1)S(1)} %get-tuple-element.28.refs_2_.refs_1_, bf16[6,64,1024]{2,1,0:T(8,128)(2,1)S(1)} %get-tuple-element.33.refs_2_, bf16[64,1024]{1,0:T(8,128)(2,1)S(1)} %get-tuple-element.29.refs_3_, ...), custom_call_target="tpu_custom_call" | custom-call | flops 2415919104 | bytes 4194304 | tf_op jit(solution)/shard_map/dgrad/pallas_call | solution.py:791
  37.8 4.2 %all-to-all-done.1.parts_ref = bf16[32,32,128]{2,1,0:T(8,128)(2,1)S(1)} async-done(((bf16[32,32,128]{2,1,0:T(8,128)(2,1)}), bf16[32,32,128]{2,1,0:T(8,128)(2,1)S(1)}, u32[]{:S(2)}, u32[]{:S(2)}) %all-to-all-start.1) | async-done | bytes 262176 | tf_op jit(solution)/shard_map/all_to_all | solution.py:830
  42.0 0.0 copy-done.2
  42.0 0.0 copy-done.3
  42.0 1.5 %adam.1 = (f32[27,128]{1,0:T(8,128)}, f32[27,128]{1,0:T(8,128)}, f32[27,128]{1,0:T(8,128)}, f32[27,128]{1,0:T(8,128)}) custom-call(bf16[32,32,128]{2,1,0:T(8,128)(2,1)S(1)} %all-to-all-done.1.parts_ref, f32[27,128]{1,0:T(8,128)S(1)} %bitcast.8, f32[27,128]{1,0:T(8,128)S(1)} %bitcast.9, f32[27,128]{1,0:T(8,128)S(1)} %bitcast.10), custom_call_target="tpu_custom_call" | custom-call | flops 4194304 | bytes 524288 | tf_op jit(solution)/shard_map/adam/pallas_call | solution.py:738
Async XLA Ops:
  0.6 2.0 %copy-start.1 = (f32[3456]{0:T(1024)S(1)}, f32[3456]{0:T(1024)}, u32[]{:S(2)}) copy-start(f32[3456]{0:T(1024)} %param.9) | copy-start | bytes 41476
  2.0 14.2 %collective-permute-start = (bf16[64,1024]{1,0:T(8,128)(2,1)S(1)}, bf16[64,1024]{1,0:T(8,128)(2,1)S(1)}, u32[]{:S(2)}, u32[]{:S(2)}) collective-permute-start(bf16[64,1024]{1,0:T(8,128)(2,1)S(1)} %get-tuple-element.27), channel_id=1, source_target_pairs={{8,16},{16,8},{9,17},{17,9},{10,18},{18,10},{11,19},{19,11},{12,20... | collective-permute-start | bytes 393224 | tf_op jit(solution)/shard_map/ppermute | solution.py:987
  2.7 14.1 %copy-start = (bf16[64,8,8,128]{3,2,1,0:T(8,128)(2,1)S(1)}, bf16[64,8,8,128]{3,2,1,0:T(8,128)(2,1)}, u32[]{:S(2)}) copy-start(bf16[64,8,8,128]{3,2,1,0:T(8,128)(2,1)} %a_ref) | copy-start | bytes 3145732
  5.6 10.6 %collective-permute-start.1 = (bf16[64,1024]{1,0:T(8,128)(2,1)S(1)}, bf16[64,1024]{1,0:T(8,128)(2,1)S(1)}, u32[]{:S(2)}, u32[]{:S(2)}) collective-permute-start(bf16[64,1024]{1,0:T(8,128)(2,1)S(1)} %get-tuple-element.30), channel_id=1, source_target_pairs={{0,8},{8,0},{16,24},{24,16},{1,9},{9,1},{17,25},{25,17},{2,10},{10... | collective-permute-start | bytes 393224 | tf_op jit(solution)/shard_map/ppermute | solution.py:987
  11.4 16.8 %all-to-all-start = ((bf16[32,32,128]{2,1,0:T(8,128)(2,1)}), bf16[32,32,128]{2,1,0:T(8,128)(2,1)S(1)}, u32[]{:S(2)}, u32[]{:S(2)}) async-start(bf16[32,32,128]{2,1,0:T(8,128)(2,1)} %get-tuple-element.42), calls=%async_computation | async-start | bytes 524288 | tf_op jit(solution)/shard_map/all_to_all | solution.py:816
  16.5 1.5 %collective-permute-start.2 = (bf16[12,64,128]{2,1,0:T(8,128)(2,1)S(1)}, bf16[12,64,128]{2,1,0:T(8,128)(2,1)S(1)}, u32[]{:S(2)}, u32[]{:S(2)}) collective-permute-start(bf16[12,64,128]{2,1,0:T(8,128)(2,1)S(1)} %get-tuple-element.36.own_ref), channel_id=1, source_target_pairs={{0,4},{4,0},{1,5},{5,1},{2,6},{6,2},{3,7},{7,3},{8,12},{12,8},{9,1... | collective-permute-start | bytes 589832 | tf_op jit(solution)/shard_map/ppermute | solution.py:980
  18.1 8.8 %collective-permute-start.3 = (bf16[3,64,128]{2,1,0:T(8,128)(2,1)S(1)}, bf16[3,64,128]{2,1,0:T(8,128)(2,1)S(1)}, u32[]{:S(2)}, u32[]{:S(2)}) collective-permute-start(bf16[3,64,128]{2,1,0:T(8,128)(2,1)S(1)} %get-tuple-element.39.refs_3_), channel_id=1, source_target_pairs={{1,2},{2,1},{5,6},{6,5},{9,10},{10,9},{13,14},{14,13},{17,18},{18,... | collective-permute-start | bytes 147464 | tf_op jit(solution)/shard_map/ppermute | solution.py:987
  18.7 8.1 %collective-permute-start.4 = (bf16[3,64,128]{2,1,0:T(8,128)(2,1)S(1)}, bf16[3,64,128]{2,1,0:T(8,128)(2,1)S(1)}, u32[]{:S(2)}, u32[]{:S(2)}) collective-permute-start(bf16[3,64,128]{2,1,0:T(8,128)(2,1)S(1)} %get-tuple-element.40.refs_2_), channel_id=1, source_target_pairs={{0,1},{1,0},{2,3},{3,2},{4,5},{5,4},{6,7},{7,6},{8,9},{9,8},{10,11... | collective-permute-start | bytes 147464 | tf_op jit(solution)/shard_map/ppermute | solution.py:987
  28.2 13.8 %all-to-all-start.1 = ((bf16[32,32,128]{2,1,0:T(8,128)(2,1)}), bf16[32,32,128]{2,1,0:T(8,128)(2,1)S(1)}, u32[]{:S(2)}, u32[]{:S(2)}) async-start(bf16[32,32,128]{2,1,0:T(8,128)(2,1)} %finish.1), calls=%async_computation.1 | async-start | bytes 524288 | tf_op jit(solution)/shard_map/all_to_all | solution.py:830
  32.7 9.3 %copy-start.2 = (f32[3456]{0:T(1024)S(1)}, f32[3456]{0:T(1024)}, u32[]{:S(2)}) copy-start(f32[3456]{0:T(1024)} %param.10) | copy-start | bytes 41476
  32.7 9.3 %copy-start.3 = (f32[3456]{0:T(1024)S(1)}, f32[3456]{0:T(1024)}, u32[]{:S(2)}) copy-start(f32[3456]{0:T(1024)} %param.11) | copy-start | bytes 41476

commit v8 on v7

--- a/solution.py
+++ b/solution.py
@@ -26,14 +26,20 @@
     return pl.CostEstimate(flops=flops, bytes_accessed=moved, transcendentals=0)
 
 
-def to_planes(value, tile, write, rows=1):
+def to_planes(value, tile, write, order=(1, 1)):
     channels, size_y, size_z = value.shape
-    count = channels // rows
+    lines, rows = order
+    count = channels // (lines * rows)
     tile[...] = value.astype(F32).reshape(channels * size_y, size_z)
     for y in range(size_y):
         for r in range(rows):
-            picked = tile[pl.ds(r * size_y + y, count, stride=rows * size_y), :]
-            write(slice(r * count, (r + 1) * count), y, picked.astype(BF16))
+            found = []
+            for e in range(lines):
+                start = (e * rows + r) * size_y + y
+                found.append(tile[pl.ds(start, count, stride=lines * rows * size_y), :])
+            at = slice(r * lines * count, (r + 1) * lines * count)
+            picked = found[0] if lines == 1 else jnp.concatenate(found, axis=0)
+            write(at, y, picked.astype(BF16))
 
 
 def masked(p, u):
@@ -50,7 +56,7 @@
         out_ref[...] = second_ref[...]
 
 
-def face_kernel(axis, rows, p_ref, u_ref, *refs):
+def face_kernel(axis, order, p_ref, u_ref, *refs):
     p_buf, u_buf, tile, sems = refs[-4:]
     out_refs, swap_refs = refs[:2], refs[2:-4]
     size_x, size_z = p_ref.shape[1], p_ref.shape[3]
@@ -70,18 +76,18 @@
         def write(at, y, value):
             out_ref[at, y * size_z : (y + 1) * size_z] = value
 
-        to_planes(masked(p_buf[k], u_buf[k]), tile.at[k], write, rows)
+        to_planes(masked(p_buf[k], u_buf[k]), tile.at[k], write, order)
     if axis is not None:
         choose(is_odd(axis), swap_refs[0], out_refs[1], out_refs[0])
 
 
-def faces(preact, upstream, axis=None, rows=1):
+def faces(preact, upstream, axis=None, order=(1, 1)):
     channels, size_x, size_y, size_z = preact.shape
     face = jax.ShapeDtypeStruct((channels, size_y * size_z), BF16)
     buffer = pltpu.VMEM((2, channels, size_y, size_z), BF16)
     count = 2 if axis is None else 3
     return pl.pallas_call(
-        functools.partial(face_kernel, axis, rows),
+        functools.partial(face_kernel, axis, order),
         in_specs=[HBM, HBM],
         out_specs=[VMEM] * count,
         out_shape=[face] * count,
@@ -97,7 +103,7 @@
     )(preact, upstream)
 
 
-def read_inner(rows, p_ref, u_ref, g_ref, p_buf, u_buf, tile, sems):
+def read_inner(order, p_ref, u_ref, g_ref, p_buf, u_buf, tile, sems):
     size_x, size_z = p_ref.shape[1], p_ref.shape[3]
     inner = size_x - 2
     copies = []
@@ -116,11 +122,11 @@
         def write(at, y, value):
             g_ref[x, at, y * size_z : (y + 1) * size_z] = value
 
-        to_planes(masked(p_buf[x], u_buf[x]), tile.at[x % 2], write, rows)
+        to_planes(masked(p_buf[x], u_buf[x]), tile.at[x % 2], write, order)
 
 
 def inner_kernel(*refs):
-    read_inner(1, *refs)
+    read_inner((1, 1), *refs)
 
 
 def inner_output(channels, size_x, size_y, size_z):
@@ -434,9 +440,10 @@
     return jnp.where(lax.axis_index("gy") == 0, high, low).astype(BF16)
 
 
-def pair_inner_kernel(rows, *refs):
+def pair_inner_kernel(order, *refs):
     first_ref, last_ref, m_ref, g_ref, side_ref, swap_ref, sent_ref = refs[2:9]
-    tile_ref, tile_sems = refs[13:]
+    tile, tile_ref, tile_sems = refs[9:]
+    size_z = side_ref.shape[-1]
     choose(is_odd("gx"), swap_ref, first_ref, last_ref)
     share = m_ref[...]
     height = tile_ref.shape[0] - share.shape[0]
@@ -449,8 +456,12 @@
     ]
     for copy in copies:
         copy.start()
-    read_inner(rows, *refs[:2], g_ref, *refs[9:13])
-    size_z = side_ref.shape[-1]
+    for x in range(g_ref.shape[0]):
+
+        def write(at, y, value):
+            g_ref[x, at, y * size_z : (y + 1) * size_z] = value
+
+        to_planes(masked(refs[0][:, x + 1], refs[1][:, x + 1]), tile.at[x % 2], write, order)
     inner, _, plane = g_ref.shape
     size_x = inner + 2
     bodies = [first_ref] + [g_ref.at[x] for x in range(inner)] + [last_ref]
@@ -465,12 +476,12 @@
         copy.wait()
 
 
-def pair_inner(preact, upstream, first, last, share, sent_shape, rows):
+def pair_inner(preact, upstream, first, last, share, sent_shape, order):
     shape = preact.shape
     channels, size_x, _, size_z = shape
     return pl.pallas_call(
-        functools.partial(pair_inner_kernel, rows),
-        in_specs=[HBM] * 2 + [VMEM] * 3,
+        functools.partial(pair_inner_kernel, order),
+        in_specs=[VMEM] * 5,
         out_specs=[VMEM] * 3 + [HBM],
         out_shape=[
             inner_output(*shape),
@@ -478,9 +489,12 @@
             jax.ShapeDtypeStruct(first.shape, BF16),
             jax.ShapeDtypeStruct(sent_shape, BF16),
         ],
-        scratch_shapes=inner_scratch(*shape)
-        + [pltpu.VMEM(sent_shape[1:], BF16), pltpu.SemaphoreType.DMA((sent_shape[0],))],
-        compiler_params=params(INNER_VMEM),
+        scratch_shapes=[
+            pltpu.VMEM((2, channels * shape[2], size_z), F32),
+            pltpu.VMEM(sent_shape[1:], BF16),
+            pltpu.SemaphoreType.DMA((sent_shape[0],)),
+        ],
+        compiler_params=params(),
         cost_estimate=cost(0, 4 * 2**20),
         name="inner",
     )(preact, upstream, first, last, share)
@@ -714,9 +728,15 @@
     source = lax.broadcasted_iota(jnp.int32, (32, 2 * LANES), 1)
     goes = lax.shift_right_logical((source & (LANES - 1)) * taps, 7)
     goes = goes + jnp.where(source < LANES, 0, 1)
-    pick = jnp.where(goes == target, 1.0, 0.0)
+    pick = jnp.where(goes == target, 1.0, 0.0).astype(BF16)
+    parts = []
+    for _ in range(3):
+        parts.append(line.astype(BF16))
+        line = line - parts[-1].astype(F32)
     return jnp.dot(
-        pick, line, preferred_element_type=F32, precision=lax.Precision.HIGHEST
+        jnp.concatenate([pick] * 3, axis=1),
+        jnp.concatenate(parts, axis=0),
+        preferred_element_type=F32,
     )[:taps]
 
 
@@ -807,13 +827,15 @@
     rows = channels // devices
     used = master.shape[0] // LANES
     block = (devices, -(-used // 16) * 16, LANES)
-    first, last, odd_sent = faces(preact, upstream, "gx", rows)
+    order = (lax.axis_size("gz"), rows)
+    partners = ("gz", "gx", "gy")
+    first, last, odd_sent = faces(preact, upstream, "gx", order)
     odd_halves = swapped(odd_sent, "gx", 1)
     inner, own, even_sent, sent = pair_inner(
-        preact, upstream, first, last, master.reshape(used, LANES), block, rows
+        preact, upstream, first, last, master.reshape(used, LANES), block, order
     )
     even_halves = swapped(even_sent, "gx", 0)
-    kernel = lax.all_to_all(sent, AXES, 0, 0, tiled=True)
+    kernel = lax.all_to_all(sent, partners, 0, 0, tiled=True)
     own, xlo, xhi = side((odd_halves, even_halves), own)
     planes = (xlo, first, inner, last, xhi)
     own, activations = lax.optimization_barrier((own, activations))
@@ -827,7 +849,7 @@
     z_received = (from_odd, from_even)
     part = finish(acc, columns, z_sent, z_received, scale, rows, (size_x, size_y), block)
     part, kernel = lax.optimization_barrier((part, kernel))
-    parts = lax.all_to_all(part, AXES, 0, 0, tiled=True)
+    parts = lax.all_to_all(part, partners, 0, 0, tiled=True)
     weights = spread(kernel, channels, rows)
     grad_input = pair_dgrad((*sources, *z_received), weights, shape)
     return grad_input, *adam(parts, master, first_moment, second_moment)

time: 43.9 us -> 45.3 us (1.032)
  local copies, waits for them, and re-layouts: 0.02 us -> 0.74 us
    unnamed x8 -> x14, local copies, waits for them, and re-layouts: 0.02 us -> 0.74 us
  transfers between devices with their start and end apart: 7 -> 7, of which waited for: 2 -> 2; matrix products, arithmetic and copies ran while one was open for 0% -> 0% of each run, Pallas kernels for 34% -> 33%
where the time goes in v8:
time: 45.3 us; the launch traced here: 44.9 us
  starting transfers between devices  20.6 us (45%)
  Pallas kernels  18 us (40%)
  waiting for transfers between devices  4.77 us (11%)
  between operations  0.81 us (2%)
  local copies, waits for them, and re-layouts  0.74 us (2%)
    ppermute x4, starting transfers between devices, swapped(): return lax.ppermute(value, axis, pairs)  11.6 us
    pallas_call x1, Pallas kernels, pair_dgrad(): pl.pallas_call(pair_dgrad_kernel, in_specs=[VMEM] * 10, out_specs=VMEM, o...  5.08 us
    all_to_all x1, starting transfers between devices, pair_program(): kernel = lax.all_to_all(sent, partners, 0, 0, tiled=True)  4.83 us
    all_to_all x1, waiting for transfers between devices, pair_program(): parts = lax.all_to_all(part, partners, 0, 0, tiled=True)  4.62 us
    all_to_all x1, starting transfers between devices, pair_program(): parts = lax.all_to_all(part, partners, 0, 0, tiled=True)  3.79 us
    pallas_call x1, Pallas kernels, pair_wgrad(): pl.pallas_call(pair_wgrad_kernel, in_specs=[VMEM] * 8, out_specs=VMEM, ou...  3.56 us
    pallas_call x1, Pallas kernels, pair_inner(): pl.pallas_call(functools.partial(pair_inner_kernel, order), in_specs=[VME...  2.93 us
    pallas_call x1, Pallas kernels, faces(): pl.pallas_call(functools.partial(face_kernel, axis, order), in_specs=[HBM...  1.61 us
  transfers between devices with their start and end apart: 7, of which 2 were waited for; matrix products, arithmetic and copies ran while one was open for 0% of the time, Pallas kernels for 33%

profile of v8, /device:TPU:0, one launch (start us, length us, event | category | flops | bytes accessed | tf_op | source)
XLA Modules:
  0.0 44.9 jit_solution(7677554218712259444)
XLA Ops:
  0.6 0.0 copy-start.1
  0.6 0.0 copy-start
  0.7 1.6 %faces.1 = (bf16[64,1024]{1,0:T(8,128)(2,1)S(1)}, bf16[64,1024]{1,0:T(8,128)(2,1)S(1)}, bf16[64,1024]{1,0:T(8,128)(2,1)S(1)}) custom-call(bf16[64,8,8,128]{3,2,1,0:T(8,128)(2,1)} %refs_0_.1, bf16[64,8,8,128]{3,2,1,0:T(8,128)(2,1)} %refs_1_.1), custom_call_target="tpu_custom_call" | custom-call | bytes 1048576 | tf_op jit(solution)/shard_map/faces/pallas_call | solution.py:89
  2.3 0.7 %collective-permute-start = (bf16[64,1024]{1,0:T(8,128)(2,1)S(1)}, bf16[64,1024]{1,0:T(8,128)(2,1)S(1)}, u32[]{:S(2)}, u32[]{:S(2)}) collective-permute-start(bf16[64,1024]{1,0:T(8,128)(2,1)S(1)} %get-tuple-element.27), channel_id=1, source_target_pairs={{8,16},{16,8},{9,17},{17,9},{10,18},{18,10},{11,19},{19,11},{12,20... | collective-permute-start | bytes 393224 | tf_op jit(solution)/shard_map/ppermute | solution.py:1009
  3.0 0.0 copy-start.3
  3.0 0.7 %copy-done.3 = f32[3456]{0:T(1024)S(1)} copy-done((f32[3456]{0:T(1024)S(1)}, f32[3456]{0:T(1024)}, u32[]{:S(2)}) %copy-start.3) | copy-done | bytes 13848
  3.7 2.9 %inner.1 = (bf16[6,64,1024]{2,1,0:T(8,128)(2,1)S(1)}, bf16[10,64,128]{2,1,0:T(8,128)(2,1)S(1)}, bf16[64,1024]{1,0:T(8,128)(2,1)S(1)}, bf16[32,32,128]{2,1,0:T(8,128)(2,1)}) custom-call(bf16[64,8,8,128]{3,2,1,0:T(8,128)(2,1)S(1)} %copy-done, bf16[64,8,8,128]{3,2,1,0:T(8,128)(2,1)S(1)} %copy-done.1, bf16[64,1024]{1,0:T(8,128)(2,1)S(1)} %get-tuple-element.28.refs_2_.refs_1_, ...), custom_call_target="tpu_custom_call" | custom-call | bytes 4194304 | tf_op jit(solution)/shard_map/inner/pallas_call | solution.py:482
  6.6 5.7 %collective-permute-start.1 = (bf16[64,1024]{1,0:T(8,128)(2,1)S(1)}, bf16[64,1024]{1,0:T(8,128)(2,1)S(1)}, u32[]{:S(2)}, u32[]{:S(2)}) collective-permute-start(bf16[64,1024]{1,0:T(8,128)(2,1)S(1)} %get-tuple-element.30), channel_id=1, source_target_pairs={{0,8},{8,0},{16,24},{24,16},{1,9},{9,1},{17,25},{25,17},{2,10},{10... | collective-permute-start | bytes 393224 | tf_op jit(solution)/shard_map/ppermute | solution.py:1009
  12.4 4.8 %all-to-all-start = ((bf16[32,32,128]{2,1,0:T(8,128)(2,1)}), bf16[32,32,128]{2,1,0:T(8,128)(2,1)S(1)}, u32[]{:S(2)}, u32[]{:S(2)}) async-start(bf16[32,32,128]{2,1,0:T(8,128)(2,1)} %get-tuple-element.42), calls=%async_computation | async-start | bytes 524288 | tf_op jit(solution)/shard_map/all_to_all | solution.py:838
  17.2 0.0 collective-permute-done.odd_ref
  17.2 0.0 collective-permute-done.1.even_ref
  17.2 0.2 side.1
  17.5 0.3 collective-permute-start.2
  17.8 1.0 %inputs.1 = (bf16[8,64,1024]{2,1,0:T(8,128)(2,1)S(1)}, bf16[64,128]{1,0:T(8,128)(2,1)S(1)}) custom-call(bf16[64,8,8,128]{3,2,1,0:T(8,128)(2,1)S(1)} %copy-done.2), custom_call_target="tpu_custom_call" | custom-call | bytes 2097152 | tf_op jit(solution)/shard_map/inputs/pallas_call | solution.py:178
  18.8 0.1 collective-permute-done.2.other_ref.refs_5_.refs_6_
  19.0 0.1 join.1
  19.1 0.7 %collective-permute-start.3 = (bf16[3,64,128]{2,1,0:T(8,128)(2,1)S(1)}, bf16[3,64,128]{2,1,0:T(8,128)(2,1)S(1)}, u32[]{:S(2)}, u32[]{:S(2)}) collective-permute-start(bf16[3,64,128]{2,1,0:T(8,128)(2,1)S(1)} %get-tuple-element.39.refs_3_), channel_id=1, source_target_pairs={{1,2},{2,1},{5,6},{6,5},{9,10},{10,9},{13,14},{14,13},{17,18},{18,... | collective-permute-start | bytes 147464 | tf_op jit(solution)/shard_map/ppermute | solution.py:1009
  19.7 4.5 %collective-permute-start.4 = (bf16[3,64,128]{2,1,0:T(8,128)(2,1)S(1)}, bf16[3,64,128]{2,1,0:T(8,128)(2,1)S(1)}, u32[]{:S(2)}, u32[]{:S(2)}) collective-permute-start(bf16[3,64,128]{2,1,0:T(8,128)(2,1)S(1)} %get-tuple-element.40.refs_2_), channel_id=1, source_target_pairs={{0,1},{1,0},{2,3},{3,2},{4,5},{5,4},{6,7},{7,6},{8,9},{9,8},{10,11... | collective-permute-start | bytes 147464 | tf_op jit(solution)/shard_map/ppermute | solution.py:1009
  24.3 3.6 %wgrad.1.refs_0_ = f32[576,192]{1,0:T(8,128)S(1)} custom-call(bf16[64,1024]{1,0:T(8,128)(2,1)S(1)} %get-tuple-element.32.refs_0_, bf16[64,1024]{1,0:T(8,128)(2,1)S(1)} %get-tuple-element.28.refs_2_.refs_1_, bf16[6,64,1024]{2,1,0:T(8,128)(2,1)S(1)} %get-tuple-element.33.refs_2_, bf16[64,1024]{1,0:T(8,128)(2,1)S(1)} %get-tuple-element.29.refs_3_, ...), custom_call_target="tpu_custom_call" | custom-call | flops 2264924160 | bytes 4194304 | tf_op jit(solution)/shard_map/wgrad/pallas_call | solution.py:607
  27.8 0.0 collective-permute-done.3.refs_4_.refs_7_
  27.9 0.0 collective-permute-done.4.refs_5_.refs_8_
  27.9 1.3 %finish.1 = bf16[32,32,128]{2,1,0:T(8,128)(2,1)} custom-call(f32[576,192]{1,0:T(8,128)S(1)} %wgrad.1.refs_0_, bf16[64,128]{1,0:T(8,128)(2,1)S(1)} %get-tuple-element.38.columns_ref.refs_1_, bf16[3,64,128]{2,1,0:T(8,128)(2,1)S(1)} %get-tuple-element.40.refs_2_, bf16[3,64,128]{2,1,0:T(8,128)(2,1)S(1)} %get-tuple-element.39.refs_3_, ...), custom_call_target="tpu_custom_call" | custom-call | flops 134217728 | bytes 2097152 | tf_op jit(solution)/shard_map/finish/pallas_call | solution.py:679
  29.2 0.0 all-to-all-done.w_ref
  29.2 3.8 %all-to-all-start.1 = ((bf16[32,32,128]{2,1,0:T(8,128)(2,1)}), bf16[32,32,128]{2,1,0:T(8,128)(2,1)S(1)}, u32[]{:S(2)}, u32[]{:S(2)}) async-start(bf16[32,32,128]{2,1,0:T(8,128)(2,1)} %finish.1), calls=%async_computation.1 | async-start | bytes 524288 | tf_op jit(solution)/shard_map/all_to_all | solution.py:852
  33.0 0.7 %spread.1.refs_9_ = bf16[3,128,768]{2,1,0:T(8,128)(2,1)S(1)} custom-call(bf16[32,32,128]{2,1,0:T(8,128)(2,1)S(1)} %all-to-all-done.w_ref), custom_call_target="tpu_custom_call" | custom-call | flops 1048576 | bytes 2097152 | tf_op jit(solution)/shard_map/spread/pallas_call | solution.py:787
  33.7 0.0 copy-start.4
  33.7 0.0 copy-start.5
  33.7 0.0 copy-start.6
  33.7 5.1 %dgrad.1 = bf16[64,8,8,128]{3,2,1,0:T(8,128)(2,1)} custom-call(bf16[64,1024]{1,0:T(8,128)(2,1)S(1)} %get-tuple-element.32.refs_0_, bf16[64,1024]{1,0:T(8,128)(2,1)S(1)} %get-tuple-element.28.refs_2_.refs_1_, bf16[6,64,1024]{2,1,0:T(8,128)(2,1)S(1)} %get-tuple-element.33.refs_2_, bf16[64,1024]{1,0:T(8,128)(2,1)S(1)} %get-tuple-element.29.refs_3_, ...), custom_call_target="tpu_custom_call" | custom-call | flops 2415919104 | bytes 4194304 | tf_op jit(solution)/shard_map/dgrad/pallas_call | solution.py:811
  38.8 4.6 %all-to-all-done.1.parts_ref = bf16[32,32,128]{2,1,0:T(8,128)(2,1)S(1)} async-done(((bf16[32,32,128]{2,1,0:T(8,128)(2,1)}), bf16[32,32,128]{2,1,0:T(8,128)(2,1)S(1)}, u32[]{:S(2)}, u32[]{:S(2)}) %all-to-all-start.1) | async-done | bytes 262176 | tf_op jit(solution)/shard_map/all_to_all | solution.py:852
  43.4 0.0 copy-done.4
  43.4 1.5 %adam.1 = (f32[27,128]{1,0:T(8,128)}, f32[27,128]{1,0:T(8,128)}, f32[27,128]{1,0:T(8,128)}, f32[27,128]{1,0:T(8,128)}) custom-call(bf16[32,32,128]{2,1,0:T(8,128)(2,1)S(1)} %all-to-all-done.1.parts_ref, f32[27,128]{1,0:T(8,128)S(1)} %bitcast.8, f32[27,128]{1,0:T(8,128)S(1)} %bitcast.9, f32[27,128]{1,0:T(8,128)S(1)} %bitcast.10), custom_call_target="tpu_custom_call" | custom-call | flops 4194304 | bytes 524288 | tf_op jit(solution)/shard_map/adam/pallas_call | solution.py:758
  (6 shorter events, 0.0 us)
Async XLA Ops:
  0.6 2.3 %copy-start.1 = (bf16[64,8,8,128]{3,2,1,0:T(8,128)(2,1)S(1)}, bf16[64,8,8,128]{3,2,1,0:T(8,128)(2,1)}, u32[]{:S(2)}) copy-start(bf16[64,8,8,128]{3,2,1,0:T(8,128)(2,1)} %refs_1_.1) | copy-start | bytes 3145732
  0.6 2.3 %copy-start = (bf16[64,8,8,128]{3,2,1,0:T(8,128)(2,1)S(1)}, bf16[64,8,8,128]{3,2,1,0:T(8,128)(2,1)}, u32[]{:S(2)}) copy-start(bf16[64,8,8,128]{3,2,1,0:T(8,128)(2,1)} %refs_0_.1) | copy-start | bytes 3145732
  2.3 14.9 %collective-permute-start = (bf16[64,1024]{1,0:T(8,128)(2,1)S(1)}, bf16[64,1024]{1,0:T(8,128)(2,1)S(1)}, u32[]{:S(2)}, u32[]{:S(2)}) collective-permute-start(bf16[64,1024]{1,0:T(8,128)(2,1)S(1)} %get-tuple-element.27), channel_id=1, source_target_pairs={{8,16},{16,8},{9,17},{17,9},{10,18},{18,10},{11,19},{19,11},{12,20... | collective-permute-start | bytes 393224 | tf_op jit(solution)/shard_map/ppermute | solution.py:1009
  3.0 0.7 %copy-start.3 = (f32[3456]{0:T(1024)S(1)}, f32[3456]{0:T(1024)}, u32[]{:S(2)}) copy-start(f32[3456]{0:T(1024)} %param.9) | copy-start | bytes 41476
  3.7 14.1 %copy-start.2 = (bf16[64,8,8,128]{3,2,1,0:T(8,128)(2,1)S(1)}, bf16[64,8,8,128]{3,2,1,0:T(8,128)(2,1)}, u32[]{:S(2)}) copy-start(bf16[64,8,8,128]{3,2,1,0:T(8,128)(2,1)} %a_ref) | copy-start | bytes 3145732
  6.6 10.6 %collective-permute-start.1 = (bf16[64,1024]{1,0:T(8,128)(2,1)S(1)}, bf16[64,1024]{1,0:T(8,128)(2,1)S(1)}, u32[]{:S(2)}, u32[]{:S(2)}) collective-permute-start(bf16[64,1024]{1,0:T(8,128)(2,1)S(1)} %get-tuple-element.30), channel_id=1, source_target_pairs={{0,8},{8,0},{16,24},{24,16},{1,9},{9,1},{17,25},{25,17},{2,10},{10... | collective-permute-start | bytes 393224 | tf_op jit(solution)/shard_map/ppermute | solution.py:1009
  12.4 16.8 %all-to-all-start = ((bf16[32,32,128]{2,1,0:T(8,128)(2,1)}), bf16[32,32,128]{2,1,0:T(8,128)(2,1)S(1)}, u32[]{:S(2)}, u32[]{:S(2)}) async-start(bf16[32,32,128]{2,1,0:T(8,128)(2,1)} %get-tuple-element.42), calls=%async_computation | async-start | bytes 524288 | tf_op jit(solution)/shard_map/all_to_all | solution.py:838
  17.5 1.5 %collective-permute-start.2 = (bf16[12,64,128]{2,1,0:T(8,128)(2,1)S(1)}, bf16[12,64,128]{2,1,0:T(8,128)(2,1)S(1)}, u32[]{:S(2)}, u32[]{:S(2)}) collective-permute-start(bf16[12,64,128]{2,1,0:T(8,128)(2,1)S(1)} %get-tuple-element.36.own_ref), channel_id=1, source_target_pairs={{0,4},{4,0},{1,5},{5,1},{2,6},{6,2},{3,7},{7,3},{8,12},{12,8},{9,1... | collective-permute-start | bytes 589832 | tf_op jit(solution)/shard_map/ppermute | solution.py:1002
  19.1 8.8 %collective-permute-start.3 = (bf16[3,64,128]{2,1,0:T(8,128)(2,1)S(1)}, bf16[3,64,128]{2,1,0:T(8,128)(2,1)S(1)}, u32[]{:S(2)}, u32[]{:S(2)}) collective-permute-start(bf16[3,64,128]{2,1,0:T(8,128)(2,1)S(1)} %get-tuple-element.39.refs_3_), channel_id=1, source_target_pairs={{1,2},{2,1},{5,6},{6,5},{9,10},{10,9},{13,14},{14,13},{17,18},{18,... | collective-permute-start | bytes 147464 | tf_op jit(solution)/shard_map/ppermute | solution.py:1009
  19.7 8.1 %collective-permute-start.4 = (bf16[3,64,128]{2,1,0:T(8,128)(2,1)S(1)}, bf16[3,64,128]{2,1,0:T(8,128)(2,1)S(1)}, u32[]{:S(2)}, u32[]{:S(2)}) collective-permute-start(bf16[3,64,128]{2,1,0:T(8,128)(2,1)S(1)} %get-tuple-element.40.refs_2_), channel_id=1, source_target_pairs={{0,1},{1,0},{2,3},{3,2},{4,5},{5,4},{6,7},{7,6},{8,9},{9,8},{10,11... | collective-permute-start | bytes 147464 | tf_op jit(solution)/shard_map/ppermute | solution.py:1009
  29.2 14.2 %all-to-all-start.1 = ((bf16[32,32,128]{2,1,0:T(8,128)(2,1)}), bf16[32,32,128]{2,1,0:T(8,128)(2,1)S(1)}, u32[]{:S(2)}, u32[]{:S(2)}) async-start(bf16[32,32,128]{2,1,0:T(8,128)(2,1)} %finish.1), calls=%async_computation.1 | async-start | bytes 524288 | tf_op jit(solution)/shard_map/all_to_all | solution.py:852
  33.7 9.7 %copy-start.4 = (f32[3456]{0:T(1024)S(1)}, f32[3456]{0:T(1024)}, u32[]{:S(2)}) copy-start(f32[3456]{0:T(1024)} %param.9) | copy-start | bytes 41476
  33.7 9.7 %copy-start.5 = (f32[3456]{0:T(1024)S(1)}, f32[3456]{0:T(1024)}, u32[]{:S(2)}) copy-start(f32[3456]{0:T(1024)} %param.10) | copy-start | bytes 41476
  33.7 9.7 %copy-start.6 = (f32[3456]{0:T(1024)S(1)}, f32[3456]{0:T(1024)}, u32[]{:S(2)}) copy-start(f32[3456]{0:T(1024)} %param.11) | copy-start | bytes 41476

commit v9 on v7

--- a/solution.py
+++ b/solution.py
@@ -436,19 +436,17 @@
 
 def pair_inner_kernel(rows, *refs):
     first_ref, last_ref, m_ref, g_ref, side_ref, swap_ref, sent_ref = refs[2:9]
-    tile_ref, tile_sems = refs[13:]
+    sent_buf, sent_sem = refs[13:]
     choose(is_odd("gx"), swap_ref, first_ref, last_ref)
     share = m_ref[...]
-    height = tile_ref.shape[0] - share.shape[0]
+    height = sent_ref.shape[1] - share.shape[0]
     if height:
         share = jnp.concatenate([share, jnp.zeros((height, share.shape[1]), F32)], axis=0)
-    tile_ref[...] = share.astype(BF16)
-    copies = [
-        pltpu.make_async_copy(tile_ref, sent_ref.at[device], tile_sems.at[device])
-        for device in range(sent_ref.shape[0])
-    ]
-    for copy in copies:
-        copy.start()
+    share = share.astype(BF16)
+    for device in range(sent_ref.shape[0]):
+        sent_buf[device] = share
+    send = pltpu.make_async_copy(sent_buf, sent_ref, sent_sem)
+    send.start()
     read_inner(rows, *refs[:2], g_ref, *refs[9:13])
     size_z = side_ref.shape[-1]
     inner, _, plane = g_ref.shape
@@ -461,8 +459,7 @@
     )
     side_ref[size_x] = low.astype(BF16)
     side_ref[size_x + 1] = high.astype(BF16)
-    for copy in copies:
-        copy.wait()
+    send.wait()
 
 
 def pair_inner(preact, upstream, first, last, share, sent_shape, rows):
@@ -479,7 +476,7 @@
             jax.ShapeDtypeStruct(sent_shape, BF16),
         ],
         scratch_shapes=inner_scratch(*shape)
-        + [pltpu.VMEM(sent_shape[1:], BF16), pltpu.SemaphoreType.DMA((sent_shape[0],))],
+        + [pltpu.VMEM(sent_shape, BF16), pltpu.SemaphoreType.DMA(())],
         compiler_params=params(INNER_VMEM),
         cost_estimate=cost(0, 4 * 2**20),
         name="inner",
@@ -604,7 +601,7 @@
 
 def finish_kernel(scale, rows, sizes, *refs):
     acc_ref, columns_ref, even_ref, odd_ref, from_odd_ref, from_even_ref = refs[:6]
-    part_ref, chunks = refs[6:]
+    part_ref, chunks, part_buf, sems = refs[6:]
     size_x, size_y = sizes
     channels = columns_ref.shape[0]
     area = size_x * size_y
@@ -657,7 +654,17 @@
                 chunks[pl.ds(at * pieces + k, count, stride=height), :] = line[
                     :, k * width : (k + 1) * width
                 ]
-    part_ref[...] = chunks[...].reshape(part_ref.shape).astype(BF16)
+    pieces = sems.shape[0]
+    step = count // pieces
+    copies = []
+    for k in range(pieces):
+        piece = chunks[k * step * height : (k + 1) * step * height, :]
+        at = pl.ds(k * step, step)
+        part_buf[at] = piece.reshape(step, height, width).astype(BF16)
+        copies.append(pltpu.make_async_copy(part_buf.at[at], part_ref.at[at], sems.at[k]))
+        copies[-1].start()
+    for copy in copies:
+        copy.wait()
 
 
 def finish(acc, columns, sent, received, scale, rows, sizes, part_shape):
@@ -665,9 +672,13 @@
     return pl.pallas_call(
         functools.partial(finish_kernel, scale, rows, sizes),
         in_specs=[VMEM] * 6,
-        out_specs=VMEM,
+        out_specs=HBM,
         out_shape=jax.ShapeDtypeStruct(part_shape, BF16),
-        scratch_shapes=[pltpu.VMEM((part_shape[0] * part_shape[1], part_shape[2]), F32)],
+        scratch_shapes=[
+            pltpu.VMEM((part_shape[0] * part_shape[1], part_shape[2]), F32),
+            pltpu.VMEM(part_shape, BF16),
+            pltpu.SemaphoreType.DMA((4,)),
+        ],
         compiler_params=params(),
         cost_estimate=cost(2**27, 2**21),
         name="finish",
@@ -703,9 +714,16 @@
     line = places[...].T
     number = lax.broadcasted_iota(jnp.int32, (LANES, LANES), 0) * taps
     column = lax.broadcasted_iota(jnp.int32, (LANES, LANES), 1)
-    for bit in range(7):
-        turn = 1 << bit
-        line = jnp.where((number & turn) != 0, pltpu.roll(line, turn, 1), line)
+    turned = []
+    for group in range(LANES // 8):
+        piece = line[8 * group : 8 * (group + 1)]
+        rest = 8 * group * taps % LANES
+        for step in range(3):
+            turn = rest // (3 - step)
+            rest -= turn
+            piece = pltpu.roll(piece, turn, 1, stride=taps // 3, stride_axis=0)
+        turned.append(piece)
+    line = jnp.concatenate(turned, axis=0)
     start = number & (LANES - 1)
     line = jnp.concatenate(
         [jnp.where(column >= start, line, 0.0), jnp.where(column < start, line, 0.0)], axis=0
@@ -714,9 +732,15 @@
     source = lax.broadcasted_iota(jnp.int32, (32, 2 * LANES), 1)
     goes = lax.shift_right_logical((source & (LANES - 1)) * taps, 7)
     goes = goes + jnp.where(source < LANES, 0, 1)
-    pick = jnp.where(goes == target, 1.0, 0.0)
+    pick = jnp.where(goes == target, 1.0, 0.0).astype(BF16)
+    parts = []
+    for _ in range(3):
+        parts.append(line.astype(BF16))
+        line = line - parts[-1].astype(F32)
     return jnp.dot(
-        pick, line, preferred_element_type=F32, precision=lax.Precision.HIGHEST
+        jnp.concatenate([pick] * 3, axis=1),
+        jnp.concatenate(parts, axis=0),
+        preferred_element_type=F32,
     )[:taps]
 
 

time: 43.9 us -> 43.3 us (0.986)
  Pallas kernels: 17.8 us -> 17.2 us
where the time goes in v9:
time: 43.3 us; the launch traced here: 42.9 us
  starting transfers between devices  20.4 us (47%)
  Pallas kernels  17.2 us (40%)
  waiting for transfers between devices  4.55 us (11%)
  between operations  0.8 us (2%)
    ppermute x4, starting transfers between devices, swapped(): return lax.ppermute(value, axis, pairs)  11.6 us
    pallas_call x1, Pallas kernels, pair_dgrad(): pl.pallas_call(pair_dgrad_kernel, in_specs=[VMEM] * 10, out_specs=VMEM, o...  5.09 us
    all_to_all x1, starting transfers between devices, pair_program(): kernel = lax.all_to_all(sent, AXES, 0, 0, tiled=True)  4.84 us
    all_to_all x1, waiting for transfers between devices, pair_program(): parts = lax.all_to_all(part, AXES, 0, 0, tiled=True)  4.4 us
    all_to_all x1, starting transfers between devices, pair_program(): parts = lax.all_to_all(part, AXES, 0, 0, tiled=True)  3.61 us
    pallas_call x1, Pallas kernels, pair_wgrad(): pl.pallas_call(pair_wgrad_kernel, in_specs=[VMEM] * 8, out_specs=VMEM, ou...  3.56 us
    pallas_call x1, Pallas kernels, pair_inner(): pl.pallas_call(functools.partial(pair_inner_kernel, rows), in_specs=[HBM]...  2.61 us
    pallas_call x1, Pallas kernels, faces(): pl.pallas_call(functools.partial(face_kernel, axis, rows), in_specs=[HBM,...  1.33 us
  transfers between devices with their start and end apart: 7, of which 2 were waited for; matrix products, arithmetic and copies ran while one was open for 0% of the time, Pallas kernels for 34%

profile of v9, /device:TPU:0, one launch (start us, length us, event | category | flops | bytes accessed | tf_op | source)
XLA Modules:
  0.0 42.9 jit_solution(12409951184745107366)
XLA Ops:
  0.6 0.0 copy-start.1
  0.6 1.3 %faces.1 = (bf16[64,1024]{1,0:T(8,128)(2,1)S(1)}, bf16[64,1024]{1,0:T(8,128)(2,1)S(1)}, bf16[64,1024]{1,0:T(8,128)(2,1)S(1)}) custom-call(bf16[64,8,8,128]{3,2,1,0:T(8,128)(2,1)} %refs_0_.1, bf16[64,8,8,128]{3,2,1,0:T(8,128)(2,1)} %refs_1_.1), custom_call_target="tpu_custom_call" | custom-call | bytes 1048576 | tf_op jit(solution)/shard_map/faces/pallas_call | solution.py:83
  2.0 0.7 %collective-permute-start = (bf16[64,1024]{1,0:T(8,128)(2,1)S(1)}, bf16[64,1024]{1,0:T(8,128)(2,1)S(1)}, u32[]{:S(2)}, u32[]{:S(2)}) collective-permute-start(bf16[64,1024]{1,0:T(8,128)(2,1)S(1)} %get-tuple-element.27), channel_id=1, source_target_pairs={{8,16},{16,8},{9,17},{17,9},{10,18},{18,10},{11,19},{19,11},{12,20... | collective-permute-start | bytes 393224 | tf_op jit(solution)/shard_map/ppermute | solution.py:1011
  2.7 0.0 copy-done.1
  2.7 0.0 copy-start
  2.7 2.6 %inner.1 = (bf16[6,64,1024]{2,1,0:T(8,128)(2,1)S(1)}, bf16[10,64,128]{2,1,0:T(8,128)(2,1)S(1)}, bf16[64,1024]{1,0:T(8,128)(2,1)S(1)}, bf16[32,32,128]{2,1,0:T(8,128)(2,1)}) custom-call(bf16[64,8,8,128]{3,2,1,0:T(8,128)(2,1)} %refs_0_.1, bf16[64,8,8,128]{3,2,1,0:T(8,128)(2,1)} %refs_1_.1, bf16[64,1024]{1,0:T(8,128)(2,1)S(1)} %get-tuple-element.28.refs_2_.refs_1_, ...), custom_call_target="tpu_custom_call" | custom-call | bytes 4194304 | tf_op jit(solution)/shard_map/inner/pallas_call | solution.py:468
  5.3 5.7 %collective-permute-start.1 = (bf16[64,1024]{1,0:T(8,128)(2,1)S(1)}, bf16[64,1024]{1,0:T(8,128)(2,1)S(1)}, u32[]{:S(2)}, u32[]{:S(2)}) collective-permute-start(bf16[64,1024]{1,0:T(8,128)(2,1)S(1)} %get-tuple-element.30), channel_id=1, source_target_pairs={{0,8},{8,0},{16,24},{24,16},{1,9},{9,1},{17,25},{25,17},{2,10},{10... | collective-permute-start | bytes 393224 | tf_op jit(solution)/shard_map/ppermute | solution.py:1011
  11.0 4.8 %all-to-all-start = ((bf16[32,32,128]{2,1,0:T(8,128)(2,1)}), bf16[32,32,128]{2,1,0:T(8,128)(2,1)S(1)}, u32[]{:S(2)}, u32[]{:S(2)}) async-start(bf16[32,32,128]{2,1,0:T(8,128)(2,1)} %get-tuple-element.42), calls=%async_computation | async-start | bytes 524288 | tf_op jit(solution)/shard_map/all_to_all | solution.py:840
  15.9 0.0 collective-permute-done.odd_ref
  15.9 0.0 collective-permute-done.1.even_ref
  15.9 0.2 side.1
  16.1 0.3 collective-permute-start.2
  16.5 0.0 copy-done
  16.5 1.0 %inputs.1 = (bf16[8,64,1024]{2,1,0:T(8,128)(2,1)S(1)}, bf16[64,128]{1,0:T(8,128)(2,1)S(1)}) custom-call(bf16[64,8,8,128]{3,2,1,0:T(8,128)(2,1)S(1)} %copy-done), custom_call_target="tpu_custom_call" | custom-call | bytes 2097152 | tf_op jit(solution)/shard_map/inputs/pallas_call | solution.py:172
  17.5 0.1 collective-permute-done.2.other_ref.refs_5_.refs_6_
  17.6 0.1 join.1
  17.7 0.7 %collective-permute-start.3 = (bf16[3,64,128]{2,1,0:T(8,128)(2,1)S(1)}, bf16[3,64,128]{2,1,0:T(8,128)(2,1)S(1)}, u32[]{:S(2)}, u32[]{:S(2)}) collective-permute-start(bf16[3,64,128]{2,1,0:T(8,128)(2,1)S(1)} %get-tuple-element.39.refs_3_), channel_id=1, source_target_pairs={{1,2},{2,1},{5,6},{6,5},{9,10},{10,9},{13,14},{14,13},{17,18},{18,... | collective-permute-start | bytes 147464 | tf_op jit(solution)/shard_map/ppermute | solution.py:1011
  18.4 4.5 %collective-permute-start.4 = (bf16[3,64,128]{2,1,0:T(8,128)(2,1)S(1)}, bf16[3,64,128]{2,1,0:T(8,128)(2,1)S(1)}, u32[]{:S(2)}, u32[]{:S(2)}) collective-permute-start(bf16[3,64,128]{2,1,0:T(8,128)(2,1)S(1)} %get-tuple-element.40.refs_2_), channel_id=1, source_target_pairs={{0,1},{1,0},{2,3},{3,2},{4,5},{5,4},{6,7},{7,6},{8,9},{9,8},{10,11... | collective-permute-start | bytes 147464 | tf_op jit(solution)/shard_map/ppermute | solution.py:1011
  22.9 3.6 %wgrad.1.refs_0_ = f32[576,192]{1,0:T(8,128)S(1)} custom-call(bf16[64,1024]{1,0:T(8,128)(2,1)S(1)} %get-tuple-element.32.refs_0_, bf16[64,1024]{1,0:T(8,128)(2,1)S(1)} %get-tuple-element.28.refs_2_.refs_1_, bf16[6,64,1024]{2,1,0:T(8,128)(2,1)S(1)} %get-tuple-element.33.refs_2_, bf16[64,1024]{1,0:T(8,128)(2,1)S(1)} %get-tuple-element.29.refs_3_, ...), custom_call_target="tpu_custom_call" | custom-call | flops 2264924160 | bytes 4194304 | tf_op jit(solution)/shard_map/wgrad/pallas_call | solution.py:590
  26.5 0.0 collective-permute-done.3.refs_4_.refs_7_
  26.5 0.0 collective-permute-done.4.refs_5_.refs_8_
  26.5 1.3 %finish.1 = bf16[32,32,128]{2,1,0:T(8,128)(2,1)} custom-call(f32[576,192]{1,0:T(8,128)S(1)} %wgrad.1.refs_0_, bf16[64,128]{1,0:T(8,128)(2,1)S(1)} %get-tuple-element.38.columns_ref.refs_1_, bf16[3,64,128]{2,1,0:T(8,128)(2,1)S(1)} %get-tuple-element.40.refs_2_, bf16[3,64,128]{2,1,0:T(8,128)(2,1)S(1)} %get-tuple-element.39.refs_3_, ...), custom_call_target="tpu_custom_call" | custom-call | flops 134217728 | bytes 2097152 | tf_op jit(solution)/shard_map/finish/pallas_call | solution.py:672
  27.9 0.0 all-to-all-done.w_ref
  27.9 3.6 %all-to-all-start.1 = ((bf16[32,32,128]{2,1,0:T(8,128)(2,1)}), bf16[32,32,128]{2,1,0:T(8,128)(2,1)S(1)}, u32[]{:S(2)}, u32[]{:S(2)}) async-start(bf16[32,32,128]{2,1,0:T(8,128)(2,1)} %finish.1), calls=%async_computation.1 | async-start | bytes 524288 | tf_op jit(solution)/shard_map/all_to_all | solution.py:854
  31.5 0.7 %spread.1.refs_9_ = bf16[3,128,768]{2,1,0:T(8,128)(2,1)S(1)} custom-call(bf16[32,32,128]{2,1,0:T(8,128)(2,1)S(1)} %all-to-all-done.w_ref), custom_call_target="tpu_custom_call" | custom-call | flops 1048576 | bytes 2097152 | tf_op jit(solution)/shard_map/spread/pallas_call | solution.py:791
  32.2 0.0 copy-start.2
  32.2 0.0 copy-start.3
  32.2 5.1 %dgrad.1 = bf16[64,8,8,128]{3,2,1,0:T(8,128)(2,1)} custom-call(bf16[64,1024]{1,0:T(8,128)(2,1)S(1)} %get-tuple-element.32.refs_0_, bf16[64,1024]{1,0:T(8,128)(2,1)S(1)} %get-tuple-element.28.refs_2_.refs_1_, bf16[6,64,1024]{2,1,0:T(8,128)(2,1)S(1)} %get-tuple-element.33.refs_2_, bf16[64,1024]{1,0:T(8,128)(2,1)S(1)} %get-tuple-element.29.refs_3_, ...), custom_call_target="tpu_custom_call" | custom-call | flops 2415919104 | bytes 4194304 | tf_op jit(solution)/shard_map/dgrad/pallas_call | solution.py:815
  37.3 4.4 %all-to-all-done.1.parts_ref = bf16[32,32,128]{2,1,0:T(8,128)(2,1)S(1)} async-done(((bf16[32,32,128]{2,1,0:T(8,128)(2,1)}), bf16[32,32,128]{2,1,0:T(8,128)(2,1)S(1)}, u32[]{:S(2)}, u32[]{:S(2)}) %all-to-all-start.1) | async-done | bytes 262176 | tf_op jit(solution)/shard_map/all_to_all | solution.py:854
  41.7 0.0 copy-done.2
  41.7 0.0 copy-done.3
  41.7 1.2 %adam.1 = (f32[27,128]{1,0:T(8,128)}, f32[27,128]{1,0:T(8,128)}, f32[27,128]{1,0:T(8,128)}, f32[27,128]{1,0:T(8,128)}) custom-call(bf16[32,32,128]{2,1,0:T(8,128)(2,1)S(1)} %all-to-all-done.1.parts_ref, f32[27,128]{1,0:T(8,128)S(1)} %bitcast.8, f32[27,128]{1,0:T(8,128)S(1)} %bitcast.9, f32[27,128]{1,0:T(8,128)S(1)} %bitcast.10), custom_call_target="tpu_custom_call" | custom-call | flops 4194304 | bytes 524288 | tf_op jit(solution)/shard_map/adam/pallas_call | solution.py:762
Async XLA Ops:
  0.6 2.0 %copy-start.1 = (f32[3456]{0:T(1024)S(1)}, f32[3456]{0:T(1024)}, u32[]{:S(2)}) copy-start(f32[3456]{0:T(1024)} %param.9) | copy-start | bytes 41476
  2.0 13.9 %collective-permute-start = (bf16[64,1024]{1,0:T(8,128)(2,1)S(1)}, bf16[64,1024]{1,0:T(8,128)(2,1)S(1)}, u32[]{:S(2)}, u32[]{:S(2)}) collective-permute-start(bf16[64,1024]{1,0:T(8,128)(2,1)S(1)} %get-tuple-element.27), channel_id=1, source_target_pairs={{8,16},{16,8},{9,17},{17,9},{10,18},{18,10},{11,19},{19,11},{12,20... | collective-permute-start | bytes 393224 | tf_op jit(solution)/shard_map/ppermute | solution.py:1011
  2.7 13.8 %copy-start = (bf16[64,8,8,128]{3,2,1,0:T(8,128)(2,1)S(1)}, bf16[64,8,8,128]{3,2,1,0:T(8,128)(2,1)}, u32[]{:S(2)}) copy-start(bf16[64,8,8,128]{3,2,1,0:T(8,128)(2,1)} %a_ref) | copy-start | bytes 3145732
  5.3 10.6 %collective-permute-start.1 = (bf16[64,1024]{1,0:T(8,128)(2,1)S(1)}, bf16[64,1024]{1,0:T(8,128)(2,1)S(1)}, u32[]{:S(2)}, u32[]{:S(2)}) collective-permute-start(bf16[64,1024]{1,0:T(8,128)(2,1)S(1)} %get-tuple-element.30), channel_id=1, source_target_pairs={{0,8},{8,0},{16,24},{24,16},{1,9},{9,1},{17,25},{25,17},{2,10},{10... | collective-permute-start | bytes 393224 | tf_op jit(solution)/shard_map/ppermute | solution.py:1011
  11.0 16.9 %all-to-all-start = ((bf16[32,32,128]{2,1,0:T(8,128)(2,1)}), bf16[32,32,128]{2,1,0:T(8,128)(2,1)S(1)}, u32[]{:S(2)}, u32[]{:S(2)}) async-start(bf16[32,32,128]{2,1,0:T(8,128)(2,1)} %get-tuple-element.42), calls=%async_computation | async-start | bytes 524288 | tf_op jit(solution)/shard_map/all_to_all | solution.py:840
  16.1 1.5 %collective-permute-start.2 = (bf16[12,64,128]{2,1,0:T(8,128)(2,1)S(1)}, bf16[12,64,128]{2,1,0:T(8,128)(2,1)S(1)}, u32[]{:S(2)}, u32[]{:S(2)}) collective-permute-start(bf16[12,64,128]{2,1,0:T(8,128)(2,1)S(1)} %get-tuple-element.36.own_ref), channel_id=1, source_target_pairs={{0,4},{4,0},{1,5},{5,1},{2,6},{6,2},{3,7},{7,3},{8,12},{12,8},{9,1... | collective-permute-start | bytes 589832 | tf_op jit(solution)/shard_map/ppermute | solution.py:1004
  17.7 8.8 %collective-permute-start.3 = (bf16[3,64,128]{2,1,0:T(8,128)(2,1)S(1)}, bf16[3,64,128]{2,1,0:T(8,128)(2,1)S(1)}, u32[]{:S(2)}, u32[]{:S(2)}) collective-permute-start(bf16[3,64,128]{2,1,0:T(8,128)(2,1)S(1)} %get-tuple-element.39.refs_3_), channel_id=1, source_target_pairs={{1,2},{2,1},{5,6},{6,5},{9,10},{10,9},{13,14},{14,13},{17,18},{18,... | collective-permute-start | bytes 147464 | tf_op jit(solution)/shard_map/ppermute | solution.py:1011
  18.4 8.1 %collective-permute-start.4 = (bf16[3,64,128]{2,1,0:T(8,128)(2,1)S(1)}, bf16[3,64,128]{2,1,0:T(8,128)(2,1)S(1)}, u32[]{:S(2)}, u32[]{:S(2)}) collective-permute-start(bf16[3,64,128]{2,1,0:T(8,128)(2,1)S(1)} %get-tuple-element.40.refs_2_), channel_id=1, source_target_pairs={{0,1},{1,0},{2,3},{3,2},{4,5},{5,4},{6,7},{7,6},{8,9},{9,8},{10,11... | collective-permute-start | bytes 147464 | tf_op jit(solution)/shard_map/ppermute | solution.py:1011
  27.9 13.8 %all-to-all-start.1 = ((bf16[32,32,128]{2,1,0:T(8,128)(2,1)}), bf16[32,32,128]{2,1,0:T(8,128)(2,1)S(1)}, u32[]{:S(2)}, u32[]{:S(2)}) async-start(bf16[32,32,128]{2,1,0:T(8,128)(2,1)} %finish.1), calls=%async_computation.1 | async-start | bytes 524288 | tf_op jit(solution)/shard_map/all_to_all | solution.py:854
  32.2 9.5 %copy-start.2 = (f32[3456]{0:T(1024)S(1)}, f32[3456]{0:T(1024)}, u32[]{:S(2)}) copy-start(f32[3456]{0:T(1024)} %param.10) | copy-start | bytes 41476
  32.2 9.5 %copy-start.3 = (f32[3456]{0:T(1024)S(1)}, f32[3456]{0:T(1024)}, u32[]{:S(2)}) copy-start(f32[3456]{0:T(1024)} %param.11) | copy-start | bytes 41476

commit v10 on v9

--- a/solution.py
+++ b/solution.py
@@ -241,11 +241,11 @@
     return put_columns(columns, lambda number: number, rows_y, size_z)
 
 
-def pair_z_halo(odd_ref, even_ref, planes, size_y, size_z):
-    me, odd = lax.axis_index("gy"), is_odd("gz")
+def pair_z_halo(low_ref, high_ref, planes, size_y, size_z):
+    me = lax.axis_index("gy")
     sides = []
-    for low, high in ((even_ref, odd_ref), (odd_ref, even_ref)):
-        first, second = (either(odd, low[k], high[k]) for k in range(2))
+    for ref in (low_ref, high_ref):
+        first, second = ref[0].astype(F32), ref[1].astype(F32)
         lane = lax.broadcasted_iota(jnp.int32, first.shape, 1)
         own = jnp.where(me == 0, first, second)
         before = jnp.where(me == 0, 0.0, first)
@@ -306,22 +306,26 @@
     group = 3 * channels
     zero = jnp.zeros((channels, 2 * size_z), BF16)
     done = 0
-    for x in range(size_x):
-        while done < x + 3:
+    for x in range(0, size_x, 2):
+        while done < x + 4:
             shifted_plane(done, refs, halo, g3)
             done += 1
-        value = x_ref[x]
-        for b in range(3):
-            at = slice(b * channels, (b + 1) * channels)
-            start = (2 - b) * size_z
-            x3[x, at, start : start + plane] = value
-            if start:
-                x3[x, at, :start] = zero[:, :start]
-            if start < 2 * size_z:
-                x3[x, at, start + plane :] = zero[:, start:]
+        for plane_x in (x, x + 1):
+            value = x_ref[plane_x]
+            for b in range(3):
+                at = slice(b * channels, (b + 1) * channels)
+                start = (2 - b) * size_z
+                x3[plane_x, at, start : start + plane] = value
+                if start:
+                    x3[plane_x, at, :start] = zero[:, :start]
+                if start < 2 * size_z:
+                    x3[plane_x, at, start + plane :] = zero[:, start:]
         product = lax.dot_general(
-            g3[x * group : (x + 3) * group, :],
-            x3[x],
+            jnp.concatenate(
+                [g3[x * group : (x + 3) * group, :], g3[(x + 1) * group : (x + 4) * group, :]],
+                axis=1,
+            ),
+            jnp.concatenate([x3[x], x3[x + 1]], axis=1),
             (((1,), (1,)), ((), ())),
             preferred_element_type=F32,
         )
@@ -428,6 +432,18 @@
     return cost(72 * channels * channels * size_x * size_y * size_z, 4 * 2**20)
 
 
+def turned_columns(planes, low, high, size_y, size_z):
+    lane = lax.broadcasted_iota(jnp.int32, low.shape, 1)
+    for number, plane in planes:
+        for y in range(size_y):
+            at = number * size_y + y
+            head = plane[:, y * size_z : y * size_z + LANES]
+            tail = plane[:, (y + 1) * size_z - LANES : (y + 1) * size_z]
+            low = jnp.where(lane == at, pltpu.roll(head, at, 1), low)
+            high = jnp.where(lane == at, pltpu.roll(tail, at + 1, 1), high)
+    return low, high
+
+
 def row_for_other(body, size_z):
     plane = body.shape[-1]
     low, high = body[:, :size_z].astype(F32), body[:, plane - size_z :].astype(F32)
@@ -454,11 +470,12 @@
     bodies = [first_ref] + [g_ref.at[x] for x in range(inner)] + [last_ref]
     for x, body in enumerate(bodies):
         side_ref[x] = row_for_other(body, size_z)
-    low, high = z_tiles(
-        [body[...] for body in bodies], plane // size_z, size_z, range(1, size_x + 1)
+    low = jnp.zeros((first_ref.shape[0], LANES), BF16)
+    low, high = turned_columns(
+        [(x + 1, body) for x, body in enumerate(bodies)], low, low, plane // size_z, size_z
     )
-    side_ref[size_x] = low.astype(BF16)
-    side_ref[size_x + 1] = high.astype(BF16)
+    side_ref[size_x] = low
+    side_ref[size_x + 1] = high
     send.wait()
 
 
@@ -504,15 +521,9 @@
     for x in range(size_x):
         sent_ref[x + 1] = own_ref[x]
     sent_ref[size_x + 1] = row_for_other(high, size_z)
-    lane = lax.broadcasted_iota(jnp.int32, (low.shape[0], LANES), 1)
-    first, second = own_ref[size_x], own_ref[size_x + 1]
-    for number, plane in ((0, low), (size_x + 1, high)):
-        for y in range(size_y):
-            at = number * size_y + y
-            head = plane[:, y * size_z : y * size_z + LANES]
-            tail = plane[:, (y + 1) * size_z - LANES : (y + 1) * size_z]
-            first = jnp.where(lane == at, pltpu.roll(head, at, 1), first)
-            second = jnp.where(lane == at, pltpu.roll(tail, at + 1, 1), second)
+    first, second = turned_columns(
+        ((0, low), (size_x + 1, high)), own_ref[size_x], own_ref[size_x + 1], size_y, size_z
+    )
     sent_ref[size_x + 2] = first
     sent_ref[size_x + 3] = second
 
@@ -545,27 +556,13 @@
     return jnp.where(me == 0, first, second)
 
 
-def join_kernel(area, own_ref, other_ref, columns_ref, even_ref, odd_ref):
+def join_kernel(area, own_ref, other_ref, columns_ref, down_ref, up_ref):
     at = own_ref.shape[0] - 2
     me = lax.axis_index("gy")
-    last = own_columns(columns_ref[...], 1, area).astype(BF16)
-
-    def fill(up_ref, down_ref):
-        for k, out_ref in enumerate((down_ref, up_ref)):
-            out_ref[me] = own_ref[at + k]
-            out_ref[1 - me] = other_ref[at + k]
-        up_ref[2] = last
-        down_ref[2] = last
-
-    odd = is_odd("gz")
-
-    @pl.when(odd)
-    def _():
-        fill(odd_ref, even_ref)
-
-    @pl.when(jnp.logical_not(odd))
-    def _():
-        fill(even_ref, odd_ref)
+    for k, out_ref in enumerate((down_ref, up_ref)):
+        out_ref[me] = own_ref[at + k]
+        out_ref[1 - me] = other_ref[at + k]
+    up_ref[2] = own_columns(columns_ref[...], 1, area).astype(BF16)
 
 
 def join(own, other, columns, area):
@@ -573,7 +570,7 @@
         functools.partial(join_kernel, area),
         in_specs=[VMEM] * 3,
         out_specs=[VMEM] * 2,
-        out_shape=[jax.ShapeDtypeStruct((3, *own.shape[1:]), BF16)] * 2,
+        out_shape=[jax.ShapeDtypeStruct((n, *own.shape[1:]), BF16) for n in (2, 3)],
         compiler_params=params(),
         cost_estimate=cost(0, 2**17),
         name="join",
@@ -600,17 +597,16 @@
 
 
 def finish_kernel(scale, rows, sizes, *refs):
-    acc_ref, columns_ref, even_ref, odd_ref, from_odd_ref, from_even_ref = refs[:6]
-    part_ref, chunks, part_buf, sems = refs[6:]
+    acc_ref, columns_ref, down_ref, from_below_ref = refs[:4]
+    part_ref, chunks, part_buf, sems = refs[4:]
     size_x, size_y = sizes
     channels = columns_ref.shape[0]
     area = size_x * size_y
-    odd = is_odd("gz")
     lane = lax.broadcasted_iota(jnp.int32, (channels, LANES), 1)
     row = lane % size_y
     jump = area - size_y + 1
-    below = [either(odd, from_even_ref[k], from_odd_ref[k]) for k in range(3)]
-    own = [either(odd, even_ref[k], odd_ref[k]) for k in range(2)]
+    below = [from_below_ref[k].astype(F32) for k in range(3)]
+    own = [down_ref[k].astype(F32) for k in range(2)]
     pairs = ((below[:2], own_columns(columns_ref[...], 0, area)), (own, below[2]))
     edges = []
     for tiles, value in pairs:
@@ -667,11 +663,11 @@
         copy.wait()
 
 
-def finish(acc, columns, sent, received, scale, rows, sizes, part_shape):
+def finish(acc, columns, down, below, scale, rows, sizes, part_shape):
     channels = columns.shape[0]
     return pl.pallas_call(
         functools.partial(finish_kernel, scale, rows, sizes),
-        in_specs=[VMEM] * 6,
+        in_specs=[VMEM] * 4,
         out_specs=HBM,
         out_shape=jax.ShapeDtypeStruct(part_shape, BF16),
         scratch_shapes=[
@@ -682,7 +678,7 @@
         compiler_params=params(),
         cost_estimate=cost(2**27, 2**21),
         name="finish",
-    )(acc, columns, *sent, *received)
+    )(acc, columns, down, below)
 
 
 def adam_step(master, first, second, weight_grad):
@@ -776,31 +772,46 @@
     return tuple(out.reshape(share) for out in outs)
 
 
-def spread_kernel(rows, w_ref, weights_ref, turned, chunks):
+def lines_kernel(rows, w_ref, whole_ref, chunks):
     count, height, width = w_ref.shape
-    taps = 27 * rows * count
+    taps = whole_ref.shape[1]
     chunks[...] = w_ref[...].astype(F32).reshape(chunks.shape)
     line = jnp.concatenate(
         [chunks[pl.ds(k, count, stride=height), :] for k in range(rows * taps // width)], axis=1
     )
-    whole = jnp.concatenate([line[:, r * taps : (r + 1) * taps] for r in range(rows)], axis=0)
-    spread_weights(whole, turned, weights_ref)
-
-
-def spread(kernel, channels, rows):
-    return pl.pallas_call(
-        functools.partial(spread_kernel, rows),
+    for r in range(rows):
+        whole_ref[r * count : (r + 1) * count, :] = line[:, r * taps : (r + 1) * taps]
+
+
+def lines(kernel, channels, rows):
+    return pl.pallas_call(
+        functools.partial(lines_kernel, rows),
+        in_specs=[VMEM],
+        out_specs=VMEM,
+        out_shape=jax.ShapeDtypeStruct((channels, 27 * channels), F32),
+        scratch_shapes=[pltpu.VMEM((kernel.shape[0] * kernel.shape[1], kernel.shape[2]), F32)],
+        compiler_params=params(),
+        cost_estimate=cost(0, 2**20),
+        name="lines",
+    )(kernel)
+
+
+def spread_kernel(whole_ref, weights_ref, turned):
+    spread_weights(whole_ref[...], turned, weights_ref)
+
+
+def spread(whole):
+    channels = whole.shape[0]
+    return pl.pallas_call(
+        spread_kernel,
         in_specs=[VMEM],
         out_specs=VMEM,
         out_shape=jax.ShapeDtypeStruct((3, 2 * channels, 12 * channels), BF16),
-        scratch_shapes=[
-            flat_scratch(channels),
-            pltpu.VMEM((kernel.shape[0] * kernel.shape[1], kernel.shape[2]), F32),
-        ],
+        scratch_shapes=[flat_scratch(channels)],
         compiler_params=params(),
         cost_estimate=cost(2**20, 2**21),
         name="spread",
-    )(kernel)
+    )(whole)
 
 
 def pair_dgrad_kernel(*refs):
@@ -819,7 +830,7 @@
         out_shape=jax.ShapeDtypeStruct(shape, BF16),
         scratch_shapes=[g3_scratch(*shape), pltpu.VMEM((2, channels * size_y, size_z), F32)],
         compiler_params=params(32 * 2**20),
-        cost_estimate=dgrad_cost(*shape),
+        cost_estimate=cost(0, 2**10),
         name="dgrad",
     )(*sources, weights)
 
@@ -843,17 +854,17 @@
     own, activations = lax.optimization_barrier((own, activations))
     other = shifted(own, {"gy": "swap"})
     planes_x, columns = input_planes(activations, True)
-    z_sent = join(own, other, columns, size_x * size_y)
-    from_odd = swapped(z_sent[1], "gz", 1)
-    from_even = swapped(z_sent[0], "gz", 0)
+    down, up = join(own, other, columns, size_x * size_y)
+    below = shifted(up, {"gz": 1})
     sources = (*planes, other, other)
     acc = pair_wgrad(sources, planes_x, shape)
-    z_received = (from_odd, from_even)
-    part = finish(acc, columns, z_sent, z_received, scale, rows, (size_x, size_y), block)
+    part = finish(acc, columns, down, below, scale, rows, (size_x, size_y), block)
     part, kernel = lax.optimization_barrier((part, kernel))
     parts = lax.all_to_all(part, AXES, 0, 0, tiled=True)
-    weights = spread(kernel, channels, rows)
-    grad_input = pair_dgrad((*sources, *z_received), weights, shape)
+    whole = lines(kernel, channels, rows)
+    whole, down = lax.optimization_barrier((whole, down))
+    above = shifted(down, {"gz": -1})
+    grad_input = pair_dgrad((*sources, below, above), spread(whole), shape)
     return grad_input, *adam(parts, master, first_moment, second_moment)
 
 

time: 43.3 us -> 45.3 us (1.046)
  the two profiles are of different devices: /device:TPU:0 before, /device:TPU:8 now
where the time goes in v10:
time: 45.3 us; the launch traced here: 45 us
  starting transfers between devices  20.7 us (46%)
  Pallas kernels  17.4 us (38%)
  waiting for transfers between devices  6.08 us (13%)
  between operations  0.8 us (2%)
    ppermute x3, waiting for transfers between devices, shifted(): return lax.ppermute(value, names if len(names) > 1 else names[0], pairs)  6.07 us
    ppermute x3, starting transfers between devices, shifted(): return lax.ppermute(value, names if len(names) > 1 else names[0], pairs)  5.74 us
    pallas_call x1, Pallas kernels, pair_dgrad(): pl.pallas_call(pair_dgrad_kernel, in_specs=[VMEM] * 10, out_specs=VMEM, o...  5.07 us
    all_to_all x1, starting transfers between devices, pair_program(): kernel = lax.all_to_all(sent, AXES, 0, 0, tiled=True)  5.03 us
    all_to_all x1, starting transfers between devices, pair_program(): parts = lax.all_to_all(part, AXES, 0, 0, tiled=True)  4.96 us
    ppermute x2, starting transfers between devices, swapped(): return lax.ppermute(value, axis, pairs)  4.96 us
    pallas_call x1, Pallas kernels, pair_wgrad(): pl.pallas_call(pair_wgrad_kernel, in_specs=[VMEM] * 8, out_specs=VMEM, ou...  3.46 us
    pallas_call x1, Pallas kernels, pair_inner(): pl.pallas_call(functools.partial(pair_inner_kernel, rows), in_specs=[HBM]...  2.75 us
  transfers between devices with their start and end apart: 7, of which 2 were waited for; matrix products, arithmetic and copies ran while one was open for 0% of the time, Pallas kernels for 33%

profile of v10, /device:TPU:8, one launch (start us, length us, event | category | flops | bytes accessed | tf_op | source)
XLA Modules:
  0.0 45.0 jit_solution(12751796277432110884)
XLA Ops:
  0.6 0.0 copy-start.1
  0.6 1.3 %faces.1 = (bf16[64,1024]{1,0:T(8,128)(2,1)S(1)}, bf16[64,1024]{1,0:T(8,128)(2,1)S(1)}, bf16[64,1024]{1,0:T(8,128)(2,1)S(1)}) custom-call(bf16[64,8,8,128]{3,2,1,0:T(8,128)(2,1)} %refs_0_.1, bf16[64,8,8,128]{3,2,1,0:T(8,128)(2,1)} %refs_1_.1), custom_call_target="tpu_custom_call" | custom-call | bytes 1048576 | tf_op jit(solution)/shard_map/faces/pallas_call | solution.py:83
  2.0 0.7 %collective-permute-start = (bf16[64,1024]{1,0:T(8,128)(2,1)S(1)}, bf16[64,1024]{1,0:T(8,128)(2,1)S(1)}, u32[]{:S(2)}, u32[]{:S(2)}) collective-permute-start(bf16[64,1024]{1,0:T(8,128)(2,1)S(1)} %get-tuple-element.29), channel_id=1, source_target_pairs={{8,16},{16,8},{9,17},{17,9},{10,18},{18,10},{11,19},{19,11},{12,20... | collective-permute-start | bytes 393224 | tf_op jit(solution)/shard_map/ppermute | solution.py:1022
  2.7 0.0 copy-done.1
  2.7 0.0 copy-start
  2.7 2.8 %inner.1 = (bf16[6,64,1024]{2,1,0:T(8,128)(2,1)S(1)}, bf16[10,64,128]{2,1,0:T(8,128)(2,1)S(1)}, bf16[64,1024]{1,0:T(8,128)(2,1)S(1)}, bf16[32,32,128]{2,1,0:T(8,128)(2,1)}) custom-call(bf16[64,8,8,128]{3,2,1,0:T(8,128)(2,1)} %refs_0_.1, bf16[64,8,8,128]{3,2,1,0:T(8,128)(2,1)} %refs_1_.1, bf16[64,1024]{1,0:T(8,128)(2,1)S(1)} %get-tuple-element.30.refs_2_.refs_1_, ...), custom_call_target="tpu_custom_call" | custom-call | bytes 4194304 | tf_op jit(solution)/shard_map/inner/pallas_call | solution.py:485
  5.4 4.3 %collective-permute-start.1 = (bf16[64,1024]{1,0:T(8,128)(2,1)S(1)}, bf16[64,1024]{1,0:T(8,128)(2,1)S(1)}, u32[]{:S(2)}, u32[]{:S(2)}) collective-permute-start(bf16[64,1024]{1,0:T(8,128)(2,1)S(1)} %get-tuple-element.32), channel_id=1, source_target_pairs={{0,8},{8,0},{16,24},{24,16},{1,9},{9,1},{17,25},{25,17},{2,10},{10... | collective-permute-start | bytes 393224 | tf_op jit(solution)/shard_map/ppermute | solution.py:1022
  9.7 5.0 %all-to-all-start = ((bf16[32,32,128]{2,1,0:T(8,128)(2,1)}), bf16[32,32,128]{2,1,0:T(8,128)(2,1)S(1)}, u32[]{:S(2)}, u32[]{:S(2)}) async-start(bf16[32,32,128]{2,1,0:T(8,128)(2,1)} %get-tuple-element.44), calls=%async_computation | async-start | bytes 524288 | tf_op jit(solution)/shard_map/all_to_all | solution.py:851
  14.8 0.0 collective-permute-done.odd_ref
  14.8 0.0 collective-permute-done.1.even_ref
  14.8 0.2 side.1
  15.0 0.2 collective-permute-start.2
  15.2 0.0 copy-done
  15.2 1.0 %inputs.1 = (bf16[8,64,1024]{2,1,0:T(8,128)(2,1)S(1)}, bf16[64,128]{1,0:T(8,128)(2,1)S(1)}) custom-call(bf16[64,8,8,128]{3,2,1,0:T(8,128)(2,1)S(1)} %copy-done), custom_call_target="tpu_custom_call" | custom-call | bytes 2097152 | tf_op jit(solution)/shard_map/inputs/pallas_call | solution.py:172
  16.3 0.2 collective-permute-done.2.other_ref.refs_5_.refs_6_
  16.5 0.1 join.1
  16.6 3.4 %collective-permute-start.3 = (bf16[3,64,128]{2,1,0:T(8,128)(2,1)S(1)}, bf16[3,64,128]{2,1,0:T(8,128)(2,1)S(1)}, u32[]{:S(2)}, u32[]{:S(2)}) collective-permute-start(bf16[3,64,128]{2,1,0:T(8,128)(2,1)S(1)} %get-tuple-element.41), channel_id=1, source_target_pairs={{0,1},{1,2},{2,3},{4,5},{5,6},{6,7},{8,9},{9,10},{10,11},{12,13},{... | collective-permute-start | bytes 147464 | tf_op jit(solution)/shard_map/ppermute | solution.py:1015
  20.0 3.5 %wgrad.1.refs_0_ = f32[576,192]{1,0:T(8,128)S(1)} custom-call(bf16[64,1024]{1,0:T(8,128)(2,1)S(1)} %get-tuple-element.34.refs_0_, bf16[64,1024]{1,0:T(8,128)(2,1)S(1)} %get-tuple-element.30.refs_2_.refs_1_, bf16[6,64,1024]{2,1,0:T(8,128)(2,1)S(1)} %get-tuple-element.35.refs_2_, bf16[64,1024]{1,0:T(8,128)(2,1)S(1)} %get-tuple-element.31.refs_3_, ...), custom_call_target="tpu_custom_call" | custom-call | flops 2264924160 | bytes 4194304 | tf_op jit(solution)/shard_map/wgrad/pallas_call | solution.py:587
  23.4 0.0 collective-permute-done.3.refs_3_.refs_7_
  23.5 1.3 %finish.1 = bf16[32,32,128]{2,1,0:T(8,128)(2,1)} custom-call(f32[576,192]{1,0:T(8,128)S(1)} %wgrad.1.refs_0_, bf16[64,128]{1,0:T(8,128)(2,1)S(1)} %get-tuple-element.40.columns_ref.refs_1_, bf16[2,64,128]{2,1,0:T(8,128)(2,1)S(1)} %get-tuple-element.46.refs_2_, bf16[3,64,128]{2,1,0:T(8,128)(2,1)S(1)} %collective-permute-done.3.refs_3_.refs_7_), custom_call_target="tpu_custom_call" | custom-call | flops 134217728 | bytes 2097152 | tf_op jit(solution)/shard_map/finish/pallas_call | solution.py:668
  24.8 0.0 all-to-all-done.w_ref
  24.8 5.0 %all-to-all-start.1 = ((bf16[32,32,128]{2,1,0:T(8,128)(2,1)}), bf16[32,32,128]{2,1,0:T(8,128)(2,1)S(1)}, u32[]{:S(2)}, u32[]{:S(2)}) async-start(bf16[32,32,128]{2,1,0:T(8,128)(2,1)} %finish.1), calls=%async_computation.1 | async-start | bytes 524288 | tf_op jit(solution)/shard_map/all_to_all | solution.py:863
  29.8 0.3 lines.1.whole_ref
  30.1 2.2 %collective-permute-start.4 = (bf16[2,64,128]{2,1,0:T(8,128)(2,1)S(1)}, bf16[2,64,128]{2,1,0:T(8,128)(2,1)S(1)}, u32[]{:S(2)}, u32[]{:S(2)}) collective-permute-start(bf16[2,64,128]{2,1,0:T(8,128)(2,1)S(1)} %get-tuple-element.46.refs_2_), channel_id=1, source_target_pairs={{1,0},{2,1},{3,2},{5,4},{6,5},{7,6},{9,8},{10,9},{11,10},{13,12},{... | collective-permute-start | bytes 98312 | tf_op jit(solution)/shard_map/ppermute | solution.py:1015
  32.3 0.5 %spread.1.refs_9_ = bf16[3,128,768]{2,1,0:T(8,128)(2,1)S(1)} custom-call(f32[64,1728]{1,0:T(8,128)S(1)} %lines.1.whole_ref), custom_call_target="tpu_custom_call" | custom-call | flops 1048576 | bytes 2097152 | tf_op jit(solution)/shard_map/spread/pallas_call | solution.py:805
  32.8 0.0 copy-start.2
  32.8 0.0 copy-start.3
  32.8 5.8 %collective-permute-done.4.refs_8_ = bf16[2,64,128]{2,1,0:T(8,128)(2,1)S(1)} collective-permute-done((bf16[2,64,128]{2,1,0:T(8,128)(2,1)S(1)}, bf16[2,64,128]{2,1,0:T(8,128)(2,1)S(1)}, u32[]{:S(2)}, u32[]{:S(2)}) %collective-permute-start.4) | collective-permute-done | bytes 32800 | tf_op jit(solution)/shard_map/ppermute | solution.py:1015
  38.6 5.1 %dgrad.1 = bf16[64,8,8,128]{3,2,1,0:T(8,128)(2,1)} custom-call(bf16[64,1024]{1,0:T(8,128)(2,1)S(1)} %get-tuple-element.34.refs_0_, bf16[64,1024]{1,0:T(8,128)(2,1)S(1)} %get-tuple-element.30.refs_2_.refs_1_, bf16[6,64,1024]{2,1,0:T(8,128)(2,1)S(1)} %get-tuple-element.35.refs_2_, bf16[64,1024]{1,0:T(8,128)(2,1)S(1)} %get-tuple-element.31.refs_3_, ...), custom_call_target="tpu_custom_call" | custom-call | bytes 1024 | tf_op jit(solution)/shard_map/dgrad/pallas_call | solution.py:826
  43.7 0.0 all-to-all-done.1.parts_ref
  43.7 0.0 copy-done.2
  43.7 1.2 %adam.1 = (f32[27,128]{1,0:T(8,128)}, f32[27,128]{1,0:T(8,128)}, f32[27,128]{1,0:T(8,128)}, f32[27,128]{1,0:T(8,128)}) custom-call(bf16[32,32,128]{2,1,0:T(8,128)(2,1)S(1)} %all-to-all-done.1.parts_ref, f32[27,128]{1,0:T(8,128)S(1)} %bitcast.8, f32[27,128]{1,0:T(8,128)S(1)} %bitcast.9, f32[27,128]{1,0:T(8,128)S(1)} %bitcast.10), custom_call_target="tpu_custom_call" | custom-call | flops 4194304 | bytes 524288 | tf_op jit(solution)/shard_map/adam/pallas_call | solution.py:758
  (1 shorter events, 0.0 us)
Async XLA Ops:
  0.6 2.0 %copy-start.1 = (f32[3456]{0:T(1024)S(1)}, f32[3456]{0:T(1024)}, u32[]{:S(2)}) copy-start(f32[3456]{0:T(1024)} %param.9) | copy-start | bytes 41476
  2.0 12.8 %collective-permute-start = (bf16[64,1024]{1,0:T(8,128)(2,1)S(1)}, bf16[64,1024]{1,0:T(8,128)(2,1)S(1)}, u32[]{:S(2)}, u32[]{:S(2)}) collective-permute-start(bf16[64,1024]{1,0:T(8,128)(2,1)S(1)} %get-tuple-element.29), channel_id=1, source_target_pairs={{8,16},{16,8},{9,17},{17,9},{10,18},{18,10},{11,19},{19,11},{12,20... | collective-permute-start | bytes 393224 | tf_op jit(solution)/shard_map/ppermute | solution.py:1022
  2.7 12.6 %copy-start = (bf16[64,8,8,128]{3,2,1,0:T(8,128)(2,1)S(1)}, bf16[64,8,8,128]{3,2,1,0:T(8,128)(2,1)}, u32[]{:S(2)}) copy-start(bf16[64,8,8,128]{3,2,1,0:T(8,128)(2,1)} %a_ref) | copy-start | bytes 3145732
  5.4 9.3 %collective-permute-start.1 = (bf16[64,1024]{1,0:T(8,128)(2,1)S(1)}, bf16[64,1024]{1,0:T(8,128)(2,1)S(1)}, u32[]{:S(2)}, u32[]{:S(2)}) collective-permute-start(bf16[64,1024]{1,0:T(8,128)(2,1)S(1)} %get-tuple-element.32), channel_id=1, source_target_pairs={{0,8},{8,0},{16,24},{24,16},{1,9},{9,1},{17,25},{25,17},{2,10},{10... | collective-permute-start | bytes 393224 | tf_op jit(solution)/shard_map/ppermute | solution.py:1022
  9.7 15.1 %all-to-all-start = ((bf16[32,32,128]{2,1,0:T(8,128)(2,1)}), bf16[32,32,128]{2,1,0:T(8,128)(2,1)S(1)}, u32[]{:S(2)}, u32[]{:S(2)}) async-start(bf16[32,32,128]{2,1,0:T(8,128)(2,1)} %get-tuple-element.44), calls=%async_computation | async-start | bytes 524288 | tf_op jit(solution)/shard_map/all_to_all | solution.py:851
  15.0 1.5 %collective-permute-start.2 = (bf16[12,64,128]{2,1,0:T(8,128)(2,1)S(1)}, bf16[12,64,128]{2,1,0:T(8,128)(2,1)S(1)}, u32[]{:S(2)}, u32[]{:S(2)}) collective-permute-start(bf16[12,64,128]{2,1,0:T(8,128)(2,1)S(1)} %get-tuple-element.38.own_ref), channel_id=1, source_target_pairs={{0,4},{4,0},{1,5},{5,1},{2,6},{6,2},{3,7},{7,3},{8,12},{12,8},{9,1... | collective-permute-start | bytes 589832 | tf_op jit(solution)/shard_map/ppermute | solution.py:1015
  16.6 6.8 %collective-permute-start.3 = (bf16[3,64,128]{2,1,0:T(8,128)(2,1)S(1)}, bf16[3,64,128]{2,1,0:T(8,128)(2,1)S(1)}, u32[]{:S(2)}, u32[]{:S(2)}) collective-permute-start(bf16[3,64,128]{2,1,0:T(8,128)(2,1)S(1)} %get-tuple-element.41), channel_id=1, source_target_pairs={{0,1},{1,2},{2,3},{4,5},{5,6},{6,7},{8,9},{9,10},{10,11},{12,13},{... | collective-permute-start | bytes 147464 | tf_op jit(solution)/shard_map/ppermute | solution.py:1015
  24.8 18.9 %all-to-all-start.1 = ((bf16[32,32,128]{2,1,0:T(8,128)(2,1)}), bf16[32,32,128]{2,1,0:T(8,128)(2,1)S(1)}, u32[]{:S(2)}, u32[]{:S(2)}) async-start(bf16[32,32,128]{2,1,0:T(8,128)(2,1)} %finish.1), calls=%async_computation.1 | async-start | bytes 524288 | tf_op jit(solution)/shard_map/all_to_all | solution.py:863
  30.1 8.5 %collective-permute-start.4 = (bf16[2,64,128]{2,1,0:T(8,128)(2,1)S(1)}, bf16[2,64,128]{2,1,0:T(8,128)(2,1)S(1)}, u32[]{:S(2)}, u32[]{:S(2)}) collective-permute-start(bf16[2,64,128]{2,1,0:T(8,128)(2,1)S(1)} %get-tuple-element.46.refs_2_), channel_id=1, source_target_pairs={{1,0},{2,1},{3,2},{5,4},{6,5},{7,6},{9,8},{10,9},{11,10},{13,12},{... | collective-permute-start | bytes 98312 | tf_op jit(solution)/shard_map/ppermute | solution.py:1015
  32.8 10.9 %copy-start.2 = (f32[3456]{0:T(1024)S(1)}, f32[3456]{0:T(1024)}, u32[]{:S(2)}) copy-start(f32[3456]{0:T(1024)} %param.10) | copy-start | bytes 41476
  32.8 10.9 %copy-start.3 = (f32[3456]{0:T(1024)S(1)}, f32[3456]{0:T(1024)}, u32[]{:S(2)}) copy-start(f32[3456]{0:T(1024)} %param.11) | copy-start | bytes 41476

commit v11 on v9

--- a/solution.py
+++ b/solution.py
@@ -34,6 +34,14 @@
         for r in range(rows):
             picked = tile[pl.ds(r * size_y + y, count, stride=rows * size_y), :]
             write(slice(r * count, (r + 1) * count), y, picked.astype(BF16))
+
+
+QUAD = 4
+
+
+def to_quads(rows, write):
+    for k in range(rows.shape[-2] // QUAD):
+        write(slice(k * LANES, (k + 1) * LANES), rows[..., k * QUAD : (k + 1) * QUAD, :])
 
 
 def masked(p, u):
@@ -306,22 +314,26 @@
     group = 3 * channels
     zero = jnp.zeros((channels, 2 * size_z), BF16)
     done = 0
-    for x in range(size_x):
-        while done < x + 3:
+    for x in range(0, size_x, 2):
+        while done < x + 4:
             shifted_plane(done, refs, halo, g3)
             done += 1
-        value = x_ref[x]
-        for b in range(3):
-            at = slice(b * channels, (b + 1) * channels)
-            start = (2 - b) * size_z
-            x3[x, at, start : start + plane] = value
-            if start:
-                x3[x, at, :start] = zero[:, :start]
-            if start < 2 * size_z:
-                x3[x, at, start + plane :] = zero[:, start:]
+        for plane_x in (x, x + 1):
+            value = x_ref[plane_x]
+            for b in range(3):
+                at = slice(b * channels, (b + 1) * channels)
+                start = (2 - b) * size_z
+                x3[plane_x, at, start : start + plane] = value
+                if start:
+                    x3[plane_x, at, :start] = zero[:, :start]
+                if start < 2 * size_z:
+                    x3[plane_x, at, start + plane :] = zero[:, start:]
         product = lax.dot_general(
-            g3[x * group : (x + 3) * group, :],
-            x3[x],
+            jnp.concatenate(
+                [g3[x * group : (x + 3) * group, :], g3[(x + 1) * group : (x + 4) * group, :]],
+                axis=1,
+            ),
+            jnp.concatenate([x3[x], x3[x + 1]], axis=1),
             (((1,), (1,)), ((), ())),
             preferred_element_type=F32,
         )
@@ -439,12 +451,15 @@
     sent_buf, sent_sem = refs[13:]
     choose(is_odd("gx"), swap_ref, first_ref, last_ref)
     share = m_ref[...]
-    height = sent_ref.shape[1] - share.shape[0]
-    if height:
-        share = jnp.concatenate([share, jnp.zeros((height, share.shape[1]), F32)], axis=0)
-    share = share.astype(BF16)
-    for device in range(sent_ref.shape[0]):
-        sent_buf[device] = share
+    share = jnp.concatenate(
+        [share, jnp.zeros((-share.shape[0] % QUAD, share.shape[1]), F32)], axis=0
+    )
+
+    def write(at, quad):
+        quad = quad.astype(BF16)
+        sent_buf[:, :, at] = jnp.broadcast_to(quad[None], (sent_buf.shape[0], *quad.shape))
+
+    to_quads(share, write)
     send = pltpu.make_async_copy(sent_buf, sent_ref, sent_sem)
     send.start()
     read_inner(rows, *refs[:2], g_ref, *refs[9:13])
@@ -601,7 +616,7 @@
 
 def finish_kernel(scale, rows, sizes, *refs):
     acc_ref, columns_ref, even_ref, odd_ref, from_odd_ref, from_even_ref = refs[:6]
-    part_ref, chunks, part_buf, sems = refs[6:]
+    part_ref, chunks = refs[6:]
     size_x, size_y = sizes
     channels = columns_ref.shape[0]
     area = size_x * size_y
@@ -637,7 +652,8 @@
                 preferred_element_type=F32,
             )
         )
-    count, height, width = part_ref.shape
+    count = part_ref.shape[0]
+    height, width = chunks.shape[0] // count, LANES
     chunks[...] = jnp.zeros_like(chunks)
     pieces = rows * acc_ref.shape[1] // width
     for a in range(3):
@@ -654,17 +670,12 @@
                 chunks[pl.ds(at * pieces + k, count, stride=height), :] = line[
                     :, k * width : (k + 1) * width
                 ]
-    pieces = sems.shape[0]
-    step = count // pieces
-    copies = []
-    for k in range(pieces):
-        piece = chunks[k * step * height : (k + 1) * step * height, :]
-        at = pl.ds(k * step, step)
-        part_buf[at] = piece.reshape(step, height, width).astype(BF16)
-        copies.append(pltpu.make_async_copy(part_buf.at[at], part_ref.at[at], sems.at[k]))
-        copies[-1].start()
-    for copy in copies:
-        copy.wait()
+
+    def write(at, quads):
+        part_ref[:, :, at] = quads.astype(BF16)
+
+    whole = chunks[...].reshape(count, height, width)
+    to_quads(whole[:, : part_ref.shape[2] // LANES * QUAD], write)
 
 
 def finish(acc, columns, sent, received, scale, rows, sizes, part_shape):
@@ -672,12 +683,10 @@
     return pl.pallas_call(
         functools.partial(finish_kernel, scale, rows, sizes),
         in_specs=[VMEM] * 6,
-        out_specs=HBM,
+        out_specs=VMEM,
         out_shape=jax.ShapeDtypeStruct(part_shape, BF16),
         scratch_shapes=[
-            pltpu.VMEM((part_shape[0] * part_shape[1], part_shape[2]), F32),
-            pltpu.VMEM(part_shape, BF16),
-            pltpu.SemaphoreType.DMA((4,)),
+            pltpu.VMEM((part_shape[0] * -(-part_shape[2] // LANES * QUAD // 8) * 8, LANES), F32),
         ],
         compiler_params=params(),
         cost_estimate=cost(2**27, 2**21),
@@ -697,7 +706,8 @@
 def in_flat_order(value, rows, places, spread_rows):
     taps = 27
     lane = lax.broadcasted_iota(jnp.int32, (9, LANES), 1)
-    rows[: value.shape[0], :] = value
+    for k in range(value.shape[1] // LANES):
+        rows[k * QUAD : (k + 1) * QUAD, :] = value[:, k * LANES : (k + 1) * LANES]
     thirds = [rows[pl.ds(k, 9, stride=3), :] for k in range(3)]
     half = LANES // 2
     by_y = (
@@ -765,7 +775,7 @@
         out_specs=[VMEM] * 4,
         out_shape=[result] * 4,
         scratch_shapes=[
-            pltpu.VMEM(parts.shape[1:], F32),
+            pltpu.VMEM((32, LANES), F32),
             pltpu.VMEM((LANES, LANES), F32),
             pltpu.VMEM((3, 16, LANES), F32),
         ],
@@ -777,11 +787,17 @@
 
 
 def spread_kernel(rows, w_ref, weights_ref, turned, chunks):
-    count, height, width = w_ref.shape
+    count = w_ref.shape[0]
+    height = chunks.shape[0] // count
     taps = 27 * rows * count
-    chunks[...] = w_ref[...].astype(F32).reshape(chunks.shape)
+    quads = [
+        w_ref[:, :, k * LANES : (k + 1) * LANES].astype(F32)
+        for k in range(w_ref.shape[2] // LANES)
+    ]
+    spare = jnp.zeros((count, height - QUAD * len(quads), LANES), F32)
+    chunks[...] = jnp.concatenate(quads + [spare], axis=1).reshape(chunks.shape)
     line = jnp.concatenate(
-        [chunks[pl.ds(k, count, stride=height), :] for k in range(rows * taps // width)], axis=1
+        [chunks[pl.ds(k, count, stride=height), :] for k in range(rows * taps // LANES)], axis=1
     )
     whole = jnp.concatenate([line[:, r * taps : (r + 1) * taps] for r in range(rows)], axis=0)
     spread_weights(whole, turned, weights_ref)
@@ -795,7 +811,7 @@
         out_shape=jax.ShapeDtypeStruct((3, 2 * channels, 12 * channels), BF16),
         scratch_shapes=[
             flat_scratch(channels),
-            pltpu.VMEM((kernel.shape[0] * kernel.shape[1], kernel.shape[2]), F32),
+            pltpu.VMEM((kernel.shape[0] * 32, LANES), F32),
         ],
         compiler_params=params(),
         cost_estimate=cost(2**20, 2**21),
@@ -830,7 +846,7 @@
     devices = math.prod(lax.axis_size(a) for a in AXES)
     rows = channels // devices
     used = master.shape[0] // LANES
-    block = (devices, -(-used // 16) * 16, LANES)
+    block = (devices, QUAD, -(-used // QUAD) * LANES)
     first, last, odd_sent = faces(preact, upstream, "gx", rows)
     odd_halves = swapped(odd_sent, "gx", 1)
     inner, own, even_sent, sent = pair_inner(

time: 43.3 us -> 42.8 us (0.988)
  no operation moved by 1% of the time
where the time goes in v11:
time: 42.8 us; the launch traced here: 42.5 us
  starting transfers between devices  20.4 us (48%)
  Pallas kernels  17.2 us (40%)
  waiting for transfers between devices  4.12 us (10%)
  between operations  0.78 us (2%)
    ppermute x4, starting transfers between devices, swapped(): return lax.ppermute(value, axis, pairs)  11.6 us
    pallas_call x1, Pallas kernels, pair_dgrad(): pl.pallas_call(pair_dgrad_kernel, in_specs=[VMEM] * 10, out_specs=VMEM, o...  5.08 us
    all_to_all x1, starting transfers between devices, pair_program(): kernel = lax.all_to_all(sent, AXES, 0, 0, tiled=True)  4.83 us
    all_to_all x1, waiting for transfers between devices, pair_program(): parts = lax.all_to_all(part, AXES, 0, 0, tiled=True)  3.97 us
    all_to_all x1, starting transfers between devices, pair_program(): parts = lax.all_to_all(part, AXES, 0, 0, tiled=True)  3.6 us
    pallas_call x1, Pallas kernels, pair_wgrad(): pl.pallas_call(pair_wgrad_kernel, in_specs=[VMEM] * 8, out_specs=VMEM, ou...  3.45 us
    pallas_call x1, Pallas kernels, pair_inner(): pl.pallas_call(functools.partial(pair_inner_kernel, rows), in_specs=[HBM]...  2.63 us
    pallas_call x1, Pallas kernels, finish(): pl.pallas_call(functools.partial(finish_kernel, scale, rows, sizes), in_s...  1.38 us
  transfers between devices with their start and end apart: 7, of which 2 were waited for; matrix products, arithmetic and copies ran while one was open for 0% of the time, Pallas kernels for 34%

profile of v11, /device:TPU:0, one launch (start us, length us, event | category | flops | bytes accessed | tf_op | source)
XLA Modules:
  0.0 42.5 jit_solution(7378566086130716304)
XLA Ops:
  0.6 0.0 copy-start.1
  0.6 1.3 %faces.1 = (bf16[64,1024]{1,0:T(8,128)(2,1)S(1)}, bf16[64,1024]{1,0:T(8,128)(2,1)S(1)}, bf16[64,1024]{1,0:T(8,128)(2,1)S(1)}) custom-call(bf16[64,8,8,128]{3,2,1,0:T(8,128)(2,1)} %refs_0_.1, bf16[64,8,8,128]{3,2,1,0:T(8,128)(2,1)} %refs_1_.1), custom_call_target="tpu_custom_call" | custom-call | bytes 1048576 | tf_op jit(solution)/shard_map/faces/pallas_call | solution.py:91
  2.0 0.7 %collective-permute-start = (bf16[64,1024]{1,0:T(8,128)(2,1)S(1)}, bf16[64,1024]{1,0:T(8,128)(2,1)S(1)}, u32[]{:S(2)}, u32[]{:S(2)}) collective-permute-start(bf16[64,1024]{1,0:T(8,128)(2,1)S(1)} %get-tuple-element.27), channel_id=1, source_target_pairs={{8,16},{16,8},{9,17},{17,9},{10,18},{18,10},{11,19},{19,11},{12,20... | collective-permute-start | bytes 393224 | tf_op jit(solution)/shard_map/ppermute | solution.py:1027
  2.7 0.0 copy-done.1
  2.7 0.0 copy-start
  2.7 2.6 %inner.1 = (bf16[6,64,1024]{2,1,0:T(8,128)(2,1)S(1)}, bf16[10,64,128]{2,1,0:T(8,128)(2,1)S(1)}, bf16[64,1024]{1,0:T(8,128)(2,1)S(1)}, bf16[32,4,896]{2,1,0:T(4,128)(2,1)}) custom-call(bf16[64,8,8,128]{3,2,1,0:T(8,128)(2,1)} %refs_0_.1, bf16[64,8,8,128]{3,2,1,0:T(8,128)(2,1)} %refs_1_.1, bf16[64,1024]{1,0:T(8,128)(2,1)S(1)} %get-tuple-element.28.refs_2_.refs_1_, ...), custom_call_target="tpu_custom_call" | custom-call | bytes 4194304 | tf_op jit(solution)/shard_map/inner/pallas_call | solution.py:483
  5.3 5.7 %collective-permute-start.1 = (bf16[64,1024]{1,0:T(8,128)(2,1)S(1)}, bf16[64,1024]{1,0:T(8,128)(2,1)S(1)}, u32[]{:S(2)}, u32[]{:S(2)}) collective-permute-start(bf16[64,1024]{1,0:T(8,128)(2,1)S(1)} %get-tuple-element.30), channel_id=1, source_target_pairs={{0,8},{8,0},{16,24},{24,16},{1,9},{9,1},{17,25},{25,17},{2,10},{10... | collective-permute-start | bytes 393224 | tf_op jit(solution)/shard_map/ppermute | solution.py:1027
  11.1 4.8 %all-to-all-start = ((bf16[32,4,896]{2,1,0:T(4,128)(2,1)}), bf16[32,4,896]{2,1,0:T(4,128)(2,1)S(1)}, u32[]{:S(2)}, u32[]{:S(2)}) async-start(bf16[32,4,896]{2,1,0:T(4,128)(2,1)} %get-tuple-element.42), calls=%async_computation | async-start | bytes 458752 | tf_op jit(solution)/shard_map/all_to_all | solution.py:856
  15.9 0.0 collective-permute-done.odd_ref
  15.9 0.0 collective-permute-done.1.even_ref
  15.9 0.2 side.1
  16.2 0.3 collective-permute-start.2
  16.5 0.0 copy-done
  16.5 1.0 %inputs.1 = (bf16[8,64,1024]{2,1,0:T(8,128)(2,1)S(1)}, bf16[64,128]{1,0:T(8,128)(2,1)S(1)}) custom-call(bf16[64,8,8,128]{3,2,1,0:T(8,128)(2,1)S(1)} %copy-done), custom_call_target="tpu_custom_call" | custom-call | bytes 2097152 | tf_op jit(solution)/shard_map/inputs/pallas_call | solution.py:180
  17.5 0.1 collective-permute-done.2.other_ref.refs_5_.refs_6_
  17.7 0.1 join.1
  17.8 0.7 %collective-permute-start.3 = (bf16[3,64,128]{2,1,0:T(8,128)(2,1)S(1)}, bf16[3,64,128]{2,1,0:T(8,128)(2,1)S(1)}, u32[]{:S(2)}, u32[]{:S(2)}) collective-permute-start(bf16[3,64,128]{2,1,0:T(8,128)(2,1)S(1)} %get-tuple-element.39.refs_3_), channel_id=1, source_target_pairs={{1,2},{2,1},{5,6},{6,5},{9,10},{10,9},{13,14},{14,13},{17,18},{18,... | collective-permute-start | bytes 147464 | tf_op jit(solution)/shard_map/ppermute | solution.py:1027
  18.4 4.5 %collective-permute-start.4 = (bf16[3,64,128]{2,1,0:T(8,128)(2,1)S(1)}, bf16[3,64,128]{2,1,0:T(8,128)(2,1)S(1)}, u32[]{:S(2)}, u32[]{:S(2)}) collective-permute-start(bf16[3,64,128]{2,1,0:T(8,128)(2,1)S(1)} %get-tuple-element.40.refs_2_), channel_id=1, source_target_pairs={{0,1},{1,0},{2,3},{3,2},{4,5},{5,4},{6,7},{7,6},{8,9},{9,8},{10,11... | collective-permute-start | bytes 147464 | tf_op jit(solution)/shard_map/ppermute | solution.py:1027
  23.0 3.5 %wgrad.1.refs_0_ = f32[576,192]{1,0:T(8,128)S(1)} custom-call(bf16[64,1024]{1,0:T(8,128)(2,1)S(1)} %get-tuple-element.32.refs_0_, bf16[64,1024]{1,0:T(8,128)(2,1)S(1)} %get-tuple-element.28.refs_2_.refs_1_, bf16[6,64,1024]{2,1,0:T(8,128)(2,1)S(1)} %get-tuple-element.33.refs_2_, bf16[64,1024]{1,0:T(8,128)(2,1)S(1)} %get-tuple-element.29.refs_3_, ...), custom_call_target="tpu_custom_call" | custom-call | flops 2264924160 | bytes 4194304 | tf_op jit(solution)/shard_map/wgrad/pallas_call | solution.py:605
  26.4 0.0 collective-permute-done.3.refs_4_.refs_7_
  26.4 0.0 collective-permute-done.4.refs_5_.refs_8_
  26.5 1.4 %finish.1 = bf16[32,4,896]{2,1,0:T(4,128)(2,1)} custom-call(f32[576,192]{1,0:T(8,128)S(1)} %wgrad.1.refs_0_, bf16[64,128]{1,0:T(8,128)(2,1)S(1)} %get-tuple-element.38.columns_ref.refs_1_, bf16[3,64,128]{2,1,0:T(8,128)(2,1)S(1)} %get-tuple-element.40.refs_2_, bf16[3,64,128]{2,1,0:T(8,128)(2,1)S(1)} %get-tuple-element.39.refs_3_, ...), custom_call_target="tpu_custom_call" | custom-call | flops 134217728 | bytes 2097152 | tf_op jit(solution)/shard_map/finish/pallas_call | solution.py:683
  27.8 0.0 all-to-all-done.w_ref
  27.8 3.6 %all-to-all-start.1 = ((bf16[32,4,896]{2,1,0:T(4,128)(2,1)}), bf16[32,4,896]{2,1,0:T(4,128)(2,1)S(1)}, u32[]{:S(2)}, u32[]{:S(2)}) async-start(bf16[32,4,896]{2,1,0:T(4,128)(2,1)} %finish.1), calls=%async_computation.1 | async-start | bytes 458752 | tf_op jit(solution)/shard_map/all_to_all | solution.py:870
  31.4 0.7 %spread.1.refs_9_ = bf16[3,128,768]{2,1,0:T(8,128)(2,1)S(1)} custom-call(bf16[32,4,896]{2,1,0:T(4,128)(2,1)S(1)} %all-to-all-done.w_ref), custom_call_target="tpu_custom_call" | custom-call | flops 1048576 | bytes 2097152 | tf_op jit(solution)/shard_map/spread/pallas_call | solution.py:807
  32.2 0.0 copy-start.2
  32.2 0.0 copy-start.3
  32.2 5.1 %dgrad.1 = bf16[64,8,8,128]{3,2,1,0:T(8,128)(2,1)} custom-call(bf16[64,1024]{1,0:T(8,128)(2,1)S(1)} %get-tuple-element.32.refs_0_, bf16[64,1024]{1,0:T(8,128)(2,1)S(1)} %get-tuple-element.28.refs_2_.refs_1_, bf16[6,64,1024]{2,1,0:T(8,128)(2,1)S(1)} %get-tuple-element.33.refs_2_, bf16[64,1024]{1,0:T(8,128)(2,1)S(1)} %get-tuple-element.29.refs_3_, ...), custom_call_target="tpu_custom_call" | custom-call | flops 2415919104 | bytes 4194304 | tf_op jit(solution)/shard_map/dgrad/pallas_call | solution.py:831
  37.3 4.0 %all-to-all-done.1.parts_ref = bf16[32,4,896]{2,1,0:T(4,128)(2,1)S(1)} async-done(((bf16[32,4,896]{2,1,0:T(4,128)(2,1)}), bf16[32,4,896]{2,1,0:T(4,128)(2,1)S(1)}, u32[]{:S(2)}, u32[]{:S(2)}) %all-to-all-start.1) | async-done | bytes 229408 | tf_op jit(solution)/shard_map/all_to_all | solution.py:870
  41.2 0.0 copy-done.2
  41.2 0.0 copy-done.3
  41.2 1.2 %adam.1 = (f32[27,128]{1,0:T(8,128)}, f32[27,128]{1,0:T(8,128)}, f32[27,128]{1,0:T(8,128)}, f32[27,128]{1,0:T(8,128)}) custom-call(bf16[32,4,896]{2,1,0:T(4,128)(2,1)S(1)} %all-to-all-done.1.parts_ref, f32[27,128]{1,0:T(8,128)S(1)} %bitcast.8, f32[27,128]{1,0:T(8,128)S(1)} %bitcast.9, f32[27,128]{1,0:T(8,128)S(1)} %bitcast.10), custom_call_target="tpu_custom_call" | custom-call | flops 4194304 | bytes 524288 | tf_op jit(solution)/shard_map/adam/pallas_call | solution.py:772
Async XLA Ops:
  0.6 2.0 %copy-start.1 = (f32[3456]{0:T(1024)S(1)}, f32[3456]{0:T(1024)}, u32[]{:S(2)}) copy-start(f32[3456]{0:T(1024)} %param.9) | copy-start | bytes 41476
  2.0 13.9 %collective-permute-start = (bf16[64,1024]{1,0:T(8,128)(2,1)S(1)}, bf16[64,1024]{1,0:T(8,128)(2,1)S(1)}, u32[]{:S(2)}, u32[]{:S(2)}) collective-permute-start(bf16[64,1024]{1,0:T(8,128)(2,1)S(1)} %get-tuple-element.27), channel_id=1, source_target_pairs={{8,16},{16,8},{9,17},{17,9},{10,18},{18,10},{11,19},{19,11},{12,20... | collective-permute-start | bytes 393224 | tf_op jit(solution)/shard_map/ppermute | solution.py:1027
  2.7 13.8 %copy-start = (bf16[64,8,8,128]{3,2,1,0:T(8,128)(2,1)S(1)}, bf16[64,8,8,128]{3,2,1,0:T(8,128)(2,1)}, u32[]{:S(2)}) copy-start(bf16[64,8,8,128]{3,2,1,0:T(8,128)(2,1)} %a_ref) | copy-start | bytes 3145732
  5.3 10.6 %collective-permute-start.1 = (bf16[64,1024]{1,0:T(8,128)(2,1)S(1)}, bf16[64,1024]{1,0:T(8,128)(2,1)S(1)}, u32[]{:S(2)}, u32[]{:S(2)}) collective-permute-start(bf16[64,1024]{1,0:T(8,128)(2,1)S(1)} %get-tuple-element.30), channel_id=1, source_target_pairs={{0,8},{8,0},{16,24},{24,16},{1,9},{9,1},{17,25},{25,17},{2,10},{10... | collective-permute-start | bytes 393224 | tf_op jit(solution)/shard_map/ppermute | solution.py:1027
  11.1 16.8 %all-to-all-start = ((bf16[32,4,896]{2,1,0:T(4,128)(2,1)}), bf16[32,4,896]{2,1,0:T(4,128)(2,1)S(1)}, u32[]{:S(2)}, u32[]{:S(2)}) async-start(bf16[32,4,896]{2,1,0:T(4,128)(2,1)} %get-tuple-element.42), calls=%async_computation | async-start | bytes 458752 | tf_op jit(solution)/shard_map/all_to_all | solution.py:856
  16.2 1.5 %collective-permute-start.2 = (bf16[12,64,128]{2,1,0:T(8,128)(2,1)S(1)}, bf16[12,64,128]{2,1,0:T(8,128)(2,1)S(1)}, u32[]{:S(2)}, u32[]{:S(2)}) collective-permute-start(bf16[12,64,128]{2,1,0:T(8,128)(2,1)S(1)} %get-tuple-element.36.own_ref), channel_id=1, source_target_pairs={{0,4},{4,0},{1,5},{5,1},{2,6},{6,2},{3,7},{7,3},{8,12},{12,8},{9,1... | collective-permute-start | bytes 589832 | tf_op jit(solution)/shard_map/ppermute | solution.py:1020
  17.8 8.7 %collective-permute-start.3 = (bf16[3,64,128]{2,1,0:T(8,128)(2,1)S(1)}, bf16[3,64,128]{2,1,0:T(8,128)(2,1)S(1)}, u32[]{:S(2)}, u32[]{:S(2)}) collective-permute-start(bf16[3,64,128]{2,1,0:T(8,128)(2,1)S(1)} %get-tuple-element.39.refs_3_), channel_id=1, source_target_pairs={{1,2},{2,1},{5,6},{6,5},{9,10},{10,9},{13,14},{14,13},{17,18},{18,... | collective-permute-start | bytes 147464 | tf_op jit(solution)/shard_map/ppermute | solution.py:1027
  18.4 8.0 %collective-permute-start.4 = (bf16[3,64,128]{2,1,0:T(8,128)(2,1)S(1)}, bf16[3,64,128]{2,1,0:T(8,128)(2,1)S(1)}, u32[]{:S(2)}, u32[]{:S(2)}) collective-permute-start(bf16[3,64,128]{2,1,0:T(8,128)(2,1)S(1)} %get-tuple-element.40.refs_2_), channel_id=1, source_target_pairs={{0,1},{1,0},{2,3},{3,2},{4,5},{5,4},{6,7},{7,6},{8,9},{9,8},{10,11... | collective-permute-start | bytes 147464 | tf_op jit(solution)/shard_map/ppermute | solution.py:1027
  27.8 13.4 %all-to-all-start.1 = ((bf16[32,4,896]{2,1,0:T(4,128)(2,1)}), bf16[32,4,896]{2,1,0:T(4,128)(2,1)S(1)}, u32[]{:S(2)}, u32[]{:S(2)}) async-start(bf16[32,4,896]{2,1,0:T(4,128)(2,1)} %finish.1), calls=%async_computation.1 | async-start | bytes 458752 | tf_op jit(solution)/shard_map/all_to_all | solution.py:870
  32.2 9.1 %copy-start.2 = (f32[3456]{0:T(1024)S(1)}, f32[3456]{0:T(1024)}, u32[]{:S(2)}) copy-start(f32[3456]{0:T(1024)} %param.10) | copy-start | bytes 41476
  32.2 9.1 %copy-start.3 = (f32[3456]{0:T(1024)S(1)}, f32[3456]{0:T(1024)}, u32[]{:S(2)}) copy-start(f32[3456]{0:T(1024)} %param.11) | copy-start | bytes 41476

commit v12 on v11

--- a/solution.py
+++ b/solution.py
@@ -16,6 +16,8 @@
 BF16 = jnp.bfloat16
 FACES_VMEM = 55_900_000
 INNER_VMEM = 54_800_000
+ENDS_VMEM = 54_800_000
+MIDDLES_VMEM = 53_600_000
 
 
 def params(limit=24 * 2**20):
@@ -446,23 +448,13 @@
     return jnp.where(lax.axis_index("gy") == 0, high, low).astype(BF16)
 
 
-def pair_inner_kernel(rows, *refs):
-    first_ref, last_ref, m_ref, g_ref, side_ref, swap_ref, sent_ref = refs[2:9]
-    sent_buf, sent_sem = refs[13:]
-    choose(is_odd("gx"), swap_ref, first_ref, last_ref)
-    share = m_ref[...]
-    share = jnp.concatenate(
-        [share, jnp.zeros((-share.shape[0] % QUAD, share.shape[1]), F32)], axis=0
-    )
-
-    def write(at, quad):
-        quad = quad.astype(BF16)
-        sent_buf[:, :, at] = jnp.broadcast_to(quad[None], (sent_buf.shape[0], *quad.shape))
-
-    to_quads(share, write)
-    send = pltpu.make_async_copy(sent_buf, sent_ref, sent_sem)
-    send.start()
-    read_inner(rows, *refs[:2], g_ref, *refs[9:13])
+def in_odd_swaps(axis):
+    me, count = lax.axis_index(axis), lax.axis_size(axis)
+    return (me > 0) & (me < count - 1 + count % 2)
+
+
+def own_planes(order, p_ref, u_ref, first_ref, last_ref, g_ref, side_ref, *scratch):
+    read_inner(order, p_ref, u_ref, g_ref, *scratch)
     size_z = side_ref.shape[-1]
     inner, _, plane = g_ref.shape
     size_x = inner + 2
@@ -474,28 +466,74 @@
     )
     side_ref[size_x] = low.astype(BF16)
     side_ref[size_x + 1] = high.astype(BF16)
+
+
+def ends_kernel(order, *refs):
+    choose(is_odd("gx"), refs[6], refs[2], refs[3])
+
+    @pl.when(jnp.logical_not(in_odd_swaps("gx")))
+    def _():
+        own_planes(order, *refs[:6], *refs[7:])
+
+
+def middles_kernel(order, *refs):
+    m_ref, g_before_ref, side_before_ref, g_ref, side_ref, sent_ref = refs[4:10]
+    sent_buf, sent_sem = refs[14:]
+    share = m_ref[...]
+    share = jnp.concatenate(
+        [share, jnp.zeros((-share.shape[0] % QUAD, share.shape[1]), F32)], axis=0
+    )
+
+    def write(at, quad):
+        quad = quad.astype(BF16)
+        sent_buf[:, :, at] = jnp.broadcast_to(quad[None], (sent_buf.shape[0], *quad.shape))
+
+    to_quads(share, write)
+    send = pltpu.make_async_copy(sent_buf, sent_ref, sent_sem)
+    send.start()
+    middle = in_odd_swaps("gx")
+
+    @pl.when(middle)
+    def _():
+        own_planes(order, *refs[:4], g_ref, side_ref, *refs[10:14])
+
+    @pl.when(jnp.logical_not(middle))
+    def _():
+        g_ref[...] = g_before_ref[...]
+        side_ref[...] = side_before_ref[...]
+
     send.wait()
 
 
-def pair_inner(preact, upstream, first, last, share, sent_shape, rows):
+def pair_inner(preact, upstream, first, last, share, sent_shape, order):
     shape = preact.shape
     channels, size_x, _, size_z = shape
-    return pl.pallas_call(
-        functools.partial(pair_inner_kernel, rows),
-        in_specs=[HBM] * 2 + [VMEM] * 3,
-        out_specs=[VMEM] * 3 + [HBM],
-        out_shape=[
-            inner_output(*shape),
-            jax.ShapeDtypeStruct((size_x + 2, channels, size_z), BF16),
-            jax.ShapeDtypeStruct(first.shape, BF16),
-            jax.ShapeDtypeStruct(sent_shape, BF16),
-        ],
+    made = [
+        inner_output(*shape),
+        jax.ShapeDtypeStruct((size_x + 2, channels, size_z), BF16),
+    ]
+    *before, swap = pl.pallas_call(
+        functools.partial(ends_kernel, order),
+        in_specs=[HBM] * 2 + [VMEM] * 2,
+        out_specs=[VMEM] * 3,
+        out_shape=made + [jax.ShapeDtypeStruct(first.shape, BF16)],
+        scratch_shapes=inner_scratch(*shape),
+        compiler_params=params(ENDS_VMEM),
+        cost_estimate=cost(0, 2**20),
+        name="ends",
+    )(preact, upstream, first, last)
+    g, side_rows, sent = pl.pallas_call(
+        functools.partial(middles_kernel, order),
+        in_specs=[HBM] * 2 + [VMEM] * 5,
+        out_specs=[VMEM] * 2 + [HBM],
+        out_shape=made + [jax.ShapeDtypeStruct(sent_shape, BF16)],
         scratch_shapes=inner_scratch(*shape)
         + [pltpu.VMEM(sent_shape, BF16), pltpu.SemaphoreType.DMA(())],
-        compiler_params=params(INNER_VMEM),
+        compiler_params=params(MIDDLES_VMEM),
         cost_estimate=cost(0, 4 * 2**20),
-        name="inner",
-    )(preact, upstream, first, last, share)
+        name="middles",
+    )(preact, upstream, first, last, share, *before)
+    return g, side_rows, swap, sent
 
 
 def is_odd(axis):

time: 42.8 us -> 42.6 us (level)
  Pallas kernels: 17.2 us -> 17.9 us
  starting transfers between devices: 20.4 us -> 19.7 us
    ppermute x4, starting transfers between devices: 11.6 us -> 9.29 us  [swapped(): return lax.ppermute(value, axis, pairs)]
    all_to_all x1, starting transfers between devices: 4.83 us -> 6.28 us  [pair_program(): kernel = lax.all_to_all(sent, AXES, 0, 0, tiled=True)]
    pallas_call x1 -> x2, Pallas kernels: 2.63 us -> 3.33 us  [the longest x1 2.47 us: pair_inner(): pl.pallas_call(functools.partial(ends_kernel, order), in_specs=[HBM] * 2...]
  transfers between devices with their start and end apart: 7 -> 7, of which waited for: 2 -> 2; matrix products, arithmetic and copies ran while one was open for 0% -> 0% of each run, Pallas kernels for 34% -> 36%
where the time goes in v12:
time: 42.6 us; the launch traced here: 42.3 us
  starting transfers between devices  19.7 us (46%)
  Pallas kernels  17.9 us (42%)
  waiting for transfers between devices  3.93 us (9%)
  between operations  0.78 us (2%)
    ppermute x4, starting transfers between devices, swapped(): return lax.ppermute(value, axis, pairs)  9.29 us
    all_to_all x1, starting transfers between devices, pair_program(): kernel = lax.all_to_all(sent, AXES, 0, 0, tiled=True)  6.28 us
    pallas_call x1, Pallas kernels, pair_dgrad(): pl.pallas_call(pair_dgrad_kernel, in_specs=[VMEM] * 10, out_specs=VMEM, o...  5.08 us
    all_to_all x1, starting transfers between devices, pair_program(): parts = lax.all_to_all(part, AXES, 0, 0, tiled=True)  3.79 us
    all_to_all x1, waiting for transfers between devices, pair_program(): parts = lax.all_to_all(part, AXES, 0, 0, tiled=True)  3.78 us
    pallas_call x1, Pallas kernels, pair_wgrad(): pl.pallas_call(pair_wgrad_kernel, in_specs=[VMEM] * 8, out_specs=VMEM, ou...  3.45 us
    pallas_call x1, Pallas kernels, pair_inner(): pl.pallas_call(functools.partial(ends_kernel, order), in_specs=[HBM] * 2...  2.47 us
    pallas_call x1, Pallas kernels, finish(): pl.pallas_call(functools.partial(finish_kernel, scale, rows, sizes), in_s...  1.36 us
  transfers between devices with their start and end apart: 7, of which 2 were waited for; matrix products, arithmetic and copies ran while one was open for 0% of the time, Pallas kernels for 36%

profile of v12, /device:TPU:0, one launch (start us, length us, event | category | flops | bytes accessed | tf_op | source)
XLA Modules:
  0.0 42.3 jit_solution(11578884779961355334)
XLA Ops:
  0.6 1.3 %faces.1 = (bf16[64,1024]{1,0:T(8,128)(2,1)S(1)}, bf16[64,1024]{1,0:T(8,128)(2,1)S(1)}, bf16[64,1024]{1,0:T(8,128)(2,1)S(1)}) custom-call(bf16[64,8,8,128]{3,2,1,0:T(8,128)(2,1)} %refs_0_.3, bf16[64,8,8,128]{3,2,1,0:T(8,128)(2,1)} %refs_1_.3), custom_call_target="tpu_custom_call" | custom-call | bytes 1048576 | tf_op jit(solution)/shard_map/faces/pallas_call | solution.py:93
  2.0 0.7 %collective-permute-start = (bf16[64,1024]{1,0:T(8,128)(2,1)S(1)}, bf16[64,1024]{1,0:T(8,128)(2,1)S(1)}, u32[]{:S(2)}, u32[]{:S(2)}) collective-permute-start(bf16[64,1024]{1,0:T(8,128)(2,1)S(1)} %get-tuple-element.29), channel_id=1, source_target_pairs={{8,16},{16,8},{9,17},{17,9},{10,18},{18,10},{11,19},{19,11},{12,20... | collective-permute-start | bytes 393224 | tf_op jit(solution)/shard_map/ppermute | solution.py:1065
  2.6 0.0 copy-start.1
  2.7 2.5 %ends.1 = (bf16[6,64,1024]{2,1,0:T(8,128)(2,1)S(1)}, bf16[10,64,128]{2,1,0:T(8,128)(2,1)S(1)}, bf16[64,1024]{1,0:T(8,128)(2,1)S(1)}) custom-call(bf16[64,8,8,128]{3,2,1,0:T(8,128)(2,1)} %refs_0_.3, bf16[64,8,8,128]{3,2,1,0:T(8,128)(2,1)} %refs_1_.3, bf16[64,1024]{1,0:T(8,128)(2,1)S(1)} %get-tuple-element.30.refs_2_.refs_1_, ...), custom_call_target="tpu_custom_call" | custom-call | bytes 1048576 | tf_op jit(solution)/shard_map/ends/pallas_call | solution.py:515
  5.1 3.4 %collective-permute-start.1 = (bf16[64,1024]{1,0:T(8,128)(2,1)S(1)}, bf16[64,1024]{1,0:T(8,128)(2,1)S(1)}, u32[]{:S(2)}, u32[]{:S(2)}) collective-permute-start(bf16[64,1024]{1,0:T(8,128)(2,1)S(1)} %get-tuple-element.32), channel_id=1, source_target_pairs={{0,8},{8,0},{16,24},{24,16},{1,9},{9,1},{17,25},{25,17},{2,10},{10... | collective-permute-start | bytes 393224 | tf_op jit(solution)/shard_map/ppermute | solution.py:1065
  8.5 0.0 copy-done.1
  8.5 0.9 %middles.1 = (bf16[6,64,1024]{2,1,0:T(8,128)(2,1)S(1)}, bf16[10,64,128]{2,1,0:T(8,128)(2,1)S(1)}, bf16[32,4,896]{2,1,0:T(4,128)(2,1)}) custom-call(bf16[64,8,8,128]{3,2,1,0:T(8,128)(2,1)} %refs_0_.3, bf16[64,8,8,128]{3,2,1,0:T(8,128)(2,1)} %refs_1_.3, bf16[64,1024]{1,0:T(8,128)(2,1)S(1)} %get-tuple-element.30.refs_2_.refs_1_, ...), custom_call_target="tpu_custom_call" | custom-call | bytes 4194304 | tf_op jit(solution)/shard_map/middles/pallas_call | solution.py:525
  9.4 6.3 %all-to-all-start = ((bf16[32,4,896]{2,1,0:T(4,128)(2,1)}), bf16[32,4,896]{2,1,0:T(4,128)(2,1)S(1)}, u32[]{:S(2)}, u32[]{:S(2)}) async-start(bf16[32,4,896]{2,1,0:T(4,128)(2,1)} %get-tuple-element.46), calls=%async_computation | async-start | bytes 458752 | tf_op jit(solution)/shard_map/all_to_all | solution.py:894
  15.7 0.0 collective-permute-done.odd_ref
  15.7 0.0 collective-permute-done.1.even_ref
  15.7 0.2 side.1
  16.0 0.3 collective-permute-start.2
  16.3 0.0 copy-done
  16.3 1.0 %inputs.1 = (bf16[8,64,1024]{2,1,0:T(8,128)(2,1)S(1)}, bf16[64,128]{1,0:T(8,128)(2,1)S(1)}) custom-call(bf16[64,8,8,128]{3,2,1,0:T(8,128)(2,1)S(1)} %copy-done), custom_call_target="tpu_custom_call" | custom-call | bytes 2097152 | tf_op jit(solution)/shard_map/inputs/pallas_call | solution.py:182
  17.3 0.1 collective-permute-done.2.other_ref.refs_5_.refs_6_
  17.5 0.1 join.1
  17.6 0.7 %collective-permute-start.3 = (bf16[3,64,128]{2,1,0:T(8,128)(2,1)S(1)}, bf16[3,64,128]{2,1,0:T(8,128)(2,1)S(1)}, u32[]{:S(2)}, u32[]{:S(2)}) collective-permute-start(bf16[3,64,128]{2,1,0:T(8,128)(2,1)S(1)} %get-tuple-element.43.refs_3_), channel_id=1, source_target_pairs={{1,2},{2,1},{5,6},{6,5},{9,10},{10,9},{13,14},{14,13},{17,18},{18,... | collective-permute-start | bytes 147464 | tf_op jit(solution)/shard_map/ppermute | solution.py:1065
  18.2 4.5 %collective-permute-start.4 = (bf16[3,64,128]{2,1,0:T(8,128)(2,1)S(1)}, bf16[3,64,128]{2,1,0:T(8,128)(2,1)S(1)}, u32[]{:S(2)}, u32[]{:S(2)}) collective-permute-start(bf16[3,64,128]{2,1,0:T(8,128)(2,1)S(1)} %get-tuple-element.44.refs_2_), channel_id=1, source_target_pairs={{0,1},{1,0},{2,3},{3,2},{4,5},{5,4},{6,7},{7,6},{8,9},{9,8},{10,11... | collective-permute-start | bytes 147464 | tf_op jit(solution)/shard_map/ppermute | solution.py:1065
  22.8 3.5 %wgrad.1.refs_0_ = f32[576,192]{1,0:T(8,128)S(1)} custom-call(bf16[64,1024]{1,0:T(8,128)(2,1)S(1)} %get-tuple-element.36.refs_0_, bf16[64,1024]{1,0:T(8,128)(2,1)S(1)} %get-tuple-element.30.refs_2_.refs_1_, bf16[6,64,1024]{2,1,0:T(8,128)(2,1)S(1)} %get-tuple-element.37.refs_2_, bf16[64,1024]{1,0:T(8,128)(2,1)S(1)} %get-tuple-element.31.refs_3_, ...), custom_call_target="tpu_custom_call" | custom-call | flops 2264924160 | bytes 4194304 | tf_op jit(solution)/shard_map/wgrad/pallas_call | solution.py:643
  26.2 0.0 collective-permute-done.3.refs_4_.refs_7_
  26.3 0.0 collective-permute-done.4.refs_5_.refs_8_
  26.3 1.4 %finish.1 = bf16[32,4,896]{2,1,0:T(4,128)(2,1)} custom-call(f32[576,192]{1,0:T(8,128)S(1)} %wgrad.1.refs_0_, bf16[64,128]{1,0:T(8,128)(2,1)S(1)} %get-tuple-element.42.columns_ref.refs_1_, bf16[3,64,128]{2,1,0:T(8,128)(2,1)S(1)} %get-tuple-element.44.refs_2_, bf16[3,64,128]{2,1,0:T(8,128)(2,1)S(1)} %get-tuple-element.43.refs_3_, ...), custom_call_target="tpu_custom_call" | custom-call | flops 134217728 | bytes 2097152 | tf_op jit(solution)/shard_map/finish/pallas_call | solution.py:721
  27.6 0.0 all-to-all-done.w_ref
  27.6 3.8 %all-to-all-start.1 = ((bf16[32,4,896]{2,1,0:T(4,128)(2,1)}), bf16[32,4,896]{2,1,0:T(4,128)(2,1)S(1)}, u32[]{:S(2)}, u32[]{:S(2)}) async-start(bf16[32,4,896]{2,1,0:T(4,128)(2,1)} %finish.1), calls=%async_computation.1 | async-start | bytes 458752 | tf_op jit(solution)/shard_map/all_to_all | solution.py:908
  31.4 0.7 %spread.1.refs_9_ = bf16[3,128,768]{2,1,0:T(8,128)(2,1)S(1)} custom-call(bf16[32,4,896]{2,1,0:T(4,128)(2,1)S(1)} %all-to-all-done.w_ref), custom_call_target="tpu_custom_call" | custom-call | flops 1048576 | bytes 2097152 | tf_op jit(solution)/shard_map/spread/pallas_call | solution.py:845
  32.1 0.0 copy-start.2
  32.2 0.0 copy-start.3
  32.2 5.1 %dgrad.1 = bf16[64,8,8,128]{3,2,1,0:T(8,128)(2,1)} custom-call(bf16[64,1024]{1,0:T(8,128)(2,1)S(1)} %get-tuple-element.36.refs_0_, bf16[64,1024]{1,0:T(8,128)(2,1)S(1)} %get-tuple-element.30.refs_2_.refs_1_, bf16[6,64,1024]{2,1,0:T(8,128)(2,1)S(1)} %get-tuple-element.37.refs_2_, bf16[64,1024]{1,0:T(8,128)(2,1)S(1)} %get-tuple-element.31.refs_3_, ...), custom_call_target="tpu_custom_call" | custom-call | flops 2415919104 | bytes 4194304 | tf_op jit(solution)/shard_map/dgrad/pallas_call | solution.py:869
  37.3 3.8 %all-to-all-done.1.parts_ref = bf16[32,4,896]{2,1,0:T(4,128)(2,1)S(1)} async-done(((bf16[32,4,896]{2,1,0:T(4,128)(2,1)}), bf16[32,4,896]{2,1,0:T(4,128)(2,1)S(1)}, u32[]{:S(2)}, u32[]{:S(2)}) %all-to-all-start.1) | async-done | bytes 229408 | tf_op jit(solution)/shard_map/all_to_all | solution.py:908
  41.0 0.0 copy-done.2
  41.0 0.0 copy-done.3
  41.0 1.2 %adam.1 = (f32[27,128]{1,0:T(8,128)}, f32[27,128]{1,0:T(8,128)}, f32[27,128]{1,0:T(8,128)}, f32[27,128]{1,0:T(8,128)}) custom-call(bf16[32,4,896]{2,1,0:T(4,128)(2,1)S(1)} %all-to-all-done.1.parts_ref, f32[27,128]{1,0:T(8,128)S(1)} %bitcast.8, f32[27,128]{1,0:T(8,128)S(1)} %bitcast.9, f32[27,128]{1,0:T(8,128)S(1)} %bitcast.10), custom_call_target="tpu_custom_call" | custom-call | flops 4194304 | bytes 524288 | tf_op jit(solution)/shard_map/adam/pallas_call | solution.py:810
  (1 shorter events, 0.0 us)
Async XLA Ops:
  2.0 13.7 %collective-permute-start = (bf16[64,1024]{1,0:T(8,128)(2,1)S(1)}, bf16[64,1024]{1,0:T(8,128)(2,1)S(1)}, u32[]{:S(2)}, u32[]{:S(2)}) collective-permute-start(bf16[64,1024]{1,0:T(8,128)(2,1)S(1)} %get-tuple-element.29), channel_id=1, source_target_pairs={{8,16},{16,8},{9,17},{17,9},{10,18},{18,10},{11,19},{19,11},{12,20... | collective-permute-start | bytes 393224 | tf_op jit(solution)/shard_map/ppermute | solution.py:1065
  2.6 5.9 %copy-start.1 = (f32[3456]{0:T(1024)S(1)}, f32[3456]{0:T(1024)}, u32[]{:S(2)}) copy-start(f32[3456]{0:T(1024)} %param.9) | copy-start | bytes 41476
  5.1 10.6 %collective-permute-start.1 = (bf16[64,1024]{1,0:T(8,128)(2,1)S(1)}, bf16[64,1024]{1,0:T(8,128)(2,1)S(1)}, u32[]{:S(2)}, u32[]{:S(2)}) collective-permute-start(bf16[64,1024]{1,0:T(8,128)(2,1)S(1)} %get-tuple-element.32), channel_id=1, source_target_pairs={{0,8},{8,0},{16,24},{24,16},{1,9},{9,1},{17,25},{25,17},{2,10},{10... | collective-permute-start | bytes 393224 | tf_op jit(solution)/shard_map/ppermute | solution.py:1065
  8.5 7.7 %copy-start = (bf16[64,8,8,128]{3,2,1,0:T(8,128)(2,1)S(1)}, bf16[64,8,8,128]{3,2,1,0:T(8,128)(2,1)}, u32[]{:S(2)}) copy-start(bf16[64,8,8,128]{3,2,1,0:T(8,128)(2,1)} %a_ref) | copy-start | bytes 3145732
  9.4 18.2 %all-to-all-start = ((bf16[32,4,896]{2,1,0:T(4,128)(2,1)}), bf16[32,4,896]{2,1,0:T(4,128)(2,1)S(1)}, u32[]{:S(2)}, u32[]{:S(2)}) async-start(bf16[32,4,896]{2,1,0:T(4,128)(2,1)} %get-tuple-element.46), calls=%async_computation | async-start | bytes 458752 | tf_op jit(solution)/shard_map/all_to_all | solution.py:894
  16.0 1.5 %collective-permute-start.2 = (bf16[12,64,128]{2,1,0:T(8,128)(2,1)S(1)}, bf16[12,64,128]{2,1,0:T(8,128)(2,1)S(1)}, u32[]{:S(2)}, u32[]{:S(2)}) collective-permute-start(bf16[12,64,128]{2,1,0:T(8,128)(2,1)S(1)} %get-tuple-element.40.own_ref), channel_id=1, source_target_pairs={{0,4},{4,0},{1,5},{5,1},{2,6},{6,2},{3,7},{7,3},{8,12},{12,8},{9,1... | collective-permute-start | bytes 589832 | tf_op jit(solution)/shard_map/ppermute | solution.py:1058
  17.6 8.7 %collective-permute-start.3 = (bf16[3,64,128]{2,1,0:T(8,128)(2,1)S(1)}, bf16[3,64,128]{2,1,0:T(8,128)(2,1)S(1)}, u32[]{:S(2)}, u32[]{:S(2)}) collective-permute-start(bf16[3,64,128]{2,1,0:T(8,128)(2,1)S(1)} %get-tuple-element.43.refs_3_), channel_id=1, source_target_pairs={{1,2},{2,1},{5,6},{6,5},{9,10},{10,9},{13,14},{14,13},{17,18},{18,... | collective-permute-start | bytes 147464 | tf_op jit(solution)/shard_map/ppermute | solution.py:1065
  18.2 8.0 %collective-permute-start.4 = (bf16[3,64,128]{2,1,0:T(8,128)(2,1)S(1)}, bf16[3,64,128]{2,1,0:T(8,128)(2,1)S(1)}, u32[]{:S(2)}, u32[]{:S(2)}) collective-permute-start(bf16[3,64,128]{2,1,0:T(8,128)(2,1)S(1)} %get-tuple-element.44.refs_2_), channel_id=1, source_target_pairs={{0,1},{1,0},{2,3},{3,2},{4,5},{5,4},{6,7},{7,6},{8,9},{9,8},{10,11... | collective-permute-start | bytes 147464 | tf_op jit(solution)/shard_map/ppermute | solution.py:1065
  27.6 13.4 %all-to-all-start.1 = ((bf16[32,4,896]{2,1,0:T(4,128)(2,1)}), bf16[32,4,896]{2,1,0:T(4,128)(2,1)S(1)}, u32[]{:S(2)}, u32[]{:S(2)}) async-start(bf16[32,4,896]{2,1,0:T(4,128)(2,1)} %finish.1), calls=%async_computation.1 | async-start | bytes 458752 | tf_op jit(solution)/shard_map/all_to_all | solution.py:908
  32.1 8.9 %copy-start.2 = (f32[3456]{0:T(1024)S(1)}, f32[3456]{0:T(1024)}, u32[]{:S(2)}) copy-start(f32[3456]{0:T(1024)} %param.10) | copy-start | bytes 41476
  32.2 8.9 %copy-start.3 = (f32[3456]{0:T(1024)S(1)}, f32[3456]{0:T(1024)}, u32[]{:S(2)}) copy-start(f32[3456]{0:T(1024)} %param.11) | copy-start | bytes 41476

commit v13 on v12

--- a/solution.py
+++ b/solution.py
@@ -17,7 +17,7 @@
 FACES_VMEM = 55_900_000
 INNER_VMEM = 54_800_000
 ENDS_VMEM = 54_800_000
-MIDDLES_VMEM = 53_600_000
+MIDDLES_VMEM = 54_600_000
 
 
 def params(limit=24 * 2**20):
@@ -107,30 +107,38 @@
     )(preact, upstream)
 
 
-def read_inner(rows, p_ref, u_ref, g_ref, p_buf, u_buf, tile, sems):
-    size_x, size_z = p_ref.shape[1], p_ref.shape[3]
-    inner = size_x - 2
+def fetch(planes, p_ref, u_ref, p_buf, u_buf, sems):
     copies = []
-    for x in range(inner):
+    for x in planes:
         pair = (
-            pltpu.make_async_copy(p_ref.at[:, x + 1], p_buf.at[x], sems.at[x]),
-            pltpu.make_async_copy(u_ref.at[:, x + 1], u_buf.at[x], sems.at[inner + x]),
+            pltpu.make_async_copy(p_ref.at[:, x + 1], p_buf.at[x], sems.at[2 * x]),
+            pltpu.make_async_copy(u_ref.at[:, x + 1], u_buf.at[x], sems.at[2 * x + 1]),
         )
         for copy in pair:
             copy.start()
         copies.append(pair)
-    for x in range(inner):
-        for copy in copies[x]:
+    return copies
+
+
+def settle(order, planes, copies, g_ref, p_buf, u_buf, tile):
+    size_z = p_buf.shape[-1]
+    for x, pair in zip(planes, copies):
+        for copy in pair:
             copy.wait()
 
         def write(at, y, value):
             g_ref[x, at, y * size_z : (y + 1) * size_z] = value
 
-        to_planes(masked(p_buf[x], u_buf[x]), tile.at[x % 2], write, rows)
+        to_planes(masked(p_buf[x], u_buf[x]), tile.at[x % 2], write, order)
+
+
+def read_inner(order, planes, p_ref, u_ref, g_ref, p_buf, u_buf, tile, sems):
+    copies = fetch(planes, p_ref, u_ref, p_buf, u_buf, sems)
+    settle(order, planes, copies, g_ref, p_buf, u_buf, tile)
 
 
 def inner_kernel(*refs):
-    read_inner(1, *refs)
+    read_inner(1, range(refs[2].shape[0]), *refs)
 
 
 def inner_output(channels, size_x, size_y, size_z):
@@ -453,10 +461,45 @@
     return (me > 0) & (me < count - 1 + count % 2)
 
 
-def own_planes(order, p_ref, u_ref, first_ref, last_ref, g_ref, side_ref, *scratch):
-    read_inner(order, p_ref, u_ref, g_ref, *scratch)
+def ends_kernel(order, *refs):
+    choose(is_odd("gx"), refs[5], refs[2], refs[3])
+
+    @pl.when(jnp.logical_not(in_odd_swaps("gx")))
+    def _():
+        read_inner(order, range(refs[4].shape[0]), *refs[:2], refs[4], *refs[6:])
+
+
+def middles_kernel(order, *refs):
+    p_ref, u_ref, first_ref, last_ref, m_ref, before_ref, g_ref, side_ref, sent_ref = refs[:9]
+    p_buf, u_buf, tile, sems, sent_buf, sent_sem = refs[9:]
+    half = before_ref.shape[0]
+    inner, _, plane = g_ref.shape
+    later = range(half, inner)
+    copies = fetch(later, p_ref, u_ref, p_buf, u_buf, sems)
+    share = m_ref[...]
+    share = jnp.concatenate(
+        [share, jnp.zeros((-share.shape[0] % QUAD, share.shape[1]), F32)], axis=0
+    )
+
+    def write(at, quad):
+        quad = quad.astype(BF16)
+        sent_buf[:, :, at] = jnp.broadcast_to(quad[None], (sent_buf.shape[0], *quad.shape))
+
+    to_quads(share, write)
+    send = pltpu.make_async_copy(sent_buf, sent_ref, sent_sem)
+    send.start()
+    middle = in_odd_swaps("gx")
+
+    @pl.when(middle)
+    def _():
+        read_inner(order, range(half), p_ref, u_ref, g_ref, p_buf, u_buf, tile, sems)
+
+    @pl.when(jnp.logical_not(middle))
+    def _():
+        g_ref[:half] = before_ref[...]
+
+    settle(order, later, copies, g_ref, p_buf, u_buf, tile)
     size_z = side_ref.shape[-1]
-    inner, _, plane = g_ref.shape
     size_x = inner + 2
     bodies = [first_ref] + [g_ref.at[x] for x in range(inner)] + [last_ref]
     for x, body in enumerate(bodies):
@@ -466,42 +509,6 @@
     )
     side_ref[size_x] = low.astype(BF16)
     side_ref[size_x + 1] = high.astype(BF16)
-
-
-def ends_kernel(order, *refs):
-    choose(is_odd("gx"), refs[6], refs[2], refs[3])
-
-    @pl.when(jnp.logical_not(in_odd_swaps("gx")))
-    def _():
-        own_planes(order, *refs[:6], *refs[7:])
-
-
-def middles_kernel(order, *refs):
-    m_ref, g_before_ref, side_before_ref, g_ref, side_ref, sent_ref = refs[4:10]
-    sent_buf, sent_sem = refs[14:]
-    share = m_ref[...]
-    share = jnp.concatenate(
-        [share, jnp.zeros((-share.shape[0] % QUAD, share.shape[1]), F32)], axis=0
-    )
-
-    def write(at, quad):
-        quad = quad.astype(BF16)
-        sent_buf[:, :, at] = jnp.broadcast_to(quad[None], (sent_buf.shape[0], *quad.shape))
-
-    to_quads(share, write)
-    send = pltpu.make_async_copy(sent_buf, sent_ref, sent_sem)
-    send.start()
-    middle = in_odd_swaps("gx")
-
-    @pl.when(middle)
-    def _():
-        own_planes(order, *refs[:4], g_ref, side_ref, *refs[10:14])
-
-    @pl.when(jnp.logical_not(middle))
-    def _():
-        g_ref[...] = g_before_ref[...]
-        side_ref[...] = side_before_ref[...]
-
     send.wait()
 
 
@@ -512,11 +519,12 @@
         inner_output(*shape),
         jax.ShapeDtypeStruct((size_x + 2, channels, size_z), BF16),
     ]
-    *before, swap = pl.pallas_call(
+    half = jax.ShapeDtypeStruct((made[0].shape[0] // 2, *made[0].shape[1:]), BF16)
+    before, swap = pl.pallas_call(
         functools.partial(ends_kernel, order),
         in_specs=[HBM] * 2 + [VMEM] * 2,
-        out_specs=[VMEM] * 3,
-        out_shape=made + [jax.ShapeDtypeStruct(first.shape, BF16)],
+        out_specs=[VMEM] * 2,
+        out_shape=[half, jax.ShapeDtypeStruct(first.shape, BF16)],
         scratch_shapes=inner_scratch(*shape),
         compiler_params=params(ENDS_VMEM),
         cost_estimate=cost(0, 2**20),
@@ -524,7 +532,7 @@
     )(preact, upstream, first, last)
     g, side_rows, sent = pl.pallas_call(
         functools.partial(middles_kernel, order),
-        in_specs=[HBM] * 2 + [VMEM] * 5,
+        in_specs=[HBM] * 2 + [VMEM] * 4,
         out_specs=[VMEM] * 2 + [HBM],
         out_shape=made + [jax.ShapeDtypeStruct(sent_shape, BF16)],
         scratch_shapes=inner_scratch(*shape)
@@ -532,7 +540,7 @@
         compiler_params=params(MIDDLES_VMEM),
         cost_estimate=cost(0, 4 * 2**20),
         name="middles",
-    )(preact, upstream, first, last, share, *before)
+    )(preact, upstream, first, last, share, before)
     return g, side_rows, swap, sent
 
 

time: 42.6 us -> 42.4 us (level)
  starting transfers between devices: 19.7 us -> 19.1 us
    all_to_all x1, starting transfers between devices: 6.28 us -> 4.84 us  [pair_program(): kernel = lax.all_to_all(sent, AXES, 0, 0, tiled=True)]
    pallas_call x1, Pallas kernels: 0.86 us -> 2.13 us  [pair_inner(): pl.pallas_call(functools.partial(middles_kernel, order), in_specs=[HBM] *...]
    pallas_call x1, Pallas kernels: 2.47 us -> 1.58 us  [pair_inner(): pl.pallas_call(functools.partial(ends_kernel, order), in_specs=[HBM] * 2...]
    ppermute x4, starting transfers between devices: 9.29 us -> 10.2 us  [swapped(): return lax.ppermute(value, axis, pairs)]
  transfers between devices with their start and end apart: 7 -> 7, of which waited for: 2 -> 2; matrix products, arithmetic and copies ran while one was open for 0% -> 0% of each run, Pallas kernels for 36% -> 37%
where the time goes in v13:
time: 42.4 us; the launch traced here: 42.1 us
  starting transfers between devices  19.1 us (45%)
  Pallas kernels  18.2 us (43%)
  waiting for transfers between devices  3.94 us (9%)
  between operations  0.78 us (2%)
    ppermute x4, starting transfers between devices, swapped(): return lax.ppermute(value, axis, pairs)  10.2 us
    pallas_call x1, Pallas kernels, pair_dgrad(): pl.pallas_call(pair_dgrad_kernel, in_specs=[VMEM] * 10, out_specs=VMEM, o...  5.08 us
    all_to_all x1, starting transfers between devices, pair_program(): kernel = lax.all_to_all(sent, AXES, 0, 0, tiled=True)  4.84 us
    all_to_all x1, waiting for transfers between devices, pair_program(): parts = lax.all_to_all(part, AXES, 0, 0, tiled=True)  3.79 us
    all_to_all x1, starting transfers between devices, pair_program(): parts = lax.all_to_all(part, AXES, 0, 0, tiled=True)  3.78 us
    pallas_call x1, Pallas kernels, pair_wgrad(): pl.pallas_call(pair_wgrad_kernel, in_specs=[VMEM] * 8, out_specs=VMEM, ou...  3.45 us
    pallas_call x1, Pallas kernels, pair_inner(): pl.pallas_call(functools.partial(middles_kernel, order), in_specs=[HBM] *...  2.13 us
    pallas_call x1, Pallas kernels, pair_inner(): pl.pallas_call(functools.partial(ends_kernel, order), in_specs=[HBM] * 2...  1.58 us
  transfers between devices with their start and end apart: 7, of which 2 were waited for; matrix products, arithmetic and copies ran while one was open for 0% of the time, Pallas kernels for 37%

profile of v13, /device:TPU:0, one launch (start us, length us, event | category | flops | bytes accessed | tf_op | source)
XLA Modules:
  0.0 42.1 jit_solution(300122910290607468)
XLA Ops:
  0.6 1.3 %faces.1 = (bf16[64,1024]{1,0:T(8,128)(2,1)S(1)}, bf16[64,1024]{1,0:T(8,128)(2,1)S(1)}, bf16[64,1024]{1,0:T(8,128)(2,1)S(1)}) custom-call(bf16[64,8,8,128]{3,2,1,0:T(8,128)(2,1)} %refs_0_.3, bf16[64,8,8,128]{3,2,1,0:T(8,128)(2,1)} %refs_1_.3), custom_call_target="tpu_custom_call" | custom-call | bytes 1048576 | tf_op jit(solution)/shard_map/faces/pallas_call | solution.py:93
  2.0 0.7 %collective-permute-start = (bf16[64,1024]{1,0:T(8,128)(2,1)S(1)}, bf16[64,1024]{1,0:T(8,128)(2,1)S(1)}, u32[]{:S(2)}, u32[]{:S(2)}) collective-permute-start(bf16[64,1024]{1,0:T(8,128)(2,1)S(1)} %get-tuple-element.28), channel_id=1, source_target_pairs={{8,16},{16,8},{9,17},{17,9},{10,18},{18,10},{11,19},{19,11},{12,20... | collective-permute-start | bytes 393224 | tf_op jit(solution)/shard_map/ppermute | solution.py:1073
  2.6 0.0 copy-start.1
  2.7 1.6 %ends.1 = (bf16[3,64,1024]{2,1,0:T(8,128)(2,1)S(1)}, bf16[64,1024]{1,0:T(8,128)(2,1)S(1)}) custom-call(bf16[64,8,8,128]{3,2,1,0:T(8,128)(2,1)} %refs_0_.3, bf16[64,8,8,128]{3,2,1,0:T(8,128)(2,1)} %refs_1_.3, bf16[64,1024]{1,0:T(8,128)(2,1)S(1)} %get-tuple-element.29.refs_2_.refs_1_, bf16[64,1024]{1,0:T(8,128)(2,1)S(1)} %get-tuple-element.30.refs_3_), custom_call_target="tpu_custom_call" | custom-call | bytes 1048576 | tf_op jit(solution)/shard_map/ends/pallas_call | solution.py:523
  4.2 4.3 %collective-permute-start.1 = (bf16[64,1024]{1,0:T(8,128)(2,1)S(1)}, bf16[64,1024]{1,0:T(8,128)(2,1)S(1)}, u32[]{:S(2)}, u32[]{:S(2)}) collective-permute-start(bf16[64,1024]{1,0:T(8,128)(2,1)S(1)} %get-tuple-element.31), channel_id=1, source_target_pairs={{0,8},{8,0},{16,24},{24,16},{1,9},{9,1},{17,25},{25,17},{2,10},{10... | collective-permute-start | bytes 393224 | tf_op jit(solution)/shard_map/ppermute | solution.py:1073
  8.5 0.0 copy-done.1
  8.5 2.1 %middles.1 = (bf16[6,64,1024]{2,1,0:T(8,128)(2,1)S(1)}, bf16[10,64,128]{2,1,0:T(8,128)(2,1)S(1)}, bf16[32,4,896]{2,1,0:T(4,128)(2,1)}) custom-call(bf16[64,8,8,128]{3,2,1,0:T(8,128)(2,1)} %refs_0_.3, bf16[64,8,8,128]{3,2,1,0:T(8,128)(2,1)} %refs_1_.3, bf16[64,1024]{1,0:T(8,128)(2,1)S(1)} %get-tuple-element.29.refs_2_.refs_1_, ...), custom_call_target="tpu_custom_call" | custom-call | bytes 4194304 | tf_op jit(solution)/shard_map/middles/pallas_call | solution.py:533
  10.7 4.8 %all-to-all-start = ((bf16[32,4,896]{2,1,0:T(4,128)(2,1)}), bf16[32,4,896]{2,1,0:T(4,128)(2,1)S(1)}, u32[]{:S(2)}, u32[]{:S(2)}) async-start(bf16[32,4,896]{2,1,0:T(4,128)(2,1)} %get-tuple-element.44), calls=%async_computation | async-start | bytes 458752 | tf_op jit(solution)/shard_map/all_to_all | solution.py:902
  15.5 0.0 collective-permute-done.odd_ref
  15.5 0.0 collective-permute-done.1.even_ref
  15.5 0.2 side.1
  15.8 0.3 collective-permute-start.2
  16.1 0.0 copy-done
  16.1 1.0 %inputs.1 = (bf16[8,64,1024]{2,1,0:T(8,128)(2,1)S(1)}, bf16[64,128]{1,0:T(8,128)(2,1)S(1)}) custom-call(bf16[64,8,8,128]{3,2,1,0:T(8,128)(2,1)S(1)} %copy-done), custom_call_target="tpu_custom_call" | custom-call | bytes 2097152 | tf_op jit(solution)/shard_map/inputs/pallas_call | solution.py:190
  17.2 0.1 collective-permute-done.2.other_ref.refs_5_.refs_6_
  17.3 0.1 join.1
  17.4 0.7 %collective-permute-start.3 = (bf16[3,64,128]{2,1,0:T(8,128)(2,1)S(1)}, bf16[3,64,128]{2,1,0:T(8,128)(2,1)S(1)}, u32[]{:S(2)}, u32[]{:S(2)}) collective-permute-start(bf16[3,64,128]{2,1,0:T(8,128)(2,1)S(1)} %get-tuple-element.41.refs_3_), channel_id=1, source_target_pairs={{1,2},{2,1},{5,6},{6,5},{9,10},{10,9},{13,14},{14,13},{17,18},{18,... | collective-permute-start | bytes 147464 | tf_op jit(solution)/shard_map/ppermute | solution.py:1073
  18.1 4.5 %collective-permute-start.4 = (bf16[3,64,128]{2,1,0:T(8,128)(2,1)S(1)}, bf16[3,64,128]{2,1,0:T(8,128)(2,1)S(1)}, u32[]{:S(2)}, u32[]{:S(2)}) collective-permute-start(bf16[3,64,128]{2,1,0:T(8,128)(2,1)S(1)} %get-tuple-element.42.refs_2_), channel_id=1, source_target_pairs={{0,1},{1,0},{2,3},{3,2},{4,5},{5,4},{6,7},{7,6},{8,9},{9,8},{10,11... | collective-permute-start | bytes 147464 | tf_op jit(solution)/shard_map/ppermute | solution.py:1073
  22.6 3.5 %wgrad.1.refs_0_ = f32[576,192]{1,0:T(8,128)S(1)} custom-call(bf16[64,1024]{1,0:T(8,128)(2,1)S(1)} %get-tuple-element.34.refs_0_, bf16[64,1024]{1,0:T(8,128)(2,1)S(1)} %get-tuple-element.29.refs_2_.refs_1_, bf16[6,64,1024]{2,1,0:T(8,128)(2,1)S(1)} %get-tuple-element.35.refs_2_, bf16[64,1024]{1,0:T(8,128)(2,1)S(1)} %get-tuple-element.30.refs_3_, ...), custom_call_target="tpu_custom_call" | custom-call | flops 2264924160 | bytes 4194304 | tf_op jit(solution)/shard_map/wgrad/pallas_call | solution.py:651
  26.1 0.0 collective-permute-done.3.refs_4_.refs_7_
  26.1 0.0 collective-permute-done.4.refs_5_.refs_8_
  26.1 1.4 %finish.1 = bf16[32,4,896]{2,1,0:T(4,128)(2,1)} custom-call(f32[576,192]{1,0:T(8,128)S(1)} %wgrad.1.refs_0_, bf16[64,128]{1,0:T(8,128)(2,1)S(1)} %get-tuple-element.40.columns_ref.refs_1_, bf16[3,64,128]{2,1,0:T(8,128)(2,1)S(1)} %get-tuple-element.42.refs_2_, bf16[3,64,128]{2,1,0:T(8,128)(2,1)S(1)} %get-tuple-element.41.refs_3_, ...), custom_call_target="tpu_custom_call" | custom-call | flops 134217728 | bytes 2097152 | tf_op jit(solution)/shard_map/finish/pallas_call | solution.py:729
  27.4 0.0 all-to-all-done.w_ref
  27.5 3.8 %all-to-all-start.1 = ((bf16[32,4,896]{2,1,0:T(4,128)(2,1)}), bf16[32,4,896]{2,1,0:T(4,128)(2,1)S(1)}, u32[]{:S(2)}, u32[]{:S(2)}) async-start(bf16[32,4,896]{2,1,0:T(4,128)(2,1)} %finish.1), calls=%async_computation.1 | async-start | bytes 458752 | tf_op jit(solution)/shard_map/all_to_all | solution.py:916
  31.2 0.7 %spread.1.refs_9_ = bf16[3,128,768]{2,1,0:T(8,128)(2,1)S(1)} custom-call(bf16[32,4,896]{2,1,0:T(4,128)(2,1)S(1)} %all-to-all-done.w_ref), custom_call_target="tpu_custom_call" | custom-call | flops 1048576 | bytes 2097152 | tf_op jit(solution)/shard_map/spread/pallas_call | solution.py:853
  32.0 0.0 copy-start.2
  32.0 0.0 copy-start.3
  32.0 5.1 %dgrad.1 = bf16[64,8,8,128]{3,2,1,0:T(8,128)(2,1)} custom-call(bf16[64,1024]{1,0:T(8,128)(2,1)S(1)} %get-tuple-element.34.refs_0_, bf16[64,1024]{1,0:T(8,128)(2,1)S(1)} %get-tuple-element.29.refs_2_.refs_1_, bf16[6,64,1024]{2,1,0:T(8,128)(2,1)S(1)} %get-tuple-element.35.refs_2_, bf16[64,1024]{1,0:T(8,128)(2,1)S(1)} %get-tuple-element.30.refs_3_, ...), custom_call_target="tpu_custom_call" | custom-call | flops 2415919104 | bytes 4194304 | tf_op jit(solution)/shard_map/dgrad/pallas_call | solution.py:877
  37.1 3.8 %all-to-all-done.1.parts_ref = bf16[32,4,896]{2,1,0:T(4,128)(2,1)S(1)} async-done(((bf16[32,4,896]{2,1,0:T(4,128)(2,1)}), bf16[32,4,896]{2,1,0:T(4,128)(2,1)S(1)}, u32[]{:S(2)}, u32[]{:S(2)}) %all-to-all-start.1) | async-done | bytes 229408 | tf_op jit(solution)/shard_map/all_to_all | solution.py:916
  40.9 0.0 copy-done.2
  40.9 0.0 copy-done.3
  40.9 1.2 %adam.1 = (f32[27,128]{1,0:T(8,128)}, f32[27,128]{1,0:T(8,128)}, f32[27,128]{1,0:T(8,128)}, f32[27,128]{1,0:T(8,128)}) custom-call(bf16[32,4,896]{2,1,0:T(4,128)(2,1)S(1)} %all-to-all-done.1.parts_ref, f32[27,128]{1,0:T(8,128)S(1)} %bitcast.8, f32[27,128]{1,0:T(8,128)S(1)} %bitcast.9, f32[27,128]{1,0:T(8,128)S(1)} %bitcast.10), custom_call_target="tpu_custom_call" | custom-call | flops 4194304 | bytes 524288 | tf_op jit(solution)/shard_map/adam/pallas_call | solution.py:818
  (1 shorter events, 0.0 us)
Async XLA Ops:
  2.0 13.6 %collective-permute-start = (bf16[64,1024]{1,0:T(8,128)(2,1)S(1)}, bf16[64,1024]{1,0:T(8,128)(2,1)S(1)}, u32[]{:S(2)}, u32[]{:S(2)}) collective-permute-start(bf16[64,1024]{1,0:T(8,128)(2,1)S(1)} %get-tuple-element.28), channel_id=1, source_target_pairs={{8,16},{16,8},{9,17},{17,9},{10,18},{18,10},{11,19},{19,11},{12,20... | collective-permute-start | bytes 393224 | tf_op jit(solution)/shard_map/ppermute | solution.py:1073
  2.6 5.9 %copy-start.1 = (f32[3456]{0:T(1024)S(1)}, f32[3456]{0:T(1024)}, u32[]{:S(2)}) copy-start(f32[3456]{0:T(1024)} %param.9) | copy-start | bytes 41476
  4.2 11.3 %collective-permute-start.1 = (bf16[64,1024]{1,0:T(8,128)(2,1)S(1)}, bf16[64,1024]{1,0:T(8,128)(2,1)S(1)}, u32[]{:S(2)}, u32[]{:S(2)}) collective-permute-start(bf16[64,1024]{1,0:T(8,128)(2,1)S(1)} %get-tuple-element.31), channel_id=1, source_target_pairs={{0,8},{8,0},{16,24},{24,16},{1,9},{9,1},{17,25},{25,17},{2,10},{10... | collective-permute-start | bytes 393224 | tf_op jit(solution)/shard_map/ppermute | solution.py:1073
  8.5 7.6 %copy-start = (bf16[64,8,8,128]{3,2,1,0:T(8,128)(2,1)S(1)}, bf16[64,8,8,128]{3,2,1,0:T(8,128)(2,1)}, u32[]{:S(2)}) copy-start(bf16[64,8,8,128]{3,2,1,0:T(8,128)(2,1)} %a_ref) | copy-start | bytes 3145732
  10.7 16.8 %all-to-all-start = ((bf16[32,4,896]{2,1,0:T(4,128)(2,1)}), bf16[32,4,896]{2,1,0:T(4,128)(2,1)S(1)}, u32[]{:S(2)}, u32[]{:S(2)}) async-start(bf16[32,4,896]{2,1,0:T(4,128)(2,1)} %get-tuple-element.44), calls=%async_computation | async-start | bytes 458752 | tf_op jit(solution)/shard_map/all_to_all | solution.py:902
  15.8 1.5 %collective-permute-start.2 = (bf16[12,64,128]{2,1,0:T(8,128)(2,1)S(1)}, bf16[12,64,128]{2,1,0:T(8,128)(2,1)S(1)}, u32[]{:S(2)}, u32[]{:S(2)}) collective-permute-start(bf16[12,64,128]{2,1,0:T(8,128)(2,1)S(1)} %get-tuple-element.38.own_ref), channel_id=1, source_target_pairs={{0,4},{4,0},{1,5},{5,1},{2,6},{6,2},{3,7},{7,3},{8,12},{12,8},{9,1... | collective-permute-start | bytes 589832 | tf_op jit(solution)/shard_map/ppermute | solution.py:1066
  17.4 8.7 %collective-permute-start.3 = (bf16[3,64,128]{2,1,0:T(8,128)(2,1)S(1)}, bf16[3,64,128]{2,1,0:T(8,128)(2,1)S(1)}, u32[]{:S(2)}, u32[]{:S(2)}) collective-permute-start(bf16[3,64,128]{2,1,0:T(8,128)(2,1)S(1)} %get-tuple-element.41.refs_3_), channel_id=1, source_target_pairs={{1,2},{2,1},{5,6},{6,5},{9,10},{10,9},{13,14},{14,13},{17,18},{18,... | collective-permute-start | bytes 147464 | tf_op jit(solution)/shard_map/ppermute | solution.py:1073
  18.1 8.0 %collective-permute-start.4 = (bf16[3,64,128]{2,1,0:T(8,128)(2,1)S(1)}, bf16[3,64,128]{2,1,0:T(8,128)(2,1)S(1)}, u32[]{:S(2)}, u32[]{:S(2)}) collective-permute-start(bf16[3,64,128]{2,1,0:T(8,128)(2,1)S(1)} %get-tuple-element.42.refs_2_), channel_id=1, source_target_pairs={{0,1},{1,0},{2,3},{3,2},{4,5},{5,4},{6,7},{7,6},{8,9},{9,8},{10,11... | collective-permute-start | bytes 147464 | tf_op jit(solution)/shard_map/ppermute | solution.py:1073
  27.5 13.4 %all-to-all-start.1 = ((bf16[32,4,896]{2,1,0:T(4,128)(2,1)}), bf16[32,4,896]{2,1,0:T(4,128)(2,1)S(1)}, u32[]{:S(2)}, u32[]{:S(2)}) async-start(bf16[32,4,896]{2,1,0:T(4,128)(2,1)} %finish.1), calls=%async_computation.1 | async-start | bytes 458752 | tf_op jit(solution)/shard_map/all_to_all | solution.py:916
  32.0 8.9 %copy-start.2 = (f32[3456]{0:T(1024)S(1)}, f32[3456]{0:T(1024)}, u32[]{:S(2)}) copy-start(f32[3456]{0:T(1024)} %param.10) | copy-start | bytes 41476
  32.0 8.9 %copy-start.3 = (f32[3456]{0:T(1024)S(1)}, f32[3456]{0:T(1024)}, u32[]{:S(2)}) copy-start(f32[3456]{0:T(1024)} %param.11) | copy-start | bytes 41476

commit v14 on v13

--- a/solution.py
+++ b/solution.py
@@ -17,7 +17,7 @@
 FACES_VMEM = 55_900_000
 INNER_VMEM = 54_800_000
 ENDS_VMEM = 54_800_000
-MIDDLES_VMEM = 54_600_000
+MIDDLES_VMEM = 53_600_000
 
 
 def params(limit=24 * 2**20):

time: 42.4 us -> 42.6 us (level)
  no operation moved by 1% of the time
where the time goes in v14:
time: 42.6 us; the launch traced here: 42.3 us
  starting transfers between devices  19.3 us (45%)
  Pallas kernels  18.2 us (43%)
  waiting for transfers between devices  3.94 us (9%)
  between operations  0.79 us (2%)
    ppermute x4, starting transfers between devices, swapped(): return lax.ppermute(value, axis, pairs)  10.1 us
    all_to_all x1, starting transfers between devices, pair_program(): kernel = lax.all_to_all(sent, AXES, 0, 0, tiled=True)  5.13 us
    pallas_call x1, Pallas kernels, pair_dgrad(): pl.pallas_call(pair_dgrad_kernel, in_specs=[VMEM] * 10, out_specs=VMEM, o...  5.08 us
    all_to_all x1, waiting for transfers between devices, pair_program(): parts = lax.all_to_all(part, AXES, 0, 0, tiled=True)  3.79 us
    all_to_all x1, starting transfers between devices, pair_program(): parts = lax.all_to_all(part, AXES, 0, 0, tiled=True)  3.78 us
    pallas_call x1, Pallas kernels, pair_wgrad(): pl.pallas_call(pair_wgrad_kernel, in_specs=[VMEM] * 8, out_specs=VMEM, ou...  3.45 us
    pallas_call x1, Pallas kernels, pair_inner(): pl.pallas_call(functools.partial(middles_kernel, order), in_specs=[HBM] *...  2.04 us
    pallas_call x1, Pallas kernels, pair_inner(): pl.pallas_call(functools.partial(ends_kernel, order), in_specs=[HBM] * 2...  1.66 us
  transfers between devices with their start and end apart: 7, of which 2 were waited for; matrix products, arithmetic and copies ran while one was open for 0% of the time, Pallas kernels for 37%

profile of v14, /device:TPU:0, one launch (start us, length us, event | category | flops | bytes accessed | tf_op | source)
XLA Modules:
  0.0 42.3 jit_solution(10008591882660527523)
XLA Ops:
  0.6 1.3 %faces.1 = (bf16[64,1024]{1,0:T(8,128)(2,1)S(1)}, bf16[64,1024]{1,0:T(8,128)(2,1)S(1)}, bf16[64,1024]{1,0:T(8,128)(2,1)S(1)}) custom-call(bf16[64,8,8,128]{3,2,1,0:T(8,128)(2,1)} %refs_0_.3, bf16[64,8,8,128]{3,2,1,0:T(8,128)(2,1)} %refs_1_.3), custom_call_target="tpu_custom_call" | custom-call | bytes 1048576 | tf_op jit(solution)/shard_map/faces/pallas_call | solution.py:93
  2.0 0.7 %collective-permute-start = (bf16[64,1024]{1,0:T(8,128)(2,1)S(1)}, bf16[64,1024]{1,0:T(8,128)(2,1)S(1)}, u32[]{:S(2)}, u32[]{:S(2)}) collective-permute-start(bf16[64,1024]{1,0:T(8,128)(2,1)S(1)} %get-tuple-element.28), channel_id=1, source_target_pairs={{8,16},{16,8},{9,17},{17,9},{10,18},{18,10},{11,19},{19,11},{12,20... | collective-permute-start | bytes 393224 | tf_op jit(solution)/shard_map/ppermute | solution.py:1073
  2.6 0.0 copy-start
  2.7 0.0 copy-start.2
  2.7 1.7 %ends.1 = (bf16[3,64,1024]{2,1,0:T(8,128)(2,1)S(1)}, bf16[64,1024]{1,0:T(8,128)(2,1)S(1)}) custom-call(bf16[64,8,8,128]{3,2,1,0:T(8,128)(2,1)} %refs_0_.3, bf16[64,8,8,128]{3,2,1,0:T(8,128)(2,1)} %refs_1_.3, bf16[64,1024]{1,0:T(8,128)(2,1)S(1)} %get-tuple-element.29.refs_2_.refs_1_, bf16[64,1024]{1,0:T(8,128)(2,1)S(1)} %get-tuple-element.30.refs_3_), custom_call_target="tpu_custom_call" | custom-call | bytes 1048576 | tf_op jit(solution)/shard_map/ends/pallas_call | solution.py:523
  4.3 4.2 %collective-permute-start.1 = (bf16[64,1024]{1,0:T(8,128)(2,1)S(1)}, bf16[64,1024]{1,0:T(8,128)(2,1)S(1)}, u32[]{:S(2)}, u32[]{:S(2)}) collective-permute-start(bf16[64,1024]{1,0:T(8,128)(2,1)S(1)} %get-tuple-element.31), channel_id=1, source_target_pairs={{0,8},{8,0},{16,24},{24,16},{1,9},{9,1},{17,25},{25,17},{2,10},{10... | collective-permute-start | bytes 393224 | tf_op jit(solution)/shard_map/ppermute | solution.py:1073
  8.6 0.0 copy-done
  8.6 2.0 %middles.1 = (bf16[6,64,1024]{2,1,0:T(8,128)(2,1)S(1)}, bf16[10,64,128]{2,1,0:T(8,128)(2,1)S(1)}, bf16[32,4,896]{2,1,0:T(4,128)(2,1)}) custom-call(bf16[64,8,8,128]{3,2,1,0:T(8,128)(2,1)S(1)} %copy-done, bf16[64,8,8,128]{3,2,1,0:T(8,128)(2,1)} %refs_1_.3, bf16[64,1024]{1,0:T(8,128)(2,1)S(1)} %get-tuple-element.29.refs_2_.refs_1_, ...), custom_call_target="tpu_custom_call" | custom-call | bytes 4194304 | tf_op jit(solution)/shard_map/middles/pallas_call | solution.py:533
  10.6 5.1 %all-to-all-start = ((bf16[32,4,896]{2,1,0:T(4,128)(2,1)}), bf16[32,4,896]{2,1,0:T(4,128)(2,1)S(1)}, u32[]{:S(2)}, u32[]{:S(2)}) async-start(bf16[32,4,896]{2,1,0:T(4,128)(2,1)} %get-tuple-element.44), calls=%async_computation | async-start | bytes 458752 | tf_op jit(solution)/shard_map/all_to_all | solution.py:902
  15.8 0.0 collective-permute-done.odd_ref
  15.8 0.0 collective-permute-done.1.even_ref
  15.8 0.2 side.1
  16.0 0.3 collective-permute-start.2
  16.3 0.0 copy-done.1
  16.3 1.0 %inputs.1 = (bf16[8,64,1024]{2,1,0:T(8,128)(2,1)S(1)}, bf16[64,128]{1,0:T(8,128)(2,1)S(1)}) custom-call(bf16[64,8,8,128]{3,2,1,0:T(8,128)(2,1)S(1)} %copy-done.1), custom_call_target="tpu_custom_call" | custom-call | bytes 2097152 | tf_op jit(solution)/shard_map/inputs/pallas_call | solution.py:190
  17.4 0.1 collective-permute-done.2.other_ref.refs_5_.refs_6_
  17.5 0.1 join.1
  17.6 0.7 %collective-permute-start.3 = (bf16[3,64,128]{2,1,0:T(8,128)(2,1)S(1)}, bf16[3,64,128]{2,1,0:T(8,128)(2,1)S(1)}, u32[]{:S(2)}, u32[]{:S(2)}) collective-permute-start(bf16[3,64,128]{2,1,0:T(8,128)(2,1)S(1)} %get-tuple-element.41.refs_3_), channel_id=1, source_target_pairs={{1,2},{2,1},{5,6},{6,5},{9,10},{10,9},{13,14},{14,13},{17,18},{18,... | collective-permute-start | bytes 147464 | tf_op jit(solution)/shard_map/ppermute | solution.py:1073
  18.3 4.5 %collective-permute-start.4 = (bf16[3,64,128]{2,1,0:T(8,128)(2,1)S(1)}, bf16[3,64,128]{2,1,0:T(8,128)(2,1)S(1)}, u32[]{:S(2)}, u32[]{:S(2)}) collective-permute-start(bf16[3,64,128]{2,1,0:T(8,128)(2,1)S(1)} %get-tuple-element.42.refs_2_), channel_id=1, source_target_pairs={{0,1},{1,0},{2,3},{3,2},{4,5},{5,4},{6,7},{7,6},{8,9},{9,8},{10,11... | collective-permute-start | bytes 147464 | tf_op jit(solution)/shard_map/ppermute | solution.py:1073
  22.8 3.5 %wgrad.1.refs_0_ = f32[576,192]{1,0:T(8,128)S(1)} custom-call(bf16[64,1024]{1,0:T(8,128)(2,1)S(1)} %get-tuple-element.34.refs_0_, bf16[64,1024]{1,0:T(8,128)(2,1)S(1)} %get-tuple-element.29.refs_2_.refs_1_, bf16[6,64,1024]{2,1,0:T(8,128)(2,1)S(1)} %get-tuple-element.35.refs_2_, bf16[64,1024]{1,0:T(8,128)(2,1)S(1)} %get-tuple-element.30.refs_3_, ...), custom_call_target="tpu_custom_call" | custom-call | flops 2264924160 | bytes 4194304 | tf_op jit(solution)/shard_map/wgrad/pallas_call | solution.py:651
  26.3 0.0 collective-permute-done.3.refs_4_.refs_7_
  26.3 0.0 collective-permute-done.4.refs_5_.refs_8_
  26.3 1.4 %finish.1 = bf16[32,4,896]{2,1,0:T(4,128)(2,1)} custom-call(f32[576,192]{1,0:T(8,128)S(1)} %wgrad.1.refs_0_, bf16[64,128]{1,0:T(8,128)(2,1)S(1)} %get-tuple-element.40.columns_ref.refs_1_, bf16[3,64,128]{2,1,0:T(8,128)(2,1)S(1)} %get-tuple-element.42.refs_2_, bf16[3,64,128]{2,1,0:T(8,128)(2,1)S(1)} %get-tuple-element.41.refs_3_, ...), custom_call_target="tpu_custom_call" | custom-call | flops 134217728 | bytes 2097152 | tf_op jit(solution)/shard_map/finish/pallas_call | solution.py:729
  27.7 0.0 all-to-all-done.w_ref
  27.7 3.8 %all-to-all-start.1 = ((bf16[32,4,896]{2,1,0:T(4,128)(2,1)}), bf16[32,4,896]{2,1,0:T(4,128)(2,1)S(1)}, u32[]{:S(2)}, u32[]{:S(2)}) async-start(bf16[32,4,896]{2,1,0:T(4,128)(2,1)} %finish.1), calls=%async_computation.1 | async-start | bytes 458752 | tf_op jit(solution)/shard_map/all_to_all | solution.py:916
  31.5 0.7 %spread.1.refs_9_ = bf16[3,128,768]{2,1,0:T(8,128)(2,1)S(1)} custom-call(bf16[32,4,896]{2,1,0:T(4,128)(2,1)S(1)} %all-to-all-done.w_ref), custom_call_target="tpu_custom_call" | custom-call | flops 1048576 | bytes 2097152 | tf_op jit(solution)/shard_map/spread/pallas_call | solution.py:853
  32.2 0.0 copy-start.3
  32.2 0.0 copy-start.4
  32.2 5.1 %dgrad.1 = bf16[64,8,8,128]{3,2,1,0:T(8,128)(2,1)} custom-call(bf16[64,1024]{1,0:T(8,128)(2,1)S(1)} %get-tuple-element.34.refs_0_, bf16[64,1024]{1,0:T(8,128)(2,1)S(1)} %get-tuple-element.29.refs_2_.refs_1_, bf16[6,64,1024]{2,1,0:T(8,128)(2,1)S(1)} %get-tuple-element.35.refs_2_, bf16[64,1024]{1,0:T(8,128)(2,1)S(1)} %get-tuple-element.30.refs_3_, ...), custom_call_target="tpu_custom_call" | custom-call | flops 2415919104 | bytes 4194304 | tf_op jit(solution)/shard_map/dgrad/pallas_call | solution.py:877
  37.3 3.8 %all-to-all-done.1.parts_ref = bf16[32,4,896]{2,1,0:T(4,128)(2,1)S(1)} async-done(((bf16[32,4,896]{2,1,0:T(4,128)(2,1)}), bf16[32,4,896]{2,1,0:T(4,128)(2,1)S(1)}, u32[]{:S(2)}, u32[]{:S(2)}) %all-to-all-start.1) | async-done | bytes 229408 | tf_op jit(solution)/shard_map/all_to_all | solution.py:916
  41.1 0.0 copy-done.4
  41.1 1.2 %adam.1 = (f32[27,128]{1,0:T(8,128)}, f32[27,128]{1,0:T(8,128)}, f32[27,128]{1,0:T(8,128)}, f32[27,128]{1,0:T(8,128)}) custom-call(bf16[32,4,896]{2,1,0:T(4,128)(2,1)S(1)} %all-to-all-done.1.parts_ref, f32[27,128]{1,0:T(8,128)S(1)} %bitcast.8, f32[27,128]{1,0:T(8,128)S(1)} %bitcast.9, f32[27,128]{1,0:T(8,128)S(1)} %bitcast.10), custom_call_target="tpu_custom_call" | custom-call | flops 4194304 | bytes 524288 | tf_op jit(solution)/shard_map/adam/pallas_call | solution.py:818
  (3 shorter events, 0.0 us)
Async XLA Ops:
  2.0 13.8 %collective-permute-start = (bf16[64,1024]{1,0:T(8,128)(2,1)S(1)}, bf16[64,1024]{1,0:T(8,128)(2,1)S(1)}, u32[]{:S(2)}, u32[]{:S(2)}) collective-permute-start(bf16[64,1024]{1,0:T(8,128)(2,1)S(1)} %get-tuple-element.28), channel_id=1, source_target_pairs={{8,16},{16,8},{9,17},{17,9},{10,18},{18,10},{11,19},{19,11},{12,20... | collective-permute-start | bytes 393224 | tf_op jit(solution)/shard_map/ppermute | solution.py:1073
  2.6 5.9 %copy-start = (bf16[64,8,8,128]{3,2,1,0:T(8,128)(2,1)S(1)}, bf16[64,8,8,128]{3,2,1,0:T(8,128)(2,1)}, u32[]{:S(2)}) copy-start(bf16[64,8,8,128]{3,2,1,0:T(8,128)(2,1)} %refs_0_.3) | copy-start | bytes 3145732
  2.7 5.9 %copy-start.2 = (f32[3456]{0:T(1024)S(1)}, f32[3456]{0:T(1024)}, u32[]{:S(2)}) copy-start(f32[3456]{0:T(1024)} %param.9) | copy-start | bytes 41476
  4.3 11.4 %collective-permute-start.1 = (bf16[64,1024]{1,0:T(8,128)(2,1)S(1)}, bf16[64,1024]{1,0:T(8,128)(2,1)S(1)}, u32[]{:S(2)}, u32[]{:S(2)}) collective-permute-start(bf16[64,1024]{1,0:T(8,128)(2,1)S(1)} %get-tuple-element.31), channel_id=1, source_target_pairs={{0,8},{8,0},{16,24},{24,16},{1,9},{9,1},{17,25},{25,17},{2,10},{10... | collective-permute-start | bytes 393224 | tf_op jit(solution)/shard_map/ppermute | solution.py:1073
  8.6 7.8 %copy-start.1 = (bf16[64,8,8,128]{3,2,1,0:T(8,128)(2,1)S(1)}, bf16[64,8,8,128]{3,2,1,0:T(8,128)(2,1)}, u32[]{:S(2)}) copy-start(bf16[64,8,8,128]{3,2,1,0:T(8,128)(2,1)} %a_ref) | copy-start | bytes 3145732
  10.6 17.1 %all-to-all-start = ((bf16[32,4,896]{2,1,0:T(4,128)(2,1)}), bf16[32,4,896]{2,1,0:T(4,128)(2,1)S(1)}, u32[]{:S(2)}, u32[]{:S(2)}) async-start(bf16[32,4,896]{2,1,0:T(4,128)(2,1)} %get-tuple-element.44), calls=%async_computation | async-start | bytes 458752 | tf_op jit(solution)/shard_map/all_to_all | solution.py:902
  16.0 1.5 %collective-permute-start.2 = (bf16[12,64,128]{2,1,0:T(8,128)(2,1)S(1)}, bf16[12,64,128]{2,1,0:T(8,128)(2,1)S(1)}, u32[]{:S(2)}, u32[]{:S(2)}) collective-permute-start(bf16[12,64,128]{2,1,0:T(8,128)(2,1)S(1)} %get-tuple-element.38.own_ref), channel_id=1, source_target_pairs={{0,4},{4,0},{1,5},{5,1},{2,6},{6,2},{3,7},{7,3},{8,12},{12,8},{9,1... | collective-permute-start | bytes 589832 | tf_op jit(solution)/shard_map/ppermute | solution.py:1066
  17.6 8.7 %collective-permute-start.3 = (bf16[3,64,128]{2,1,0:T(8,128)(2,1)S(1)}, bf16[3,64,128]{2,1,0:T(8,128)(2,1)S(1)}, u32[]{:S(2)}, u32[]{:S(2)}) collective-permute-start(bf16[3,64,128]{2,1,0:T(8,128)(2,1)S(1)} %get-tuple-element.41.refs_3_), channel_id=1, source_target_pairs={{1,2},{2,1},{5,6},{6,5},{9,10},{10,9},{13,14},{14,13},{17,18},{18,... | collective-permute-start | bytes 147464 | tf_op jit(solution)/shard_map/ppermute | solution.py:1073
  18.3 8.0 %collective-permute-start.4 = (bf16[3,64,128]{2,1,0:T(8,128)(2,1)S(1)}, bf16[3,64,128]{2,1,0:T(8,128)(2,1)S(1)}, u32[]{:S(2)}, u32[]{:S(2)}) collective-permute-start(bf16[3,64,128]{2,1,0:T(8,128)(2,1)S(1)} %get-tuple-element.42.refs_2_), channel_id=1, source_target_pairs={{0,1},{1,0},{2,3},{3,2},{4,5},{5,4},{6,7},{7,6},{8,9},{9,8},{10,11... | collective-permute-start | bytes 147464 | tf_op jit(solution)/shard_map/ppermute | solution.py:1073
  27.7 13.4 %all-to-all-start.1 = ((bf16[32,4,896]{2,1,0:T(4,128)(2,1)}), bf16[32,4,896]{2,1,0:T(4,128)(2,1)S(1)}, u32[]{:S(2)}, u32[]{:S(2)}) async-start(bf16[32,4,896]{2,1,0:T(4,128)(2,1)} %finish.1), calls=%async_computation.1 | async-start | bytes 458752 | tf_op jit(solution)/shard_map/all_to_all | solution.py:916
  32.2 8.9 %copy-start.3 = (f32[3456]{0:T(1024)S(1)}, f32[3456]{0:T(1024)}, u32[]{:S(2)}) copy-start(f32[3456]{0:T(1024)} %param.10) | copy-start | bytes 41476
  32.2 8.9 %copy-start.4 = (f32[3456]{0:T(1024)S(1)}, f32[3456]{0:T(1024)}, u32[]{:S(2)}) copy-start(f32[3456]{0:T(1024)} %param.11) | copy-start | bytes 41476

commit v15 on v13

--- a/solution.py
+++ b/solution.py
@@ -47,7 +47,7 @@
 
 
 def masked(p, u):
-    return jnp.where(p > 0, u, jnp.zeros_like(u))
+    return jnp.where(p.astype(F32) > 0, u.astype(F32), 0.0)
 
 
 def choose(condition, out_ref, first_ref, second_ref):

time: 42.4 us -> 42.4 us (level)
  no operation moved by 1% of the time
where the time goes in v15:
time: 42.4 us; the launch traced here: 42 us
  starting transfers between devices  19.2 us (45%)
  Pallas kernels  18.1 us (43%)
  waiting for transfers between devices  3.93 us (9%)
  between operations  0.78 us (2%)
    ppermute x4, starting transfers between devices, swapped(): return lax.ppermute(value, axis, pairs)  10.2 us
    pallas_call x1, Pallas kernels, pair_dgrad(): pl.pallas_call(pair_dgrad_kernel, in_specs=[VMEM] * 10, out_specs=VMEM, o...  5.08 us
    all_to_all x1, starting transfers between devices, pair_program(): kernel = lax.all_to_all(sent, AXES, 0, 0, tiled=True)  4.84 us
    all_to_all x1, starting transfers between devices, pair_program(): parts = lax.all_to_all(part, AXES, 0, 0, tiled=True)  3.79 us
    all_to_all x1, waiting for transfers between devices, pair_program(): parts = lax.all_to_all(part, AXES, 0, 0, tiled=True)  3.78 us
    pallas_call x1, Pallas kernels, pair_wgrad(): pl.pallas_call(pair_wgrad_kernel, in_specs=[VMEM] * 8, out_specs=VMEM, ou...  3.45 us
    pallas_call x1, Pallas kernels, pair_inner(): pl.pallas_call(functools.partial(middles_kernel, order), in_specs=[HBM] *...  2.11 us
    pallas_call x1, Pallas kernels, pair_inner(): pl.pallas_call(functools.partial(ends_kernel, order), in_specs=[HBM] * 2...  1.53 us
  transfers between devices with their start and end apart: 7, of which 2 were waited for; matrix products, arithmetic and copies ran while one was open for 0% of the time, Pallas kernels for 37%

profile of v15, /device:TPU:0, one launch (start us, length us, event | category | flops | bytes accessed | tf_op | source)
XLA Modules:
  0.0 42.0 jit_solution(122300780063833509)
XLA Ops:
  0.6 1.3 %faces.1 = (bf16[64,1024]{1,0:T(8,128)(2,1)S(1)}, bf16[64,1024]{1,0:T(8,128)(2,1)S(1)}, bf16[64,1024]{1,0:T(8,128)(2,1)S(1)}) custom-call(bf16[64,8,8,128]{3,2,1,0:T(8,128)(2,1)} %refs_0_.3, bf16[64,8,8,128]{3,2,1,0:T(8,128)(2,1)} %refs_1_.3), custom_call_target="tpu_custom_call" | custom-call | bytes 1048576 | tf_op jit(solution)/shard_map/faces/pallas_call | solution.py:93
  1.9 0.7 %collective-permute-start = (bf16[64,1024]{1,0:T(8,128)(2,1)S(1)}, bf16[64,1024]{1,0:T(8,128)(2,1)S(1)}, u32[]{:S(2)}, u32[]{:S(2)}) collective-permute-start(bf16[64,1024]{1,0:T(8,128)(2,1)S(1)} %get-tuple-element.28), channel_id=1, source_target_pairs={{8,16},{16,8},{9,17},{17,9},{10,18},{18,10},{11,19},{19,11},{12,20... | collective-permute-start | bytes 393224 | tf_op jit(solution)/shard_map/ppermute | solution.py:1073
  2.6 0.0 copy-start.1
  2.6 1.5 %ends.1 = (bf16[3,64,1024]{2,1,0:T(8,128)(2,1)S(1)}, bf16[64,1024]{1,0:T(8,128)(2,1)S(1)}) custom-call(bf16[64,8,8,128]{3,2,1,0:T(8,128)(2,1)} %refs_0_.3, bf16[64,8,8,128]{3,2,1,0:T(8,128)(2,1)} %refs_1_.3, bf16[64,1024]{1,0:T(8,128)(2,1)S(1)} %get-tuple-element.29.refs_2_.refs_1_, bf16[64,1024]{1,0:T(8,128)(2,1)S(1)} %get-tuple-element.30.refs_3_), custom_call_target="tpu_custom_call" | custom-call | bytes 1048576 | tf_op jit(solution)/shard_map/ends/pallas_call | solution.py:523
  4.2 4.3 %collective-permute-start.1 = (bf16[64,1024]{1,0:T(8,128)(2,1)S(1)}, bf16[64,1024]{1,0:T(8,128)(2,1)S(1)}, u32[]{:S(2)}, u32[]{:S(2)}) collective-permute-start(bf16[64,1024]{1,0:T(8,128)(2,1)S(1)} %get-tuple-element.31), channel_id=1, source_target_pairs={{0,8},{8,0},{16,24},{24,16},{1,9},{9,1},{17,25},{25,17},{2,10},{10... | collective-permute-start | bytes 393224 | tf_op jit(solution)/shard_map/ppermute | solution.py:1073
  8.5 0.0 copy-done.1
  8.5 2.1 %middles.1 = (bf16[6,64,1024]{2,1,0:T(8,128)(2,1)S(1)}, bf16[10,64,128]{2,1,0:T(8,128)(2,1)S(1)}, bf16[32,4,896]{2,1,0:T(4,128)(2,1)}) custom-call(bf16[64,8,8,128]{3,2,1,0:T(8,128)(2,1)} %refs_0_.3, bf16[64,8,8,128]{3,2,1,0:T(8,128)(2,1)} %refs_1_.3, bf16[64,1024]{1,0:T(8,128)(2,1)S(1)} %get-tuple-element.29.refs_2_.refs_1_, ...), custom_call_target="tpu_custom_call" | custom-call | bytes 4194304 | tf_op jit(solution)/shard_map/middles/pallas_call | solution.py:533
  10.6 4.8 %all-to-all-start = ((bf16[32,4,896]{2,1,0:T(4,128)(2,1)}), bf16[32,4,896]{2,1,0:T(4,128)(2,1)S(1)}, u32[]{:S(2)}, u32[]{:S(2)}) async-start(bf16[32,4,896]{2,1,0:T(4,128)(2,1)} %get-tuple-element.44), calls=%async_computation | async-start | bytes 458752 | tf_op jit(solution)/shard_map/all_to_all | solution.py:902
  15.5 0.0 collective-permute-done.odd_ref
  15.5 0.0 collective-permute-done.1.even_ref
  15.5 0.2 side.1
  15.7 0.3 collective-permute-start.2
  16.1 0.0 copy-done
  16.1 1.0 %inputs.1 = (bf16[8,64,1024]{2,1,0:T(8,128)(2,1)S(1)}, bf16[64,128]{1,0:T(8,128)(2,1)S(1)}) custom-call(bf16[64,8,8,128]{3,2,1,0:T(8,128)(2,1)S(1)} %copy-done), custom_call_target="tpu_custom_call" | custom-call | bytes 2097152 | tf_op jit(solution)/shard_map/inputs/pallas_call | solution.py:190
  17.1 0.1 collective-permute-done.2.other_ref.refs_5_.refs_6_
  17.3 0.1 join.1
  17.3 0.7 %collective-permute-start.3 = (bf16[3,64,128]{2,1,0:T(8,128)(2,1)S(1)}, bf16[3,64,128]{2,1,0:T(8,128)(2,1)S(1)}, u32[]{:S(2)}, u32[]{:S(2)}) collective-permute-start(bf16[3,64,128]{2,1,0:T(8,128)(2,1)S(1)} %get-tuple-element.41.refs_3_), channel_id=1, source_target_pairs={{1,2},{2,1},{5,6},{6,5},{9,10},{10,9},{13,14},{14,13},{17,18},{18,... | collective-permute-start | bytes 147464 | tf_op jit(solution)/shard_map/ppermute | solution.py:1073
  18.0 4.5 %collective-permute-start.4 = (bf16[3,64,128]{2,1,0:T(8,128)(2,1)S(1)}, bf16[3,64,128]{2,1,0:T(8,128)(2,1)S(1)}, u32[]{:S(2)}, u32[]{:S(2)}) collective-permute-start(bf16[3,64,128]{2,1,0:T(8,128)(2,1)S(1)} %get-tuple-element.42.refs_2_), channel_id=1, source_target_pairs={{0,1},{1,0},{2,3},{3,2},{4,5},{5,4},{6,7},{7,6},{8,9},{9,8},{10,11... | collective-permute-start | bytes 147464 | tf_op jit(solution)/shard_map/ppermute | solution.py:1073
  22.6 3.5 %wgrad.1.refs_0_ = f32[576,192]{1,0:T(8,128)S(1)} custom-call(bf16[64,1024]{1,0:T(8,128)(2,1)S(1)} %get-tuple-element.34.refs_0_, bf16[64,1024]{1,0:T(8,128)(2,1)S(1)} %get-tuple-element.29.refs_2_.refs_1_, bf16[6,64,1024]{2,1,0:T(8,128)(2,1)S(1)} %get-tuple-element.35.refs_2_, bf16[64,1024]{1,0:T(8,128)(2,1)S(1)} %get-tuple-element.30.refs_3_, ...), custom_call_target="tpu_custom_call" | custom-call | flops 2264924160 | bytes 4194304 | tf_op jit(solution)/shard_map/wgrad/pallas_call | solution.py:651
  26.0 0.0 collective-permute-done.3.refs_4_.refs_7_
  26.0 0.0 collective-permute-done.4.refs_5_.refs_8_
  26.0 1.4 %finish.1 = bf16[32,4,896]{2,1,0:T(4,128)(2,1)} custom-call(f32[576,192]{1,0:T(8,128)S(1)} %wgrad.1.refs_0_, bf16[64,128]{1,0:T(8,128)(2,1)S(1)} %get-tuple-element.40.columns_ref.refs_1_, bf16[3,64,128]{2,1,0:T(8,128)(2,1)S(1)} %get-tuple-element.42.refs_2_, bf16[3,64,128]{2,1,0:T(8,128)(2,1)S(1)} %get-tuple-element.41.refs_3_, ...), custom_call_target="tpu_custom_call" | custom-call | flops 134217728 | bytes 2097152 | tf_op jit(solution)/shard_map/finish/pallas_call | solution.py:729
  27.4 0.0 all-to-all-done.w_ref
  27.4 3.8 %all-to-all-start.1 = ((bf16[32,4,896]{2,1,0:T(4,128)(2,1)}), bf16[32,4,896]{2,1,0:T(4,128)(2,1)S(1)}, u32[]{:S(2)}, u32[]{:S(2)}) async-start(bf16[32,4,896]{2,1,0:T(4,128)(2,1)} %finish.1), calls=%async_computation.1 | async-start | bytes 458752 | tf_op jit(solution)/shard_map/all_to_all | solution.py:916
  31.2 0.7 %spread.1.refs_9_ = bf16[3,128,768]{2,1,0:T(8,128)(2,1)S(1)} custom-call(bf16[32,4,896]{2,1,0:T(4,128)(2,1)S(1)} %all-to-all-done.w_ref), custom_call_target="tpu_custom_call" | custom-call | flops 1048576 | bytes 2097152 | tf_op jit(solution)/shard_map/spread/pallas_call | solution.py:853
  31.9 0.0 copy-start.2
  31.9 0.0 copy-start.3
  31.9 5.1 %dgrad.1 = bf16[64,8,8,128]{3,2,1,0:T(8,128)(2,1)} custom-call(bf16[64,1024]{1,0:T(8,128)(2,1)S(1)} %get-tuple-element.34.refs_0_, bf16[64,1024]{1,0:T(8,128)(2,1)S(1)} %get-tuple-element.29.refs_2_.refs_1_, bf16[6,64,1024]{2,1,0:T(8,128)(2,1)S(1)} %get-tuple-element.35.refs_2_, bf16[64,1024]{1,0:T(8,128)(2,1)S(1)} %get-tuple-element.30.refs_3_, ...), custom_call_target="tpu_custom_call" | custom-call | flops 2415919104 | bytes 4194304 | tf_op jit(solution)/shard_map/dgrad/pallas_call | solution.py:877
  37.0 3.8 %all-to-all-done.1.parts_ref = bf16[32,4,896]{2,1,0:T(4,128)(2,1)S(1)} async-done(((bf16[32,4,896]{2,1,0:T(4,128)(2,1)}), bf16[32,4,896]{2,1,0:T(4,128)(2,1)S(1)}, u32[]{:S(2)}, u32[]{:S(2)}) %all-to-all-start.1) | async-done | bytes 229408 | tf_op jit(solution)/shard_map/all_to_all | solution.py:916
  40.8 0.0 copy-done.2
  40.8 0.0 copy-done.3
  40.8 1.2 %adam.1 = (f32[27,128]{1,0:T(8,128)}, f32[27,128]{1,0:T(8,128)}, f32[27,128]{1,0:T(8,128)}, f32[27,128]{1,0:T(8,128)}) custom-call(bf16[32,4,896]{2,1,0:T(4,128)(2,1)S(1)} %all-to-all-done.1.parts_ref, f32[27,128]{1,0:T(8,128)S(1)} %bitcast.8, f32[27,128]{1,0:T(8,128)S(1)} %bitcast.9, f32[27,128]{1,0:T(8,128)S(1)} %bitcast.10), custom_call_target="tpu_custom_call" | custom-call | flops 4194304 | bytes 524288 | tf_op jit(solution)/shard_map/adam/pallas_call | solution.py:818
  (1 shorter events, 0.0 us)
Async XLA Ops:
  1.9 13.6 %collective-permute-start = (bf16[64,1024]{1,0:T(8,128)(2,1)S(1)}, bf16[64,1024]{1,0:T(8,128)(2,1)S(1)}, u32[]{:S(2)}, u32[]{:S(2)}) collective-permute-start(bf16[64,1024]{1,0:T(8,128)(2,1)S(1)} %get-tuple-element.28), channel_id=1, source_target_pairs={{8,16},{16,8},{9,17},{17,9},{10,18},{18,10},{11,19},{19,11},{12,20... | collective-permute-start | bytes 393224 | tf_op jit(solution)/shard_map/ppermute | solution.py:1073
  2.6 5.9 %copy-start.1 = (f32[3456]{0:T(1024)S(1)}, f32[3456]{0:T(1024)}, u32[]{:S(2)}) copy-start(f32[3456]{0:T(1024)} %param.9) | copy-start | bytes 41476
  4.2 11.3 %collective-permute-start.1 = (bf16[64,1024]{1,0:T(8,128)(2,1)S(1)}, bf16[64,1024]{1,0:T(8,128)(2,1)S(1)}, u32[]{:S(2)}, u32[]{:S(2)}) collective-permute-start(bf16[64,1024]{1,0:T(8,128)(2,1)S(1)} %get-tuple-element.31), channel_id=1, source_target_pairs={{0,8},{8,0},{16,24},{24,16},{1,9},{9,1},{17,25},{25,17},{2,10},{10... | collective-permute-start | bytes 393224 | tf_op jit(solution)/shard_map/ppermute | solution.py:1073
  8.5 7.6 %copy-start = (bf16[64,8,8,128]{3,2,1,0:T(8,128)(2,1)S(1)}, bf16[64,8,8,128]{3,2,1,0:T(8,128)(2,1)}, u32[]{:S(2)}) copy-start(bf16[64,8,8,128]{3,2,1,0:T(8,128)(2,1)} %a_ref) | copy-start | bytes 3145732
  10.6 16.8 %all-to-all-start = ((bf16[32,4,896]{2,1,0:T(4,128)(2,1)}), bf16[32,4,896]{2,1,0:T(4,128)(2,1)S(1)}, u32[]{:S(2)}, u32[]{:S(2)}) async-start(bf16[32,4,896]{2,1,0:T(4,128)(2,1)} %get-tuple-element.44), calls=%async_computation | async-start | bytes 458752 | tf_op jit(solution)/shard_map/all_to_all | solution.py:902
  15.7 1.5 %collective-permute-start.2 = (bf16[12,64,128]{2,1,0:T(8,128)(2,1)S(1)}, bf16[12,64,128]{2,1,0:T(8,128)(2,1)S(1)}, u32[]{:S(2)}, u32[]{:S(2)}) collective-permute-start(bf16[12,64,128]{2,1,0:T(8,128)(2,1)S(1)} %get-tuple-element.38.own_ref), channel_id=1, source_target_pairs={{0,4},{4,0},{1,5},{5,1},{2,6},{6,2},{3,7},{7,3},{8,12},{12,8},{9,1... | collective-permute-start | bytes 589832 | tf_op jit(solution)/shard_map/ppermute | solution.py:1066
  17.3 8.7 %collective-permute-start.3 = (bf16[3,64,128]{2,1,0:T(8,128)(2,1)S(1)}, bf16[3,64,128]{2,1,0:T(8,128)(2,1)S(1)}, u32[]{:S(2)}, u32[]{:S(2)}) collective-permute-start(bf16[3,64,128]{2,1,0:T(8,128)(2,1)S(1)} %get-tuple-element.41.refs_3_), channel_id=1, source_target_pairs={{1,2},{2,1},{5,6},{6,5},{9,10},{10,9},{13,14},{14,13},{17,18},{18,... | collective-permute-start | bytes 147464 | tf_op jit(solution)/shard_map/ppermute | solution.py:1073
  18.0 8.0 %collective-permute-start.4 = (bf16[3,64,128]{2,1,0:T(8,128)(2,1)S(1)}, bf16[3,64,128]{2,1,0:T(8,128)(2,1)S(1)}, u32[]{:S(2)}, u32[]{:S(2)}) collective-permute-start(bf16[3,64,128]{2,1,0:T(8,128)(2,1)S(1)} %get-tuple-element.42.refs_2_), channel_id=1, source_target_pairs={{0,1},{1,0},{2,3},{3,2},{4,5},{5,4},{6,7},{7,6},{8,9},{9,8},{10,11... | collective-permute-start | bytes 147464 | tf_op jit(solution)/shard_map/ppermute | solution.py:1073
  27.4 13.4 %all-to-all-start.1 = ((bf16[32,4,896]{2,1,0:T(4,128)(2,1)}), bf16[32,4,896]{2,1,0:T(4,128)(2,1)S(1)}, u32[]{:S(2)}, u32[]{:S(2)}) async-start(bf16[32,4,896]{2,1,0:T(4,128)(2,1)} %finish.1), calls=%async_computation.1 | async-start | bytes 458752 | tf_op jit(solution)/shard_map/all_to_all | solution.py:916
  31.9 8.9 %copy-start.2 = (f32[3456]{0:T(1024)S(1)}, f32[3456]{0:T(1024)}, u32[]{:S(2)}) copy-start(f32[3456]{0:T(1024)} %param.10) | copy-start | bytes 41476
  31.9 8.9 %copy-start.3 = (f32[3456]{0:T(1024)S(1)}, f32[3456]{0:T(1024)}, u32[]{:S(2)}) copy-start(f32[3456]{0:T(1024)} %param.11) | copy-start | bytes 41476

commit v16 on v15

--- a/solution.py
+++ b/solution.py
@@ -107,17 +107,20 @@
     )(preact, upstream)
 
 
-def fetch(planes, p_ref, u_ref, p_buf, u_buf, sems):
-    copies = []
-    for x in planes:
-        pair = (
+def fetches(planes, p_ref, u_ref, p_buf, u_buf, sems):
+    return [
+        (
             pltpu.make_async_copy(p_ref.at[:, x + 1], p_buf.at[x], sems.at[2 * x]),
             pltpu.make_async_copy(u_ref.at[:, x + 1], u_buf.at[x], sems.at[2 * x + 1]),
         )
+        for x in planes
+    ]
+
+
+def start(copies):
+    for pair in copies:
         for copy in pair:
             copy.start()
-        copies.append(pair)
-    return copies
 
 
 def settle(order, planes, copies, g_ref, p_buf, u_buf, tile):
@@ -133,7 +136,8 @@
 
 
 def read_inner(order, planes, p_ref, u_ref, g_ref, p_buf, u_buf, tile, sems):
-    copies = fetch(planes, p_ref, u_ref, p_buf, u_buf, sems)
+    copies = fetches(planes, p_ref, u_ref, p_buf, u_buf, sems)
+    start(copies)
     settle(order, planes, copies, g_ref, p_buf, u_buf, tile)
 
 
@@ -475,7 +479,15 @@
     half = before_ref.shape[0]
     inner, _, plane = g_ref.shape
     later = range(half, inner)
-    copies = fetch(later, p_ref, u_ref, p_buf, u_buf, sems)
+    middle = in_odd_swaps("gx")
+    first_copies = fetches(range(half), p_ref, u_ref, p_buf, u_buf, sems)
+    later_copies = fetches(later, p_ref, u_ref, p_buf, u_buf, sems)
+
+    @pl.when(middle)
+    def _():
+        start(first_copies)
+
+    start(later_copies)
     share = m_ref[...]
     share = jnp.concatenate(
         [share, jnp.zeros((-share.shape[0] % QUAD, share.shape[1]), F32)], axis=0
@@ -488,17 +500,16 @@
     to_quads(share, write)
     send = pltpu.make_async_copy(sent_buf, sent_ref, sent_sem)
     send.start()
-    middle = in_odd_swaps("gx")
 
     @pl.when(middle)
     def _():
-        read_inner(order, range(half), p_ref, u_ref, g_ref, p_buf, u_buf, tile, sems)
+        settle(order, range(half), first_copies, g_ref, p_buf, u_buf, tile)
 
     @pl.when(jnp.logical_not(middle))
     def _():
         g_ref[:half] = before_ref[...]
 
-    settle(order, later, copies, g_ref, p_buf, u_buf, tile)
+    settle(order, later, later_copies, g_ref, p_buf, u_buf, tile)
     size_z = side_ref.shape[-1]
     size_x = inner + 2
     bodies = [first_ref] + [g_ref.at[x] for x in range(inner)] + [last_ref]
@@ -519,7 +530,7 @@
         inner_output(*shape),
         jax.ShapeDtypeStruct((size_x + 2, channels, size_z), BF16),
     ]
-    half = jax.ShapeDtypeStruct((made[0].shape[0] // 2, *made[0].shape[1:]), BF16)
+    half = jax.ShapeDtypeStruct((made[0].shape[0] * 2 // 3, *made[0].shape[1:]), BF16)
     before, swap = pl.pallas_call(
         functools.partial(ends_kernel, order),
         in_specs=[HBM] * 2 + [VMEM] * 2,

time: 42.4 us -> 43.2 us (1.019)
  Pallas kernels: 18.1 us -> 19 us
    pallas_call x1, Pallas kernels: 2.11 us -> 2.85 us  [pair_inner(): pl.pallas_call(functools.partial(middles_kernel, order), in_specs=[HBM] *...]
  transfers between devices with their start and end apart: 7 -> 7, of which waited for: 2 -> 2; matrix products, arithmetic and copies ran while one was open for 0% -> 0% of each run, Pallas kernels for 37% -> 39%
where the time goes in v16:
time: 43.2 us; the launch traced here: 42.8 us
  Pallas kernels  19 us (44%)
  starting transfers between devices  19 us (44%)
  waiting for transfers between devices  3.94 us (9%)
  between operations  0.79 us (2%)
    ppermute x4, starting transfers between devices, swapped(): return lax.ppermute(value, axis, pairs)  10.1 us
    pallas_call x1, Pallas kernels, pair_dgrad(): pl.pallas_call(pair_dgrad_kernel, in_specs=[VMEM] * 10, out_specs=VMEM, o...  5.08 us
    all_to_all x1, starting transfers between devices, pair_program(): kernel = lax.all_to_all(sent, AXES, 0, 0, tiled=True)  4.84 us
    all_to_all x1, waiting for transfers between devices, pair_program(): parts = lax.all_to_all(part, AXES, 0, 0, tiled=True)  3.79 us
    all_to_all x1, starting transfers between devices, pair_program(): parts = lax.all_to_all(part, AXES, 0, 0, tiled=True)  3.78 us
    pallas_call x1, Pallas kernels, pair_wgrad(): pl.pallas_call(pair_wgrad_kernel, in_specs=[VMEM] * 8, out_specs=VMEM, ou...  3.45 us
    pallas_call x1, Pallas kernels, pair_inner(): pl.pallas_call(functools.partial(middles_kernel, order), in_specs=[HBM] *...  2.85 us
    pallas_call x1, Pallas kernels, pair_inner(): pl.pallas_call(functools.partial(ends_kernel, order), in_specs=[HBM] * 2...  1.67 us
  transfers between devices with their start and end apart: 7, of which 2 were waited for; matrix products, arithmetic and copies ran while one was open for 0% of the time, Pallas kernels for 39%

profile of v16, /device:TPU:0, one launch (start us, length us, event | category | flops | bytes accessed | tf_op | source)
XLA Modules:
  0.0 42.8 jit_solution(14746275511880184732)
XLA Ops:
  0.6 1.3 %faces.1 = (bf16[64,1024]{1,0:T(8,128)(2,1)S(1)}, bf16[64,1024]{1,0:T(8,128)(2,1)S(1)}, bf16[64,1024]{1,0:T(8,128)(2,1)S(1)}) custom-call(bf16[64,8,8,128]{3,2,1,0:T(8,128)(2,1)} %refs_0_.3, bf16[64,8,8,128]{3,2,1,0:T(8,128)(2,1)} %refs_1_.3), custom_call_target="tpu_custom_call" | custom-call | bytes 1048576 | tf_op jit(solution)/shard_map/faces/pallas_call | solution.py:93
  1.9 0.7 %collective-permute-start = (bf16[64,1024]{1,0:T(8,128)(2,1)S(1)}, bf16[64,1024]{1,0:T(8,128)(2,1)S(1)}, u32[]{:S(2)}, u32[]{:S(2)}) collective-permute-start(bf16[64,1024]{1,0:T(8,128)(2,1)S(1)} %get-tuple-element.28), channel_id=1, source_target_pairs={{8,16},{16,8},{9,17},{17,9},{10,18},{18,10},{11,19},{19,11},{12,20... | collective-permute-start | bytes 393224 | tf_op jit(solution)/shard_map/ppermute | solution.py:1084
  2.6 0.0 copy-start.1
  2.6 1.7 %ends.1 = (bf16[4,64,1024]{2,1,0:T(8,128)(2,1)S(1)}, bf16[64,1024]{1,0:T(8,128)(2,1)S(1)}) custom-call(bf16[64,8,8,128]{3,2,1,0:T(8,128)(2,1)} %refs_0_.3, bf16[64,8,8,128]{3,2,1,0:T(8,128)(2,1)} %refs_1_.3, bf16[64,1024]{1,0:T(8,128)(2,1)S(1)} %get-tuple-element.29.refs_2_.refs_1_, bf16[64,1024]{1,0:T(8,128)(2,1)S(1)} %get-tuple-element.30.refs_3_), custom_call_target="tpu_custom_call" | custom-call | bytes 1048576 | tf_op jit(solution)/shard_map/ends/pallas_call | solution.py:534
  4.3 4.2 %collective-permute-start.1 = (bf16[64,1024]{1,0:T(8,128)(2,1)S(1)}, bf16[64,1024]{1,0:T(8,128)(2,1)S(1)}, u32[]{:S(2)}, u32[]{:S(2)}) collective-permute-start(bf16[64,1024]{1,0:T(8,128)(2,1)S(1)} %get-tuple-element.31), channel_id=1, source_target_pairs={{0,8},{8,0},{16,24},{24,16},{1,9},{9,1},{17,25},{25,17},{2,10},{10... | collective-permute-start | bytes 393224 | tf_op jit(solution)/shard_map/ppermute | solution.py:1084
  8.5 0.0 copy-done.1
  8.5 2.8 %middles.1 = (bf16[6,64,1024]{2,1,0:T(8,128)(2,1)}, bf16[10,64,128]{2,1,0:T(8,128)(2,1)S(1)}, bf16[32,4,896]{2,1,0:T(4,128)(2,1)}) custom-call(bf16[64,8,8,128]{3,2,1,0:T(8,128)(2,1)} %refs_0_.3, bf16[64,8,8,128]{3,2,1,0:T(8,128)(2,1)} %refs_1_.3, bf16[64,1024]{1,0:T(8,128)(2,1)S(1)} %get-tuple-element.29.refs_2_.refs_1_, ...), custom_call_target="tpu_custom_call" | custom-call | bytes 4194304 | tf_op jit(solution)/shard_map/middles/pallas_call | solution.py:544
  11.4 4.8 %all-to-all-start = ((bf16[32,4,896]{2,1,0:T(4,128)(2,1)}), bf16[32,4,896]{2,1,0:T(4,128)(2,1)S(1)}, u32[]{:S(2)}, u32[]{:S(2)}) async-start(bf16[32,4,896]{2,1,0:T(4,128)(2,1)} %get-tuple-element.44), calls=%async_computation | async-start | bytes 458752 | tf_op jit(solution)/shard_map/all_to_all | solution.py:913
  16.2 0.0 collective-permute-done.odd_ref
  16.2 0.0 collective-permute-done.1.even_ref
  16.2 0.2 side.1
  16.5 0.0 copy-start.4
  16.5 0.3 collective-permute-start.2
  16.8 1.0 %inputs.1 = (bf16[8,64,1024]{2,1,0:T(8,128)(2,1)S(1)}, bf16[64,128]{1,0:T(8,128)(2,1)S(1)}) custom-call(bf16[64,8,8,128]{3,2,1,0:T(8,128)(2,1)S(1)} %copy-done), custom_call_target="tpu_custom_call" | custom-call | bytes 2097152 | tf_op jit(solution)/shard_map/inputs/pallas_call | solution.py:194
  17.9 0.1 collective-permute-done.2.other_ref.refs_5_.refs_6_
  18.0 0.1 join.1
  18.1 0.7 %collective-permute-start.3 = (bf16[3,64,128]{2,1,0:T(8,128)(2,1)S(1)}, bf16[3,64,128]{2,1,0:T(8,128)(2,1)S(1)}, u32[]{:S(2)}, u32[]{:S(2)}) collective-permute-start(bf16[3,64,128]{2,1,0:T(8,128)(2,1)S(1)} %get-tuple-element.41.refs_3_), channel_id=1, source_target_pairs={{1,2},{2,1},{5,6},{6,5},{9,10},{10,9},{13,14},{14,13},{17,18},{18,... | collective-permute-start | bytes 147464 | tf_op jit(solution)/shard_map/ppermute | solution.py:1084
  18.8 4.5 %collective-permute-start.4 = (bf16[3,64,128]{2,1,0:T(8,128)(2,1)S(1)}, bf16[3,64,128]{2,1,0:T(8,128)(2,1)S(1)}, u32[]{:S(2)}, u32[]{:S(2)}) collective-permute-start(bf16[3,64,128]{2,1,0:T(8,128)(2,1)S(1)} %get-tuple-element.42.refs_2_), channel_id=1, source_target_pairs={{0,1},{1,0},{2,3},{3,2},{4,5},{5,4},{6,7},{7,6},{8,9},{9,8},{10,11... | collective-permute-start | bytes 147464 | tf_op jit(solution)/shard_map/ppermute | solution.py:1084
  23.3 0.0 copy-done.4
  23.3 3.5 %wgrad.1.refs_0_ = f32[576,192]{1,0:T(8,128)S(1)} custom-call(bf16[64,1024]{1,0:T(8,128)(2,1)S(1)} %get-tuple-element.34.refs_0_, bf16[64,1024]{1,0:T(8,128)(2,1)S(1)} %get-tuple-element.29.refs_2_.refs_1_, bf16[6,64,1024]{2,1,0:T(8,128)(2,1)S(1)} %copy-done.4, bf16[64,1024]{1,0:T(8,128)(2,1)S(1)} %get-tuple-element.30.refs_3_, ...), custom_call_target="tpu_custom_call" | custom-call | flops 2264924160 | bytes 4194304 | tf_op jit(solution)/shard_map/wgrad/pallas_call | solution.py:662
  26.8 0.0 collective-permute-done.3.refs_4_.refs_7_
  26.8 0.0 collective-permute-done.4.refs_5_.refs_8_
  26.8 1.4 %finish.1 = bf16[32,4,896]{2,1,0:T(4,128)(2,1)} custom-call(f32[576,192]{1,0:T(8,128)S(1)} %wgrad.1.refs_0_, bf16[64,128]{1,0:T(8,128)(2,1)S(1)} %get-tuple-element.40.columns_ref.refs_1_, bf16[3,64,128]{2,1,0:T(8,128)(2,1)S(1)} %get-tuple-element.42.refs_2_, bf16[3,64,128]{2,1,0:T(8,128)(2,1)S(1)} %get-tuple-element.41.refs_3_, ...), custom_call_target="tpu_custom_call" | custom-call | flops 134217728 | bytes 2097152 | tf_op jit(solution)/shard_map/finish/pallas_call | solution.py:740
  28.2 0.0 all-to-all-done.w_ref
  28.2 3.8 %all-to-all-start.1 = ((bf16[32,4,896]{2,1,0:T(4,128)(2,1)}), bf16[32,4,896]{2,1,0:T(4,128)(2,1)S(1)}, u32[]{:S(2)}, u32[]{:S(2)}) async-start(bf16[32,4,896]{2,1,0:T(4,128)(2,1)} %finish.1), calls=%async_computation.1 | async-start | bytes 458752 | tf_op jit(solution)/shard_map/all_to_all | solution.py:927
  32.0 0.7 %spread.1.refs_9_ = bf16[3,128,768]{2,1,0:T(8,128)(2,1)S(1)} custom-call(bf16[32,4,896]{2,1,0:T(4,128)(2,1)S(1)} %all-to-all-done.w_ref), custom_call_target="tpu_custom_call" | custom-call | flops 1048576 | bytes 2097152 | tf_op jit(solution)/shard_map/spread/pallas_call | solution.py:864
  32.7 0.0 copy-start.2
  32.7 0.0 copy-start.3
  32.7 5.1 %dgrad.1 = bf16[64,8,8,128]{3,2,1,0:T(8,128)(2,1)} custom-call(bf16[64,1024]{1,0:T(8,128)(2,1)S(1)} %get-tuple-element.34.refs_0_, bf16[64,1024]{1,0:T(8,128)(2,1)S(1)} %get-tuple-element.29.refs_2_.refs_1_, bf16[6,64,1024]{2,1,0:T(8,128)(2,1)S(1)} %copy-done.4, bf16[64,1024]{1,0:T(8,128)(2,1)S(1)} %get-tuple-element.30.refs_3_, ...), custom_call_target="tpu_custom_call" | custom-call | flops 2415919104 | bytes 4194304 | tf_op jit(solution)/shard_map/dgrad/pallas_call | solution.py:888
  37.8 3.8 %all-to-all-done.1.parts_ref = bf16[32,4,896]{2,1,0:T(4,128)(2,1)S(1)} async-done(((bf16[32,4,896]{2,1,0:T(4,128)(2,1)}), bf16[32,4,896]{2,1,0:T(4,128)(2,1)S(1)}, u32[]{:S(2)}, u32[]{:S(2)}) %all-to-all-start.1) | async-done | bytes 229408 | tf_op jit(solution)/shard_map/all_to_all | solution.py:927
  41.6 0.0 copy-done.2
  41.6 1.2 %adam.1 = (f32[27,128]{1,0:T(8,128)}, f32[27,128]{1,0:T(8,128)}, f32[27,128]{1,0:T(8,128)}, f32[27,128]{1,0:T(8,128)}) custom-call(bf16[32,4,896]{2,1,0:T(4,128)(2,1)S(1)} %all-to-all-done.1.parts_ref, f32[27,128]{1,0:T(8,128)S(1)} %bitcast.8, f32[27,128]{1,0:T(8,128)S(1)} %bitcast.9, f32[27,128]{1,0:T(8,128)S(1)} %bitcast.10), custom_call_target="tpu_custom_call" | custom-call | flops 4194304 | bytes 524288 | tf_op jit(solution)/shard_map/adam/pallas_call | solution.py:829
  (3 shorter events, 0.0 us)
Async XLA Ops:
  1.9 14.3 %collective-permute-start = (bf16[64,1024]{1,0:T(8,128)(2,1)S(1)}, bf16[64,1024]{1,0:T(8,128)(2,1)S(1)}, u32[]{:S(2)}, u32[]{:S(2)}) collective-permute-start(bf16[64,1024]{1,0:T(8,128)(2,1)S(1)} %get-tuple-element.28), channel_id=1, source_target_pairs={{8,16},{16,8},{9,17},{17,9},{10,18},{18,10},{11,19},{19,11},{12,20... | collective-permute-start | bytes 393224 | tf_op jit(solution)/shard_map/ppermute | solution.py:1084
  2.6 5.9 %copy-start.1 = (f32[3456]{0:T(1024)S(1)}, f32[3456]{0:T(1024)}, u32[]{:S(2)}) copy-start(f32[3456]{0:T(1024)} %param.9) | copy-start | bytes 41476
  4.3 11.9 %collective-permute-start.1 = (bf16[64,1024]{1,0:T(8,128)(2,1)S(1)}, bf16[64,1024]{1,0:T(8,128)(2,1)S(1)}, u32[]{:S(2)}, u32[]{:S(2)}) collective-permute-start(bf16[64,1024]{1,0:T(8,128)(2,1)S(1)} %get-tuple-element.31), channel_id=1, source_target_pairs={{0,8},{8,0},{16,24},{24,16},{1,9},{9,1},{17,25},{25,17},{2,10},{10... | collective-permute-start | bytes 393224 | tf_op jit(solution)/shard_map/ppermute | solution.py:1084
  8.5 8.3 %copy-start = (bf16[64,8,8,128]{3,2,1,0:T(8,128)(2,1)S(1)}, bf16[64,8,8,128]{3,2,1,0:T(8,128)(2,1)}, u32[]{:S(2)}) copy-start(bf16[64,8,8,128]{3,2,1,0:T(8,128)(2,1)} %a_ref) | copy-start | bytes 3145732
  11.4 16.8 %all-to-all-start = ((bf16[32,4,896]{2,1,0:T(4,128)(2,1)}), bf16[32,4,896]{2,1,0:T(4,128)(2,1)S(1)}, u32[]{:S(2)}, u32[]{:S(2)}) async-start(bf16[32,4,896]{2,1,0:T(4,128)(2,1)} %get-tuple-element.44), calls=%async_computation | async-start | bytes 458752 | tf_op jit(solution)/shard_map/all_to_all | solution.py:913
  16.5 6.8 %copy-start.4 = (bf16[6,64,1024]{2,1,0:T(8,128)(2,1)S(1)}, bf16[6,64,1024]{2,1,0:T(8,128)(2,1)}, u32[]{:S(2)}) copy-start(bf16[6,64,1024]{2,1,0:T(8,128)(2,1)} %get-tuple-element.35.refs_2_) | copy-start | bytes 2359300
  16.5 1.5 %collective-permute-start.2 = (bf16[12,64,128]{2,1,0:T(8,128)(2,1)S(1)}, bf16[12,64,128]{2,1,0:T(8,128)(2,1)S(1)}, u32[]{:S(2)}, u32[]{:S(2)}) collective-permute-start(bf16[12,64,128]{2,1,0:T(8,128)(2,1)S(1)} %get-tuple-element.38.own_ref), channel_id=1, source_target_pairs={{0,4},{4,0},{1,5},{5,1},{2,6},{6,2},{3,7},{7,3},{8,12},{12,8},{9,1... | collective-permute-start | bytes 589832 | tf_op jit(solution)/shard_map/ppermute | solution.py:1077
  18.1 8.7 %collective-permute-start.3 = (bf16[3,64,128]{2,1,0:T(8,128)(2,1)S(1)}, bf16[3,64,128]{2,1,0:T(8,128)(2,1)S(1)}, u32[]{:S(2)}, u32[]{:S(2)}) collective-permute-start(bf16[3,64,128]{2,1,0:T(8,128)(2,1)S(1)} %get-tuple-element.41.refs_3_), channel_id=1, source_target_pairs={{1,2},{2,1},{5,6},{6,5},{9,10},{10,9},{13,14},{14,13},{17,18},{18,... | collective-permute-start | bytes 147464 | tf_op jit(solution)/shard_map/ppermute | solution.py:1084
  18.8 8.0 %collective-permute-start.4 = (bf16[3,64,128]{2,1,0:T(8,128)(2,1)S(1)}, bf16[3,64,128]{2,1,0:T(8,128)(2,1)S(1)}, u32[]{:S(2)}, u32[]{:S(2)}) collective-permute-start(bf16[3,64,128]{2,1,0:T(8,128)(2,1)S(1)} %get-tuple-element.42.refs_2_), channel_id=1, source_target_pairs={{0,1},{1,0},{2,3},{3,2},{4,5},{5,4},{6,7},{7,6},{8,9},{9,8},{10,11... | collective-permute-start | bytes 147464 | tf_op jit(solution)/shard_map/ppermute | solution.py:1084
  28.2 13.4 %all-to-all-start.1 = ((bf16[32,4,896]{2,1,0:T(4,128)(2,1)}), bf16[32,4,896]{2,1,0:T(4,128)(2,1)S(1)}, u32[]{:S(2)}, u32[]{:S(2)}) async-start(bf16[32,4,896]{2,1,0:T(4,128)(2,1)} %finish.1), calls=%async_computation.1 | async-start | bytes 458752 | tf_op jit(solution)/shard_map/all_to_all | solution.py:927
  32.7 8.9 %copy-start.2 = (f32[3456]{0:T(1024)S(1)}, f32[3456]{0:T(1024)}, u32[]{:S(2)}) copy-start(f32[3456]{0:T(1024)} %param.10) | copy-start | bytes 41476
  32.7 8.9 %copy-start.3 = (f32[3456]{0:T(1024)S(1)}, f32[3456]{0:T(1024)}, u32[]{:S(2)}) copy-start(f32[3456]{0:T(1024)} %param.11) | copy-start | bytes 41476

commit v17 on v16

--- a/solution.py
+++ b/solution.py
@@ -17,7 +17,7 @@
 FACES_VMEM = 55_900_000
 INNER_VMEM = 54_800_000
 ENDS_VMEM = 54_800_000
-MIDDLES_VMEM = 54_600_000
+MIDDLES_VMEM = 54_300_000
 
 
 def params(limit=24 * 2**20):

time: 43.2 us -> 42.3 us (0.979)
  Pallas kernels: 19 us -> 18.1 us
    pallas_call x1, Pallas kernels: 2.85 us -> 1.97 us  [pair_inner(): pl.pallas_call(functools.partial(middles_kernel, order), in_specs=[HBM] *...]
  transfers between devices with their start and end apart: 7 -> 7, of which waited for: 2 -> 2; matrix products, arithmetic and copies ran while one was open for 0% -> 0% of each run, Pallas kernels for 39% -> 37%
where the time goes in v17:
time: 42.3 us; the launch traced here: 41.9 us
  starting transfers between devices  19 us (45%)
  Pallas kernels  18.1 us (43%)
  waiting for transfers between devices  3.94 us (9%)
  between operations  0.78 us (2%)
    ppermute x4, starting transfers between devices, swapped(): return lax.ppermute(value, axis, pairs)  10.1 us
    pallas_call x1, Pallas kernels, pair_dgrad(): pl.pallas_call(pair_dgrad_kernel, in_specs=[VMEM] * 10, out_specs=VMEM, o...  5.08 us
    all_to_all x1, starting transfers between devices, pair_program(): kernel = lax.all_to_all(sent, AXES, 0, 0, tiled=True)  4.84 us
    all_to_all x1, waiting for transfers between devices, pair_program(): parts = lax.all_to_all(part, AXES, 0, 0, tiled=True)  3.79 us
    all_to_all x1, starting transfers between devices, pair_program(): parts = lax.all_to_all(part, AXES, 0, 0, tiled=True)  3.78 us
    pallas_call x1, Pallas kernels, pair_wgrad(): pl.pallas_call(pair_wgrad_kernel, in_specs=[VMEM] * 8, out_specs=VMEM, ou...  3.45 us
    pallas_call x1, Pallas kernels, pair_inner(): pl.pallas_call(functools.partial(middles_kernel, order), in_specs=[HBM] *...  1.97 us
    pallas_call x1, Pallas kernels, pair_inner(): pl.pallas_call(functools.partial(ends_kernel, order), in_specs=[HBM] * 2...  1.67 us
  transfers between devices with their start and end apart: 7, of which 2 were waited for; matrix products, arithmetic and copies ran while one was open for 0% of the time, Pallas kernels for 37%

profile of v17, /device:TPU:0, one launch (start us, length us, event | category | flops | bytes accessed | tf_op | source)
XLA Modules:
  0.0 41.9 jit_solution(353538789171377626)
XLA Ops:
  0.6 1.3 %faces.1 = (bf16[64,1024]{1,0:T(8,128)(2,1)S(1)}, bf16[64,1024]{1,0:T(8,128)(2,1)S(1)}, bf16[64,1024]{1,0:T(8,128)(2,1)S(1)}) custom-call(bf16[64,8,8,128]{3,2,1,0:T(8,128)(2,1)} %refs_0_.3, bf16[64,8,8,128]{3,2,1,0:T(8,128)(2,1)} %refs_1_.3), custom_call_target="tpu_custom_call" | custom-call | bytes 1048576 | tf_op jit(solution)/shard_map/faces/pallas_call | solution.py:93
  1.9 0.7 %collective-permute-start = (bf16[64,1024]{1,0:T(8,128)(2,1)S(1)}, bf16[64,1024]{1,0:T(8,128)(2,1)S(1)}, u32[]{:S(2)}, u32[]{:S(2)}) collective-permute-start(bf16[64,1024]{1,0:T(8,128)(2,1)S(1)} %get-tuple-element.28), channel_id=1, source_target_pairs={{8,16},{16,8},{9,17},{17,9},{10,18},{18,10},{11,19},{19,11},{12,20... | collective-permute-start | bytes 393224 | tf_op jit(solution)/shard_map/ppermute | solution.py:1084
  2.6 0.0 copy-start.1
  2.6 1.7 %ends.1 = (bf16[4,64,1024]{2,1,0:T(8,128)(2,1)S(1)}, bf16[64,1024]{1,0:T(8,128)(2,1)S(1)}) custom-call(bf16[64,8,8,128]{3,2,1,0:T(8,128)(2,1)} %refs_0_.3, bf16[64,8,8,128]{3,2,1,0:T(8,128)(2,1)} %refs_1_.3, bf16[64,1024]{1,0:T(8,128)(2,1)S(1)} %get-tuple-element.29.refs_2_.refs_1_, bf16[64,1024]{1,0:T(8,128)(2,1)S(1)} %get-tuple-element.30.refs_3_), custom_call_target="tpu_custom_call" | custom-call | bytes 1048576 | tf_op jit(solution)/shard_map/ends/pallas_call | solution.py:534
  4.3 4.2 %collective-permute-start.1 = (bf16[64,1024]{1,0:T(8,128)(2,1)S(1)}, bf16[64,1024]{1,0:T(8,128)(2,1)S(1)}, u32[]{:S(2)}, u32[]{:S(2)}) collective-permute-start(bf16[64,1024]{1,0:T(8,128)(2,1)S(1)} %get-tuple-element.31), channel_id=1, source_target_pairs={{0,8},{8,0},{16,24},{24,16},{1,9},{9,1},{17,25},{25,17},{2,10},{10... | collective-permute-start | bytes 393224 | tf_op jit(solution)/shard_map/ppermute | solution.py:1084
  8.5 0.0 copy-done.1
  8.5 2.0 %middles.1 = (bf16[6,64,1024]{2,1,0:T(8,128)(2,1)S(1)}, bf16[10,64,128]{2,1,0:T(8,128)(2,1)S(1)}, bf16[32,4,896]{2,1,0:T(4,128)(2,1)}) custom-call(bf16[64,8,8,128]{3,2,1,0:T(8,128)(2,1)} %refs_0_.3, bf16[64,8,8,128]{3,2,1,0:T(8,128)(2,1)} %refs_1_.3, bf16[64,1024]{1,0:T(8,128)(2,1)S(1)} %get-tuple-element.29.refs_2_.refs_1_, ...), custom_call_target="tpu_custom_call" | custom-call | bytes 4194304 | tf_op jit(solution)/shard_map/middles/pallas_call | solution.py:544
  10.5 4.8 %all-to-all-start = ((bf16[32,4,896]{2,1,0:T(4,128)(2,1)}), bf16[32,4,896]{2,1,0:T(4,128)(2,1)S(1)}, u32[]{:S(2)}, u32[]{:S(2)}) async-start(bf16[32,4,896]{2,1,0:T(4,128)(2,1)} %get-tuple-element.44), calls=%async_computation | async-start | bytes 458752 | tf_op jit(solution)/shard_map/all_to_all | solution.py:913
  15.3 0.0 collective-permute-done.odd_ref
  15.4 0.0 collective-permute-done.1.even_ref
  15.4 0.2 side.1
  15.6 0.3 collective-permute-start.2
  15.9 0.0 copy-done
  15.9 1.0 %inputs.1 = (bf16[8,64,1024]{2,1,0:T(8,128)(2,1)S(1)}, bf16[64,128]{1,0:T(8,128)(2,1)S(1)}) custom-call(bf16[64,8,8,128]{3,2,1,0:T(8,128)(2,1)S(1)} %copy-done), custom_call_target="tpu_custom_call" | custom-call | bytes 2097152 | tf_op jit(solution)/shard_map/inputs/pallas_call | solution.py:194
  17.0 0.1 collective-permute-done.2.other_ref.refs_5_.refs_6_
  17.1 0.1 join.1
  17.2 0.7 %collective-permute-start.3 = (bf16[3,64,128]{2,1,0:T(8,128)(2,1)S(1)}, bf16[3,64,128]{2,1,0:T(8,128)(2,1)S(1)}, u32[]{:S(2)}, u32[]{:S(2)}) collective-permute-start(bf16[3,64,128]{2,1,0:T(8,128)(2,1)S(1)} %get-tuple-element.41.refs_3_), channel_id=1, source_target_pairs={{1,2},{2,1},{5,6},{6,5},{9,10},{10,9},{13,14},{14,13},{17,18},{18,... | collective-permute-start | bytes 147464 | tf_op jit(solution)/shard_map/ppermute | solution.py:1084
  17.9 4.5 %collective-permute-start.4 = (bf16[3,64,128]{2,1,0:T(8,128)(2,1)S(1)}, bf16[3,64,128]{2,1,0:T(8,128)(2,1)S(1)}, u32[]{:S(2)}, u32[]{:S(2)}) collective-permute-start(bf16[3,64,128]{2,1,0:T(8,128)(2,1)S(1)} %get-tuple-element.42.refs_2_), channel_id=1, source_target_pairs={{0,1},{1,0},{2,3},{3,2},{4,5},{5,4},{6,7},{7,6},{8,9},{9,8},{10,11... | collective-permute-start | bytes 147464 | tf_op jit(solution)/shard_map/ppermute | solution.py:1084
  22.4 3.5 %wgrad.1.refs_0_ = f32[576,192]{1,0:T(8,128)S(1)} custom-call(bf16[64,1024]{1,0:T(8,128)(2,1)S(1)} %get-tuple-element.34.refs_0_, bf16[64,1024]{1,0:T(8,128)(2,1)S(1)} %get-tuple-element.29.refs_2_.refs_1_, bf16[6,64,1024]{2,1,0:T(8,128)(2,1)S(1)} %get-tuple-element.35.refs_2_, bf16[64,1024]{1,0:T(8,128)(2,1)S(1)} %get-tuple-element.30.refs_3_, ...), custom_call_target="tpu_custom_call" | custom-call | flops 2264924160 | bytes 4194304 | tf_op jit(solution)/shard_map/wgrad/pallas_call | solution.py:662
  25.9 0.0 collective-permute-done.3.refs_4_.refs_7_
  25.9 0.0 collective-permute-done.4.refs_5_.refs_8_
  25.9 1.4 %finish.1 = bf16[32,4,896]{2,1,0:T(4,128)(2,1)} custom-call(f32[576,192]{1,0:T(8,128)S(1)} %wgrad.1.refs_0_, bf16[64,128]{1,0:T(8,128)(2,1)S(1)} %get-tuple-element.40.columns_ref.refs_1_, bf16[3,64,128]{2,1,0:T(8,128)(2,1)S(1)} %get-tuple-element.42.refs_2_, bf16[3,64,128]{2,1,0:T(8,128)(2,1)S(1)} %get-tuple-element.41.refs_3_, ...), custom_call_target="tpu_custom_call" | custom-call | flops 134217728 | bytes 2097152 | tf_op jit(solution)/shard_map/finish/pallas_call | solution.py:740
  27.3 0.0 all-to-all-done.w_ref
  27.3 3.8 %all-to-all-start.1 = ((bf16[32,4,896]{2,1,0:T(4,128)(2,1)}), bf16[32,4,896]{2,1,0:T(4,128)(2,1)S(1)}, u32[]{:S(2)}, u32[]{:S(2)}) async-start(bf16[32,4,896]{2,1,0:T(4,128)(2,1)} %finish.1), calls=%async_computation.1 | async-start | bytes 458752 | tf_op jit(solution)/shard_map/all_to_all | solution.py:927
  31.1 0.7 %spread.1.refs_9_ = bf16[3,128,768]{2,1,0:T(8,128)(2,1)S(1)} custom-call(bf16[32,4,896]{2,1,0:T(4,128)(2,1)S(1)} %all-to-all-done.w_ref), custom_call_target="tpu_custom_call" | custom-call | flops 1048576 | bytes 2097152 | tf_op jit(solution)/shard_map/spread/pallas_call | solution.py:864
  31.8 0.0 copy-start.2
  31.8 0.0 copy-start.3
  31.8 5.1 %dgrad.1 = bf16[64,8,8,128]{3,2,1,0:T(8,128)(2,1)} custom-call(bf16[64,1024]{1,0:T(8,128)(2,1)S(1)} %get-tuple-element.34.refs_0_, bf16[64,1024]{1,0:T(8,128)(2,1)S(1)} %get-tuple-element.29.refs_2_.refs_1_, bf16[6,64,1024]{2,1,0:T(8,128)(2,1)S(1)} %get-tuple-element.35.refs_2_, bf16[64,1024]{1,0:T(8,128)(2,1)S(1)} %get-tuple-element.30.refs_3_, ...), custom_call_target="tpu_custom_call" | custom-call | flops 2415919104 | bytes 4194304 | tf_op jit(solution)/shard_map/dgrad/pallas_call | solution.py:888
  36.9 3.8 %all-to-all-done.1.parts_ref = bf16[32,4,896]{2,1,0:T(4,128)(2,1)S(1)} async-done(((bf16[32,4,896]{2,1,0:T(4,128)(2,1)}), bf16[32,4,896]{2,1,0:T(4,128)(2,1)S(1)}, u32[]{:S(2)}, u32[]{:S(2)}) %all-to-all-start.1) | async-done | bytes 229408 | tf_op jit(solution)/shard_map/all_to_all | solution.py:927
  40.7 0.0 copy-done.2
  40.7 0.0 copy-done.3
  40.7 1.2 %adam.1 = (f32[27,128]{1,0:T(8,128)}, f32[27,128]{1,0:T(8,128)}, f32[27,128]{1,0:T(8,128)}, f32[27,128]{1,0:T(8,128)}) custom-call(bf16[32,4,896]{2,1,0:T(4,128)(2,1)S(1)} %all-to-all-done.1.parts_ref, f32[27,128]{1,0:T(8,128)S(1)} %bitcast.8, f32[27,128]{1,0:T(8,128)S(1)} %bitcast.9, f32[27,128]{1,0:T(8,128)S(1)} %bitcast.10), custom_call_target="tpu_custom_call" | custom-call | flops 4194304 | bytes 524288 | tf_op jit(solution)/shard_map/adam/pallas_call | solution.py:829
  (1 shorter events, 0.0 us)
Async XLA Ops:
  1.9 13.4 %collective-permute-start = (bf16[64,1024]{1,0:T(8,128)(2,1)S(1)}, bf16[64,1024]{1,0:T(8,128)(2,1)S(1)}, u32[]{:S(2)}, u32[]{:S(2)}) collective-permute-start(bf16[64,1024]{1,0:T(8,128)(2,1)S(1)} %get-tuple-element.28), channel_id=1, source_target_pairs={{8,16},{16,8},{9,17},{17,9},{10,18},{18,10},{11,19},{19,11},{12,20... | collective-permute-start | bytes 393224 | tf_op jit(solution)/shard_map/ppermute | solution.py:1084
  2.6 5.9 %copy-start.1 = (f32[3456]{0:T(1024)S(1)}, f32[3456]{0:T(1024)}, u32[]{:S(2)}) copy-start(f32[3456]{0:T(1024)} %param.9) | copy-start | bytes 41476
  4.3 11.0 %collective-permute-start.1 = (bf16[64,1024]{1,0:T(8,128)(2,1)S(1)}, bf16[64,1024]{1,0:T(8,128)(2,1)S(1)}, u32[]{:S(2)}, u32[]{:S(2)}) collective-permute-start(bf16[64,1024]{1,0:T(8,128)(2,1)S(1)} %get-tuple-element.31), channel_id=1, source_target_pairs={{0,8},{8,0},{16,24},{24,16},{1,9},{9,1},{17,25},{25,17},{2,10},{10... | collective-permute-start | bytes 393224 | tf_op jit(solution)/shard_map/ppermute | solution.py:1084
  8.5 7.4 %copy-start = (bf16[64,8,8,128]{3,2,1,0:T(8,128)(2,1)S(1)}, bf16[64,8,8,128]{3,2,1,0:T(8,128)(2,1)}, u32[]{:S(2)}) copy-start(bf16[64,8,8,128]{3,2,1,0:T(8,128)(2,1)} %a_ref) | copy-start | bytes 3145732
  10.5 16.8 %all-to-all-start = ((bf16[32,4,896]{2,1,0:T(4,128)(2,1)}), bf16[32,4,896]{2,1,0:T(4,128)(2,1)S(1)}, u32[]{:S(2)}, u32[]{:S(2)}) async-start(bf16[32,4,896]{2,1,0:T(4,128)(2,1)} %get-tuple-element.44), calls=%async_computation | async-start | bytes 458752 | tf_op jit(solution)/shard_map/all_to_all | solution.py:913
  15.6 1.5 %collective-permute-start.2 = (bf16[12,64,128]{2,1,0:T(8,128)(2,1)S(1)}, bf16[12,64,128]{2,1,0:T(8,128)(2,1)S(1)}, u32[]{:S(2)}, u32[]{:S(2)}) collective-permute-start(bf16[12,64,128]{2,1,0:T(8,128)(2,1)S(1)} %get-tuple-element.38.own_ref), channel_id=1, source_target_pairs={{0,4},{4,0},{1,5},{5,1},{2,6},{6,2},{3,7},{7,3},{8,12},{12,8},{9,1... | collective-permute-start | bytes 589832 | tf_op jit(solution)/shard_map/ppermute | solution.py:1077
  17.2 8.7 %collective-permute-start.3 = (bf16[3,64,128]{2,1,0:T(8,128)(2,1)S(1)}, bf16[3,64,128]{2,1,0:T(8,128)(2,1)S(1)}, u32[]{:S(2)}, u32[]{:S(2)}) collective-permute-start(bf16[3,64,128]{2,1,0:T(8,128)(2,1)S(1)} %get-tuple-element.41.refs_3_), channel_id=1, source_target_pairs={{1,2},{2,1},{5,6},{6,5},{9,10},{10,9},{13,14},{14,13},{17,18},{18,... | collective-permute-start | bytes 147464 | tf_op jit(solution)/shard_map/ppermute | solution.py:1084
  17.9 8.0 %collective-permute-start.4 = (bf16[3,64,128]{2,1,0:T(8,128)(2,1)S(1)}, bf16[3,64,128]{2,1,0:T(8,128)(2,1)S(1)}, u32[]{:S(2)}, u32[]{:S(2)}) collective-permute-start(bf16[3,64,128]{2,1,0:T(8,128)(2,1)S(1)} %get-tuple-element.42.refs_2_), channel_id=1, source_target_pairs={{0,1},{1,0},{2,3},{3,2},{4,5},{5,4},{6,7},{7,6},{8,9},{9,8},{10,11... | collective-permute-start | bytes 147464 | tf_op jit(solution)/shard_map/ppermute | solution.py:1084
  27.3 13.4 %all-to-all-start.1 = ((bf16[32,4,896]{2,1,0:T(4,128)(2,1)}), bf16[32,4,896]{2,1,0:T(4,128)(2,1)S(1)}, u32[]{:S(2)}, u32[]{:S(2)}) async-start(bf16[32,4,896]{2,1,0:T(4,128)(2,1)} %finish.1), calls=%async_computation.1 | async-start | bytes 458752 | tf_op jit(solution)/shard_map/all_to_all | solution.py:927
  31.8 8.9 %copy-start.2 = (f32[3456]{0:T(1024)S(1)}, f32[3456]{0:T(1024)}, u32[]{:S(2)}) copy-start(f32[3456]{0:T(1024)} %param.10) | copy-start | bytes 41476
  31.8 8.9 %copy-start.3 = (f32[3456]{0:T(1024)S(1)}, f32[3456]{0:T(1024)}, u32[]{:S(2)}) copy-start(f32[3456]{0:T(1024)} %param.11) | copy-start | bytes 41476

commit v18 on v17

--- a/solution.py
+++ b/solution.py
@@ -17,7 +17,7 @@
 FACES_VMEM = 55_900_000
 INNER_VMEM = 54_800_000
 ENDS_VMEM = 54_800_000
-MIDDLES_VMEM = 54_300_000
+MIDDLES_VMEM = 54_000_000
 
 
 def params(limit=24 * 2**20):
@@ -530,7 +530,7 @@
         inner_output(*shape),
         jax.ShapeDtypeStruct((size_x + 2, channels, size_z), BF16),
     ]
-    half = jax.ShapeDtypeStruct((made[0].shape[0] * 2 // 3, *made[0].shape[1:]), BF16)
+    half = jax.ShapeDtypeStruct((made[0].shape[0], *made[0].shape[1:]), BF16)
     before, swap = pl.pallas_call(
         functools.partial(ends_kernel, order),
         in_specs=[HBM] * 2 + [VMEM] * 2,

time: 42.3 us -> 42.1 us (level)
  Pallas kernels: 18.1 us -> 17.3 us
  starting transfers between devices: 19 us -> 19.7 us
    pallas_call x1, Pallas kernels: 1.97 us -> 0.86 us  [pair_inner(): pl.pallas_call(functools.partial(middles_kernel, order), in_specs=[HBM] *...]
    all_to_all x1, starting transfers between devices: 4.84 us -> 5.81 us  [pair_program(): kernel = lax.all_to_all(sent, AXES, 0, 0, tiled=True)]
  transfers between devices with their start and end apart: 7 -> 7, of which waited for: 2 -> 2; matrix products, arithmetic and copies ran while one was open for 0% -> 0% of each run, Pallas kernels for 37% -> 35%
where the time goes in v18:
time: 42.1 us; the launch traced here: 41.8 us
  starting transfers between devices  19.7 us (47%)
  Pallas kernels  17.3 us (41%)
  waiting for transfers between devices  3.93 us (9%)
  between operations  0.78 us (2%)
    ppermute x4, starting transfers between devices, swapped(): return lax.ppermute(value, axis, pairs)  9.8 us
    all_to_all x1, starting transfers between devices, pair_program(): kernel = lax.all_to_all(sent, AXES, 0, 0, tiled=True)  5.81 us
    pallas_call x1, Pallas kernels, pair_dgrad(): pl.pallas_call(pair_dgrad_kernel, in_specs=[VMEM] * 10, out_specs=VMEM, o...  5.09 us
    all_to_all x1, starting transfers between devices, pair_program(): parts = lax.all_to_all(part, AXES, 0, 0, tiled=True)  3.78 us
    all_to_all x1, waiting for transfers between devices, pair_program(): parts = lax.all_to_all(part, AXES, 0, 0, tiled=True)  3.78 us
    pallas_call x1, Pallas kernels, pair_wgrad(): pl.pallas_call(pair_wgrad_kernel, in_specs=[VMEM] * 8, out_specs=VMEM, ou...  3.45 us
    pallas_call x1, Pallas kernels, pair_inner(): pl.pallas_call(functools.partial(ends_kernel, order), in_specs=[HBM] * 2...  1.96 us
    pallas_call x1, Pallas kernels, finish(): pl.pallas_call(functools.partial(finish_kernel, scale, rows, sizes), in_s...  1.36 us
  transfers between devices with their start and end apart: 7, of which 2 were waited for; matrix products, arithmetic and copies ran while one was open for 0% of the time, Pallas kernels for 35%

profile of v18, /device:TPU:0, one launch (start us, length us, event | category | flops | bytes accessed | tf_op | source)
XLA Modules:
  0.0 41.8 jit_solution(5819563254124201594)
XLA Ops:
  0.6 1.3 %faces.1 = (bf16[64,1024]{1,0:T(8,128)(2,1)S(1)}, bf16[64,1024]{1,0:T(8,128)(2,1)S(1)}, bf16[64,1024]{1,0:T(8,128)(2,1)S(1)}) custom-call(bf16[64,8,8,128]{3,2,1,0:T(8,128)(2,1)} %refs_0_.3, bf16[64,8,8,128]{3,2,1,0:T(8,128)(2,1)} %refs_1_.3), custom_call_target="tpu_custom_call" | custom-call | bytes 1048576 | tf_op jit(solution)/shard_map/faces/pallas_call | solution.py:93
  1.9 0.7 %collective-permute-start = (bf16[64,1024]{1,0:T(8,128)(2,1)S(1)}, bf16[64,1024]{1,0:T(8,128)(2,1)S(1)}, u32[]{:S(2)}, u32[]{:S(2)}) collective-permute-start(bf16[64,1024]{1,0:T(8,128)(2,1)S(1)} %get-tuple-element.28), channel_id=1, source_target_pairs={{8,16},{16,8},{9,17},{17,9},{10,18},{18,10},{11,19},{19,11},{12,20... | collective-permute-start | bytes 393224 | tf_op jit(solution)/shard_map/ppermute | solution.py:1084
  2.6 0.0 copy-start.1
  2.6 2.0 %ends.1 = (bf16[6,64,1024]{2,1,0:T(8,128)(2,1)S(1)}, bf16[64,1024]{1,0:T(8,128)(2,1)S(1)}) custom-call(bf16[64,8,8,128]{3,2,1,0:T(8,128)(2,1)} %refs_0_.3, bf16[64,8,8,128]{3,2,1,0:T(8,128)(2,1)} %refs_1_.3, bf16[64,1024]{1,0:T(8,128)(2,1)S(1)} %get-tuple-element.29.refs_2_.refs_1_, bf16[64,1024]{1,0:T(8,128)(2,1)S(1)} %get-tuple-element.30.refs_3_), custom_call_target="tpu_custom_call" | custom-call | bytes 1048576 | tf_op jit(solution)/shard_map/ends/pallas_call | solution.py:534
  4.6 3.9 %collective-permute-start.1 = (bf16[64,1024]{1,0:T(8,128)(2,1)S(1)}, bf16[64,1024]{1,0:T(8,128)(2,1)S(1)}, u32[]{:S(2)}, u32[]{:S(2)}) collective-permute-start(bf16[64,1024]{1,0:T(8,128)(2,1)S(1)} %get-tuple-element.31), channel_id=1, source_target_pairs={{0,8},{8,0},{16,24},{24,16},{1,9},{9,1},{17,25},{25,17},{2,10},{10... | collective-permute-start | bytes 393224 | tf_op jit(solution)/shard_map/ppermute | solution.py:1084
  8.5 0.0 copy-done.1
  8.5 0.9 %middles.1 = (bf16[6,64,1024]{2,1,0:T(8,128)(2,1)S(1)}, bf16[10,64,128]{2,1,0:T(8,128)(2,1)S(1)}, bf16[32,4,896]{2,1,0:T(4,128)(2,1)}) custom-call(bf16[64,8,8,128]{3,2,1,0:T(8,128)(2,1)} %refs_0_.3, bf16[64,8,8,128]{3,2,1,0:T(8,128)(2,1)} %refs_1_.3, bf16[64,1024]{1,0:T(8,128)(2,1)S(1)} %get-tuple-element.29.refs_2_.refs_1_, ...), custom_call_target="tpu_custom_call" | custom-call | bytes 4194304 | tf_op jit(solution)/shard_map/middles/pallas_call | solution.py:544
  9.4 5.8 %all-to-all-start = ((bf16[32,4,896]{2,1,0:T(4,128)(2,1)}), bf16[32,4,896]{2,1,0:T(4,128)(2,1)S(1)}, u32[]{:S(2)}, u32[]{:S(2)}) async-start(bf16[32,4,896]{2,1,0:T(4,128)(2,1)} %get-tuple-element.44), calls=%async_computation | async-start | bytes 458752 | tf_op jit(solution)/shard_map/all_to_all | solution.py:913
  15.2 0.0 collective-permute-done.odd_ref
  15.2 0.0 collective-permute-done.1.even_ref
  15.2 0.2 side.1
  15.5 0.3 collective-permute-start.2
  15.8 0.0 copy-done
  15.8 1.0 %inputs.1 = (bf16[8,64,1024]{2,1,0:T(8,128)(2,1)S(1)}, bf16[64,128]{1,0:T(8,128)(2,1)S(1)}) custom-call(bf16[64,8,8,128]{3,2,1,0:T(8,128)(2,1)S(1)} %copy-done), custom_call_target="tpu_custom_call" | custom-call | bytes 2097152 | tf_op jit(solution)/shard_map/inputs/pallas_call | solution.py:194
  16.8 0.1 collective-permute-done.2.other_ref.refs_5_.refs_6_
  17.0 0.1 join.1
  17.1 0.7 %collective-permute-start.3 = (bf16[3,64,128]{2,1,0:T(8,128)(2,1)S(1)}, bf16[3,64,128]{2,1,0:T(8,128)(2,1)S(1)}, u32[]{:S(2)}, u32[]{:S(2)}) collective-permute-start(bf16[3,64,128]{2,1,0:T(8,128)(2,1)S(1)} %get-tuple-element.41.refs_3_), channel_id=1, source_target_pairs={{1,2},{2,1},{5,6},{6,5},{9,10},{10,9},{13,14},{14,13},{17,18},{18,... | collective-permute-start | bytes 147464 | tf_op jit(solution)/shard_map/ppermute | solution.py:1084
  17.7 4.5 %collective-permute-start.4 = (bf16[3,64,128]{2,1,0:T(8,128)(2,1)S(1)}, bf16[3,64,128]{2,1,0:T(8,128)(2,1)S(1)}, u32[]{:S(2)}, u32[]{:S(2)}) collective-permute-start(bf16[3,64,128]{2,1,0:T(8,128)(2,1)S(1)} %get-tuple-element.42.refs_2_), channel_id=1, source_target_pairs={{0,1},{1,0},{2,3},{3,2},{4,5},{5,4},{6,7},{7,6},{8,9},{9,8},{10,11... | collective-permute-start | bytes 147464 | tf_op jit(solution)/shard_map/ppermute | solution.py:1084
  22.3 3.5 %wgrad.1.refs_0_ = f32[576,192]{1,0:T(8,128)S(1)} custom-call(bf16[64,1024]{1,0:T(8,128)(2,1)S(1)} %get-tuple-element.34.refs_0_, bf16[64,1024]{1,0:T(8,128)(2,1)S(1)} %get-tuple-element.29.refs_2_.refs_1_, bf16[6,64,1024]{2,1,0:T(8,128)(2,1)S(1)} %get-tuple-element.35.refs_2_, bf16[64,1024]{1,0:T(8,128)(2,1)S(1)} %get-tuple-element.30.refs_3_, ...), custom_call_target="tpu_custom_call" | custom-call | flops 2264924160 | bytes 4194304 | tf_op jit(solution)/shard_map/wgrad/pallas_call | solution.py:662
  25.7 0.0 collective-permute-done.3.refs_4_.refs_7_
  25.8 0.0 collective-permute-done.4.refs_5_.refs_8_
  25.8 1.4 %finish.1 = bf16[32,4,896]{2,1,0:T(4,128)(2,1)} custom-call(f32[576,192]{1,0:T(8,128)S(1)} %wgrad.1.refs_0_, bf16[64,128]{1,0:T(8,128)(2,1)S(1)} %get-tuple-element.40.columns_ref.refs_1_, bf16[3,64,128]{2,1,0:T(8,128)(2,1)S(1)} %get-tuple-element.42.refs_2_, bf16[3,64,128]{2,1,0:T(8,128)(2,1)S(1)} %get-tuple-element.41.refs_3_, ...), custom_call_target="tpu_custom_call" | custom-call | flops 134217728 | bytes 2097152 | tf_op jit(solution)/shard_map/finish/pallas_call | solution.py:740
  27.1 0.0 all-to-all-done.w_ref
  27.1 3.8 %all-to-all-start.1 = ((bf16[32,4,896]{2,1,0:T(4,128)(2,1)}), bf16[32,4,896]{2,1,0:T(4,128)(2,1)S(1)}, u32[]{:S(2)}, u32[]{:S(2)}) async-start(bf16[32,4,896]{2,1,0:T(4,128)(2,1)} %finish.1), calls=%async_computation.1 | async-start | bytes 458752 | tf_op jit(solution)/shard_map/all_to_all | solution.py:927
  30.9 0.7 %spread.1.refs_9_ = bf16[3,128,768]{2,1,0:T(8,128)(2,1)S(1)} custom-call(bf16[32,4,896]{2,1,0:T(4,128)(2,1)S(1)} %all-to-all-done.w_ref), custom_call_target="tpu_custom_call" | custom-call | flops 1048576 | bytes 2097152 | tf_op jit(solution)/shard_map/spread/pallas_call | solution.py:864
  31.6 0.0 copy-start.2
  31.7 0.0 copy-start.3
  31.7 5.1 %dgrad.1 = bf16[64,8,8,128]{3,2,1,0:T(8,128)(2,1)} custom-call(bf16[64,1024]{1,0:T(8,128)(2,1)S(1)} %get-tuple-element.34.refs_0_, bf16[64,1024]{1,0:T(8,128)(2,1)S(1)} %get-tuple-element.29.refs_2_.refs_1_, bf16[6,64,1024]{2,1,0:T(8,128)(2,1)S(1)} %get-tuple-element.35.refs_2_, bf16[64,1024]{1,0:T(8,128)(2,1)S(1)} %get-tuple-element.30.refs_3_, ...), custom_call_target="tpu_custom_call" | custom-call | flops 2415919104 | bytes 4194304 | tf_op jit(solution)/shard_map/dgrad/pallas_call | solution.py:888
  36.8 3.8 %all-to-all-done.1.parts_ref = bf16[32,4,896]{2,1,0:T(4,128)(2,1)S(1)} async-done(((bf16[32,4,896]{2,1,0:T(4,128)(2,1)}), bf16[32,4,896]{2,1,0:T(4,128)(2,1)S(1)}, u32[]{:S(2)}, u32[]{:S(2)}) %all-to-all-start.1) | async-done | bytes 229408 | tf_op jit(solution)/shard_map/all_to_all | solution.py:927
  40.5 0.0 copy-done.2
  40.5 0.0 copy-done.3
  40.5 1.2 %adam.1 = (f32[27,128]{1,0:T(8,128)}, f32[27,128]{1,0:T(8,128)}, f32[27,128]{1,0:T(8,128)}, f32[27,128]{1,0:T(8,128)}) custom-call(bf16[32,4,896]{2,1,0:T(4,128)(2,1)S(1)} %all-to-all-done.1.parts_ref, f32[27,128]{1,0:T(8,128)S(1)} %bitcast.8, f32[27,128]{1,0:T(8,128)S(1)} %bitcast.9, f32[27,128]{1,0:T(8,128)S(1)} %bitcast.10), custom_call_target="tpu_custom_call" | custom-call | flops 4194304 | bytes 524288 | tf_op jit(solution)/shard_map/adam/pallas_call | solution.py:829
  (1 shorter events, 0.0 us)
Async XLA Ops:
  1.9 13.3 %collective-permute-start = (bf16[64,1024]{1,0:T(8,128)(2,1)S(1)}, bf16[64,1024]{1,0:T(8,128)(2,1)S(1)}, u32[]{:S(2)}, u32[]{:S(2)}) collective-permute-start(bf16[64,1024]{1,0:T(8,128)(2,1)S(1)} %get-tuple-element.28), channel_id=1, source_target_pairs={{8,16},{16,8},{9,17},{17,9},{10,18},{18,10},{11,19},{19,11},{12,20... | collective-permute-start | bytes 393224 | tf_op jit(solution)/shard_map/ppermute | solution.py:1084
  2.6 5.9 %copy-start.1 = (f32[3456]{0:T(1024)S(1)}, f32[3456]{0:T(1024)}, u32[]{:S(2)}) copy-start(f32[3456]{0:T(1024)} %param.9) | copy-start | bytes 41476
  4.6 10.6 %collective-permute-start.1 = (bf16[64,1024]{1,0:T(8,128)(2,1)S(1)}, bf16[64,1024]{1,0:T(8,128)(2,1)S(1)}, u32[]{:S(2)}, u32[]{:S(2)}) collective-permute-start(bf16[64,1024]{1,0:T(8,128)(2,1)S(1)} %get-tuple-element.31), channel_id=1, source_target_pairs={{0,8},{8,0},{16,24},{24,16},{1,9},{9,1},{17,25},{25,17},{2,10},{10... | collective-permute-start | bytes 393224 | tf_op jit(solution)/shard_map/ppermute | solution.py:1084
  8.5 7.3 %copy-start = (bf16[64,8,8,128]{3,2,1,0:T(8,128)(2,1)S(1)}, bf16[64,8,8,128]{3,2,1,0:T(8,128)(2,1)}, u32[]{:S(2)}) copy-start(bf16[64,8,8,128]{3,2,1,0:T(8,128)(2,1)} %a_ref) | copy-start | bytes 3145732
  9.4 17.7 %all-to-all-start = ((bf16[32,4,896]{2,1,0:T(4,128)(2,1)}), bf16[32,4,896]{2,1,0:T(4,128)(2,1)S(1)}, u32[]{:S(2)}, u32[]{:S(2)}) async-start(bf16[32,4,896]{2,1,0:T(4,128)(2,1)} %get-tuple-element.44), calls=%async_computation | async-start | bytes 458752 | tf_op jit(solution)/shard_map/all_to_all | solution.py:913
  15.5 1.5 %collective-permute-start.2 = (bf16[12,64,128]{2,1,0:T(8,128)(2,1)S(1)}, bf16[12,64,128]{2,1,0:T(8,128)(2,1)S(1)}, u32[]{:S(2)}, u32[]{:S(2)}) collective-permute-start(bf16[12,64,128]{2,1,0:T(8,128)(2,1)S(1)} %get-tuple-element.38.own_ref), channel_id=1, source_target_pairs={{0,4},{4,0},{1,5},{5,1},{2,6},{6,2},{3,7},{7,3},{8,12},{12,8},{9,1... | collective-permute-start | bytes 589832 | tf_op jit(solution)/shard_map/ppermute | solution.py:1077
  17.1 8.7 %collective-permute-start.3 = (bf16[3,64,128]{2,1,0:T(8,128)(2,1)S(1)}, bf16[3,64,128]{2,1,0:T(8,128)(2,1)S(1)}, u32[]{:S(2)}, u32[]{:S(2)}) collective-permute-start(bf16[3,64,128]{2,1,0:T(8,128)(2,1)S(1)} %get-tuple-element.41.refs_3_), channel_id=1, source_target_pairs={{1,2},{2,1},{5,6},{6,5},{9,10},{10,9},{13,14},{14,13},{17,18},{18,... | collective-permute-start | bytes 147464 | tf_op jit(solution)/shard_map/ppermute | solution.py:1084
  17.7 8.0 %collective-permute-start.4 = (bf16[3,64,128]{2,1,0:T(8,128)(2,1)S(1)}, bf16[3,64,128]{2,1,0:T(8,128)(2,1)S(1)}, u32[]{:S(2)}, u32[]{:S(2)}) collective-permute-start(bf16[3,64,128]{2,1,0:T(8,128)(2,1)S(1)} %get-tuple-element.42.refs_2_), channel_id=1, source_target_pairs={{0,1},{1,0},{2,3},{3,2},{4,5},{5,4},{6,7},{7,6},{8,9},{9,8},{10,11... | collective-permute-start | bytes 147464 | tf_op jit(solution)/shard_map/ppermute | solution.py:1084
  27.1 13.4 %all-to-all-start.1 = ((bf16[32,4,896]{2,1,0:T(4,128)(2,1)}), bf16[32,4,896]{2,1,0:T(4,128)(2,1)S(1)}, u32[]{:S(2)}, u32[]{:S(2)}) async-start(bf16[32,4,896]{2,1,0:T(4,128)(2,1)} %finish.1), calls=%async_computation.1 | async-start | bytes 458752 | tf_op jit(solution)/shard_map/all_to_all | solution.py:927
  31.6 8.9 %copy-start.2 = (f32[3456]{0:T(1024)S(1)}, f32[3456]{0:T(1024)}, u32[]{:S(2)}) copy-start(f32[3456]{0:T(1024)} %param.10) | copy-start | bytes 41476
  31.7 8.9 %copy-start.3 = (f32[3456]{0:T(1024)S(1)}, f32[3456]{0:T(1024)}, u32[]{:S(2)}) copy-start(f32[3456]{0:T(1024)} %param.11) | copy-start | bytes 41476

commit v19 on v18

--- a/solution.py
+++ b/solution.py
@@ -711,8 +711,9 @@
         )
     count = part_ref.shape[0]
     height, width = chunks.shape[0] // count, LANES
-    chunks[...] = jnp.zeros_like(chunks)
     pieces = rows * acc_ref.shape[1] // width
+    for k in range(9 * pieces, part_ref.shape[2] // LANES * QUAD):
+        chunks[pl.ds(k, count, stride=height), :] = jnp.zeros((count, width), F32)
     for a in range(3):
         for c in range(3):
             at = 3 * a + c
@@ -813,10 +814,10 @@
 
 def adam_kernel(parts_ref, master_ref, first_ref, second_ref, *refs):
     out_refs, scratch = refs[:4], refs[4:]
-    total = parts_ref[0].astype(F32)
-    for source in range(1, parts_ref.shape[0]):
-        total = total + parts_ref[source].astype(F32)
-    weight_grad = in_flat_order(total, *scratch)
+    sums = [parts_ref[source].astype(F32) for source in range(parts_ref.shape[0])]
+    while len(sums) > 1:
+        sums = [sum(sums[k : k + 2][1:], sums[k]) for k in range(0, len(sums), 2)]
+    weight_grad = in_flat_order(sums[0], *scratch)
     results = adam_step(master_ref[...], first_ref[...], second_ref[...], weight_grad)
     for out_ref, result in zip(out_refs, (weight_grad, *results)):
         out_ref[...] = result

time: 42.1 us -> 42.1 us (level)
  no operation moved by 1% of the time
where the time goes in v19:
time: 42.1 us; the launch traced here: 41.8 us
  starting transfers between devices  19.7 us (47%)
  Pallas kernels  17.3 us (41%)
  waiting for transfers between devices  3.94 us (9%)
  between operations  0.78 us (2%)
    ppermute x4, starting transfers between devices, swapped(): return lax.ppermute(value, axis, pairs)  9.8 us
    all_to_all x1, starting transfers between devices, pair_program(): kernel = lax.all_to_all(sent, AXES, 0, 0, tiled=True)  5.81 us
    pallas_call x1, Pallas kernels, pair_dgrad(): pl.pallas_call(pair_dgrad_kernel, in_specs=[VMEM] * 10, out_specs=VMEM, o...  5.08 us
    all_to_all x1, waiting for transfers between devices, pair_program(): parts = lax.all_to_all(part, AXES, 0, 0, tiled=True)  3.79 us
    all_to_all x1, starting transfers between devices, pair_program(): parts = lax.all_to_all(part, AXES, 0, 0, tiled=True)  3.78 us
    pallas_call x1, Pallas kernels, pair_wgrad(): pl.pallas_call(pair_wgrad_kernel, in_specs=[VMEM] * 8, out_specs=VMEM, ou...  3.45 us
    pallas_call x1, Pallas kernels, pair_inner(): pl.pallas_call(functools.partial(ends_kernel, order), in_specs=[HBM] * 2...  1.96 us
    pallas_call x1, Pallas kernels, finish(): pl.pallas_call(functools.partial(finish_kernel, scale, rows, sizes), in_s...  1.37 us
  transfers between devices with their start and end apart: 7, of which 2 were waited for; matrix products, arithmetic and copies ran while one was open for 0% of the time, Pallas kernels for 35%

profile of v19, /device:TPU:0, one launch (start us, length us, event | category | flops | bytes accessed | tf_op | source)
XLA Modules:
  0.0 41.8 jit_solution(11935699073002107143)
XLA Ops:
  0.6 1.3 %faces.1 = (bf16[64,1024]{1,0:T(8,128)(2,1)S(1)}, bf16[64,1024]{1,0:T(8,128)(2,1)S(1)}, bf16[64,1024]{1,0:T(8,128)(2,1)S(1)}) custom-call(bf16[64,8,8,128]{3,2,1,0:T(8,128)(2,1)} %refs_0_.3, bf16[64,8,8,128]{3,2,1,0:T(8,128)(2,1)} %refs_1_.3), custom_call_target="tpu_custom_call" | custom-call | bytes 1048576 | tf_op jit(solution)/shard_map/faces/pallas_call | solution.py:93
  1.9 0.7 %collective-permute-start = (bf16[64,1024]{1,0:T(8,128)(2,1)S(1)}, bf16[64,1024]{1,0:T(8,128)(2,1)S(1)}, u32[]{:S(2)}, u32[]{:S(2)}) collective-permute-start(bf16[64,1024]{1,0:T(8,128)(2,1)S(1)} %get-tuple-element.28), channel_id=1, source_target_pairs={{8,16},{16,8},{9,17},{17,9},{10,18},{18,10},{11,19},{19,11},{12,20... | collective-permute-start | bytes 393224 | tf_op jit(solution)/shard_map/ppermute | solution.py:1085
  2.6 0.0 copy-start.1
  2.6 2.0 %ends.1 = (bf16[6,64,1024]{2,1,0:T(8,128)(2,1)S(1)}, bf16[64,1024]{1,0:T(8,128)(2,1)S(1)}) custom-call(bf16[64,8,8,128]{3,2,1,0:T(8,128)(2,1)} %refs_0_.3, bf16[64,8,8,128]{3,2,1,0:T(8,128)(2,1)} %refs_1_.3, bf16[64,1024]{1,0:T(8,128)(2,1)S(1)} %get-tuple-element.29.refs_2_.refs_1_, bf16[64,1024]{1,0:T(8,128)(2,1)S(1)} %get-tuple-element.30.refs_3_), custom_call_target="tpu_custom_call" | custom-call | bytes 1048576 | tf_op jit(solution)/shard_map/ends/pallas_call | solution.py:534
  4.6 3.9 %collective-permute-start.1 = (bf16[64,1024]{1,0:T(8,128)(2,1)S(1)}, bf16[64,1024]{1,0:T(8,128)(2,1)S(1)}, u32[]{:S(2)}, u32[]{:S(2)}) collective-permute-start(bf16[64,1024]{1,0:T(8,128)(2,1)S(1)} %get-tuple-element.31), channel_id=1, source_target_pairs={{0,8},{8,0},{16,24},{24,16},{1,9},{9,1},{17,25},{25,17},{2,10},{10... | collective-permute-start | bytes 393224 | tf_op jit(solution)/shard_map/ppermute | solution.py:1085
  8.5 0.0 copy-done.1
  8.5 0.9 %middles.1 = (bf16[6,64,1024]{2,1,0:T(8,128)(2,1)S(1)}, bf16[10,64,128]{2,1,0:T(8,128)(2,1)S(1)}, bf16[32,4,896]{2,1,0:T(4,128)(2,1)}) custom-call(bf16[64,8,8,128]{3,2,1,0:T(8,128)(2,1)} %refs_0_.3, bf16[64,8,8,128]{3,2,1,0:T(8,128)(2,1)} %refs_1_.3, bf16[64,1024]{1,0:T(8,128)(2,1)S(1)} %get-tuple-element.29.refs_2_.refs_1_, ...), custom_call_target="tpu_custom_call" | custom-call | bytes 4194304 | tf_op jit(solution)/shard_map/middles/pallas_call | solution.py:544
  9.4 5.8 %all-to-all-start = ((bf16[32,4,896]{2,1,0:T(4,128)(2,1)}), bf16[32,4,896]{2,1,0:T(4,128)(2,1)S(1)}, u32[]{:S(2)}, u32[]{:S(2)}) async-start(bf16[32,4,896]{2,1,0:T(4,128)(2,1)} %get-tuple-element.44), calls=%async_computation | async-start | bytes 458752 | tf_op jit(solution)/shard_map/all_to_all | solution.py:914
  15.2 0.0 collective-permute-done.odd_ref
  15.2 0.0 collective-permute-done.1.even_ref
  15.2 0.2 side.1
  15.5 0.3 collective-permute-start.2
  15.8 0.0 copy-done
  15.8 1.0 %inputs.1 = (bf16[8,64,1024]{2,1,0:T(8,128)(2,1)S(1)}, bf16[64,128]{1,0:T(8,128)(2,1)S(1)}) custom-call(bf16[64,8,8,128]{3,2,1,0:T(8,128)(2,1)S(1)} %copy-done), custom_call_target="tpu_custom_call" | custom-call | bytes 2097152 | tf_op jit(solution)/shard_map/inputs/pallas_call | solution.py:194
  16.8 0.1 collective-permute-done.2.other_ref.refs_5_.refs_6_
  17.0 0.1 join.1
  17.1 0.7 %collective-permute-start.3 = (bf16[3,64,128]{2,1,0:T(8,128)(2,1)S(1)}, bf16[3,64,128]{2,1,0:T(8,128)(2,1)S(1)}, u32[]{:S(2)}, u32[]{:S(2)}) collective-permute-start(bf16[3,64,128]{2,1,0:T(8,128)(2,1)S(1)} %get-tuple-element.41.refs_3_), channel_id=1, source_target_pairs={{1,2},{2,1},{5,6},{6,5},{9,10},{10,9},{13,14},{14,13},{17,18},{18,... | collective-permute-start | bytes 147464 | tf_op jit(solution)/shard_map/ppermute | solution.py:1085
  17.7 4.5 %collective-permute-start.4 = (bf16[3,64,128]{2,1,0:T(8,128)(2,1)S(1)}, bf16[3,64,128]{2,1,0:T(8,128)(2,1)S(1)}, u32[]{:S(2)}, u32[]{:S(2)}) collective-permute-start(bf16[3,64,128]{2,1,0:T(8,128)(2,1)S(1)} %get-tuple-element.42.refs_2_), channel_id=1, source_target_pairs={{0,1},{1,0},{2,3},{3,2},{4,5},{5,4},{6,7},{7,6},{8,9},{9,8},{10,11... | collective-permute-start | bytes 147464 | tf_op jit(solution)/shard_map/ppermute | solution.py:1085
  22.3 3.5 %wgrad.1.refs_0_ = f32[576,192]{1,0:T(8,128)S(1)} custom-call(bf16[64,1024]{1,0:T(8,128)(2,1)S(1)} %get-tuple-element.34.refs_0_, bf16[64,1024]{1,0:T(8,128)(2,1)S(1)} %get-tuple-element.29.refs_2_.refs_1_, bf16[6,64,1024]{2,1,0:T(8,128)(2,1)S(1)} %get-tuple-element.35.refs_2_, bf16[64,1024]{1,0:T(8,128)(2,1)S(1)} %get-tuple-element.30.refs_3_, ...), custom_call_target="tpu_custom_call" | custom-call | flops 2264924160 | bytes 4194304 | tf_op jit(solution)/shard_map/wgrad/pallas_call | solution.py:662
  25.7 0.0 collective-permute-done.3.refs_4_.refs_7_
  25.8 0.0 collective-permute-done.4.refs_5_.refs_8_
  25.8 1.4 %finish.1 = bf16[32,4,896]{2,1,0:T(4,128)(2,1)} custom-call(f32[576,192]{1,0:T(8,128)S(1)} %wgrad.1.refs_0_, bf16[64,128]{1,0:T(8,128)(2,1)S(1)} %get-tuple-element.40.columns_ref.refs_1_, bf16[3,64,128]{2,1,0:T(8,128)(2,1)S(1)} %get-tuple-element.42.refs_2_, bf16[3,64,128]{2,1,0:T(8,128)(2,1)S(1)} %get-tuple-element.41.refs_3_, ...), custom_call_target="tpu_custom_call" | custom-call | flops 134217728 | bytes 2097152 | tf_op jit(solution)/shard_map/finish/pallas_call | solution.py:741
  27.1 0.0 all-to-all-done.w_ref
  27.1 3.8 %all-to-all-start.1 = ((bf16[32,4,896]{2,1,0:T(4,128)(2,1)}), bf16[32,4,896]{2,1,0:T(4,128)(2,1)S(1)}, u32[]{:S(2)}, u32[]{:S(2)}) async-start(bf16[32,4,896]{2,1,0:T(4,128)(2,1)} %finish.1), calls=%async_computation.1 | async-start | bytes 458752 | tf_op jit(solution)/shard_map/all_to_all | solution.py:928
  30.9 0.7 %spread.1.refs_9_ = bf16[3,128,768]{2,1,0:T(8,128)(2,1)S(1)} custom-call(bf16[32,4,896]{2,1,0:T(4,128)(2,1)S(1)} %all-to-all-done.w_ref), custom_call_target="tpu_custom_call" | custom-call | flops 1048576 | bytes 2097152 | tf_op jit(solution)/shard_map/spread/pallas_call | solution.py:865
  31.6 0.0 copy-start.2
  31.7 0.0 copy-start.3
  31.7 5.1 %dgrad.1 = bf16[64,8,8,128]{3,2,1,0:T(8,128)(2,1)} custom-call(bf16[64,1024]{1,0:T(8,128)(2,1)S(1)} %get-tuple-element.34.refs_0_, bf16[64,1024]{1,0:T(8,128)(2,1)S(1)} %get-tuple-element.29.refs_2_.refs_1_, bf16[6,64,1024]{2,1,0:T(8,128)(2,1)S(1)} %get-tuple-element.35.refs_2_, bf16[64,1024]{1,0:T(8,128)(2,1)S(1)} %get-tuple-element.30.refs_3_, ...), custom_call_target="tpu_custom_call" | custom-call | flops 2415919104 | bytes 4194304 | tf_op jit(solution)/shard_map/dgrad/pallas_call | solution.py:889
  36.7 3.8 %all-to-all-done.1.parts_ref = bf16[32,4,896]{2,1,0:T(4,128)(2,1)S(1)} async-done(((bf16[32,4,896]{2,1,0:T(4,128)(2,1)}), bf16[32,4,896]{2,1,0:T(4,128)(2,1)S(1)}, u32[]{:S(2)}, u32[]{:S(2)}) %all-to-all-start.1) | async-done | bytes 229408 | tf_op jit(solution)/shard_map/all_to_all | solution.py:928
  40.5 0.0 copy-done.2
  40.5 0.0 copy-done.3
  40.5 1.2 %adam.1 = (f32[27,128]{1,0:T(8,128)}, f32[27,128]{1,0:T(8,128)}, f32[27,128]{1,0:T(8,128)}, f32[27,128]{1,0:T(8,128)}) custom-call(bf16[32,4,896]{2,1,0:T(4,128)(2,1)S(1)} %all-to-all-done.1.parts_ref, f32[27,128]{1,0:T(8,128)S(1)} %bitcast.8, f32[27,128]{1,0:T(8,128)S(1)} %bitcast.9, f32[27,128]{1,0:T(8,128)S(1)} %bitcast.10), custom_call_target="tpu_custom_call" | custom-call | flops 4194304 | bytes 524288 | tf_op jit(solution)/shard_map/adam/pallas_call | solution.py:830
  (1 shorter events, 0.0 us)
Async XLA Ops:
  1.9 13.3 %collective-permute-start = (bf16[64,1024]{1,0:T(8,128)(2,1)S(1)}, bf16[64,1024]{1,0:T(8,128)(2,1)S(1)}, u32[]{:S(2)}, u32[]{:S(2)}) collective-permute-start(bf16[64,1024]{1,0:T(8,128)(2,1)S(1)} %get-tuple-element.28), channel_id=1, source_target_pairs={{8,16},{16,8},{9,17},{17,9},{10,18},{18,10},{11,19},{19,11},{12,20... | collective-permute-start | bytes 393224 | tf_op jit(solution)/shard_map/ppermute | solution.py:1085
  2.6 5.9 %copy-start.1 = (f32[3456]{0:T(1024)S(1)}, f32[3456]{0:T(1024)}, u32[]{:S(2)}) copy-start(f32[3456]{0:T(1024)} %param.9) | copy-start | bytes 41476
  4.6 10.6 %collective-permute-start.1 = (bf16[64,1024]{1,0:T(8,128)(2,1)S(1)}, bf16[64,1024]{1,0:T(8,128)(2,1)S(1)}, u32[]{:S(2)}, u32[]{:S(2)}) collective-permute-start(bf16[64,1024]{1,0:T(8,128)(2,1)S(1)} %get-tuple-element.31), channel_id=1, source_target_pairs={{0,8},{8,0},{16,24},{24,16},{1,9},{9,1},{17,25},{25,17},{2,10},{10... | collective-permute-start | bytes 393224 | tf_op jit(solution)/shard_map/ppermute | solution.py:1085
  8.5 7.3 %copy-start = (bf16[64,8,8,128]{3,2,1,0:T(8,128)(2,1)S(1)}, bf16[64,8,8,128]{3,2,1,0:T(8,128)(2,1)}, u32[]{:S(2)}) copy-start(bf16[64,8,8,128]{3,2,1,0:T(8,128)(2,1)} %a_ref) | copy-start | bytes 3145732
  9.4 17.7 %all-to-all-start = ((bf16[32,4,896]{2,1,0:T(4,128)(2,1)}), bf16[32,4,896]{2,1,0:T(4,128)(2,1)S(1)}, u32[]{:S(2)}, u32[]{:S(2)}) async-start(bf16[32,4,896]{2,1,0:T(4,128)(2,1)} %get-tuple-element.44), calls=%async_computation | async-start | bytes 458752 | tf_op jit(solution)/shard_map/all_to_all | solution.py:914
  15.5 1.5 %collective-permute-start.2 = (bf16[12,64,128]{2,1,0:T(8,128)(2,1)S(1)}, bf16[12,64,128]{2,1,0:T(8,128)(2,1)S(1)}, u32[]{:S(2)}, u32[]{:S(2)}) collective-permute-start(bf16[12,64,128]{2,1,0:T(8,128)(2,1)S(1)} %get-tuple-element.38.own_ref), channel_id=1, source_target_pairs={{0,4},{4,0},{1,5},{5,1},{2,6},{6,2},{3,7},{7,3},{8,12},{12,8},{9,1... | collective-permute-start | bytes 589832 | tf_op jit(solution)/shard_map/ppermute | solution.py:1078
  17.1 8.7 %collective-permute-start.3 = (bf16[3,64,128]{2,1,0:T(8,128)(2,1)S(1)}, bf16[3,64,128]{2,1,0:T(8,128)(2,1)S(1)}, u32[]{:S(2)}, u32[]{:S(2)}) collective-permute-start(bf16[3,64,128]{2,1,0:T(8,128)(2,1)S(1)} %get-tuple-element.41.refs_3_), channel_id=1, source_target_pairs={{1,2},{2,1},{5,6},{6,5},{9,10},{10,9},{13,14},{14,13},{17,18},{18,... | collective-permute-start | bytes 147464 | tf_op jit(solution)/shard_map/ppermute | solution.py:1085
  17.7 8.0 %collective-permute-start.4 = (bf16[3,64,128]{2,1,0:T(8,128)(2,1)S(1)}, bf16[3,64,128]{2,1,0:T(8,128)(2,1)S(1)}, u32[]{:S(2)}, u32[]{:S(2)}) collective-permute-start(bf16[3,64,128]{2,1,0:T(8,128)(2,1)S(1)} %get-tuple-element.42.refs_2_), channel_id=1, source_target_pairs={{0,1},{1,0},{2,3},{3,2},{4,5},{5,4},{6,7},{7,6},{8,9},{9,8},{10,11... | collective-permute-start | bytes 147464 | tf_op jit(solution)/shard_map/ppermute | solution.py:1085
  27.1 13.4 %all-to-all-start.1 = ((bf16[32,4,896]{2,1,0:T(4,128)(2,1)}), bf16[32,4,896]{2,1,0:T(4,128)(2,1)S(1)}, u32[]{:S(2)}, u32[]{:S(2)}) async-start(bf16[32,4,896]{2,1,0:T(4,128)(2,1)} %finish.1), calls=%async_computation.1 | async-start | bytes 458752 | tf_op jit(solution)/shard_map/all_to_all | solution.py:928
  31.6 8.9 %copy-start.2 = (f32[3456]{0:T(1024)S(1)}, f32[3456]{0:T(1024)}, u32[]{:S(2)}) copy-start(f32[3456]{0:T(1024)} %param.10) | copy-start | bytes 41476
  31.7 8.9 %copy-start.3 = (f32[3456]{0:T(1024)S(1)}, f32[3456]{0:T(1024)}, u32[]{:S(2)}) copy-start(f32[3456]{0:T(1024)} %param.11) | copy-start | bytes 41476
